TPU v7x, 128 devices: a whole 4x4x4 slice. The times are simulated.
128 devices in a mesh: dp: 16 (over x, y), mp: 8 (over z, core).
Axes of the slice: x: 4, y: 4, z: 4, core: 2. Of those that a mesh axis runs over, the one named last changes fastest.
Arguments:
- tokens: bfloat16 [12288, 3072], P('dp', 'mp'), may hold values from -50 to 50
- target: bfloat16 [12288, 12288], P('dp', 'mp'), may hold values from -90 to 90
- weight: bfloat16 [3072, 12288], P('dp', 'mp'), may hold values from -0.0234375 to 0.0234375
Outputs:
- update: float32 [3072, 12288], P('dp', 'mp')
All inputs are finite; a program needn't handle non-finite values.
Results may differ from a plain program's by a relative error of at most 0.029.
Values may be sent and summed in bfloat16 or wider, within the bound.
No kernel may reach another device: no remote copies, remote signals or barrier semaphores. Data moves between devices by JAX's collectives and lax.ppermute only.
A program may use at most 128 MiB of HBM per device.

v0:
```python
import math

import jax
import jax.numpy as jnp
from jax import lax
from jax.experimental import pallas as pl
from jax.experimental.pallas import tpu as pltpu
from jax.sharding import Mesh, PartitionSpec as P

BF16, F32 = jnp.bfloat16, jnp.float32
N = 4
NT = (((1,), (1,)), ((), ()))
PARAMS = pltpu.CompilerParams(vmem_limit_bytes=52 << 20)


def shift(value, axis, step):
    return lax.ppermute(value, axis, [(i, (i + step) % N) for i in range(N)])


def slope_of(hidden, target):
    root = math.sqrt(2.0 / math.pi)
    square = hidden * hidden
    bend = jnp.tanh(hidden * (root + (root * 0.044715) * square))
    half = 0.5 + 0.5 * bend
    deriv = half + (hidden * (1.0 - bend * bend)) * (0.5 * root + (1.5 * root * 0.044715) * square)
    return ((hidden * half - target.astype(F32)) * deriv).astype(BF16)


def joined(x_ref):
    return jnp.concatenate([x_ref[k] for k in range(x_ref.shape[0])], axis=1)


def cost(rows, deep, cols, exps=0):
    return pl.CostEstimate(
        flops=2 * rows * deep * cols, bytes_accessed=2 * deep * (rows + cols) + 4 * rows * cols, transcendentals=exps
    )


def first_kernel(x_ref, w_ref, t_ref, h_ref, s_ref):
    hidden = lax.dot_general(w_ref[...], joined(x_ref), NT, preferred_element_type=F32)
    h_ref[...] = hidden
    s_ref[...] = slope_of(hidden, t_ref[...])


def first_slopes(x, w, t):
    blocks, rows, wide = x.shape
    cols = w.shape[0]
    tile = rows // N
    out = pl.BlockSpec((cols, tile), lambda i: (0, i))
    return pl.pallas_call(
        first_kernel,
        grid=(N,),
        in_specs=[
            pl.BlockSpec((blocks, tile, wide), lambda i: (0, i, 0)),
            pl.BlockSpec(w.shape, lambda i: (0, 0)),
            out,
        ],
        out_specs=[out, out],
        out_shape=[jax.ShapeDtypeStruct((cols, rows), F32), jax.ShapeDtypeStruct((cols, rows), BF16)],
        compiler_params=PARAMS,
        cost_estimate=cost(cols, blocks * wide, rows, rows * cols),
    )(x, w, t)


def moved_kernel(count, started, last, *refs):
    refs = list(refs[1:])
    xs, fs = refs[:count], refs[count : 2 * count]
    rest = refs[2 * count :]
    part = sum(
        lax.dot_general(f[...], joined(x), NT, preferred_element_type=F32) for x, f in zip(xs, fs)
    )
    if started:
        part = part + rest.pop(0)[...]
    if last:
        scale, hidden, target, out = rest
        out[...] = slope_of(hidden[...] + scale[0, 0] * part, target[...])
    else:
        rest[0][...] = part


def moved(x, pieces, which, part=None, last=None):
    blocks, rows, wide = x.shape
    cols, deep = pieces[0].shape
    per = deep // wide
    tile = rows // N
    count = len(pieces)
    at = lambda j: pl.BlockSpec((per, tile, wide), lambda i, which: (which[j], i, 0))
    out = pl.BlockSpec((cols, tile), lambda i, which: (0, i))
    specs = [at(j) for j in range(count)] + [pl.BlockSpec((cols, deep), lambda i, which: (0, 0))] * count
    args = [x] * count + list(pieces)
    alias = {}
    if part is not None:
        if last is None:
            alias = {1 + len(args): 0}
        specs.append(out)
        args.append(part)
    if last is not None:
        specs += [pl.BlockSpec(memory_space=pltpu.SMEM), out, out]
        args += list(last)

    def kernel(*refs):
        moved_kernel(count, part is not None, last is not None, *refs)

    return pl.pallas_call(
        kernel,
        grid_spec=pltpu.PrefetchScalarGridSpec(
            num_scalar_prefetch=1, grid=(N,), in_specs=specs, out_specs=out
        ),
        out_shape=jax.ShapeDtypeStruct((cols, rows), F32 if last is None else BF16),
        input_output_aliases=alias,
        compiler_params=PARAMS,
        cost_estimate=cost(cols, deep * count, rows, 0 if last is None else rows * cols),
    )(jnp.stack(which).astype(jnp.int32), *args)


def term_kernel(which_ref, x_ref, s_ref, o_ref):
    part = jnp.dot(s_ref[...], joined(x_ref), preferred_element_type=F32)

    @pl.when(pl.program_id(0) == 0)
    def _():
        o_ref[...] = part

    @pl.when(pl.program_id(0) > 0)
    def _():
        o_ref[...] += part


def term(x, s, block):
    blocks, rows, wide = x.shape
    cols = s.shape[0]
    tile = rows // 2
    per = blocks // N
    return pl.pallas_call(
        term_kernel,
        grid_spec=pltpu.PrefetchScalarGridSpec(
            num_scalar_prefetch=1,
            grid=(rows // tile,),
            in_specs=[
                pl.BlockSpec((per, tile, wide), lambda i, which: (which[0], i, 0)),
                pl.BlockSpec((cols, tile), lambda i, which: (0, i)),
            ],
            out_specs=pl.BlockSpec((cols, per * wide), lambda i, which: (0, 0)),
        ),
        out_shape=jax.ShapeDtypeStruct((cols, per * wide), F32),
        compiler_params=PARAMS,
        cost_estimate=cost(cols, rows, per * wide),
    )(jnp.reshape(block, (1,)).astype(jnp.int32), x, s)


def ring_sum(part, me):
    block = lambda step: part(lax.rem(me + step, N))
    far = block(2).astype(BF16)
    half = far.shape[0] // 2
    far_next, far_prev = shift(far[:half], "x", 1), shift(far[half:], "x", -1)
    to_next, to_prev = block(1), block(3)
    next_low = shift(to_next[half:].astype(BF16), "x", 1)
    prev_high = shift(to_prev[:half].astype(BF16), "x", -1)
    next_high = shift((to_next[:half] + far_next.astype(F32)).astype(BF16), "x", 1)
    prev_low = shift((to_prev[half:] + far_prev.astype(F32)).astype(BF16), "x", -1)
    own = block(0)
    high = own[:half] + next_high.astype(F32) + prev_high.astype(F32)
    low = own[half:] + next_low.astype(F32) + prev_low.astype(F32)
    return jnp.concatenate([high, low], axis=0)


def ring_gather(value, axis):
    return [value, shift(value, axis, -1), shift(value, axis, 2), shift(value, axis, 1)]


def ring_swap(chunk, axis):
    return [chunk(0), shift(chunk(3), axis, -1), shift(chunk(2), axis, 2), shift(chunk(1), axis, 1)]


def in_order(pieces, me):
    twice = jnp.stack(pieces + pieces)
    return lax.dynamic_slice_in_dim(twice, lax.rem(N - me, N), N, axis=0)


def total_of(value):
    total = jnp.full((8, 128), jnp.sum(value * value), F32)
    total = total + lax.ppermute(total, "c", [(0, 1), (1, 0)])
    each = lax.all_to_all(
        jnp.broadcast_to(total[:1], (N * N * N, 128)), ("x", "y", "z"), split_axis=0, concat_axis=0, tiled=True
    )
    return jnp.sum(each[:, 0])


def per_device(tokens, target, weight):
    ix, iy = lax.axis_index("x"), lax.axis_index("y")
    rows, wide = tokens.shape
    cols = weight.shape[1] // N
    width = wide * 2 * N
    hidden_all = weight.shape[1] * 2 * N

    x = lax.all_gather(tokens, ("z", "c", "y"), axis=0, tiled=True).reshape(2 * N, N * rows, wide)

    def columns(array):
        return lambda k: lax.dynamic_slice_in_dim(array, lax.rem(iy + k, N) * cols, cols, axis=1)

    w_rows = in_order(ring_swap(columns(weight), "y"), iy).reshape(-1, cols)
    w = in_order(ring_gather(w_rows.T, "x"), ix)
    w = jnp.concatenate([w[k] for k in range(N)], axis=1)
    t = in_order(ring_swap(columns(target), "y"), iy)
    t = jnp.concatenate([t[k].T for k in range(N)], axis=1)

    hidden, slope = first_slopes(x, w, t)
    first = ring_sum(lambda b: term(x, slope, b), ix)
    own, after, far, before = ring_gather(first.astype(BF16), "x")
    scale = 0.5 * math.sqrt(hidden_all) / jnp.sqrt(total_of(first) + 1e-06)
    at = lambda k: lax.rem(ix + k, N)
    part = moved(x, [own, after, before], [at(0), at(1), at(3)])
    slope = moved(x, [far], [at(2)], part, (scale.reshape(1, 1), hidden, t))
    second = ring_sum(lambda b: term(x, slope, b), ix)
    total = total_of(second)
    factor = jnp.minimum(1.0, math.sqrt(width * hidden_all) / jnp.sqrt(total + 1e-06))
    held = second.astype(BF16).T.reshape(N, -1, cols)
    parts = in_order(ring_swap(lambda k: lax.dynamic_index_in_dim(held, lax.rem(iy + k, N), 0, keepdims=False), "y"), iy)
    whole = jnp.concatenate([parts[k] for k in range(N)], axis=1)
    return whole.astype(F32) * factor


def solution(mesh):
    grid = Mesh(mesh.devices.reshape(N, N, N, 2), ("x", "y", "z", "c"))
    spec = P(("x", "y"), ("z", "c"))
    return jax.shard_map(
        per_device, mesh=grid, in_specs=(spec, spec, spec), out_specs=spec, check_vma=False
    )
```

profile of v0, /device:TPU:0, one launch (start us, length us, event | category | flops | bytes accessed | tf_op | source)
XLA Modules:
  0.0 280.9 jit_solution(15576679842234379814)
XLA Ops:
  7.3 1.8 constant_dynamic-slice_fusion.5
  9.1 1.7 collective-permute-start.2
  10.8 1.6 collective-permute-start
  12.4 2.1 collective-permute-start.1
  14.4 1.9 constant_dynamic-slice_fusion
  16.3 1.1 copy.35
  19.5 1.7 collective-permute-start.7
  22.3 1.1 copy.37
  24.3 3.2 %collective-permute-start.4 = (bf16[384,768]{1,0:T(8,128)(2,1)S(1)}, bf16[384,768]{1,0:T(8,128)(2,1)S(1)}, u32[]{:S(2)}, u32[]{:S(2)}) collective-permute-start(bf16[384,768]{1,0:T(8,128)(2,1)S(1)} %bitcast.114), channel_id=1, source_target_pairs={{0,64},{32,96},{64,0},{96,32},{1,65},{33,97},{65,1},{97,33},{2,66}... | collective-permute-start | bytes 1769480 | tf_op jit(solution)/shard_map/ppermute | solution.py:17
  27.5 1.1 collective-permute-start.3
  28.6 13.1 %collective-permute-done.6 = bf16[768,384]{0,1:T(8,128)(2,1)S(1)} collective-permute-done((bf16[768,384]{0,1:T(8,128)(2,1)}, bf16[768,384]{0,1:T(8,128)(2,1)S(1)}, u32[]{:S(2)}, u32[]{:S(2)}) %collective-permute-start.6) | collective-permute-done | bytes 589856 | tf_op jit(solution)/shard_map/ppermute | solution.py:17
  41.7 1.5 collective-permute-start.5
  45.0 12.3 %collective-permute-done.8 = bf16[768,384]{0,1:T(8,128)(2,1)S(1)} collective-permute-done((bf16[768,384]{0,1:T(8,128)(2,1)}, bf16[768,384]{0,1:T(8,128)(2,1)S(1)}, u32[]{:S(2)}, u32[]{:S(2)}) %collective-permute-start.8) | collective-permute-done | bytes 589856 | tf_op jit(solution)/shard_map/ppermute | solution.py:17
  61.6 1.8 dynamic-slice_bitcast_fusion.3
  63.9 2.6 pad_maximum_fusion
  66.5 44.0 %all-gather.2.cloned.1.call-done = bf16[24576,384]{1,0:T(8,128)(2,1)} async-done(((bf16[768,384]{1,0:T(8,128)(2,1)}), bf16[24576,384]{1,0:T(8,128)(2,1)}) %all-gather.2.cloned.1.call-update) | async-done | bytes 18874384 | tf_op jit(solution)/shard_map/all_gather | solution.py:195
  110.5 15.1 %shard_map.37 = (f32[384,3072]{1,0:T(8,128)}, bf16[384,3072]{1,0:T(8,128)(2,1)}) custom-call(bf16[8,3072,384]{2,1,0:T(8,128)(2,1)} %bitcast.101, bf16[384,3072]{1,0:T(8,128)(2,1)} %get-tuple-element.40.w_ref, bf16[384,3072]{1,0:T(8,128)(2,1)} %get-tuple-element.41.t_ref.refs_6_), custom_call_target="tpu_custom_call" | custom-call | flops 7247757312 | bytes 25952256 | tf_op jit(solution)/shard_map/pallas_call | solution.py:50
  125.7 4.3 %shard_map.40 = f32[384,768]{1,0:T(8,128)S(1)} custom-call(s32[1]{0:T(128)} %bitcast.2.which_ref.refs_0_, bf16[8,3072,384]{2,1,0:T(8,128)(2,1)} %bitcast.102, bf16[384,3072]{1,0:T(8,128)(2,1)} %get-tuple-element.7.s_ref), custom_call_target="tpu_custom_call" | custom-call | flops 1811939328 | bytes 8257536 | tf_op jit(solution)/shard_map/pallas_call | solution.py:133
  130.1 1.6 collective-permute-start.9
  131.7 4.3 %shard_map.41 = f32[384,768]{1,0:T(8,128)S(1)} custom-call(s32[1]{0:T(128)} %bitcast.30.which_ref, bf16[8,3072,384]{2,1,0:T(8,128)(2,1)} %bitcast.103, bf16[384,3072]{1,0:T(8,128)(2,1)} %get-tuple-element.7.s_ref), custom_call_target="tpu_custom_call" | custom-call | flops 1811939328 | bytes 8257536 | tf_op jit(solution)/shard_map/pallas_call | solution.py:133
  136.0 1.8 collective-permute-start.11
  137.9 1.5 collective-permute-start.13
  139.4 4.3 %shard_map.39 = f32[384,768]{1,0:T(8,128)S(1)} custom-call(s32[1]{0:T(128)} %bitcast.29.which_ref, bf16[8,3072,384]{2,1,0:T(8,128)(2,1)} %bitcast.104, bf16[384,3072]{1,0:T(8,128)(2,1)} %get-tuple-element.7.s_ref), custom_call_target="tpu_custom_call" | custom-call | flops 1811939328 | bytes 8257536 | tf_op jit(solution)/shard_map/pallas_call | solution.py:133
  144.8 6.6 %collective-permute-done.13 = bf16[192,768]{1,0:T(8,128)(2,1)S(1)} collective-permute-done((bf16[192,768]{1,0:T(8,128)(2,1)S(1)}, bf16[192,768]{1,0:T(8,128)(2,1)S(1)}, u32[]{:S(2)}, u32[]{:S(2)}) %collective-permute-start.13) | collective-permute-done | bytes 294944 | tf_op jit(solution)/shard_map/ppermute | solution.py:17
  151.4 3.0 %collective-permute-start.14 = (bf16[192,768]{1,0:T(8,128)(2,1)S(1)}, bf16[192,768]{1,0:T(8,128)(2,1)S(1)}, u32[]{:S(2)}, u32[]{:S(2)}) collective-permute-start(bf16[192,768]{1,0:T(8,128)(2,1)S(1)} %fusion.7), channel_id=1, source_target_pairs={{0,96},{32,0},{64,32},{96,64},{1,97},{33,1},{65,33},{97,65},{2,98}... | collective-permute-start | bytes 884744 | tf_op jit(solution)/shard_map/ppermute | solution.py:17
  154.4 4.3 %shard_map.38 = f32[384,768]{1,0:T(8,128)S(1)} custom-call(s32[1]{0:T(128)} %bitcast.which_ref, bf16[8,3072,384]{2,1,0:T(8,128)(2,1)} %bitcast.105, bf16[384,3072]{1,0:T(8,128)(2,1)} %get-tuple-element.7.s_ref), custom_call_target="tpu_custom_call" | custom-call | flops 1811939328 | bytes 8257536 | tf_op jit(solution)/shard_map/pallas_call | solution.py:133
  161.9 1.1 collective-permute-start.17
  163.0 2.8 collective-permute-start.16
  167.0 7.4 %all-to-all-start = ((f32[64,1,128]{2,1,0:T(1,128)}), f32[64,1,128]{2,1,0:T(1,128)S(1)}, u32[]{:S(2)}, u32[]{:S(2)}) async-start(f32[64,1,128]{2,1,0:T(1,128)} %broadcast_in_dim.17), calls=%async_computation | async-start | bytes 65536 | tf_op jit(solution)/shard_map/all_to_all | solution.py:182
  174.5 3.2 %collective-permute-start.15 = (bf16[384,768]{1,0:T(8,128)(2,1)S(1)}, bf16[384,768]{1,0:T(8,128)(2,1)S(1)}, u32[]{:S(2)}, u32[]{:S(2)}) collective-permute-start(bf16[384,768]{1,0:T(8,128)(2,1)S(1)} %fusion.1.refs_4_), channel_id=1, source_target_pairs={{0,64},{32,96},{64,0},{96,32},{1,65},{33,97},{65,1},{97,33},{2,66}... | collective-permute-start | bytes 1769480 | tf_op jit(solution)/shard_map/ppermute | solution.py:17
  177.7 14.3 %all-to-all-done = f32[64,1,128]{2,1,0:T(1,128)S(1)} async-done(((f32[64,1,128]{2,1,0:T(1,128)}), f32[64,1,128]{2,1,0:T(1,128)S(1)}, u32[]{:S(2)}, u32[]{:S(2)}) %all-to-all-start) | async-done | bytes 32800 | tf_op jit(solution)/shard_map/all_to_all | solution.py:182
  193.3 11.1 %shard_map.42.refs_3_ = f32[384,3072]{1,0:T(8,128)} custom-call(s32[3]{0:T(128)S(1)} %pad_add_fusion.refs_0_, bf16[8,3072,384]{2,1,0:T(8,128)(2,1)} %bitcast.106, bf16[8,3072,384]{2,1,0:T(8,128)(2,1)} %bitcast.107, bf16[8,3072,384]{2,1,0:T(8,128)(2,1)} %bitcast.108, bf16[384,768]{1,0:T(8,128)(2,1)S(1)} %fusion.1.refs_4_, ...), custom_call_target="tpu_custom_call" | custom-call | flops 5435817984 | bytes 20643840 | tf_op jit(solution)/shard_map/pallas_call | solution.py:104
  204.4 9.4 %shard_map.43.s_ref = bf16[384,3072]{1,0:T(8,128)(2,1)} custom-call(s32[1]{0:T(128)} %bitcast.2.which_ref.refs_0_, bf16[8,3072,384]{2,1,0:T(8,128)(2,1)} %bitcast.109, bf16[384,768]{1,0:T(8,128)(2,1)S(1)} %collective-permute-done.15.refs_2_, f32[384,3072]{1,0:T(8,128)} %shard_map.42.refs_3_, f32[1,1]{1,0:T(1,128)} %bitcast.33.refs_4_, ...), custom_call_target="tpu_custom_call" | custom-call | flops 1811939328 | bytes 10027008 | tf_op jit(solution)/shard_map/pallas_call | solution.py:104
  213.8 4.4 %shard_map.46 = f32[384,768]{1,0:T(8,128)S(1)} custom-call(s32[1]{0:T(128)} %bitcast.2.which_ref.refs_0_, bf16[8,3072,384]{2,1,0:T(8,128)(2,1)} %bitcast.110, bf16[384,3072]{1,0:T(8,128)(2,1)} %shard_map.43.s_ref), custom_call_target="tpu_custom_call" | custom-call | flops 1811939328 | bytes 8257536 | tf_op jit(solution)/shard_map/pallas_call | solution.py:133
  218.4 6.7 %collective-permute-start.23 = (bf16[192,768]{1,0:T(8,128)(2,1)S(1)}, bf16[192,768]{1,0:T(8,128)(2,1)S(1)}, u32[]{:S(2)}, u32[]{:S(2)}) collective-permute-start(bf16[192,768]{1,0:T(8,128)(2,1)S(1)} %get-tuple-element.34), channel_id=1, source_target_pairs={{0,96},{32,0},{64,32},{96,64},{1,97},{33,1},{65,33},{97,65},{2,98}... | collective-permute-start | bytes 884744 | tf_op jit(solution)/shard_map/ppermute | solution.py:17
  225.1 4.3 %shard_map.47 = f32[384,768]{1,0:T(8,128)S(1)} custom-call(s32[1]{0:T(128)} %bitcast.30.which_ref, bf16[8,3072,384]{2,1,0:T(8,128)(2,1)} %bitcast.111, bf16[384,3072]{1,0:T(8,128)(2,1)} %shard_map.43.s_ref), custom_call_target="tpu_custom_call" | custom-call | flops 1811939328 | bytes 8257536 | tf_op jit(solution)/shard_map/pallas_call | solution.py:133
  229.4 4.3 %shard_map.45 = f32[384,768]{1,0:T(8,128)S(1)} custom-call(s32[1]{0:T(128)} %bitcast.29.which_ref, bf16[8,3072,384]{2,1,0:T(8,128)(2,1)} %bitcast.112, bf16[384,3072]{1,0:T(8,128)(2,1)} %shard_map.43.s_ref), custom_call_target="tpu_custom_call" | custom-call | flops 1811939328 | bytes 8257536 | tf_op jit(solution)/shard_map/pallas_call | solution.py:133
  233.8 2.1 collective-permute-start.21
  236.5 3.3 %collective-permute-start.24 = (bf16[192,768]{1,0:T(8,128)(2,1)S(1)}, bf16[192,768]{1,0:T(8,128)(2,1)S(1)}, u32[]{:S(2)}, u32[]{:S(2)}) collective-permute-start(bf16[192,768]{1,0:T(8,128)(2,1)S(1)} %fusion.3), channel_id=1, source_target_pairs={{0,96},{32,0},{64,32},{96,64},{1,97},{33,1},{65,33},{97,65},{2,98}... | collective-permute-start | bytes 884744 | tf_op jit(solution)/shard_map/ppermute | solution.py:17
  239.7 4.3 %shard_map.44 = f32[384,768]{1,0:T(8,128)S(1)} custom-call(s32[1]{0:T(128)} %bitcast.which_ref, bf16[8,3072,384]{2,1,0:T(8,128)(2,1)} %bitcast.113, bf16[384,3072]{1,0:T(8,128)(2,1)} %shard_map.43.s_ref), custom_call_target="tpu_custom_call" | custom-call | flops 1811939328 | bytes 8257536 | tf_op jit(solution)/shard_map/pallas_call | solution.py:133
  244.1 3.3 %collective-permute-done.22 = bf16[192,768]{1,0:T(8,128)(2,1)S(1)} collective-permute-done((bf16[192,768]{1,0:T(8,128)(2,1)S(1)}, bf16[192,768]{1,0:T(8,128)(2,1)S(1)}, u32[]{:S(2)}, u32[]{:S(2)}) %collective-permute-start.22) | collective-permute-done | bytes 294944 | tf_op jit(solution)/shard_map/ppermute | solution.py:17
  247.4 3.2 %collective-permute-done.20 = bf16[192,768]{1,0:T(8,128)(2,1)S(1)} collective-permute-done((bf16[192,768]{1,0:T(8,128)(2,1)S(1)}, bf16[192,768]{1,0:T(8,128)(2,1)S(1)}, u32[]{:S(2)}, u32[]{:S(2)}) %collective-permute-start.20) | collective-permute-done | bytes 294944 | tf_op jit(solution)/shard_map/ppermute | solution.py:17
  252.8 2.1 collective-permute-start.25
  256.3 5.3 %all-to-all-start.1 = ((f32[64,1,128]{2,1,0:T(1,128)}), f32[64,1,128]{2,1,0:T(1,128)S(1)}, u32[]{:S(2)}, u32[]{:S(2)}) async-start(f32[64,1,128]{2,1,0:T(1,128)} %broadcast_in_dim.19), calls=%async_computation.1 | async-start | bytes 65536 | tf_op jit(solution)/shard_map/all_to_all | solution.py:182
  261.5 1.6 collective-permute-start.27
  263.2 2.7 collective-permute-start.26
  265.8 5.2 %all-to-all-done.1 = f32[64,1,128]{2,1,0:T(1,128)S(1)} async-done(((f32[64,1,128]{2,1,0:T(1,128)}), f32[64,1,128]{2,1,0:T(1,128)S(1)}, u32[]{:S(2)}, u32[]{:S(2)}) %all-to-all-start.1) | async-done | bytes 32800 | tf_op jit(solution)/shard_map/all_to_all | solution.py:182
  272.9 1.1 convert_multiply_fusion
  (105 shorter events, 23.0 us)
Async XLA Ops:
  6.5 104.0 %all-gather.2.cloned.1.call-start = ((), (), s32[]{:S(2)}) async-start(), calls=%async_computation.2 | async-start | bytes 19464192 | tf_op jit(solution)/shard_map/all_gather | solution.py:195
  9.1 14.6 %collective-permute-start.2 = (bf16[192,384]{1,0:T(8,128)(2,1)S(1)}, bf16[192,384]{1,0:T(8,128)(2,1)S(1)}, u32[]{:S(2)}, u32[]{:S(2)}) collective-permute-start(bf16[192,384]{1,0:T(8,128)(2,1)S(1)} %get-tuple-element.37), channel_id=1, source_target_pairs={{0,8},{8,16},{16,24},{24,0},{1,9},{9,17},{17,25},{25,1},{2,10},{10... | collective-permute-start | bytes 442376 | tf_op jit(solution)/shard_map/ppermute | solution.py:17
  10.8 12.7 %collective-permute-start = (bf16[192,384]{1,0:T(8,128)(2,1)}, bf16[192,384]{1,0:T(8,128)(2,1)S(1)}, u32[]{:S(2)}, u32[]{:S(2)}) collective-permute-start(bf16[192,384]{1,0:T(8,128)(2,1)} %get-tuple-element.38), channel_id=1, source_target_pairs={{0,24},{8,0},{16,8},{24,16},{1,25},{9,1},{17,9},{25,17},{2,26},{10... | collective-permute-start | bytes 442376 | tf_op jit(solution)/shard_map/ppermute | solution.py:17
  12.4 11.3 %collective-permute-start.1 = (bf16[192,384]{1,0:T(8,128)(2,1)}, bf16[192,384]{1,0:T(8,128)(2,1)S(1)}, u32[]{:S(2)}, u32[]{:S(2)}) collective-permute-start(bf16[192,384]{1,0:T(8,128)(2,1)} %get-tuple-element.39), channel_id=1, source_target_pairs={{0,16},{8,24},{16,0},{24,8},{1,17},{9,25},{17,1},{25,9},{2,18},{10... | collective-permute-start | bytes 442376 | tf_op jit(solution)/shard_map/ppermute | solution.py:17
  17.4 24.4 %collective-permute-start.6 = (bf16[768,384]{0,1:T(8,128)(2,1)}, bf16[768,384]{0,1:T(8,128)(2,1)S(1)}, u32[]{:S(2)}, u32[]{:S(2)}) collective-permute-start(bf16[768,384]{0,1:T(8,128)(2,1)} %copy.35), channel_id=1, source_target_pairs={{0,24},{8,0},{16,8},{24,16},{1,25},{9,1},{17,9},{25,17},{2,26},{10... | collective-permute-start | bytes 1769480 | tf_op jit(solution)/shard_map/ppermute | solution.py:17
  19.5 24.6 %collective-permute-start.7 = (bf16[768,384]{0,1:T(8,128)(2,1)}, bf16[768,384]{0,1:T(8,128)(2,1)S(1)}, u32[]{:S(2)}, u32[]{:S(2)}) collective-permute-start(bf16[768,384]{0,1:T(8,128)(2,1)} %copy.36), channel_id=1, source_target_pairs={{0,16},{8,24},{16,0},{24,8},{1,17},{9,25},{17,1},{25,9},{2,18},{10... | collective-permute-start | bytes 1769480 | tf_op jit(solution)/shard_map/ppermute | solution.py:17
  21.4 2.0 copy-start
  23.5 33.8 %collective-permute-start.8 = (bf16[768,384]{0,1:T(8,128)(2,1)}, bf16[768,384]{0,1:T(8,128)(2,1)S(1)}, u32[]{:S(2)}, u32[]{:S(2)}) collective-permute-start(bf16[768,384]{0,1:T(8,128)(2,1)} %copy.37), channel_id=1, source_target_pairs={{0,8},{8,16},{16,24},{24,0},{1,9},{9,17},{17,25},{25,1},{2,10},{10... | collective-permute-start | bytes 1769480 | tf_op jit(solution)/shard_map/ppermute | solution.py:17
  24.3 39.1 %collective-permute-start.4 = (bf16[384,768]{1,0:T(8,128)(2,1)S(1)}, bf16[384,768]{1,0:T(8,128)(2,1)S(1)}, u32[]{:S(2)}, u32[]{:S(2)}) collective-permute-start(bf16[384,768]{1,0:T(8,128)(2,1)S(1)} %bitcast.114), channel_id=1, source_target_pairs={{0,64},{32,96},{64,0},{96,32},{1,65},{33,97},{65,1},{97,33},{2,66}... | collective-permute-start | bytes 1769480 | tf_op jit(solution)/shard_map/ppermute | solution.py:17
  27.5 35.9 %collective-permute-start.3 = (bf16[384,768]{1,0:T(8,128)(2,1)S(1)}, bf16[384,768]{1,0:T(8,128)(2,1)S(1)}, u32[]{:S(2)}, u32[]{:S(2)}) collective-permute-start(bf16[384,768]{1,0:T(8,128)(2,1)S(1)} %bitcast.115), channel_id=1, source_target_pairs={{0,96},{32,0},{64,32},{96,64},{1,97},{33,1},{65,33},{97,65},{2,98}... | collective-permute-start | bytes 1769480 | tf_op jit(solution)/shard_map/ppermute | solution.py:17
  41.7 21.7 %collective-permute-start.5 = (bf16[384,768]{1,0:T(8,128)(2,1)S(1)}, bf16[384,768]{1,0:T(8,128)(2,1)S(1)}, u32[]{:S(2)}, u32[]{:S(2)}) collective-permute-start(bf16[384,768]{1,0:T(8,128)(2,1)S(1)} %bitcast.116), channel_id=1, source_target_pairs={{0,32},{32,64},{64,96},{96,0},{1,33},{33,65},{65,97},{97,1},{2,34}... | collective-permute-start | bytes 1769480 | tf_op jit(solution)/shard_map/ppermute | solution.py:17
  130.1 14.2 %collective-permute-start.9 = (bf16[192,768]{1,0:T(8,128)(2,1)S(1)}, bf16[192,768]{1,0:T(8,128)(2,1)S(1)}, u32[]{:S(2)}, u32[]{:S(2)}) collective-permute-start(bf16[192,768]{1,0:T(8,128)(2,1)S(1)} %get-tuple-element.35), channel_id=1, source_target_pairs={{0,32},{32,64},{64,96},{96,0},{1,33},{33,65},{65,97},{97,1},{2,34}... | collective-permute-start | bytes 884744 | tf_op jit(solution)/shard_map/ppermute | solution.py:17
  136.0 22.7 %collective-permute-start.11 = (bf16[192,768]{1,0:T(8,128)(2,1)S(1)}, bf16[192,768]{1,0:T(8,128)(2,1)S(1)}, u32[]{:S(2)}, u32[]{:S(2)}) collective-permute-start(bf16[192,768]{1,0:T(8,128)(2,1)S(1)} %slice.191), channel_id=1, source_target_pairs={{0,96},{32,0},{64,32},{96,64},{1,97},{33,1},{65,33},{97,65},{2,98}... | collective-permute-start | bytes 884744 | tf_op jit(solution)/shard_map/ppermute | solution.py:17
  137.9 13.5 %collective-permute-start.13 = (bf16[192,768]{1,0:T(8,128)(2,1)S(1)}, bf16[192,768]{1,0:T(8,128)(2,1)S(1)}, u32[]{:S(2)}, u32[]{:S(2)}) collective-permute-start(bf16[192,768]{1,0:T(8,128)(2,1)S(1)} %get-tuple-element.36), channel_id=1, source_target_pairs={{0,96},{32,0},{64,32},{96,64},{1,97},{33,1},{65,33},{97,65},{2,98}... | collective-permute-start | bytes 884744 | tf_op jit(solution)/shard_map/ppermute | solution.py:17
  143.8 15.0 %collective-permute-start.12 = (bf16[192,768]{1,0:T(8,128)(2,1)S(1)}, bf16[192,768]{1,0:T(8,128)(2,1)S(1)}, u32[]{:S(2)}, u32[]{:S(2)}) collective-permute-start(bf16[192,768]{1,0:T(8,128)(2,1)S(1)} %slice.190), channel_id=1, source_target_pairs={{0,32},{32,64},{64,96},{96,0},{1,33},{33,65},{65,97},{97,1},{2,34}... | collective-permute-start | bytes 884744 | tf_op jit(solution)/shard_map/ppermute | solution.py:17
  144.4 15.2 %collective-permute-start.10 = (bf16[192,768]{1,0:T(8,128)(2,1)S(1)}, bf16[192,768]{1,0:T(8,128)(2,1)S(1)}, u32[]{:S(2)}, u32[]{:S(2)}) collective-permute-start(bf16[192,768]{1,0:T(8,128)(2,1)S(1)} %fusion.9), channel_id=1, source_target_pairs={{0,32},{32,64},{64,96},{96,0},{1,33},{33,65},{65,97},{97,1},{2,34}... | collective-permute-start | bytes 884744 | tf_op jit(solution)/shard_map/ppermute | solution.py:17
  151.4 8.6 %collective-permute-start.14 = (bf16[192,768]{1,0:T(8,128)(2,1)S(1)}, bf16[192,768]{1,0:T(8,128)(2,1)S(1)}, u32[]{:S(2)}, u32[]{:S(2)}) collective-permute-start(bf16[192,768]{1,0:T(8,128)(2,1)S(1)} %fusion.7), channel_id=1, source_target_pairs={{0,96},{32,0},{64,32},{96,64},{1,97},{33,1},{65,33},{97,65},{2,98}... | collective-permute-start | bytes 884744 | tf_op jit(solution)/shard_map/ppermute | solution.py:17
  161.7 4.0 %collective-permute-start.18 = (f32[8,128]{1,0:T(8,128)S(1)}, f32[8,128]{1,0:T(8,128)S(1)}, u32[]{:S(2)}, u32[]{:S(2)}) collective-permute-start(f32[8,128]{1,0:T(8,128)S(1)} %broadcast_in_dim.16), channel_id=1, source_target_pairs={{0,1},{1,0},{2,3},{3,2},{4,5},{5,4},{6,7},{7,6},{8,9},{9,8},{10,11... | collective-permute-start | bytes 12296 | tf_op jit(solution)/shard_map/ppermute | solution.py:181
  161.9 31.4 %collective-permute-start.17 = (bf16[384,768]{1,0:T(8,128)(2,1)S(1)}, bf16[384,768]{1,0:T(8,128)(2,1)S(1)}, u32[]{:S(2)}, u32[]{:S(2)}) collective-permute-start(bf16[384,768]{1,0:T(8,128)(2,1)S(1)} %fusion.1.refs_4_), channel_id=1, source_target_pairs={{0,32},{32,64},{64,96},{96,0},{1,33},{33,65},{65,97},{97,1},{2,34}... | collective-permute-start | bytes 1769480 | tf_op jit(solution)/shard_map/ppermute | solution.py:17
  163.0 30.4 %collective-permute-start.16 = (bf16[384,768]{1,0:T(8,128)(2,1)S(1)}, bf16[384,768]{1,0:T(8,128)(2,1)S(1)}, u32[]{:S(2)}, u32[]{:S(2)}) collective-permute-start(bf16[384,768]{1,0:T(8,128)(2,1)S(1)} %fusion.1.refs_4_), channel_id=1, source_target_pairs={{0,96},{32,0},{64,32},{96,64},{1,97},{33,1},{65,33},{97,65},{2,98}... | collective-permute-start | bytes 1769480 | tf_op jit(solution)/shard_map/ppermute | solution.py:17
  167.0 25.0 %all-to-all-start = ((f32[64,1,128]{2,1,0:T(1,128)}), f32[64,1,128]{2,1,0:T(1,128)S(1)}, u32[]{:S(2)}, u32[]{:S(2)}) async-start(f32[64,1,128]{2,1,0:T(1,128)} %broadcast_in_dim.17), calls=%async_computation | async-start | bytes 65536 | tf_op jit(solution)/shard_map/all_to_all | solution.py:182
  174.5 29.9 %collective-permute-start.15 = (bf16[384,768]{1,0:T(8,128)(2,1)S(1)}, bf16[384,768]{1,0:T(8,128)(2,1)S(1)}, u32[]{:S(2)}, u32[]{:S(2)}) collective-permute-start(bf16[384,768]{1,0:T(8,128)(2,1)S(1)} %fusion.1.refs_4_), channel_id=1, source_target_pairs={{0,64},{32,96},{64,0},{96,32},{1,65},{33,97},{65,1},{97,33},{2,66}... | collective-permute-start | bytes 1769480 | tf_op jit(solution)/shard_map/ppermute | solution.py:17
  218.3 18.0 %collective-permute-start.19 = (bf16[192,768]{1,0:T(8,128)(2,1)S(1)}, bf16[192,768]{1,0:T(8,128)(2,1)S(1)}, u32[]{:S(2)}, u32[]{:S(2)}) collective-permute-start(bf16[192,768]{1,0:T(8,128)(2,1)S(1)} %get-tuple-element.33), channel_id=1, source_target_pairs={{0,32},{32,64},{64,96},{96,0},{1,33},{33,65},{65,97},{97,1},{2,34}... | collective-permute-start | bytes 884744 | tf_op jit(solution)/shard_map/ppermute | solution.py:17
  218.4 18.0 %collective-permute-start.23 = (bf16[192,768]{1,0:T(8,128)(2,1)S(1)}, bf16[192,768]{1,0:T(8,128)(2,1)S(1)}, u32[]{:S(2)}, u32[]{:S(2)}) collective-permute-start(bf16[192,768]{1,0:T(8,128)(2,1)S(1)} %get-tuple-element.34), channel_id=1, source_target_pairs={{0,96},{32,0},{64,32},{96,64},{1,97},{33,1},{65,33},{97,65},{2,98}... | collective-permute-start | bytes 884744 | tf_op jit(solution)/shard_map/ppermute | solution.py:17
  233.8 10.3 %collective-permute-start.21 = (bf16[192,768]{1,0:T(8,128)(2,1)S(1)}, bf16[192,768]{1,0:T(8,128)(2,1)S(1)}, u32[]{:S(2)}, u32[]{:S(2)}) collective-permute-start(bf16[192,768]{1,0:T(8,128)(2,1)S(1)} %slice.189), channel_id=1, source_target_pairs={{0,96},{32,0},{64,32},{96,64},{1,97},{33,1},{65,33},{97,65},{2,98}... | collective-permute-start | bytes 884744 | tf_op jit(solution)/shard_map/ppermute | solution.py:17
  235.9 11.4 %collective-permute-start.22 = (bf16[192,768]{1,0:T(8,128)(2,1)S(1)}, bf16[192,768]{1,0:T(8,128)(2,1)S(1)}, u32[]{:S(2)}, u32[]{:S(2)}) collective-permute-start(bf16[192,768]{1,0:T(8,128)(2,1)S(1)} %slice.188), channel_id=1, source_target_pairs={{0,32},{32,64},{64,96},{96,0},{1,33},{33,65},{65,97},{97,1},{2,34}... | collective-permute-start | bytes 884744 | tf_op jit(solution)/shard_map/ppermute | solution.py:17
  236.3 14.3 %collective-permute-start.20 = (bf16[192,768]{1,0:T(8,128)(2,1)S(1)}, bf16[192,768]{1,0:T(8,128)(2,1)S(1)}, u32[]{:S(2)}, u32[]{:S(2)}) collective-permute-start(bf16[192,768]{1,0:T(8,128)(2,1)S(1)} %fusion.5), channel_id=1, source_target_pairs={{0,32},{32,64},{64,96},{96,0},{1,33},{33,65},{65,97},{97,1},{2,34}... | collective-permute-start | bytes 884744 | tf_op jit(solution)/shard_map/ppermute | solution.py:17
  236.5 14.1 %collective-permute-start.24 = (bf16[192,768]{1,0:T(8,128)(2,1)S(1)}, bf16[192,768]{1,0:T(8,128)(2,1)S(1)}, u32[]{:S(2)}, u32[]{:S(2)}) collective-permute-start(bf16[192,768]{1,0:T(8,128)(2,1)S(1)} %fusion.3), channel_id=1, source_target_pairs={{0,96},{32,0},{64,32},{96,64},{1,97},{33,1},{65,33},{97,65},{2,98}... | collective-permute-start | bytes 884744 | tf_op jit(solution)/shard_map/ppermute | solution.py:17
  252.7 2.3 collective-permute-start.28
  252.8 19.5 %collective-permute-start.25 = (bf16[192,384]{1,0:T(8,128)(2,1)S(1)}, bf16[192,384]{1,0:T(8,128)(2,1)S(1)}, u32[]{:S(2)}, u32[]{:S(2)}) collective-permute-start(bf16[192,384]{1,0:T(8,128)(2,1)S(1)} %get-tuple-element.32), channel_id=1, source_target_pairs={{0,24},{8,0},{16,8},{24,16},{1,25},{9,1},{17,9},{25,17},{2,26},{10... | collective-permute-start | bytes 442376 | tf_op jit(solution)/shard_map/ppermute | solution.py:17
  256.3 14.7 %all-to-all-start.1 = ((f32[64,1,128]{2,1,0:T(1,128)}), f32[64,1,128]{2,1,0:T(1,128)S(1)}, u32[]{:S(2)}, u32[]{:S(2)}) async-start(f32[64,1,128]{2,1,0:T(1,128)} %broadcast_in_dim.19), calls=%async_computation.1 | async-start | bytes 65536 | tf_op jit(solution)/shard_map/all_to_all | solution.py:182
  261.5 11.1 %collective-permute-start.27 = (bf16[192,384]{1,0:T(8,128)(2,1)S(1)}, bf16[192,384]{1,0:T(8,128)(2,1)S(1)}, u32[]{:S(2)}, u32[]{:S(2)}) collective-permute-start(bf16[192,384]{1,0:T(8,128)(2,1)S(1)} %get-tuple-element.29), channel_id=1, source_target_pairs={{0,8},{8,16},{16,24},{24,0},{1,9},{9,17},{17,25},{25,1},{2,10},{10... | collective-permute-start | bytes 442376 | tf_op jit(solution)/shard_map/ppermute | solution.py:17
  263.2 9.5 %collective-permute-start.26 = (bf16[192,384]{1,0:T(8,128)(2,1)S(1)}, bf16[192,384]{1,0:T(8,128)(2,1)S(1)}, u32[]{:S(2)}, u32[]{:S(2)}) collective-permute-start(bf16[192,384]{1,0:T(8,128)(2,1)S(1)} %get-tuple-element.31), channel_id=1, source_target_pairs={{0,16},{8,24},{16,0},{24,8},{1,17},{9,25},{17,1},{25,9},{2,18},{10... | collective-permute-start | bytes 442376 | tf_op jit(solution)/shard_map/ppermute | solution.py:17
Sparse Core Ops, SparseCore 0:
  9.6 100.8 all-gather.1
where the time goes:
time: 281 us
  waiting for transfers between devices  104 us (37%)
  Pallas kernels  70.3 us (25%)
  starting transfers between devices  61.7 us (22%)
  local copies, waits for them, and re-layouts  20.3 us (7%)
  between operations  15.4 us (5%)
  other arithmetic  8.94 us (3%)
    ppermute x27, starting transfers between devices, shift(): return lax.ppermute(value, axis, [(i, (i + step) % N) for i in range(N)])  49 us
    all_gather x1, waiting for transfers between devices, per_device(): lax.all_gather(tokens, ('z', 'c', 'y'), axis=0, tiled=True)  44 us
    ppermute x27, waiting for transfers between devices, shift(): return lax.ppermute(value, axis, [(i, (i + step) % N) for i in range(N)])  40 us
    pallas_call x8, Pallas kernels, term(): pl.pallas_call(term_kernel, grid_spec=pltpu.PrefetchScalarGridSpec(num_sc...  34.7 us
    pallas_call x2, Pallas kernels, moved(): pl.pallas_call(kernel, grid_spec=pltpu.PrefetchScalarGridSpec(num_scalar_...  20.5 us
    all_to_all x2, waiting for transfers between devices, total_of(): lax.all_to_all(jnp.broadcast_to(total[:1], (N * N * N, 128)), ('x', 'y',...  19.5 us
    pallas_call x1, Pallas kernels, first_slopes(): pl.pallas_call(first_kernel, grid=(N,), in_specs=[pl.BlockSpec((blocks, t...  15.1 us
    all_to_all x2, starting transfers between devices, total_of(): lax.all_to_all(jnp.broadcast_to(total[:1], (N * N * N, 128)), ('x', 'y',...  12.6 us
  transfers between devices with their start and end apart: 32, of which 11 were waited for; matrix products, arithmetic and copies ran while one was open for 9% of the time, Pallas kernels for 13%

commit v1 on v0

--- a/solution.py
+++ b/solution.py
@@ -15,6 +15,10 @@
 
 def shift(value, axis, step):
     return lax.ppermute(value, axis, [(i, (i + step) % N) for i in range(N)])
+
+
+def behind(value, *others):
+    return lax.optimization_barrier((value, *others))[0]
 
 
 def slope_of(hidden, target):
@@ -171,18 +175,30 @@
     return [chunk(0), shift(chunk(3), axis, -1), shift(chunk(2), axis, 2), shift(chunk(1), axis, 1)]
 
 
+def ring_swap_halves(chunk, axis):
+    far = chunk(2)
+    half = far.shape[0] // 2
+    rows = 2 * half
+    prev = shift(jnp.concatenate([chunk(1), far[:half]], axis=0), axis, 1)
+    after = shift(jnp.concatenate([chunk(3), far[half:]], axis=0), axis, -1)
+    high, low = shift(prev[rows:], axis, 1), shift(after[rows:], axis, -1)
+    return [chunk(0), after[:rows], jnp.concatenate([high, low], axis=0), prev[:rows]]
+
+
 def in_order(pieces, me):
     twice = jnp.stack(pieces + pieces)
     return lax.dynamic_slice_in_dim(twice, lax.rem(N - me, N), N, axis=0)
 
 
-def total_of(value):
+def total_of(value, beside):
     total = jnp.full((8, 128), jnp.sum(value * value), F32)
     total = total + lax.ppermute(total, "c", [(0, 1), (1, 0)])
     each = lax.all_to_all(
         jnp.broadcast_to(total[:1], (N * N * N, 128)), ("x", "y", "z"), split_axis=0, concat_axis=0, tiled=True
     )
-    return jnp.sum(each[:, 0])
+    if beside is not None:
+        each, beside = lax.optimization_barrier((each, beside))
+    return jnp.sum(each[:, 0]), beside
 
 
 def per_device(tokens, target, weight):
@@ -197,21 +213,23 @@
     def columns(array):
         return lambda k: lax.dynamic_slice_in_dim(array, lax.rem(iy + k, N) * cols, cols, axis=1)
 
-    w_rows = in_order(ring_swap(columns(weight), "y"), iy).reshape(-1, cols)
+    w_pieces = ring_swap(columns(weight), "y")
+    w_rows = in_order(w_pieces, iy).reshape(-1, cols)
     w = in_order(ring_gather(w_rows.T, "x"), ix)
     w = jnp.concatenate([w[k] for k in range(N)], axis=1)
-    t = in_order(ring_swap(columns(target), "y"), iy)
+    t = in_order(ring_swap_halves(columns(behind(target, *w_pieces)), "y"), iy)
     t = jnp.concatenate([t[k].T for k in range(N)], axis=1)
 
     hidden, slope = first_slopes(x, w, t)
     first = ring_sum(lambda b: term(x, slope, b), ix)
     own, after, far, before = ring_gather(first.astype(BF16), "x")
-    scale = 0.5 * math.sqrt(hidden_all) / jnp.sqrt(total_of(first) + 1e-06)
     at = lambda k: lax.rem(ix + k, N)
     part = moved(x, [own, after, before], [at(0), at(1), at(3)])
+    total, part = total_of(first, part)
+    scale = 0.5 * math.sqrt(hidden_all) / jnp.sqrt(total + 1e-06)
     slope = moved(x, [far], [at(2)], part, (scale.reshape(1, 1), hidden, t))
     second = ring_sum(lambda b: term(x, slope, b), ix)
-    total = total_of(second)
+    total, _ = total_of(second, None)
     factor = jnp.minimum(1.0, math.sqrt(width * hidden_all) / jnp.sqrt(total + 1e-06))
     held = second.astype(BF16).T.reshape(N, -1, cols)
     parts = in_order(ring_swap(lambda k: lax.dynamic_index_in_dim(held, lax.rem(iy + k, N), 0, keepdims=False), "y"), iy)

time: 281 us -> 266 us (0.947)
  waiting for transfers between devices: 104 us -> 83.8 us
  local copies, waits for them, and re-layouts: 20.3 us -> 27.6 us
    all_gather x1, waiting for transfers between devices: 44 us -> 18 us  [per_device(): lax.all_gather(tokens, ('z', 'c', 'y'), axis=0, tiled=True)]
    ppermute x27 -> x28, waiting for transfers between devices: 40 us -> 59.4 us  [shift(): return lax.ppermute(value, axis, [(i, (i + step) % N) for i in range(N)])]
    all_to_all x2, waiting for transfers between devices: 19.5 us -> 5.76 us  [total_of(): lax.all_to_all(jnp.broadcast_to(total[:1], (N * N * N, 128)), ('x', 'y',...]
    ppermute x27 -> x28, starting transfers between devices: 49 us -> 42.2 us  [shift(): return lax.ppermute(value, axis, [(i, (i + step) % N) for i in range(N)])]
    all_to_all x2, starting transfers between devices: 12.6 us -> 16.8 us  [total_of(): lax.all_to_all(jnp.broadcast_to(total[:1], (N * N * N, 128)), ('x', 'y',...]
    unnamed x32 -> x29, local copies, waits for them, and re-layouts: 9.96 us -> 13 us
    optimization_barrier x0 -> x1, local copies, waits for them, and re-layouts: none -> 2.85 us  [behind(): return lax.optimization_barrier((value, *others))[0]]
  transfers between devices with their start and end apart: 32 -> 33, of which waited for: 11 -> 14; matrix products, arithmetic and copies ran while one was open for 9% -> 12% of each run, Pallas kernels for 13% -> 14%
where the time goes in v1:
time: 266 us; the launch traced here: 265 us
  waiting for transfers between devices  83.8 us (32%)
  Pallas kernels  70.1 us (26%)
  starting transfers between devices  59.1 us (22%)
  local copies, waits for them, and re-layouts  27.6 us (10%)
  between operations  15.4 us (6%)
  other arithmetic  9.19 us (3%)
    ppermute x28, waiting for transfers between devices, shift(): return lax.ppermute(value, axis, [(i, (i + step) % N) for i in range(N)])  59.4 us
    ppermute x28, starting transfers between devices, shift(): return lax.ppermute(value, axis, [(i, (i + step) % N) for i in range(N)])  42.2 us
    pallas_call x8, Pallas kernels, term(): pl.pallas_call(term_kernel, grid_spec=pltpu.PrefetchScalarGridSpec(num_sc...  34.6 us
    pallas_call x2, Pallas kernels, moved(): pl.pallas_call(kernel, grid_spec=pltpu.PrefetchScalarGridSpec(num_scalar_...  20.4 us
    all_gather x1, waiting for transfers between devices, per_device(): lax.all_gather(tokens, ('z', 'c', 'y'), axis=0, tiled=True)  18 us
    all_to_all x2, starting transfers between devices, total_of(): lax.all_to_all(jnp.broadcast_to(total[:1], (N * N * N, 128)), ('x', 'y',...  16.8 us
    pallas_call x1, Pallas kernels, first_slopes(): pl.pallas_call(first_kernel, grid=(N,), in_specs=[pl.BlockSpec((blocks, t...  15.1 us
    unnamed x29, local copies, waits for them, and re-layouts  13 us
  transfers between devices with their start and end apart: 33, of which 14 were waited for; matrix products, arithmetic and copies ran while one was open for 12% of the time, Pallas kernels for 14%

profile of v1, /device:TPU:0, one launch (start us, length us, event | category | flops | bytes accessed | tf_op | source)
XLA Modules:
  0.0 265.3 jit_solution(5653676197756370648)
XLA Ops:
  8.4 3.2 %collective-permute-start = (bf16[192,384]{1,0:T(8,128)(2,1)S(1)}, bf16[192,384]{1,0:T(8,128)(2,1)S(1)}, u32[]{:S(2)}, u32[]{:S(2)}) collective-permute-start(bf16[192,384]{1,0:T(8,128)(2,1)S(1)} %get-tuple-element.46), channel_id=1, source_target_pairs={{0,24},{8,0},{16,8},{24,16},{1,25},{9,1},{17,9},{25,17},{2,26},{10... | collective-permute-start | bytes 442376 | tf_op jit(solution)/shard_map/ppermute | solution.py:17
  14.1 3.7 %collective-permute-done = bf16[192,384]{1,0:T(8,128)(2,1)S(1)} collective-permute-done((bf16[192,384]{1,0:T(8,128)(2,1)S(1)}, bf16[192,384]{1,0:T(8,128)(2,1)S(1)}, u32[]{:S(2)}, u32[]{:S(2)}) %collective-permute-start) | collective-permute-done | bytes 147488 | tf_op jit(solution)/shard_map/ppermute | solution.py:17
  17.9 2.0 collective-permute-done.1
  19.9 1.6 collective-permute-done.2
  22.0 2.8 %collective-permute-start.3 = (bf16[384,768]{1,0:T(8,128)(2,1)S(1)}, bf16[384,768]{1,0:T(8,128)(2,1)}, u32[]{:S(2)}, u32[]{:S(2)}) collective-permute-start(bf16[384,768]{1,0:T(8,128)(2,1)S(1)} %bitcast.123), channel_id=1, source_target_pairs={{0,96},{32,0},{64,32},{96,64},{1,97},{33,1},{65,33},{97,65},{2,98}... | collective-permute-start | bytes 1769480 | tf_op jit(solution)/shard_map/ppermute | solution.py:17
  26.6 2.9 %copy.27 = bf16[768,1536]{0,1:T(8,128)(2,1)S(1)} copy(bf16[768,1536]{1,0:T(8,128)(2,1)} %param.4) | data formatting | bytes 4718592 | tf_op jit(solution)/shard_map/optimization_barrier | solution.py:21
  34.4 1.3 collective-permute-start.7
  35.8 14.6 %collective-permute-done.3 = bf16[384,768]{1,0:T(8,128)(2,1)} collective-permute-done((bf16[384,768]{1,0:T(8,128)(2,1)S(1)}, bf16[384,768]{1,0:T(8,128)(2,1)}, u32[]{:S(2)}, u32[]{:S(2)}) %collective-permute-start.3) | collective-permute-done | bytes 589856 | tf_op jit(solution)/shard_map/ppermute | solution.py:17
  50.3 1.9 bitcast_dynamic-update-slice_fusion.8
  52.2 1.9 bitcast_dynamic-update-slice_fusion.6
  54.1 1.9 bitcast_dynamic-update-slice_fusion.4
  56.9 1.9 bitcast_dynamic-update-slice_fusion.9
  58.8 1.9 bitcast_dynamic-update-slice_fusion.7
  60.8 1.9 bitcast_dynamic-update-slice_fusion.5
  62.8 2.6 collective-permute-start.9
  65.7 1.8 dynamic-slice_bitcast_fusion.7
  67.5 11.2 %collective-permute-done.9 = bf16[384,384]{0,1:T(8,128)(2,1)S(1)} collective-permute-done((bf16[384,384]{0,1:T(8,128)(2,1)S(1)}, bf16[384,384]{0,1:T(8,128)(2,1)S(1)}, u32[]{:S(2)}, u32[]{:S(2)}) %collective-permute-start.9) | collective-permute-done | bytes 294944 | tf_op jit(solution)/shard_map/ppermute | solution.py:17
  78.7 3.0 %collective-permute-done.8 = bf16[384,384]{0,1:T(8,128)(2,1)S(1)} collective-permute-done((bf16[384,384]{0,1:T(8,128)(2,1)S(1)}, bf16[384,384]{0,1:T(8,128)(2,1)S(1)}, u32[]{:S(2)}, u32[]{:S(2)}) %collective-permute-start.8) | collective-permute-done | bytes 294944 | tf_op jit(solution)/shard_map/ppermute | solution.py:17
  82.1 2.6 pad_maximum_fusion
  84.7 18.0 %all-gather.2.cloned.1.call-done = bf16[24576,384]{1,0:T(8,128)(2,1)} async-done(((bf16[768,384]{1,0:T(8,128)(2,1)}), bf16[24576,384]{1,0:T(8,128)(2,1)}) %all-gather.2.cloned.1.call-update) | async-done | bytes 18874384 | tf_op jit(solution)/shard_map/all_gather | solution.py:211
  102.7 15.1 %shard_map.37 = (f32[384,3072]{1,0:T(8,128)}, bf16[384,3072]{1,0:T(8,128)(2,1)}) custom-call(bf16[8,3072,384]{2,1,0:T(8,128)(2,1)} %bitcast.110, bf16[384,3072]{1,0:T(8,128)(2,1)} %get-tuple-element.48.w_ref, bf16[384,3072]{1,0:T(8,128)(2,1)} %get-tuple-element.49.t_ref.refs_6_), custom_call_target="tpu_custom_call" | custom-call | flops 7247757312 | bytes 25952256 | tf_op jit(solution)/shard_map/pallas_call | solution.py:54
  117.8 4.3 %shard_map.40 = f32[384,768]{1,0:T(8,128)S(1)} custom-call(s32[1]{0:T(128)} %bitcast.2.which_ref.refs_0_, bf16[8,3072,384]{2,1,0:T(8,128)(2,1)} %bitcast.111, bf16[384,3072]{1,0:T(8,128)(2,1)} %get-tuple-element.11.s_ref), custom_call_target="tpu_custom_call" | custom-call | flops 1811939328 | bytes 8257536 | tf_op jit(solution)/shard_map/pallas_call | solution.py:137
  122.3 1.7 collective-permute-start.10
  124.0 4.3 %shard_map.41 = f32[384,768]{1,0:T(8,128)S(1)} custom-call(s32[1]{0:T(128)} %bitcast.30.which_ref, bf16[8,3072,384]{2,1,0:T(8,128)(2,1)} %bitcast.112, bf16[384,3072]{1,0:T(8,128)(2,1)} %get-tuple-element.11.s_ref), custom_call_target="tpu_custom_call" | custom-call | flops 1811939328 | bytes 8257536 | tf_op jit(solution)/shard_map/pallas_call | solution.py:137
  128.4 1.7 collective-permute-start.12
  130.0 1.4 collective-permute-start.14
  131.4 4.3 %shard_map.39 = f32[384,768]{1,0:T(8,128)S(1)} custom-call(s32[1]{0:T(128)} %bitcast.29.which_ref, bf16[8,3072,384]{2,1,0:T(8,128)(2,1)} %bitcast.113, bf16[384,3072]{1,0:T(8,128)(2,1)} %get-tuple-element.11.s_ref), custom_call_target="tpu_custom_call" | custom-call | flops 1811939328 | bytes 8257536 | tf_op jit(solution)/shard_map/pallas_call | solution.py:137
  137.1 6.6 %collective-permute-done.14 = bf16[192,768]{1,0:T(8,128)(2,1)S(1)} collective-permute-done((bf16[192,768]{1,0:T(8,128)(2,1)S(1)}, bf16[192,768]{1,0:T(8,128)(2,1)S(1)}, u32[]{:S(2)}, u32[]{:S(2)}) %collective-permute-start.14) | collective-permute-done | bytes 294944 | tf_op jit(solution)/shard_map/ppermute | solution.py:17
  143.7 2.9 %collective-permute-start.15 = (bf16[192,768]{1,0:T(8,128)(2,1)S(1)}, bf16[192,768]{1,0:T(8,128)(2,1)S(1)}, u32[]{:S(2)}, u32[]{:S(2)}) collective-permute-start(bf16[192,768]{1,0:T(8,128)(2,1)S(1)} %fusion.7), channel_id=1, source_target_pairs={{0,96},{32,0},{64,32},{96,64},{1,97},{33,1},{65,33},{97,65},{2,98}... | collective-permute-start | bytes 884744 | tf_op jit(solution)/shard_map/ppermute | solution.py:17
  146.6 4.3 %shard_map.38 = f32[384,768]{1,0:T(8,128)S(1)} custom-call(s32[1]{0:T(128)} %bitcast.which_ref, bf16[8,3072,384]{2,1,0:T(8,128)(2,1)} %bitcast.114, bf16[384,3072]{1,0:T(8,128)(2,1)} %get-tuple-element.11.s_ref), custom_call_target="tpu_custom_call" | custom-call | flops 1811939328 | bytes 8257536 | tf_op jit(solution)/shard_map/pallas_call | solution.py:137
  152.3 3.8 %collective-permute-start.18 = (bf16[384,768]{1,0:T(8,128)(2,1)S(1)}, bf16[384,768]{1,0:T(8,128)(2,1)S(1)}, u32[]{:S(2)}, u32[]{:S(2)}) collective-permute-start(bf16[384,768]{1,0:T(8,128)(2,1)S(1)} %fusion.1.refs_4_), channel_id=1, source_target_pairs={{0,96},{32,0},{64,32},{96,64},{1,97},{33,1},{65,33},{97,65},{2,98}... | collective-permute-start | bytes 1769480 | tf_op jit(solution)/shard_map/ppermute | solution.py:17
  157.8 1.6 collective-permute-start.16
  160.7 8.4 %all-to-all-start = ((f32[64,1,128]{2,1,0:T(1,128)}), f32[64,1,128]{2,1,0:T(1,128)S(1)}, u32[]{:S(2)}, u32[]{:S(2)}) async-start(f32[64,1,128]{2,1,0:T(1,128)} %broadcast_in_dim.17), calls=%async_computation | async-start | bytes 65536 | tf_op jit(solution)/shard_map/all_to_all | solution.py:196
  169.1 10.9 %collective-permute-done.18.refs_5_ = bf16[384,768]{1,0:T(8,128)(2,1)S(1)} collective-permute-done((bf16[384,768]{1,0:T(8,128)(2,1)S(1)}, bf16[384,768]{1,0:T(8,128)(2,1)S(1)}, u32[]{:S(2)}, u32[]{:S(2)}) %collective-permute-start.18) | collective-permute-done | bytes 589856 | tf_op jit(solution)/shard_map/ppermute | solution.py:17
  179.9 3.4 %collective-permute-done.19.refs_6_ = bf16[384,768]{1,0:T(8,128)(2,1)S(1)} collective-permute-done((bf16[384,768]{1,0:T(8,128)(2,1)S(1)}, bf16[384,768]{1,0:T(8,128)(2,1)S(1)}, u32[]{:S(2)}, u32[]{:S(2)}) %collective-permute-start.19) | collective-permute-done | bytes 589856 | tf_op jit(solution)/shard_map/ppermute | solution.py:17
  183.3 11.0 %shard_map.42.refs_3_ = f32[384,3072]{1,0:T(8,128)} custom-call(s32[3]{0:T(128)S(1)} %pad_add_fusion.refs_0_, bf16[8,3072,384]{2,1,0:T(8,128)(2,1)} %bitcast.115, bf16[8,3072,384]{2,1,0:T(8,128)(2,1)} %bitcast.116, bf16[8,3072,384]{2,1,0:T(8,128)(2,1)} %bitcast.117, bf16[384,768]{1,0:T(8,128)(2,1)S(1)} %fusion.1.refs_4_, ...), custom_call_target="tpu_custom_call" | custom-call | flops 5435817984 | bytes 20643840 | tf_op jit(solution)/shard_map/pallas_call | solution.py:108
  195.6 9.4 %shard_map.43.s_ref = bf16[384,3072]{1,0:T(8,128)(2,1)} custom-call(s32[1]{0:T(128)} %bitcast.2.which_ref.refs_0_, bf16[8,3072,384]{2,1,0:T(8,128)(2,1)} %bitcast.118, bf16[384,768]{1,0:T(8,128)(2,1)S(1)} %collective-permute-done.16.refs_2_, f32[384,3072]{1,0:T(8,128)} %shard_map.42.refs_3_, f32[1,1]{1,0:T(1,128)} %bitcast.33.refs_4_, ...), custom_call_target="tpu_custom_call" | custom-call | flops 1811939328 | bytes 10027008 | tf_op jit(solution)/shard_map/pallas_call | solution.py:108
  205.0 4.3 %shard_map.46 = f32[384,768]{1,0:T(8,128)S(1)} custom-call(s32[1]{0:T(128)} %bitcast.2.which_ref.refs_0_, bf16[8,3072,384]{2,1,0:T(8,128)(2,1)} %bitcast.119, bf16[384,3072]{1,0:T(8,128)(2,1)} %shard_map.43.s_ref), custom_call_target="tpu_custom_call" | custom-call | flops 1811939328 | bytes 8257536 | tf_op jit(solution)/shard_map/pallas_call | solution.py:137
  209.6 3.2 %collective-permute-start.24 = (bf16[192,768]{1,0:T(8,128)(2,1)S(1)}, bf16[192,768]{1,0:T(8,128)(2,1)S(1)}, u32[]{:S(2)}, u32[]{:S(2)}) collective-permute-start(bf16[192,768]{1,0:T(8,128)(2,1)S(1)} %get-tuple-element.42), channel_id=1, source_target_pairs={{0,96},{32,0},{64,32},{96,64},{1,97},{33,1},{65,33},{97,65},{2,98}... | collective-permute-start | bytes 884744 | tf_op jit(solution)/shard_map/ppermute | solution.py:17
  212.8 4.3 %shard_map.47 = f32[384,768]{1,0:T(8,128)S(1)} custom-call(s32[1]{0:T(128)} %bitcast.30.which_ref, bf16[8,3072,384]{2,1,0:T(8,128)(2,1)} %bitcast.120, bf16[384,3072]{1,0:T(8,128)(2,1)} %shard_map.43.s_ref), custom_call_target="tpu_custom_call" | custom-call | flops 1811939328 | bytes 8257536 | tf_op jit(solution)/shard_map/pallas_call | solution.py:137
  217.1 4.3 %shard_map.45 = f32[384,768]{1,0:T(8,128)S(1)} custom-call(s32[1]{0:T(128)} %bitcast.29.which_ref, bf16[8,3072,384]{2,1,0:T(8,128)(2,1)} %bitcast.121, bf16[384,3072]{1,0:T(8,128)(2,1)} %shard_map.43.s_ref), custom_call_target="tpu_custom_call" | custom-call | flops 1811939328 | bytes 8257536 | tf_op jit(solution)/shard_map/pallas_call | solution.py:137
  221.7 2.3 collective-permute-start.23
  224.2 3.3 %collective-permute-start.25 = (bf16[192,768]{1,0:T(8,128)(2,1)S(1)}, bf16[192,768]{1,0:T(8,128)(2,1)S(1)}, u32[]{:S(2)}, u32[]{:S(2)}) collective-permute-start(bf16[192,768]{1,0:T(8,128)(2,1)S(1)} %fusion.3), channel_id=1, source_target_pairs={{0,96},{32,0},{64,32},{96,64},{1,97},{33,1},{65,33},{97,65},{2,98}... | collective-permute-start | bytes 884744 | tf_op jit(solution)/shard_map/ppermute | solution.py:17
  227.5 4.3 %shard_map.44 = f32[384,768]{1,0:T(8,128)S(1)} custom-call(s32[1]{0:T(128)} %bitcast.which_ref, bf16[8,3072,384]{2,1,0:T(8,128)(2,1)} %bitcast.122, bf16[384,3072]{1,0:T(8,128)(2,1)} %shard_map.43.s_ref), custom_call_target="tpu_custom_call" | custom-call | flops 1811939328 | bytes 8257536 | tf_op jit(solution)/shard_map/pallas_call | solution.py:137
  231.8 1.2 collective-permute-done.21
  237.7 8.4 %all-to-all-start.1 = ((f32[64,1,128]{2,1,0:T(1,128)}), f32[64,1,128]{2,1,0:T(1,128)S(1)}, u32[]{:S(2)}, u32[]{:S(2)}) async-start(f32[64,1,128]{2,1,0:T(1,128)} %broadcast_in_dim.19), calls=%async_computation.1 | async-start | bytes 65536 | tf_op jit(solution)/shard_map/all_to_all | solution.py:196
  246.2 3.2 %collective-permute-start.27 = (bf16[192,384]{1,0:T(8,128)(2,1)S(1)}, bf16[192,384]{1,0:T(8,128)(2,1)S(1)}, u32[]{:S(2)}, u32[]{:S(2)}) collective-permute-start(bf16[192,384]{1,0:T(8,128)(2,1)S(1)} %get-tuple-element.39), channel_id=1, source_target_pairs={{0,16},{8,24},{16,0},{24,8},{1,17},{9,25},{17,1},{25,9},{2,18},{10... | collective-permute-start | bytes 442376 | tf_op jit(solution)/shard_map/ppermute | solution.py:17
  249.9 5.8 %all-to-all-done.1 = f32[64,1,128]{2,1,0:T(1,128)S(1)} async-done(((f32[64,1,128]{2,1,0:T(1,128)}), f32[64,1,128]{2,1,0:T(1,128)S(1)}, u32[]{:S(2)}, u32[]{:S(2)}) %all-to-all-start.1) | async-done | bytes 32800 | tf_op jit(solution)/shard_map/all_to_all | solution.py:196
  (113 shorter events, 27.5 us)
Async XLA Ops:
  6.5 96.2 %all-gather.2.cloned.1.call-start = ((), (), s32[]{:S(2)}) async-start(), calls=%async_computation.2 | async-start | bytes 19464192 | tf_op jit(solution)/shard_map/all_gather | solution.py:211
  8.4 9.4 %collective-permute-start = (bf16[192,384]{1,0:T(8,128)(2,1)S(1)}, bf16[192,384]{1,0:T(8,128)(2,1)S(1)}, u32[]{:S(2)}, u32[]{:S(2)}) collective-permute-start(bf16[192,384]{1,0:T(8,128)(2,1)S(1)} %get-tuple-element.46), channel_id=1, source_target_pairs={{0,24},{8,0},{16,8},{24,16},{1,25},{9,1},{17,9},{25,17},{2,26},{10... | collective-permute-start | bytes 442376 | tf_op jit(solution)/shard_map/ppermute | solution.py:17
  11.6 8.3 %collective-permute-start.1 = (bf16[192,384]{1,0:T(8,128)(2,1)S(1)}, bf16[192,384]{1,0:T(8,128)(2,1)S(1)}, u32[]{:S(2)}, u32[]{:S(2)}) collective-permute-start(bf16[192,384]{1,0:T(8,128)(2,1)S(1)} %get-tuple-element.47), channel_id=1, source_target_pairs={{0,16},{8,24},{16,0},{24,8},{1,17},{9,25},{17,1},{25,9},{2,18},{10... | collective-permute-start | bytes 442376 | tf_op jit(solution)/shard_map/ppermute | solution.py:17
  12.2 9.3 %collective-permute-start.2 = (bf16[192,384]{1,0:T(8,128)(2,1)S(1)}, bf16[192,384]{1,0:T(8,128)(2,1)S(1)}, u32[]{:S(2)}, u32[]{:S(2)}) collective-permute-start(bf16[192,384]{1,0:T(8,128)(2,1)S(1)} %get-tuple-element.45), channel_id=1, source_target_pairs={{0,8},{8,16},{16,24},{24,0},{1,9},{9,17},{17,25},{25,1},{2,10},{10... | collective-permute-start | bytes 442376 | tf_op jit(solution)/shard_map/ppermute | solution.py:17
  22.0 28.3 %collective-permute-start.3 = (bf16[384,768]{1,0:T(8,128)(2,1)S(1)}, bf16[384,768]{1,0:T(8,128)(2,1)}, u32[]{:S(2)}, u32[]{:S(2)}) collective-permute-start(bf16[384,768]{1,0:T(8,128)(2,1)S(1)} %bitcast.123), channel_id=1, source_target_pairs={{0,96},{32,0},{64,32},{96,64},{1,97},{33,1},{65,33},{97,65},{2,98}... | collective-permute-start | bytes 1769480 | tf_op jit(solution)/shard_map/ppermute | solution.py:17
  24.9 27.4 %collective-permute-start.4 = (bf16[384,768]{1,0:T(8,128)(2,1)S(1)}, bf16[384,768]{1,0:T(8,128)(2,1)}, u32[]{:S(2)}, u32[]{:S(2)}) collective-permute-start(bf16[384,768]{1,0:T(8,128)(2,1)S(1)} %bitcast.124), channel_id=1, source_target_pairs={{0,64},{32,96},{64,0},{96,32},{1,65},{33,97},{65,1},{97,33},{2,66}... | collective-permute-start | bytes 1769480 | tf_op jit(solution)/shard_map/ppermute | solution.py:17
  25.7 28.5 %collective-permute-start.5 = (bf16[384,768]{1,0:T(8,128)(2,1)S(1)}, bf16[384,768]{1,0:T(8,128)(2,1)}, u32[]{:S(2)}, u32[]{:S(2)}) collective-permute-start(bf16[384,768]{1,0:T(8,128)(2,1)S(1)} %bitcast.125), channel_id=1, source_target_pairs={{0,32},{32,64},{64,96},{96,0},{1,33},{33,65},{65,97},{97,1},{2,34}... | collective-permute-start | bytes 1769480 | tf_op jit(solution)/shard_map/ppermute | solution.py:17
  33.2 1.1 copy-start
  33.2 1.2 copy-start.1
  33.5 29.2 %collective-permute-start.6 = (bf16[1152,384]{0,1:T(8,128)(2,1)S(1)}, bf16[1152,384]{0,1:T(8,128)(2,1)S(1)}, u32[]{:S(2)}, u32[]{:S(2)}) collective-permute-start(bf16[1152,384]{0,1:T(8,128)(2,1)S(1)} %pad_maximum_fusion.4), channel_id=1, source_target_pairs={{0,24},{8,0},{16,8},{24,16},{1,25},{9,1},{17,9},{25,17},{2,26},{10... | collective-permute-start | bytes 2654216 | tf_op jit(solution)/shard_map/ppermute | solution.py:17
  34.4 30.9 %collective-permute-start.7 = (bf16[1152,384]{0,1:T(8,128)(2,1)S(1)}, bf16[1152,384]{0,1:T(8,128)(2,1)S(1)}, u32[]{:S(2)}, u32[]{:S(2)}) collective-permute-start(bf16[1152,384]{0,1:T(8,128)(2,1)S(1)} %pad_maximum_fusion.5), channel_id=1, source_target_pairs={{0,8},{8,16},{16,24},{24,0},{1,9},{9,17},{17,25},{25,1},{2,10},{10... | collective-permute-start | bytes 2654216 | tf_op jit(solution)/shard_map/ppermute | solution.py:17
  62.8 15.9 %collective-permute-start.9 = (bf16[384,384]{0,1:T(8,128)(2,1)S(1)}, bf16[384,384]{0,1:T(8,128)(2,1)S(1)}, u32[]{:S(2)}, u32[]{:S(2)}) collective-permute-start(bf16[384,384]{0,1:T(8,128)(2,1)S(1)} %slice.164), channel_id=1, source_target_pairs={{0,24},{8,0},{16,8},{24,16},{1,25},{9,1},{17,9},{25,17},{2,26},{10... | collective-permute-start | bytes 884744 | tf_op jit(solution)/shard_map/ppermute | solution.py:17
  65.4 16.3 %collective-permute-start.8 = (bf16[384,384]{0,1:T(8,128)(2,1)S(1)}, bf16[384,384]{0,1:T(8,128)(2,1)S(1)}, u32[]{:S(2)}, u32[]{:S(2)}) collective-permute-start(bf16[384,384]{0,1:T(8,128)(2,1)S(1)} %slice.163), channel_id=1, source_target_pairs={{0,8},{8,16},{16,24},{24,0},{1,9},{9,17},{17,25},{25,1},{2,10},{10... | collective-permute-start | bytes 884744 | tf_op jit(solution)/shard_map/ppermute | solution.py:17
  122.3 14.2 %collective-permute-start.10 = (bf16[192,768]{1,0:T(8,128)(2,1)S(1)}, bf16[192,768]{1,0:T(8,128)(2,1)S(1)}, u32[]{:S(2)}, u32[]{:S(2)}) collective-permute-start(bf16[192,768]{1,0:T(8,128)(2,1)S(1)} %get-tuple-element.43), channel_id=1, source_target_pairs={{0,32},{32,64},{64,96},{96,0},{1,33},{33,65},{65,97},{97,1},{2,34}... | collective-permute-start | bytes 884744 | tf_op jit(solution)/shard_map/ppermute | solution.py:17
  128.4 22.5 %collective-permute-start.12 = (bf16[192,768]{1,0:T(8,128)(2,1)S(1)}, bf16[192,768]{1,0:T(8,128)(2,1)S(1)}, u32[]{:S(2)}, u32[]{:S(2)}) collective-permute-start(bf16[192,768]{1,0:T(8,128)(2,1)S(1)} %slice.228), channel_id=1, source_target_pairs={{0,96},{32,0},{64,32},{96,64},{1,97},{33,1},{65,33},{97,65},{2,98}... | collective-permute-start | bytes 884744 | tf_op jit(solution)/shard_map/ppermute | solution.py:17
  130.0 13.6 %collective-permute-start.14 = (bf16[192,768]{1,0:T(8,128)(2,1)S(1)}, bf16[192,768]{1,0:T(8,128)(2,1)S(1)}, u32[]{:S(2)}, u32[]{:S(2)}) collective-permute-start(bf16[192,768]{1,0:T(8,128)(2,1)S(1)} %get-tuple-element.44), channel_id=1, source_target_pairs={{0,96},{32,0},{64,32},{96,64},{1,97},{33,1},{65,33},{97,65},{2,98}... | collective-permute-start | bytes 884744 | tf_op jit(solution)/shard_map/ppermute | solution.py:17
  135.8 15.1 %collective-permute-start.13 = (bf16[192,768]{1,0:T(8,128)(2,1)S(1)}, bf16[192,768]{1,0:T(8,128)(2,1)S(1)}, u32[]{:S(2)}, u32[]{:S(2)}) collective-permute-start(bf16[192,768]{1,0:T(8,128)(2,1)S(1)} %slice.227), channel_id=1, source_target_pairs={{0,32},{32,64},{64,96},{96,0},{1,33},{33,65},{65,97},{97,1},{2,34}... | collective-permute-start | bytes 884744 | tf_op jit(solution)/shard_map/ppermute | solution.py:17
  136.6 15.1 %collective-permute-start.11 = (bf16[192,768]{1,0:T(8,128)(2,1)S(1)}, bf16[192,768]{1,0:T(8,128)(2,1)S(1)}, u32[]{:S(2)}, u32[]{:S(2)}) collective-permute-start(bf16[192,768]{1,0:T(8,128)(2,1)S(1)} %fusion.9), channel_id=1, source_target_pairs={{0,32},{32,64},{64,96},{96,0},{1,33},{33,65},{65,97},{97,1},{2,34}... | collective-permute-start | bytes 884744 | tf_op jit(solution)/shard_map/ppermute | solution.py:17
  143.7 8.4 %collective-permute-start.15 = (bf16[192,768]{1,0:T(8,128)(2,1)S(1)}, bf16[192,768]{1,0:T(8,128)(2,1)S(1)}, u32[]{:S(2)}, u32[]{:S(2)}) collective-permute-start(bf16[192,768]{1,0:T(8,128)(2,1)S(1)} %fusion.7), channel_id=1, source_target_pairs={{0,96},{32,0},{64,32},{96,64},{1,97},{33,1},{65,33},{97,65},{2,98}... | collective-permute-start | bytes 884744 | tf_op jit(solution)/shard_map/ppermute | solution.py:17
  152.3 27.6 %collective-permute-start.18 = (bf16[384,768]{1,0:T(8,128)(2,1)S(1)}, bf16[384,768]{1,0:T(8,128)(2,1)S(1)}, u32[]{:S(2)}, u32[]{:S(2)}) collective-permute-start(bf16[384,768]{1,0:T(8,128)(2,1)S(1)} %fusion.1.refs_4_), channel_id=1, source_target_pairs={{0,96},{32,0},{64,32},{96,64},{1,97},{33,1},{65,33},{97,65},{2,98}... | collective-permute-start | bytes 1769480 | tf_op jit(solution)/shard_map/ppermute | solution.py:17
  156.1 27.2 %collective-permute-start.19 = (bf16[384,768]{1,0:T(8,128)(2,1)S(1)}, bf16[384,768]{1,0:T(8,128)(2,1)S(1)}, u32[]{:S(2)}, u32[]{:S(2)}) collective-permute-start(bf16[384,768]{1,0:T(8,128)(2,1)S(1)} %fusion.1.refs_4_), channel_id=1, source_target_pairs={{0,32},{32,64},{64,96},{96,0},{1,33},{33,65},{65,97},{97,1},{2,34}... | collective-permute-start | bytes 1769480 | tf_op jit(solution)/shard_map/ppermute | solution.py:17
  157.6 1.7 collective-permute-start.17
  157.8 37.8 %collective-permute-start.16 = (bf16[384,768]{1,0:T(8,128)(2,1)S(1)}, bf16[384,768]{1,0:T(8,128)(2,1)S(1)}, u32[]{:S(2)}, u32[]{:S(2)}) collective-permute-start(bf16[384,768]{1,0:T(8,128)(2,1)S(1)} %fusion.1.refs_4_), channel_id=1, source_target_pairs={{0,64},{32,96},{64,0},{96,32},{1,65},{33,97},{65,1},{97,33},{2,66}... | collective-permute-start | bytes 1769480 | tf_op jit(solution)/shard_map/ppermute | solution.py:17
  160.7 33.6 %all-to-all-start = ((f32[64,1,128]{2,1,0:T(1,128)}), f32[64,1,128]{2,1,0:T(1,128)S(1)}, u32[]{:S(2)}, u32[]{:S(2)}) async-start(f32[64,1,128]{2,1,0:T(1,128)} %broadcast_in_dim.17), calls=%async_computation | async-start | bytes 65536 | tf_op jit(solution)/shard_map/all_to_all | solution.py:196
  209.5 14.5 %collective-permute-start.20 = (bf16[192,768]{1,0:T(8,128)(2,1)S(1)}, bf16[192,768]{1,0:T(8,128)(2,1)S(1)}, u32[]{:S(2)}, u32[]{:S(2)}) collective-permute-start(bf16[192,768]{1,0:T(8,128)(2,1)S(1)} %get-tuple-element.41), channel_id=1, source_target_pairs={{0,32},{32,64},{64,96},{96,0},{1,33},{33,65},{65,97},{97,1},{2,34}... | collective-permute-start | bytes 884744 | tf_op jit(solution)/shard_map/ppermute | solution.py:17
  209.6 14.5 %collective-permute-start.24 = (bf16[192,768]{1,0:T(8,128)(2,1)S(1)}, bf16[192,768]{1,0:T(8,128)(2,1)S(1)}, u32[]{:S(2)}, u32[]{:S(2)}) collective-permute-start(bf16[192,768]{1,0:T(8,128)(2,1)S(1)} %get-tuple-element.42), channel_id=1, source_target_pairs={{0,96},{32,0},{64,32},{96,64},{1,97},{33,1},{65,33},{97,65},{2,98}... | collective-permute-start | bytes 884744 | tf_op jit(solution)/shard_map/ppermute | solution.py:17
  221.5 10.3 %collective-permute-start.22 = (bf16[192,768]{1,0:T(8,128)(2,1)S(1)}, bf16[192,768]{1,0:T(8,128)(2,1)S(1)}, u32[]{:S(2)}, u32[]{:S(2)}) collective-permute-start(bf16[192,768]{1,0:T(8,128)(2,1)S(1)} %slice.226), channel_id=1, source_target_pairs={{0,96},{32,0},{64,32},{96,64},{1,97},{33,1},{65,33},{97,65},{2,98}... | collective-permute-start | bytes 884744 | tf_op jit(solution)/shard_map/ppermute | solution.py:17
  221.7 10.2 %collective-permute-start.23 = (bf16[192,768]{1,0:T(8,128)(2,1)S(1)}, bf16[192,768]{1,0:T(8,128)(2,1)S(1)}, u32[]{:S(2)}, u32[]{:S(2)}) collective-permute-start(bf16[192,768]{1,0:T(8,128)(2,1)S(1)} %slice.225), channel_id=1, source_target_pairs={{0,32},{32,64},{64,96},{96,0},{1,33},{33,65},{65,97},{97,1},{2,34}... | collective-permute-start | bytes 884744 | tf_op jit(solution)/shard_map/ppermute | solution.py:17
  224.0 9.0 %collective-permute-start.21 = (bf16[192,768]{1,0:T(8,128)(2,1)S(1)}, bf16[192,768]{1,0:T(8,128)(2,1)S(1)}, u32[]{:S(2)}, u32[]{:S(2)}) collective-permute-start(bf16[192,768]{1,0:T(8,128)(2,1)S(1)} %fusion.5), channel_id=1, source_target_pairs={{0,32},{32,64},{64,96},{96,0},{1,33},{33,65},{65,97},{97,1},{2,34}... | collective-permute-start | bytes 884744 | tf_op jit(solution)/shard_map/ppermute | solution.py:17
  224.2 8.9 %collective-permute-start.25 = (bf16[192,768]{1,0:T(8,128)(2,1)S(1)}, bf16[192,768]{1,0:T(8,128)(2,1)S(1)}, u32[]{:S(2)}, u32[]{:S(2)}) collective-permute-start(bf16[192,768]{1,0:T(8,128)(2,1)S(1)} %fusion.3), channel_id=1, source_target_pairs={{0,96},{32,0},{64,32},{96,64},{1,97},{33,1},{65,33},{97,65},{2,98}... | collective-permute-start | bytes 884744 | tf_op jit(solution)/shard_map/ppermute | solution.py:17
  235.1 1.3 collective-permute-start.29
  235.3 21.6 %collective-permute-start.26 = (bf16[192,384]{1,0:T(8,128)(2,1)S(1)}, bf16[192,384]{1,0:T(8,128)(2,1)S(1)}, u32[]{:S(2)}, u32[]{:S(2)}) collective-permute-start(bf16[192,384]{1,0:T(8,128)(2,1)S(1)} %get-tuple-element.40), channel_id=1, source_target_pairs={{0,24},{8,0},{16,8},{24,16},{1,25},{9,1},{17,9},{25,17},{2,26},{10... | collective-permute-start | bytes 442376 | tf_op jit(solution)/shard_map/ppermute | solution.py:17
  237.7 17.9 %all-to-all-start.1 = ((f32[64,1,128]{2,1,0:T(1,128)}), f32[64,1,128]{2,1,0:T(1,128)S(1)}, u32[]{:S(2)}, u32[]{:S(2)}) async-start(f32[64,1,128]{2,1,0:T(1,128)} %broadcast_in_dim.19), calls=%async_computation.1 | async-start | bytes 65536 | tf_op jit(solution)/shard_map/all_to_all | solution.py:196
  246.2 10.8 %collective-permute-start.27 = (bf16[192,384]{1,0:T(8,128)(2,1)S(1)}, bf16[192,384]{1,0:T(8,128)(2,1)S(1)}, u32[]{:S(2)}, u32[]{:S(2)}) collective-permute-start(bf16[192,384]{1,0:T(8,128)(2,1)S(1)} %get-tuple-element.39), channel_id=1, source_target_pairs={{0,16},{8,24},{16,0},{24,8},{1,17},{9,25},{17,1},{25,9},{2,18},{10... | collective-permute-start | bytes 442376 | tf_op jit(solution)/shard_map/ppermute | solution.py:17
  249.3 7.7 %collective-permute-start.28 = (bf16[192,384]{1,0:T(8,128)(2,1)S(1)}, bf16[192,384]{1,0:T(8,128)(2,1)S(1)}, u32[]{:S(2)}, u32[]{:S(2)}) collective-permute-start(bf16[192,384]{1,0:T(8,128)(2,1)S(1)} %get-tuple-element.37), channel_id=1, source_target_pairs={{0,8},{8,16},{16,24},{24,0},{1,9},{9,17},{17,25},{25,1},{2,10},{10... | collective-permute-start | bytes 442376 | tf_op jit(solution)/shard_map/ppermute | solution.py:17
Sparse Core Ops, SparseCore 0:
  9.6 93.0 all-gather.1

commit v2 on v1

--- a/solution.py
+++ b/solution.py
@@ -171,6 +171,13 @@
     return [value, shift(value, axis, -1), shift(value, axis, 2), shift(value, axis, 1)]
 
 
+def ring_gather_halves(value, axis):
+    half = value.shape[0] // 2
+    after, before = shift(value, axis, -1), shift(value, axis, 1)
+    far = jnp.concatenate([shift(before[:half], axis, 1), shift(after[half:], axis, -1)], axis=0)
+    return [value, after, far, before]
+
+
 def ring_swap(chunk, axis):
     return [chunk(0), shift(chunk(3), axis, -1), shift(chunk(2), axis, 2), shift(chunk(1), axis, 1)]
 
@@ -182,7 +189,7 @@
     prev = shift(jnp.concatenate([chunk(1), far[:half]], axis=0), axis, 1)
     after = shift(jnp.concatenate([chunk(3), far[half:]], axis=0), axis, -1)
     high, low = shift(prev[rows:], axis, 1), shift(after[rows:], axis, -1)
-    return [chunk(0), after[:rows], jnp.concatenate([high, low], axis=0), prev[:rows]]
+    return [chunk(0), after[:rows], jnp.concatenate([high, low], axis=0), prev[:rows]], (prev, after)
 
 
 def in_order(pieces, me):
@@ -213,16 +220,16 @@
     def columns(array):
         return lambda k: lax.dynamic_slice_in_dim(array, lax.rem(iy + k, N) * cols, cols, axis=1)
 
-    w_pieces = ring_swap(columns(weight), "y")
-    w_rows = in_order(w_pieces, iy).reshape(-1, cols)
+    t_pieces, first_hop = ring_swap_halves(columns(target), "y")
+    t = in_order(t_pieces, iy)
+    t = jnp.concatenate([t[k].T for k in range(N)], axis=1)
+
+    w_rows = in_order(ring_swap(columns(behind(weight, *first_hop)), "y"), iy).reshape(-1, cols)
     w = in_order(ring_gather(w_rows.T, "x"), ix)
     w = jnp.concatenate([w[k] for k in range(N)], axis=1)
-    t = in_order(ring_swap_halves(columns(behind(target, *w_pieces)), "y"), iy)
-    t = jnp.concatenate([t[k].T for k in range(N)], axis=1)
-
     hidden, slope = first_slopes(x, w, t)
     first = ring_sum(lambda b: term(x, slope, b), ix)
-    own, after, far, before = ring_gather(first.astype(BF16), "x")
+    own, after, far, before = ring_gather_halves(first.astype(BF16), "x")
     at = lambda k: lax.rem(ix + k, N)
     part = moved(x, [own, after, before], [at(0), at(1), at(3)])
     total, part = total_of(first, part)

time: 266 us -> 262 us (0.985)
  local copies, waits for them, and re-layouts: 27.6 us -> 18.9 us
  other arithmetic: 9.19 us -> 14.8 us
    all_gather x1, waiting for transfers between devices: 18 us -> 12.2 us  [per_device(): lax.all_gather(tokens, ('z', 'c', 'y'), axis=0, tiled=True)]
    unnamed x29 -> x37, local copies, waits for them, and re-layouts: 13 us -> 7.69 us
    unnamed x2, other arithmetic: 0.1 us -> 3.87 us
    ppermute x28 -> x29, starting transfers between devices: 42.2 us -> 45.9 us  [shift(): return lax.ppermute(value, axis, [(i, (i + step) % N) for i in range(N)])]
    optimization_barrier x1 -> x0, local copies, waits for them, and re-layouts: 2.85 us -> none  [behind(): return lax.optimization_barrier((value, *others))[0]]
    ppermute x28 -> x29, waiting for transfers between devices: 59.4 us -> 61.6 us  [shift(): return lax.ppermute(value, axis, [(i, (i + step) % N) for i in range(N)])]
  transfers between devices with their start and end apart: 33 -> 34, of which waited for: 14 -> 17; matrix products, arithmetic and copies ran while one was open for 12% -> 11% of each run, Pallas kernels for 14% -> 14%
where the time goes in v2:
time: 262 us
  waiting for transfers between devices  81.4 us (31%)
  Pallas kernels  70.3 us (27%)
  starting transfers between devices  61.1 us (23%)
  local copies, waits for them, and re-layouts  18.9 us (7%)
  between operations  15.4 us (6%)
  other arithmetic  14.8 us (6%)
    ppermute x29, waiting for transfers between devices, shift(): return lax.ppermute(value, axis, [(i, (i + step) % N) for i in range(N)])  61.6 us
    ppermute x29, starting transfers between devices, shift(): return lax.ppermute(value, axis, [(i, (i + step) % N) for i in range(N)])  45.9 us
    pallas_call x8, Pallas kernels, term(): pl.pallas_call(term_kernel, grid_spec=pltpu.PrefetchScalarGridSpec(num_sc...  34.6 us
    pallas_call x2, Pallas kernels, moved(): pl.pallas_call(kernel, grid_spec=pltpu.PrefetchScalarGridSpec(num_scalar_...  20.5 us
    pallas_call x1, Pallas kernels, first_slopes(): pl.pallas_call(first_kernel, grid=(N,), in_specs=[pl.BlockSpec((blocks, t...  15.2 us
    all_to_all x2, starting transfers between devices, total_of(): lax.all_to_all(jnp.broadcast_to(total[:1], (N * N * N, 128)), ('x', 'y',...  15 us
    all_gather x1, waiting for transfers between devices, per_device(): lax.all_gather(tokens, ('z', 'c', 'y'), axis=0, tiled=True)  12.2 us
    unnamed x37, local copies, waits for them, and re-layouts  7.69 us
  transfers between devices with their start and end apart: 34, of which 17 were waited for; matrix products, arithmetic and copies ran while one was open for 11% of the time, Pallas kernels for 14%

profile of v2, /device:TPU:0, one launch (start us, length us, event | category | flops | bytes accessed | tf_op | source)
XLA Modules:
  0.0 261.9 jit_solution(2239904767776879143)
XLA Ops:
  7.3 1.8 fusion.17
  11.1 1.3 copy.35
  13.4 1.7 collective-permute-start
  16.5 1.6 collective-permute-start.1
  19.3 26.6 %collective-permute-done = bf16[1152,384]{0,1:T(8,128)(2,1)S(1)} collective-permute-done((bf16[1152,384]{0,1:T(8,128)(2,1)}, bf16[1152,384]{0,1:T(8,128)(2,1)S(1)}, u32[]{:S(2)}, u32[]{:S(2)}) %collective-permute-start) | collective-permute-done | bytes 884768 | tf_op jit(solution)/shard_map/ppermute | solution.py:17
  45.8 1.5 collective-permute-done.1
  47.4 3.0 %collective-permute-start.2 = (bf16[192,384]{1,0:T(8,128)(2,1)S(1)}, bf16[192,384]{1,0:T(8,128)(2,1)S(1)}, u32[]{:S(2)}, u32[]{:S(2)}) collective-permute-start(bf16[192,384]{1,0:T(8,128)(2,1)S(1)} %get-tuple-element.46), channel_id=1, source_target_pairs={{0,24},{8,0},{16,8},{24,16},{1,25},{9,1},{17,9},{25,17},{2,26},{10... | collective-permute-start | bytes 442376 | tf_op jit(solution)/shard_map/ppermute | solution.py:17
  52.5 2.6 collective-permute-start.9
  57.7 2.6 collective-permute-done.3
  60.3 3.2 %collective-permute-done.4 = bf16[192,384]{1,0:T(8,128)(2,1)S(1)} collective-permute-done((bf16[192,384]{1,0:T(8,128)(2,1)S(1)}, bf16[192,384]{1,0:T(8,128)(2,1)S(1)}, u32[]{:S(2)}, u32[]{:S(2)}) %collective-permute-start.4) | collective-permute-done | bytes 147488 | tf_op jit(solution)/shard_map/ppermute | solution.py:17
  64.0 2.7 %collective-permute-start.5 = (bf16[384,768]{1,0:T(8,128)(2,1)S(1)}, bf16[384,768]{1,0:T(8,128)(2,1)S(1)}, u32[]{:S(2)}, u32[]{:S(2)}) collective-permute-start(bf16[384,768]{1,0:T(8,128)(2,1)S(1)} %bitcast.123), channel_id=1, source_target_pairs={{0,96},{32,0},{64,32},{96,64},{1,97},{33,1},{65,33},{97,65},{2,98}... | collective-permute-start | bytes 1769480 | tf_op jit(solution)/shard_map/ppermute | solution.py:17
  68.4 1.7 collective-permute-done.9
  70.1 4.8 %collective-permute-done.8 = bf16[384,384]{0,1:T(8,128)(2,1)} collective-permute-done((bf16[384,384]{0,1:T(8,128)(2,1)}, bf16[384,384]{0,1:T(8,128)(2,1)}, u32[]{:S(2)}, u32[]{:S(2)}) %collective-permute-start.8) | collective-permute-done | bytes 294944 | tf_op jit(solution)/shard_map/ppermute | solution.py:17
  74.9 1.9 fusion.15
  79.4 2.0 fusion.16
  82.2 1.9 dynamic-slice_bitcast_fusion.3
  84.0 2.5 collective-permute-done.5
  86.6 3.6 %collective-permute-done.7 = bf16[384,768]{1,0:T(8,128)(2,1)S(1)} collective-permute-done((bf16[384,768]{1,0:T(8,128)(2,1)S(1)}, bf16[384,768]{1,0:T(8,128)(2,1)S(1)}, u32[]{:S(2)}, u32[]{:S(2)}) %collective-permute-start.7) | collective-permute-done | bytes 589856 | tf_op jit(solution)/shard_map/ppermute | solution.py:17
  90.6 2.6 pad_maximum_fusion
  93.2 12.2 %all-gather.2.cloned.1.call-done = bf16[24576,384]{1,0:T(8,128)(2,1)} async-done(((bf16[768,384]{1,0:T(8,128)(2,1)}), bf16[24576,384]{1,0:T(8,128)(2,1)}) %all-gather.2.cloned.1.call-update) | async-done | bytes 18874384 | tf_op jit(solution)/shard_map/all_gather | solution.py:218
  105.5 15.2 %shard_map.37 = (f32[384,3072]{1,0:T(8,128)}, bf16[384,3072]{1,0:T(8,128)(2,1)}) custom-call(bf16[8,3072,384]{2,1,0:T(8,128)(2,1)} %bitcast.110, bf16[384,3072]{1,0:T(8,128)(2,1)} %get-tuple-element.47.w_ref, bf16[384,3072]{1,0:T(8,128)(2,1)} %get-tuple-element.48.t_ref.refs_6_), custom_call_target="tpu_custom_call" | custom-call | flops 7247757312 | bytes 25952256 | tf_op jit(solution)/shard_map/pallas_call | solution.py:54
  120.6 4.3 %shard_map.40 = f32[384,768]{1,0:T(8,128)S(1)} custom-call(s32[1]{0:T(128)} %bitcast.2.which_ref.refs_0_, bf16[8,3072,384]{2,1,0:T(8,128)(2,1)} %bitcast.111, bf16[384,3072]{1,0:T(8,128)(2,1)} %get-tuple-element.11.s_ref), custom_call_target="tpu_custom_call" | custom-call | flops 1811939328 | bytes 8257536 | tf_op jit(solution)/shard_map/pallas_call | solution.py:137
  125.1 1.5 collective-permute-start.10
  126.6 4.3 %shard_map.41 = f32[384,768]{1,0:T(8,128)S(1)} custom-call(s32[1]{0:T(128)} %bitcast.30.which_ref, bf16[8,3072,384]{2,1,0:T(8,128)(2,1)} %bitcast.112, bf16[384,3072]{1,0:T(8,128)(2,1)} %get-tuple-element.11.s_ref), custom_call_target="tpu_custom_call" | custom-call | flops 1811939328 | bytes 8257536 | tf_op jit(solution)/shard_map/pallas_call | solution.py:137
  130.9 1.9 collective-permute-start.12
  132.8 1.4 collective-permute-start.14
  134.3 4.3 %shard_map.39 = f32[384,768]{1,0:T(8,128)S(1)} custom-call(s32[1]{0:T(128)} %bitcast.29.which_ref, bf16[8,3072,384]{2,1,0:T(8,128)(2,1)} %bitcast.113, bf16[384,3072]{1,0:T(8,128)(2,1)} %get-tuple-element.11.s_ref), custom_call_target="tpu_custom_call" | custom-call | flops 1811939328 | bytes 8257536 | tf_op jit(solution)/shard_map/pallas_call | solution.py:137
  139.6 6.6 %collective-permute-done.14 = bf16[192,768]{1,0:T(8,128)(2,1)S(1)} collective-permute-done((bf16[192,768]{1,0:T(8,128)(2,1)S(1)}, bf16[192,768]{1,0:T(8,128)(2,1)S(1)}, u32[]{:S(2)}, u32[]{:S(2)}) %collective-permute-start.14) | collective-permute-done | bytes 294944 | tf_op jit(solution)/shard_map/ppermute | solution.py:17
  146.3 3.1 %collective-permute-start.15 = (bf16[192,768]{1,0:T(8,128)(2,1)S(1)}, bf16[192,768]{1,0:T(8,128)(2,1)S(1)}, u32[]{:S(2)}, u32[]{:S(2)}) collective-permute-start(bf16[192,768]{1,0:T(8,128)(2,1)S(1)} %fusion.7), channel_id=1, source_target_pairs={{0,96},{32,0},{64,32},{96,64},{1,97},{33,1},{65,33},{97,65},{2,98}... | collective-permute-start | bytes 884744 | tf_op jit(solution)/shard_map/ppermute | solution.py:17
  149.4 4.3 %shard_map.38 = f32[384,768]{1,0:T(8,128)S(1)} custom-call(s32[1]{0:T(128)} %bitcast.which_ref, bf16[8,3072,384]{2,1,0:T(8,128)(2,1)} %bitcast.114, bf16[384,3072]{1,0:T(8,128)(2,1)} %get-tuple-element.11.s_ref), custom_call_target="tpu_custom_call" | custom-call | flops 1811939328 | bytes 8257536 | tf_op jit(solution)/shard_map/pallas_call | solution.py:137
  155.1 3.8 %collective-permute-start.18 = (bf16[384,768]{1,0:T(8,128)(2,1)S(1)}, bf16[384,768]{1,0:T(8,128)(2,1)S(1)}, u32[]{:S(2)}, u32[]{:S(2)}) collective-permute-start(bf16[384,768]{1,0:T(8,128)(2,1)S(1)} %fusion.1.refs_4_), channel_id=1, source_target_pairs={{0,96},{32,0},{64,32},{96,64},{1,97},{33,1},{65,33},{97,65},{2,98}... | collective-permute-start | bytes 1769480 | tf_op jit(solution)/shard_map/ppermute | solution.py:17
  163.0 9.1 %all-to-all-start = ((f32[64,1,128]{2,1,0:T(1,128)}), f32[64,1,128]{2,1,0:T(1,128)S(1)}, u32[]{:S(2)}, u32[]{:S(2)}) async-start(f32[64,1,128]{2,1,0:T(1,128)} %broadcast_in_dim.17), calls=%async_computation | async-start | bytes 65536 | tf_op jit(solution)/shard_map/all_to_all | solution.py:203
  172.1 3.1 %collective-permute-start.19 = (bf16[192,768]{1,0:T(8,128)(2,1)S(1)}, bf16[192,768]{1,0:T(8,128)(2,1)S(1)}, u32[]{:S(2)}, u32[]{:S(2)}) collective-permute-start(bf16[192,768]{1,0:T(8,128)(2,1)S(1)} %slice.183), channel_id=1, source_target_pairs={{0,96},{32,0},{64,32},{96,64},{1,97},{33,1},{65,33},{97,65},{2,98}... | collective-permute-start | bytes 884744 | tf_op jit(solution)/shard_map/ppermute | solution.py:17
  175.3 11.1 %shard_map.42.refs_3_ = f32[384,3072]{1,0:T(8,128)} custom-call(s32[3]{0:T(128)S(1)} %pad_add_fusion.refs_0_, bf16[8,3072,384]{2,1,0:T(8,128)(2,1)} %bitcast.115, bf16[8,3072,384]{2,1,0:T(8,128)(2,1)} %bitcast.116, bf16[8,3072,384]{2,1,0:T(8,128)(2,1)} %bitcast.117, bf16[384,768]{1,0:T(8,128)(2,1)S(1)} %fusion.1.refs_4_, ...), custom_call_target="tpu_custom_call" | custom-call | flops 5435817984 | bytes 20643840 | tf_op jit(solution)/shard_map/pallas_call | solution.py:108
  187.7 9.4 %shard_map.43.s_ref = bf16[384,3072]{1,0:T(8,128)(2,1)} custom-call(s32[1]{0:T(128)} %bitcast.2.which_ref.refs_0_, bf16[8,3072,384]{2,1,0:T(8,128)(2,1)} %bitcast.118, bf16[384,768]{1,0:T(8,128)(2,1)S(1)} %pad_maximum_fusion.6.refs_2_, f32[384,3072]{1,0:T(8,128)} %shard_map.42.refs_3_, f32[1,1]{1,0:T(1,128)} %bitcast.33.refs_4_, ...), custom_call_target="tpu_custom_call" | custom-call | flops 1811939328 | bytes 10027008 | tf_op jit(solution)/shard_map/pallas_call | solution.py:108
  197.1 4.3 %shard_map.46 = f32[384,768]{1,0:T(8,128)S(1)} custom-call(s32[1]{0:T(128)} %bitcast.2.which_ref.refs_0_, bf16[8,3072,384]{2,1,0:T(8,128)(2,1)} %bitcast.119, bf16[384,3072]{1,0:T(8,128)(2,1)} %shard_map.43.s_ref), custom_call_target="tpu_custom_call" | custom-call | flops 1811939328 | bytes 8257536 | tf_op jit(solution)/shard_map/pallas_call | solution.py:137
  202.2 2.9 %collective-permute-start.25 = (bf16[192,768]{1,0:T(8,128)(2,1)S(1)}, bf16[192,768]{1,0:T(8,128)(2,1)S(1)}, u32[]{:S(2)}, u32[]{:S(2)}) collective-permute-start(bf16[192,768]{1,0:T(8,128)(2,1)S(1)} %get-tuple-element.41), channel_id=1, source_target_pairs={{0,96},{32,0},{64,32},{96,64},{1,97},{33,1},{65,33},{97,65},{2,98}... | collective-permute-start | bytes 884744 | tf_op jit(solution)/shard_map/ppermute | solution.py:17
  205.2 4.3 %shard_map.47 = f32[384,768]{1,0:T(8,128)S(1)} custom-call(s32[1]{0:T(128)} %bitcast.30.which_ref, bf16[8,3072,384]{2,1,0:T(8,128)(2,1)} %bitcast.120, bf16[384,3072]{1,0:T(8,128)(2,1)} %shard_map.43.s_ref), custom_call_target="tpu_custom_call" | custom-call | flops 1811939328 | bytes 8257536 | tf_op jit(solution)/shard_map/pallas_call | solution.py:137
  209.5 4.3 %shard_map.45 = f32[384,768]{1,0:T(8,128)S(1)} custom-call(s32[1]{0:T(128)} %bitcast.29.which_ref, bf16[8,3072,384]{2,1,0:T(8,128)(2,1)} %bitcast.121, bf16[384,3072]{1,0:T(8,128)(2,1)} %shard_map.43.s_ref), custom_call_target="tpu_custom_call" | custom-call | flops 1811939328 | bytes 8257536 | tf_op jit(solution)/shard_map/pallas_call | solution.py:137
  213.9 1.8 collective-permute-start.23
  216.3 3.3 %collective-permute-start.26 = (bf16[192,768]{1,0:T(8,128)(2,1)S(1)}, bf16[192,768]{1,0:T(8,128)(2,1)S(1)}, u32[]{:S(2)}, u32[]{:S(2)}) collective-permute-start(bf16[192,768]{1,0:T(8,128)(2,1)S(1)} %fusion.3), channel_id=1, source_target_pairs={{0,96},{32,0},{64,32},{96,64},{1,97},{33,1},{65,33},{97,65},{2,98}... | collective-permute-start | bytes 884744 | tf_op jit(solution)/shard_map/ppermute | solution.py:17
  219.6 4.3 %shard_map.44 = f32[384,768]{1,0:T(8,128)S(1)} custom-call(s32[1]{0:T(128)} %bitcast.which_ref, bf16[8,3072,384]{2,1,0:T(8,128)(2,1)} %bitcast.122, bf16[384,3072]{1,0:T(8,128)(2,1)} %shard_map.43.s_ref), custom_call_target="tpu_custom_call" | custom-call | flops 1811939328 | bytes 8257536 | tf_op jit(solution)/shard_map/pallas_call | solution.py:137
  224.0 3.0 %collective-permute-done.24 = bf16[192,768]{1,0:T(8,128)(2,1)S(1)} collective-permute-done((bf16[192,768]{1,0:T(8,128)(2,1)S(1)}, bf16[192,768]{1,0:T(8,128)(2,1)S(1)}, u32[]{:S(2)}, u32[]{:S(2)}) %collective-permute-start.24) | collective-permute-done | bytes 294944 | tf_op jit(solution)/shard_map/ppermute | solution.py:17
  226.9 3.5 %collective-permute-done.22 = bf16[192,768]{1,0:T(8,128)(2,1)S(1)} collective-permute-done((bf16[192,768]{1,0:T(8,128)(2,1)S(1)}, bf16[192,768]{1,0:T(8,128)(2,1)S(1)}, u32[]{:S(2)}, u32[]{:S(2)}) %collective-permute-start.22) | collective-permute-done | bytes 294944 | tf_op jit(solution)/shard_map/ppermute | solution.py:17
  232.7 2.8 %collective-permute-start.27 = (bf16[192,384]{1,0:T(8,128)(2,1)S(1)}, bf16[192,384]{1,0:T(8,128)(2,1)S(1)}, u32[]{:S(2)}, u32[]{:S(2)}) collective-permute-start(bf16[192,384]{1,0:T(8,128)(2,1)S(1)} %get-tuple-element.39), channel_id=1, source_target_pairs={{0,24},{8,0},{16,8},{24,16},{1,25},{9,1},{17,9},{25,17},{2,26},{10... | collective-permute-start | bytes 442376 | tf_op jit(solution)/shard_map/ppermute | solution.py:17
  236.8 6.0 %all-to-all-start.1 = ((f32[64,1,128]{2,1,0:T(1,128)}), f32[64,1,128]{2,1,0:T(1,128)S(1)}, u32[]{:S(2)}, u32[]{:S(2)}) async-start(f32[64,1,128]{2,1,0:T(1,128)} %broadcast_in_dim.19), calls=%async_computation.1 | async-start | bytes 65536 | tf_op jit(solution)/shard_map/all_to_all | solution.py:203
  242.8 3.2 %collective-permute-start.28 = (bf16[192,384]{1,0:T(8,128)(2,1)S(1)}, bf16[192,384]{1,0:T(8,128)(2,1)S(1)}, u32[]{:S(2)}, u32[]{:S(2)}) collective-permute-start(bf16[192,384]{1,0:T(8,128)(2,1)S(1)} %get-tuple-element.38), channel_id=1, source_target_pairs={{0,16},{8,24},{16,0},{24,8},{1,17},{9,25},{17,1},{25,9},{2,18},{10... | collective-permute-start | bytes 442376 | tf_op jit(solution)/shard_map/ppermute | solution.py:17
  246.5 5.8 %all-to-all-done.1 = f32[64,1,128]{2,1,0:T(1,128)S(1)} async-done(((f32[64,1,128]{2,1,0:T(1,128)}), f32[64,1,128]{2,1,0:T(1,128)S(1)}, u32[]{:S(2)}, u32[]{:S(2)}) %all-to-all-start.1) | async-done | bytes 32800 | tf_op jit(solution)/shard_map/all_to_all | solution.py:203
  (124 shorter events, 32.1 us)
Async XLA Ops:
  6.5 3.5 %copy-start = (bf16[768,1536]{1,0:T(8,128)(2,1)S(1)}, bf16[768,1536]{1,0:T(8,128)(2,1)}, u32[]{:S(2)}) copy-start(bf16[768,1536]{1,0:T(8,128)(2,1)} %param.4) | copy-start | bytes 7077892
  6.5 98.9 %all-gather.2.cloned.1.call-start = ((), (), s32[]{:S(2)}) async-start(), calls=%async_computation.2 | async-start | bytes 19464192 | tf_op jit(solution)/shard_map/all_gather | solution.py:218
  11.0 1.4 copy-start.1
  12.4 2.7 %copy-start.2 = (bf16[384,384]{1,0:T(8,128)(2,1)S(1)}, bf16[384,384]{1,0:T(8,128)(2,1)}, u32[]{:S(2)}) copy-start(bf16[384,384]{1,0:T(8,128)(2,1)} %get-tuple-element.26) | copy-start | bytes 884740
  13.4 32.4 %collective-permute-start = (bf16[1152,384]{0,1:T(8,128)(2,1)}, bf16[1152,384]{0,1:T(8,128)(2,1)S(1)}, u32[]{:S(2)}, u32[]{:S(2)}) collective-permute-start(bf16[1152,384]{0,1:T(8,128)(2,1)} %pad_maximum_fusion.4), channel_id=1, source_target_pairs={{0,8},{8,16},{16,24},{24,0},{1,9},{9,17},{17,25},{25,1},{2,10},{10... | collective-permute-start | bytes 2654216 | tf_op jit(solution)/shard_map/ppermute | solution.py:17
  16.5 30.8 %collective-permute-start.1 = (bf16[1152,384]{0,1:T(8,128)(2,1)}, bf16[1152,384]{0,1:T(8,128)(2,1)S(1)}, u32[]{:S(2)}, u32[]{:S(2)}) collective-permute-start(bf16[1152,384]{0,1:T(8,128)(2,1)} %pad_maximum_fusion.5), channel_id=1, source_target_pairs={{0,24},{8,0},{16,8},{24,16},{1,25},{9,1},{17,9},{25,17},{2,26},{10... | collective-permute-start | bytes 2654216 | tf_op jit(solution)/shard_map/ppermute | solution.py:17
  18.1 29.2 %copy-start.3 = (bf16[192,1536]{1,0:T(8,128)(2,1)S(1)}, bf16[192,1536]{1,0:T(8,128)(2,1)}, u32[]{:S(2)}) copy-start(bf16[192,1536]{1,0:T(8,128)(2,1)} %param.5) | copy-start | bytes 1769476
  47.4 10.3 %collective-permute-start.2 = (bf16[192,384]{1,0:T(8,128)(2,1)S(1)}, bf16[192,384]{1,0:T(8,128)(2,1)S(1)}, u32[]{:S(2)}, u32[]{:S(2)}) collective-permute-start(bf16[192,384]{1,0:T(8,128)(2,1)S(1)} %get-tuple-element.46), channel_id=1, source_target_pairs={{0,24},{8,0},{16,8},{24,16},{1,25},{9,1},{17,9},{25,17},{2,26},{10... | collective-permute-start | bytes 442376 | tf_op jit(solution)/shard_map/ppermute | solution.py:17
  50.4 9.9 %collective-permute-start.3 = (bf16[192,384]{1,0:T(8,128)(2,1)S(1)}, bf16[192,384]{1,0:T(8,128)(2,1)S(1)}, u32[]{:S(2)}, u32[]{:S(2)}) collective-permute-start(bf16[192,384]{1,0:T(8,128)(2,1)S(1)} %get-tuple-element.45), channel_id=1, source_target_pairs={{0,16},{8,24},{16,0},{24,8},{1,17},{9,25},{17,1},{25,9},{2,18},{10... | collective-permute-start | bytes 442376 | tf_op jit(solution)/shard_map/ppermute | solution.py:17
  51.1 12.4 %collective-permute-start.4 = (bf16[192,384]{1,0:T(8,128)(2,1)S(1)}, bf16[192,384]{1,0:T(8,128)(2,1)S(1)}, u32[]{:S(2)}, u32[]{:S(2)}) collective-permute-start(bf16[192,384]{1,0:T(8,128)(2,1)S(1)} %get-tuple-element.44), channel_id=1, source_target_pairs={{0,8},{8,16},{16,24},{24,0},{1,9},{9,17},{17,25},{25,1},{2,10},{10... | collective-permute-start | bytes 442376 | tf_op jit(solution)/shard_map/ppermute | solution.py:17
  52.5 17.6 %collective-permute-start.9 = (bf16[384,384]{0,1:T(8,128)(2,1)}, bf16[384,384]{0,1:T(8,128)(2,1)}, u32[]{:S(2)}, u32[]{:S(2)}) collective-permute-start(bf16[384,384]{0,1:T(8,128)(2,1)} %slice.172), channel_id=1, source_target_pairs={{0,24},{8,0},{16,8},{24,16},{1,25},{9,1},{17,9},{25,17},{2,26},{10... | collective-permute-start | bytes 884744 | tf_op jit(solution)/shard_map/ppermute | solution.py:17
  55.8 19.0 %collective-permute-start.8 = (bf16[384,384]{0,1:T(8,128)(2,1)}, bf16[384,384]{0,1:T(8,128)(2,1)}, u32[]{:S(2)}, u32[]{:S(2)}) collective-permute-start(bf16[384,384]{0,1:T(8,128)(2,1)} %slice.171), channel_id=1, source_target_pairs={{0,8},{8,16},{16,24},{24,0},{1,9},{9,17},{17,25},{25,1},{2,10},{10... | collective-permute-start | bytes 884744 | tf_op jit(solution)/shard_map/ppermute | solution.py:17
  64.0 22.5 %collective-permute-start.5 = (bf16[384,768]{1,0:T(8,128)(2,1)S(1)}, bf16[384,768]{1,0:T(8,128)(2,1)S(1)}, u32[]{:S(2)}, u32[]{:S(2)}) collective-permute-start(bf16[384,768]{1,0:T(8,128)(2,1)S(1)} %bitcast.123), channel_id=1, source_target_pairs={{0,96},{32,0},{64,32},{96,64},{1,97},{33,1},{65,33},{97,65},{2,98}... | collective-permute-start | bytes 1769480 | tf_op jit(solution)/shard_map/ppermute | solution.py:17
  66.7 19.9 %collective-permute-start.6 = (bf16[384,768]{1,0:T(8,128)(2,1)S(1)}, bf16[384,768]{1,0:T(8,128)(2,1)S(1)}, u32[]{:S(2)}, u32[]{:S(2)}) collective-permute-start(bf16[384,768]{1,0:T(8,128)(2,1)S(1)} %bitcast.124), channel_id=1, source_target_pairs={{0,64},{32,96},{64,0},{96,32},{1,65},{33,97},{65,1},{97,33},{2,66}... | collective-permute-start | bytes 1769480 | tf_op jit(solution)/shard_map/ppermute | solution.py:17
  67.4 22.8 %collective-permute-start.7 = (bf16[384,768]{1,0:T(8,128)(2,1)S(1)}, bf16[384,768]{1,0:T(8,128)(2,1)S(1)}, u32[]{:S(2)}, u32[]{:S(2)}) collective-permute-start(bf16[384,768]{1,0:T(8,128)(2,1)S(1)} %bitcast.125), channel_id=1, source_target_pairs={{0,32},{32,64},{64,96},{96,0},{1,33},{33,65},{65,97},{97,1},{2,34}... | collective-permute-start | bytes 1769480 | tf_op jit(solution)/shard_map/ppermute | solution.py:17
  125.1 14.2 %collective-permute-start.10 = (bf16[192,768]{1,0:T(8,128)(2,1)S(1)}, bf16[192,768]{1,0:T(8,128)(2,1)S(1)}, u32[]{:S(2)}, u32[]{:S(2)}) collective-permute-start(bf16[192,768]{1,0:T(8,128)(2,1)S(1)} %get-tuple-element.42), channel_id=1, source_target_pairs={{0,32},{32,64},{64,96},{96,0},{1,33},{33,65},{65,97},{97,1},{2,34}... | collective-permute-start | bytes 884744 | tf_op jit(solution)/shard_map/ppermute | solution.py:17
  130.9 22.8 %collective-permute-start.12 = (bf16[192,768]{1,0:T(8,128)(2,1)S(1)}, bf16[192,768]{1,0:T(8,128)(2,1)S(1)}, u32[]{:S(2)}, u32[]{:S(2)}) collective-permute-start(bf16[192,768]{1,0:T(8,128)(2,1)S(1)} %slice.238), channel_id=1, source_target_pairs={{0,96},{32,0},{64,32},{96,64},{1,97},{33,1},{65,33},{97,65},{2,98}... | collective-permute-start | bytes 884744 | tf_op jit(solution)/shard_map/ppermute | solution.py:17
  132.8 13.4 %collective-permute-start.14 = (bf16[192,768]{1,0:T(8,128)(2,1)S(1)}, bf16[192,768]{1,0:T(8,128)(2,1)S(1)}, u32[]{:S(2)}, u32[]{:S(2)}) collective-permute-start(bf16[192,768]{1,0:T(8,128)(2,1)S(1)} %get-tuple-element.43), channel_id=1, source_target_pairs={{0,96},{32,0},{64,32},{96,64},{1,97},{33,1},{65,33},{97,65},{2,98}... | collective-permute-start | bytes 884744 | tf_op jit(solution)/shard_map/ppermute | solution.py:17
  138.7 15.1 %collective-permute-start.13 = (bf16[192,768]{1,0:T(8,128)(2,1)S(1)}, bf16[192,768]{1,0:T(8,128)(2,1)S(1)}, u32[]{:S(2)}, u32[]{:S(2)}) collective-permute-start(bf16[192,768]{1,0:T(8,128)(2,1)S(1)} %slice.237), channel_id=1, source_target_pairs={{0,32},{32,64},{64,96},{96,0},{1,33},{33,65},{65,97},{97,1},{2,34}... | collective-permute-start | bytes 884744 | tf_op jit(solution)/shard_map/ppermute | solution.py:17
  139.4 15.2 %collective-permute-start.11 = (bf16[192,768]{1,0:T(8,128)(2,1)S(1)}, bf16[192,768]{1,0:T(8,128)(2,1)S(1)}, u32[]{:S(2)}, u32[]{:S(2)}) collective-permute-start(bf16[192,768]{1,0:T(8,128)(2,1)S(1)} %fusion.9), channel_id=1, source_target_pairs={{0,32},{32,64},{64,96},{96,0},{1,33},{33,65},{65,97},{97,1},{2,34}... | collective-permute-start | bytes 884744 | tf_op jit(solution)/shard_map/ppermute | solution.py:17
  146.3 8.6 %collective-permute-start.15 = (bf16[192,768]{1,0:T(8,128)(2,1)S(1)}, bf16[192,768]{1,0:T(8,128)(2,1)S(1)}, u32[]{:S(2)}, u32[]{:S(2)}) collective-permute-start(bf16[192,768]{1,0:T(8,128)(2,1)S(1)} %fusion.7), channel_id=1, source_target_pairs={{0,96},{32,0},{64,32},{96,64},{1,97},{33,1},{65,33},{97,65},{2,98}... | collective-permute-start | bytes 884744 | tf_op jit(solution)/shard_map/ppermute | solution.py:17
  155.1 16.9 %collective-permute-start.18 = (bf16[384,768]{1,0:T(8,128)(2,1)S(1)}, bf16[384,768]{1,0:T(8,128)(2,1)S(1)}, u32[]{:S(2)}, u32[]{:S(2)}) collective-permute-start(bf16[384,768]{1,0:T(8,128)(2,1)S(1)} %fusion.1.refs_4_), channel_id=1, source_target_pairs={{0,96},{32,0},{64,32},{96,64},{1,97},{33,1},{65,33},{97,65},{2,98}... | collective-permute-start | bytes 1769480 | tf_op jit(solution)/shard_map/ppermute | solution.py:17
  158.9 16.3 %collective-permute-start.16 = (bf16[384,768]{1,0:T(8,128)(2,1)S(1)}, bf16[384,768]{1,0:T(8,128)(2,1)S(1)}, u32[]{:S(2)}, u32[]{:S(2)}) collective-permute-start(bf16[384,768]{1,0:T(8,128)(2,1)S(1)} %fusion.1.refs_4_), channel_id=1, source_target_pairs={{0,32},{32,64},{64,96},{96,0},{1,33},{33,65},{65,97},{97,1},{2,34}... | collective-permute-start | bytes 1769480 | tf_op jit(solution)/shard_map/ppermute | solution.py:17
  160.5 1.2 collective-permute-start.20
  163.0 23.3 %all-to-all-start = ((f32[64,1,128]{2,1,0:T(1,128)}), f32[64,1,128]{2,1,0:T(1,128)S(1)}, u32[]{:S(2)}, u32[]{:S(2)}) async-start(f32[64,1,128]{2,1,0:T(1,128)} %broadcast_in_dim.17), calls=%async_computation | async-start | bytes 65536 | tf_op jit(solution)/shard_map/all_to_all | solution.py:203
  172.1 15.5 %collective-permute-start.19 = (bf16[192,768]{1,0:T(8,128)(2,1)S(1)}, bf16[192,768]{1,0:T(8,128)(2,1)S(1)}, u32[]{:S(2)}, u32[]{:S(2)}) collective-permute-start(bf16[192,768]{1,0:T(8,128)(2,1)S(1)} %slice.183), channel_id=1, source_target_pairs={{0,96},{32,0},{64,32},{96,64},{1,97},{33,1},{65,33},{97,65},{2,98}... | collective-permute-start | bytes 884744 | tf_op jit(solution)/shard_map/ppermute | solution.py:17
  175.2 12.5 %collective-permute-start.17 = (bf16[192,768]{1,0:T(8,128)(2,1)S(1)}, bf16[192,768]{1,0:T(8,128)(2,1)S(1)}, u32[]{:S(2)}, u32[]{:S(2)}) collective-permute-start(bf16[192,768]{1,0:T(8,128)(2,1)S(1)} %slice.182), channel_id=1, source_target_pairs={{0,32},{32,64},{64,96},{96,0},{1,33},{33,65},{65,97},{97,1},{2,34}... | collective-permute-start | bytes 884744 | tf_op jit(solution)/shard_map/ppermute | solution.py:17
  201.6 14.5 %collective-permute-start.21 = (bf16[192,768]{1,0:T(8,128)(2,1)S(1)}, bf16[192,768]{1,0:T(8,128)(2,1)S(1)}, u32[]{:S(2)}, u32[]{:S(2)}) collective-permute-start(bf16[192,768]{1,0:T(8,128)(2,1)S(1)} %get-tuple-element.40), channel_id=1, source_target_pairs={{0,32},{32,64},{64,96},{96,0},{1,33},{33,65},{65,97},{97,1},{2,34}... | collective-permute-start | bytes 884744 | tf_op jit(solution)/shard_map/ppermute | solution.py:17
  202.2 14.0 %collective-permute-start.25 = (bf16[192,768]{1,0:T(8,128)(2,1)S(1)}, bf16[192,768]{1,0:T(8,128)(2,1)S(1)}, u32[]{:S(2)}, u32[]{:S(2)}) collective-permute-start(bf16[192,768]{1,0:T(8,128)(2,1)S(1)} %get-tuple-element.41), channel_id=1, source_target_pairs={{0,96},{32,0},{64,32},{96,64},{1,97},{33,1},{65,33},{97,65},{2,98}... | collective-permute-start | bytes 884744 | tf_op jit(solution)/shard_map/ppermute | solution.py:17
  213.9 10.1 %collective-permute-start.23 = (bf16[192,768]{1,0:T(8,128)(2,1)S(1)}, bf16[192,768]{1,0:T(8,128)(2,1)S(1)}, u32[]{:S(2)}, u32[]{:S(2)}) collective-permute-start(bf16[192,768]{1,0:T(8,128)(2,1)S(1)} %slice.236), channel_id=1, source_target_pairs={{0,96},{32,0},{64,32},{96,64},{1,97},{33,1},{65,33},{97,65},{2,98}... | collective-permute-start | bytes 884744 | tf_op jit(solution)/shard_map/ppermute | solution.py:17
  215.7 11.2 %collective-permute-start.24 = (bf16[192,768]{1,0:T(8,128)(2,1)S(1)}, bf16[192,768]{1,0:T(8,128)(2,1)S(1)}, u32[]{:S(2)}, u32[]{:S(2)}) collective-permute-start(bf16[192,768]{1,0:T(8,128)(2,1)S(1)} %slice.235), channel_id=1, source_target_pairs={{0,32},{32,64},{64,96},{96,0},{1,33},{33,65},{65,97},{97,1},{2,34}... | collective-permute-start | bytes 884744 | tf_op jit(solution)/shard_map/ppermute | solution.py:17
  216.2 14.3 %collective-permute-start.22 = (bf16[192,768]{1,0:T(8,128)(2,1)S(1)}, bf16[192,768]{1,0:T(8,128)(2,1)S(1)}, u32[]{:S(2)}, u32[]{:S(2)}) collective-permute-start(bf16[192,768]{1,0:T(8,128)(2,1)S(1)} %fusion.5), channel_id=1, source_target_pairs={{0,32},{32,64},{64,96},{96,0},{1,33},{33,65},{65,97},{97,1},{2,34}... | collective-permute-start | bytes 884744 | tf_op jit(solution)/shard_map/ppermute | solution.py:17
  216.3 14.1 %collective-permute-start.26 = (bf16[192,768]{1,0:T(8,128)(2,1)S(1)}, bf16[192,768]{1,0:T(8,128)(2,1)S(1)}, u32[]{:S(2)}, u32[]{:S(2)}) collective-permute-start(bf16[192,768]{1,0:T(8,128)(2,1)S(1)} %fusion.3), channel_id=1, source_target_pairs={{0,96},{32,0},{64,32},{96,64},{1,97},{33,1},{65,33},{97,65},{2,98}... | collective-permute-start | bytes 884744 | tf_op jit(solution)/shard_map/ppermute | solution.py:17
  232.5 3.0 %collective-permute-start.30 = (f32[8,128]{1,0:T(8,128)S(1)}, f32[8,128]{1,0:T(8,128)S(1)}, u32[]{:S(2)}, u32[]{:S(2)}) collective-permute-start(f32[8,128]{1,0:T(8,128)S(1)} %broadcast_in_dim.18), channel_id=1, source_target_pairs={{0,1},{1,0},{2,3},{3,2},{4,5},{5,4},{6,7},{7,6},{8,9},{9,8},{10,11... | collective-permute-start | bytes 12296 | tf_op jit(solution)/shard_map/ppermute | solution.py:202
  232.7 20.9 %collective-permute-start.27 = (bf16[192,384]{1,0:T(8,128)(2,1)S(1)}, bf16[192,384]{1,0:T(8,128)(2,1)S(1)}, u32[]{:S(2)}, u32[]{:S(2)}) collective-permute-start(bf16[192,384]{1,0:T(8,128)(2,1)S(1)} %get-tuple-element.39), channel_id=1, source_target_pairs={{0,24},{8,0},{16,8},{24,16},{1,25},{9,1},{17,9},{25,17},{2,26},{10... | collective-permute-start | bytes 442376 | tf_op jit(solution)/shard_map/ppermute | solution.py:17
  236.8 15.5 %all-to-all-start.1 = ((f32[64,1,128]{2,1,0:T(1,128)}), f32[64,1,128]{2,1,0:T(1,128)S(1)}, u32[]{:S(2)}, u32[]{:S(2)}) async-start(f32[64,1,128]{2,1,0:T(1,128)} %broadcast_in_dim.19), calls=%async_computation.1 | async-start | bytes 65536 | tf_op jit(solution)/shard_map/all_to_all | solution.py:203
  242.8 10.8 %collective-permute-start.28 = (bf16[192,384]{1,0:T(8,128)(2,1)S(1)}, bf16[192,384]{1,0:T(8,128)(2,1)S(1)}, u32[]{:S(2)}, u32[]{:S(2)}) collective-permute-start(bf16[192,384]{1,0:T(8,128)(2,1)S(1)} %get-tuple-element.38), channel_id=1, source_target_pairs={{0,16},{8,24},{16,0},{24,8},{1,17},{9,25},{17,1},{25,9},{2,18},{10... | collective-permute-start | bytes 442376 | tf_op jit(solution)/shard_map/ppermute | solution.py:17
  246.0 7.7 %collective-permute-start.29 = (bf16[192,384]{1,0:T(8,128)(2,1)S(1)}, bf16[192,384]{1,0:T(8,128)(2,1)S(1)}, u32[]{:S(2)}, u32[]{:S(2)}) collective-permute-start(bf16[192,384]{1,0:T(8,128)(2,1)S(1)} %get-tuple-element.36), channel_id=1, source_target_pairs={{0,8},{8,16},{16,24},{24,0},{1,9},{9,17},{17,25},{25,1},{2,10},{10... | collective-permute-start | bytes 442376 | tf_op jit(solution)/shard_map/ppermute | solution.py:17
Sparse Core Ops, SparseCore 0:
  9.6 95.8 all-gather.1

commit v3 on v2

--- a/solution.py
+++ b/solution.py
@@ -70,9 +70,9 @@
     refs = list(refs[1:])
     xs, fs = refs[:count], refs[count : 2 * count]
     rest = refs[2 * count :]
-    part = sum(
-        lax.dot_general(f[...], joined(x), NT, preferred_element_type=F32) for x, f in zip(xs, fs)
-    )
+    x = jnp.concatenate([x_ref[k] for x_ref in xs for k in range(x_ref.shape[0])], axis=1)
+    f = jnp.concatenate([f_ref[...] for f_ref in fs], axis=1)
+    part = lax.dot_general(f, x, NT, preferred_element_type=F32)
     if started:
         part = part + rest.pop(0)[...]
     if last:
@@ -117,51 +117,53 @@
     )(jnp.stack(which).astype(jnp.int32), *args)
 
 
-def term_kernel(which_ref, x_ref, s_ref, o_ref):
-    part = jnp.dot(s_ref[...], joined(x_ref), preferred_element_type=F32)
-
-    @pl.when(pl.program_id(0) == 0)
-    def _():
-        o_ref[...] = part
-
-    @pl.when(pl.program_id(0) > 0)
-    def _():
-        o_ref[...] += part
-
-
-def term(x, s, block):
+def terms(x, s, which):
     blocks, rows, wide = x.shape
     cols = s.shape[0]
     tile = rows // 2
     per = blocks // N
+    count = len(which)
+    at = lambda j: pl.BlockSpec((per, tile, wide), lambda i, which: (which[j], i, 0))
+
+    def kernel(which_ref, *refs):
+        s_ref = refs[count]
+        parts = [jnp.dot(s_ref[...], joined(refs[j]), preferred_element_type=F32) for j in range(count)]
+
+        @pl.when(pl.program_id(0) == 0)
+        def _():
+            for j in range(count):
+                refs[count + 1 + j][...] = parts[j]
+
+        @pl.when(pl.program_id(0) > 0)
+        def _():
+            for j in range(count):
+                refs[count + 1 + j][...] += parts[j]
+
     return pl.pallas_call(
-        term_kernel,
+        kernel,
         grid_spec=pltpu.PrefetchScalarGridSpec(
             num_scalar_prefetch=1,
             grid=(rows // tile,),
-            in_specs=[
-                pl.BlockSpec((per, tile, wide), lambda i, which: (which[0], i, 0)),
-                pl.BlockSpec((cols, tile), lambda i, which: (0, i)),
-            ],
-            out_specs=pl.BlockSpec((cols, per * wide), lambda i, which: (0, 0)),
+            in_specs=[at(j) for j in range(count)] + [pl.BlockSpec((cols, tile), lambda i, which: (0, i))],
+            out_specs=[pl.BlockSpec((cols, per * wide), lambda i, which: (0, 0))] * count,
         ),
-        out_shape=jax.ShapeDtypeStruct((cols, per * wide), F32),
+        out_shape=[jax.ShapeDtypeStruct((cols, per * wide), F32)] * count,
         compiler_params=PARAMS,
-        cost_estimate=cost(cols, rows, per * wide),
-    )(jnp.reshape(block, (1,)).astype(jnp.int32), x, s)
-
-
-def ring_sum(part, me):
-    block = lambda step: part(lax.rem(me + step, N))
-    far = block(2).astype(BF16)
+        cost_estimate=cost(cols, rows, per * wide * count),
+    )(jnp.stack(which).astype(jnp.int32), *([x] * count), s)
+
+
+def ring_sum(parts, me):
+    at = lambda step: lax.rem(me + step, N)
+    far = parts([at(2)])[0].astype(BF16)
     half = far.shape[0] // 2
     far_next, far_prev = shift(far[:half], "x", 1), shift(far[half:], "x", -1)
-    to_next, to_prev = block(1), block(3)
+    to_next, to_prev = parts([at(1), at(3)])
     next_low = shift(to_next[half:].astype(BF16), "x", 1)
     prev_high = shift(to_prev[:half].astype(BF16), "x", -1)
     next_high = shift((to_next[:half] + far_next.astype(F32)).astype(BF16), "x", 1)
     prev_low = shift((to_prev[half:] + far_prev.astype(F32)).astype(BF16), "x", -1)
-    own = block(0)
+    own = parts([at(0)])[0]
     high = own[:half] + next_high.astype(F32) + prev_high.astype(F32)
     low = own[half:] + next_low.astype(F32) + prev_low.astype(F32)
     return jnp.concatenate([high, low], axis=0)
@@ -198,11 +200,9 @@
 
 
 def total_of(value, beside):
-    total = jnp.full((8, 128), jnp.sum(value * value), F32)
+    total = jnp.full((N * N * N, 128), jnp.sum(value * value), F32)
     total = total + lax.ppermute(total, "c", [(0, 1), (1, 0)])
-    each = lax.all_to_all(
-        jnp.broadcast_to(total[:1], (N * N * N, 128)), ("x", "y", "z"), split_axis=0, concat_axis=0, tiled=True
-    )
+    each = lax.all_to_all(total, ("x", "y", "z"), split_axis=0, concat_axis=0, tiled=True)
     if beside is not None:
         each, beside = lax.optimization_barrier((each, beside))
     return jnp.sum(each[:, 0]), beside
@@ -228,14 +228,14 @@
     w = in_order(ring_gather(w_rows.T, "x"), ix)
     w = jnp.concatenate([w[k] for k in range(N)], axis=1)
     hidden, slope = first_slopes(x, w, t)
-    first = ring_sum(lambda b: term(x, slope, b), ix)
+    first = ring_sum(lambda bs: terms(x, slope, bs), ix)
     own, after, far, before = ring_gather_halves(first.astype(BF16), "x")
     at = lambda k: lax.rem(ix + k, N)
     part = moved(x, [own, after, before], [at(0), at(1), at(3)])
     total, part = total_of(first, part)
     scale = 0.5 * math.sqrt(hidden_all) / jnp.sqrt(total + 1e-06)
     slope = moved(x, [far], [at(2)], part, (scale.reshape(1, 1), hidden, t))
-    second = ring_sum(lambda b: term(x, slope, b), ix)
+    second = ring_sum(lambda bs: terms(x, slope, bs), ix)
     total, _ = total_of(second, None)
     factor = jnp.minimum(1.0, math.sqrt(width * hidden_all) / jnp.sqrt(total + 1e-06))
     held = second.astype(BF16).T.reshape(N, -1, cols)

time: 262 us -> 260 us (level)
  starting transfers between devices: 61.1 us -> 57.5 us
    unnamed x37 -> x43, local copies, waits for them, and re-layouts: 7.69 us -> 7.31 us
    pallas_call x8 -> x6, Pallas kernels: 34.6 us -> 34.4 us  [terms(): pl.pallas_call(kernel, grid_spec=pltpu.PrefetchScalarGridSpec(num_scalar_...]
  transfers between devices with their start and end apart: 34 -> 34, of which waited for: 17 -> 17; matrix products, arithmetic and copies ran while one was open for 11% -> 12% of each run, Pallas kernels for 14% -> 14%
where the time goes in v3:
time: 260 us
  waiting for transfers between devices  81.2 us (31%)
  Pallas kernels  70 us (27%)
  starting transfers between devices  57.5 us (22%)
  local copies, waits for them, and re-layouts  19.6 us (8%)
  other arithmetic  15.9 us (6%)
  between operations  15.3 us (6%)
    ppermute x29, waiting for transfers between devices, shift(): return lax.ppermute(value, axis, [(i, (i + step) % N) for i in range(N)])  61 us
    ppermute x29, starting transfers between devices, shift(): return lax.ppermute(value, axis, [(i, (i + step) % N) for i in range(N)])  44.1 us
    pallas_call x6, Pallas kernels, terms(): pl.pallas_call(kernel, grid_spec=pltpu.PrefetchScalarGridSpec(num_scalar_...  34.4 us
    pallas_call x2, Pallas kernels, moved(): pl.pallas_call(kernel, grid_spec=pltpu.PrefetchScalarGridSpec(num_scalar_...  20.5 us
    pallas_call x1, Pallas kernels, first_slopes(): pl.pallas_call(first_kernel, grid=(N,), in_specs=[pl.BlockSpec((blocks, t...  15.1 us
    all_to_all x2, starting transfers between devices, total_of(): lax.all_to_all(total, ('x', 'y', 'z'), split_axis=0, concat_axis=0, tiled...  13.2 us
    all_gather x1, waiting for transfers between devices, per_device(): lax.all_gather(tokens, ('z', 'c', 'y'), axis=0, tiled=True)  12.6 us
    unnamed x43, local copies, waits for them, and re-layouts  7.31 us
  transfers between devices with their start and end apart: 34, of which 17 were waited for; matrix products, arithmetic and copies ran while one was open for 12% of the time, Pallas kernels for 14%

profile of v3, /device:TPU:0, one launch (start us, length us, event | category | flops | bytes accessed | tf_op | source)
XLA Modules:
  0.0 259.5 jit_solution(7114866619138893356)
XLA Ops:
  7.3 1.8 fusion.13
  13.0 1.7 collective-permute-start
  16.1 1.6 collective-permute-start.1
  18.9 26.5 %collective-permute-done = bf16[1152,384]{0,1:T(8,128)(2,1)S(1)} collective-permute-done((bf16[1152,384]{0,1:T(8,128)(2,1)}, bf16[1152,384]{0,1:T(8,128)(2,1)S(1)}, u32[]{:S(2)}, u32[]{:S(2)}) %collective-permute-start) | collective-permute-done | bytes 884768 | tf_op jit(solution)/shard_map/ppermute | solution.py:17
  45.4 1.5 collective-permute-done.1
  47.0 3.0 %collective-permute-start.2 = (bf16[192,384]{1,0:T(8,128)(2,1)S(1)}, bf16[192,384]{1,0:T(8,128)(2,1)S(1)}, u32[]{:S(2)}, u32[]{:S(2)}) collective-permute-start(bf16[192,384]{1,0:T(8,128)(2,1)S(1)} %get-tuple-element.54), channel_id=1, source_target_pairs={{0,24},{8,0},{16,8},{24,16},{1,25},{9,1},{17,9},{25,17},{2,26},{10... | collective-permute-start | bytes 442376 | tf_op jit(solution)/shard_map/ppermute | solution.py:17
  52.1 2.6 collective-permute-start.9
  57.2 2.3 collective-permute-done.3
  59.5 3.2 %collective-permute-done.4 = bf16[192,384]{1,0:T(8,128)(2,1)S(1)} collective-permute-done((bf16[192,384]{1,0:T(8,128)(2,1)S(1)}, bf16[192,384]{1,0:T(8,128)(2,1)S(1)}, u32[]{:S(2)}, u32[]{:S(2)}) %collective-permute-start.4) | collective-permute-done | bytes 147488 | tf_op jit(solution)/shard_map/ppermute | solution.py:17
  63.2 2.9 %collective-permute-start.5 = (bf16[384,768]{1,0:T(8,128)(2,1)S(1)}, bf16[384,768]{1,0:T(8,128)(2,1)S(1)}, u32[]{:S(2)}, u32[]{:S(2)}) collective-permute-start(bf16[384,768]{1,0:T(8,128)(2,1)S(1)} %bitcast.121), channel_id=1, source_target_pairs={{0,96},{32,0},{64,32},{96,64},{1,97},{33,1},{65,33},{97,65},{2,98}... | collective-permute-start | bytes 1769480 | tf_op jit(solution)/shard_map/ppermute | solution.py:17
  67.9 1.7 collective-permute-done.9
  69.5 4.7 %collective-permute-done.8 = bf16[384,384]{0,1:T(8,128)(2,1)} collective-permute-done((bf16[384,384]{0,1:T(8,128)(2,1)}, bf16[384,384]{0,1:T(8,128)(2,1)}, u32[]{:S(2)}, u32[]{:S(2)}) %collective-permute-start.8) | collective-permute-done | bytes 294944 | tf_op jit(solution)/shard_map/ppermute | solution.py:17
  74.3 1.9 fusion.11
  78.8 1.9 fusion.12
  81.6 2.0 dynamic-slice_bitcast_fusion.3
  83.6 2.3 collective-permute-done.5
  86.0 3.6 %collective-permute-done.7 = bf16[384,768]{1,0:T(8,128)(2,1)S(1)} collective-permute-done((bf16[384,768]{1,0:T(8,128)(2,1)S(1)}, bf16[384,768]{1,0:T(8,128)(2,1)S(1)}, u32[]{:S(2)}, u32[]{:S(2)}) %collective-permute-start.7) | collective-permute-done | bytes 589856 | tf_op jit(solution)/shard_map/ppermute | solution.py:17
  89.9 2.5 pad_maximum_fusion
  92.5 12.6 %all-gather.2.cloned.1.call-done = bf16[24576,384]{1,0:T(8,128)(2,1)} async-done(((bf16[768,384]{1,0:T(8,128)(2,1)}), bf16[24576,384]{1,0:T(8,128)(2,1)}) %all-gather.2.cloned.1.call-update) | async-done | bytes 18874384 | tf_op jit(solution)/shard_map/all_gather | solution.py:218
  105.1 15.1 %shard_map.37 = (f32[384,3072]{1,0:T(8,128)}, bf16[384,3072]{1,0:T(8,128)(2,1)}) custom-call(bf16[8,3072,384]{2,1,0:T(8,128)(2,1)} %bitcast.108, bf16[384,3072]{1,0:T(8,128)(2,1)} %get-tuple-element.55.w_ref, bf16[384,3072]{1,0:T(8,128)(2,1)} %get-tuple-element.56.t_ref.refs_6_), custom_call_target="tpu_custom_call" | custom-call | flops 7247757312 | bytes 25952256 | tf_op jit(solution)/shard_map/pallas_call | solution.py:54
  120.2 4.3 %shard_map.40 = f32[384,768]{1,0:T(8,128)S(1)} custom-call(s32[1]{0:T(128)} %bitcast.2.which_ref.refs_0_, bf16[8,3072,384]{2,1,0:T(8,128)(2,1)} %bitcast.109, bf16[384,3072]{1,0:T(8,128)(2,1)} %get-tuple-element.15.refs_1_.refs_2_), custom_call_target="tpu_custom_call" | custom-call | flops 1811939328 | bytes 8257536 | tf_op jit(solution)/shard_map/pallas_call | solution.py:142
  124.6 1.5 collective-permute-start.10
  126.1 1.8 collective-permute-start.14
  127.9 8.5 %shard_map.39 = (f32[384,768]{1,0:T(8,128)S(1)}, f32[384,768]{1,0:T(8,128)}) custom-call(s32[2]{0:T(128)S(1)} %pad_add_fusion.which_ref, bf16[8,3072,384]{2,1,0:T(8,128)(2,1)} %bitcast.110, bf16[8,3072,384]{2,1,0:T(8,128)(2,1)} %bitcast.111, bf16[384,3072]{1,0:T(8,128)(2,1)} %get-tuple-element.15.refs_1_.refs_2_), custom_call_target="tpu_custom_call" | custom-call | flops 3623878656 | bytes 14155776 | tf_op jit(solution)/shard_map/pallas_call | solution.py:142
  136.4 1.2 slice.210
  137.6 1.6 collective-permute-start.12
  140.2 3.1 %collective-permute-start.15 = (bf16[192,768]{1,0:T(8,128)(2,1)S(1)}, bf16[192,768]{1,0:T(8,128)(2,1)S(1)}, u32[]{:S(2)}, u32[]{:S(2)}) collective-permute-start(bf16[192,768]{1,0:T(8,128)(2,1)S(1)} %add_convert_fusion.2), channel_id=1, source_target_pairs={{0,96},{32,0},{64,32},{96,64},{1,97},{33,1},{65,33},{97,65},{2,98}... | collective-permute-start | bytes 884744 | tf_op jit(solution)/shard_map/ppermute | solution.py:17
  143.3 4.3 %shard_map.38 = f32[384,768]{1,0:T(8,128)S(1)} custom-call(s32[1]{0:T(128)} %bitcast.which_ref, bf16[8,3072,384]{2,1,0:T(8,128)(2,1)} %bitcast.112, bf16[384,3072]{1,0:T(8,128)(2,1)} %get-tuple-element.15.refs_1_.refs_2_), custom_call_target="tpu_custom_call" | custom-call | flops 1811939328 | bytes 8257536 | tf_op jit(solution)/shard_map/pallas_call | solution.py:142
  147.7 2.8 %collective-permute-done.13 = bf16[192,768]{1,0:T(8,128)(2,1)S(1)} collective-permute-done((bf16[192,768]{1,0:T(8,128)(2,1)S(1)}, bf16[192,768]{1,0:T(8,128)(2,1)S(1)}, u32[]{:S(2)}, u32[]{:S(2)}) %collective-permute-start.13) | collective-permute-done | bytes 294944 | tf_op jit(solution)/shard_map/ppermute | solution.py:17
  150.5 4.7 %collective-permute-done.11 = bf16[192,768]{1,0:T(8,128)(2,1)S(1)} collective-permute-done((bf16[192,768]{1,0:T(8,128)(2,1)S(1)}, bf16[192,768]{1,0:T(8,128)(2,1)S(1)}, u32[]{:S(2)}, u32[]{:S(2)}) %collective-permute-start.11) | collective-permute-done | bytes 294944 | tf_op jit(solution)/shard_map/ppermute | solution.py:17
  155.7 1.9 collective-permute-start.16
  161.5 7.2 %all-to-all-start = ((f32[64,1,128]{2,1,0:T(1,128)}), f32[64,1,128]{2,1,0:T(1,128)S(1)}, u32[]{:S(2)}, u32[]{:S(2)}) async-start(f32[64,1,128]{2,1,0:T(1,128)} %bitcast.31), calls=%async_computation | async-start | bytes 65536 | tf_op jit(solution)/shard_map/all_to_all | solution.py:205
  169.2 2.6 collective-permute-start.19
  171.9 11.0 %shard_map.41.refs_3_ = f32[384,3072]{1,0:T(8,128)} custom-call(s32[3]{0:T(128)S(1)} %pad_add_fusion.1.refs_0_, bf16[8,3072,384]{2,1,0:T(8,128)(2,1)} %bitcast.113, bf16[8,3072,384]{2,1,0:T(8,128)(2,1)} %bitcast.114, bf16[8,3072,384]{2,1,0:T(8,128)(2,1)} %bitcast.115, bf16[384,768]{1,0:T(8,128)(2,1)S(1)} %fusion.1.refs_4_, ...), custom_call_target="tpu_custom_call" | custom-call | flops 5435817984 | bytes 20643840 | tf_op jit(solution)/shard_map/pallas_call | solution.py:108
  184.3 9.5 %shard_map.42.refs_1_.refs_2_ = bf16[384,3072]{1,0:T(8,128)(2,1)} custom-call(s32[1]{0:T(128)} %bitcast.2.which_ref.refs_0_, bf16[8,3072,384]{2,1,0:T(8,128)(2,1)} %bitcast.116, bf16[384,768]{1,0:T(8,128)(2,1)S(1)} %pad_maximum_fusion.6.refs_2_, f32[384,3072]{1,0:T(8,128)} %shard_map.41.refs_3_, f32[1,1]{1,0:T(1,128)} %bitcast.33.refs_4_, ...), custom_call_target="tpu_custom_call" | custom-call | flops 1811939328 | bytes 10027008 | tf_op jit(solution)/shard_map/pallas_call | solution.py:108
  193.8 4.3 %shard_map.45 = f32[384,768]{1,0:T(8,128)S(1)} custom-call(s32[1]{0:T(128)} %bitcast.2.which_ref.refs_0_, bf16[8,3072,384]{2,1,0:T(8,128)(2,1)} %bitcast.117, bf16[384,3072]{1,0:T(8,128)(2,1)} %shard_map.42.refs_1_.refs_2_), custom_call_target="tpu_custom_call" | custom-call | flops 1811939328 | bytes 8257536 | tf_op jit(solution)/shard_map/pallas_call | solution.py:142
  198.9 3.0 %collective-permute-start.25 = (bf16[192,768]{1,0:T(8,128)(2,1)S(1)}, bf16[192,768]{1,0:T(8,128)(2,1)S(1)}, u32[]{:S(2)}, u32[]{:S(2)}) collective-permute-start(bf16[192,768]{1,0:T(8,128)(2,1)S(1)} %get-tuple-element.49), channel_id=1, source_target_pairs={{0,96},{32,0},{64,32},{96,64},{1,97},{33,1},{65,33},{97,65},{2,98}... | collective-permute-start | bytes 884744 | tf_op jit(solution)/shard_map/ppermute | solution.py:17
  201.9 8.5 %shard_map.44 = (f32[384,768]{1,0:T(8,128)S(1)}, f32[384,768]{1,0:T(8,128)}) custom-call(s32[2]{0:T(128)S(1)} %pad_add_fusion.which_ref, bf16[8,3072,384]{2,1,0:T(8,128)(2,1)} %bitcast.118, bf16[8,3072,384]{2,1,0:T(8,128)(2,1)} %bitcast.119, bf16[384,3072]{1,0:T(8,128)(2,1)} %shard_map.42.refs_1_.refs_2_), custom_call_target="tpu_custom_call" | custom-call | flops 3623878656 | bytes 14155776 | tf_op jit(solution)/shard_map/pallas_call | solution.py:142
  210.5 1.2 slice.208
  211.7 1.8 collective-permute-start.23
  214.1 3.3 %collective-permute-start.26 = (bf16[192,768]{1,0:T(8,128)(2,1)S(1)}, bf16[192,768]{1,0:T(8,128)(2,1)S(1)}, u32[]{:S(2)}, u32[]{:S(2)}) collective-permute-start(bf16[192,768]{1,0:T(8,128)(2,1)S(1)} %add_convert_fusion), channel_id=1, source_target_pairs={{0,96},{32,0},{64,32},{96,64},{1,97},{33,1},{65,33},{97,65},{2,98}... | collective-permute-start | bytes 884744 | tf_op jit(solution)/shard_map/ppermute | solution.py:17
  217.4 4.3 %shard_map.43 = f32[384,768]{1,0:T(8,128)S(1)} custom-call(s32[1]{0:T(128)} %bitcast.which_ref, bf16[8,3072,384]{2,1,0:T(8,128)(2,1)} %bitcast.120, bf16[384,3072]{1,0:T(8,128)(2,1)} %shard_map.42.refs_1_.refs_2_), custom_call_target="tpu_custom_call" | custom-call | flops 1811939328 | bytes 8257536 | tf_op jit(solution)/shard_map/pallas_call | solution.py:142
  221.7 3.0 %collective-permute-done.24 = bf16[192,768]{1,0:T(8,128)(2,1)S(1)} collective-permute-done((bf16[192,768]{1,0:T(8,128)(2,1)S(1)}, bf16[192,768]{1,0:T(8,128)(2,1)S(1)}, u32[]{:S(2)}, u32[]{:S(2)}) %collective-permute-start.24) | collective-permute-done | bytes 294944 | tf_op jit(solution)/shard_map/ppermute | solution.py:17
  224.7 3.5 %collective-permute-done.22 = bf16[192,768]{1,0:T(8,128)(2,1)S(1)} collective-permute-done((bf16[192,768]{1,0:T(8,128)(2,1)S(1)}, bf16[192,768]{1,0:T(8,128)(2,1)S(1)}, u32[]{:S(2)}, u32[]{:S(2)}) %collective-permute-start.22) | collective-permute-done | bytes 294944 | tf_op jit(solution)/shard_map/ppermute | solution.py:17
  230.4 2.8 %collective-permute-start.27 = (bf16[192,384]{1,0:T(8,128)(2,1)S(1)}, bf16[192,384]{1,0:T(8,128)(2,1)S(1)}, u32[]{:S(2)}, u32[]{:S(2)}) collective-permute-start(bf16[192,384]{1,0:T(8,128)(2,1)S(1)} %get-tuple-element.47), channel_id=1, source_target_pairs={{0,24},{8,0},{16,8},{24,16},{1,25},{9,1},{17,9},{25,17},{2,26},{10... | collective-permute-start | bytes 442376 | tf_op jit(solution)/shard_map/ppermute | solution.py:17
  234.3 6.0 %all-to-all-start.1 = ((f32[64,1,128]{2,1,0:T(1,128)}), f32[64,1,128]{2,1,0:T(1,128)S(1)}, u32[]{:S(2)}, u32[]{:S(2)}) async-start(f32[64,1,128]{2,1,0:T(1,128)} %bitcast.46), calls=%async_computation.1 | async-start | bytes 65536 | tf_op jit(solution)/shard_map/all_to_all | solution.py:205
  240.4 3.2 %collective-permute-start.28 = (bf16[192,384]{1,0:T(8,128)(2,1)S(1)}, bf16[192,384]{1,0:T(8,128)(2,1)S(1)}, u32[]{:S(2)}, u32[]{:S(2)}) collective-permute-start(bf16[192,384]{1,0:T(8,128)(2,1)S(1)} %get-tuple-element.46), channel_id=1, source_target_pairs={{0,16},{8,24},{16,0},{24,8},{1,17},{9,25},{17,1},{25,9},{2,18},{10... | collective-permute-start | bytes 442376 | tf_op jit(solution)/shard_map/ppermute | solution.py:17
  244.1 5.8 %all-to-all-done.1 = f32[64,1,128]{2,1,0:T(1,128)S(1)} async-done(((f32[64,1,128]{2,1,0:T(1,128)}), f32[64,1,128]{2,1,0:T(1,128)S(1)}, u32[]{:S(2)}, u32[]{:S(2)}) %all-to-all-start.1) | async-done | bytes 32800 | tf_op jit(solution)/shard_map/all_to_all | solution.py:205
  (125 shorter events, 32.1 us)
Async XLA Ops:
  6.5 3.5 %copy-start = (bf16[768,1536]{1,0:T(8,128)(2,1)S(1)}, bf16[768,1536]{1,0:T(8,128)(2,1)}, u32[]{:S(2)}) copy-start(bf16[768,1536]{1,0:T(8,128)(2,1)} %param.4) | copy-start | bytes 7077892
  6.5 98.5 %all-gather.2.cloned.1.call-start = ((), (), s32[]{:S(2)}) async-start(), calls=%async_computation.2 | async-start | bytes 19464192 | tf_op jit(solution)/shard_map/all_gather | solution.py:218
  11.0 1.0 copy-start.2
  12.0 2.7 %copy-start.3 = (bf16[384,384]{1,0:T(8,128)(2,1)S(1)}, bf16[384,384]{1,0:T(8,128)(2,1)}, u32[]{:S(2)}) copy-start(bf16[384,384]{1,0:T(8,128)(2,1)} %get-tuple-element.34) | copy-start | bytes 884740
  13.0 32.4 %collective-permute-start = (bf16[1152,384]{0,1:T(8,128)(2,1)}, bf16[1152,384]{0,1:T(8,128)(2,1)S(1)}, u32[]{:S(2)}, u32[]{:S(2)}) collective-permute-start(bf16[1152,384]{0,1:T(8,128)(2,1)} %pad_maximum_fusion.4), channel_id=1, source_target_pairs={{0,8},{8,16},{16,24},{24,0},{1,9},{9,17},{17,25},{25,1},{2,10},{10... | collective-permute-start | bytes 2654216 | tf_op jit(solution)/shard_map/ppermute | solution.py:17
  15.1 2.6 copy-start.1
  16.1 30.8 %collective-permute-start.1 = (bf16[1152,384]{0,1:T(8,128)(2,1)}, bf16[1152,384]{0,1:T(8,128)(2,1)S(1)}, u32[]{:S(2)}, u32[]{:S(2)}) collective-permute-start(bf16[1152,384]{0,1:T(8,128)(2,1)} %pad_maximum_fusion.5), channel_id=1, source_target_pairs={{0,24},{8,0},{16,8},{24,16},{1,25},{9,1},{17,9},{25,17},{2,26},{10... | collective-permute-start | bytes 2654216 | tf_op jit(solution)/shard_map/ppermute | solution.py:17
  17.7 29.2 %copy-start.4 = (bf16[192,1536]{1,0:T(8,128)(2,1)S(1)}, bf16[192,1536]{1,0:T(8,128)(2,1)}, u32[]{:S(2)}) copy-start(bf16[192,1536]{1,0:T(8,128)(2,1)} %param.5) | copy-start | bytes 1769476
  47.0 10.2 %collective-permute-start.2 = (bf16[192,384]{1,0:T(8,128)(2,1)S(1)}, bf16[192,384]{1,0:T(8,128)(2,1)S(1)}, u32[]{:S(2)}, u32[]{:S(2)}) collective-permute-start(bf16[192,384]{1,0:T(8,128)(2,1)S(1)} %get-tuple-element.54), channel_id=1, source_target_pairs={{0,24},{8,0},{16,8},{24,16},{1,25},{9,1},{17,9},{25,17},{2,26},{10... | collective-permute-start | bytes 442376 | tf_op jit(solution)/shard_map/ppermute | solution.py:17
  50.0 9.5 %collective-permute-start.3 = (bf16[192,384]{1,0:T(8,128)(2,1)S(1)}, bf16[192,384]{1,0:T(8,128)(2,1)S(1)}, u32[]{:S(2)}, u32[]{:S(2)}) collective-permute-start(bf16[192,384]{1,0:T(8,128)(2,1)S(1)} %get-tuple-element.53), channel_id=1, source_target_pairs={{0,16},{8,24},{16,0},{24,8},{1,17},{9,25},{17,1},{25,9},{2,18},{10... | collective-permute-start | bytes 442376 | tf_op jit(solution)/shard_map/ppermute | solution.py:17
  50.7 12.0 %collective-permute-start.4 = (bf16[192,384]{1,0:T(8,128)(2,1)S(1)}, bf16[192,384]{1,0:T(8,128)(2,1)S(1)}, u32[]{:S(2)}, u32[]{:S(2)}) collective-permute-start(bf16[192,384]{1,0:T(8,128)(2,1)S(1)} %get-tuple-element.52), channel_id=1, source_target_pairs={{0,8},{8,16},{16,24},{24,0},{1,9},{9,17},{17,25},{25,1},{2,10},{10... | collective-permute-start | bytes 442376 | tf_op jit(solution)/shard_map/ppermute | solution.py:17
  52.1 17.4 %collective-permute-start.9 = (bf16[384,384]{0,1:T(8,128)(2,1)}, bf16[384,384]{0,1:T(8,128)(2,1)}, u32[]{:S(2)}, u32[]{:S(2)}) collective-permute-start(bf16[384,384]{0,1:T(8,128)(2,1)} %slice.158), channel_id=1, source_target_pairs={{0,24},{8,0},{16,8},{24,16},{1,25},{9,1},{17,9},{25,17},{2,26},{10... | collective-permute-start | bytes 884744 | tf_op jit(solution)/shard_map/ppermute | solution.py:17
  55.5 18.8 %collective-permute-start.8 = (bf16[384,384]{0,1:T(8,128)(2,1)}, bf16[384,384]{0,1:T(8,128)(2,1)}, u32[]{:S(2)}, u32[]{:S(2)}) collective-permute-start(bf16[384,384]{0,1:T(8,128)(2,1)} %slice.157), channel_id=1, source_target_pairs={{0,8},{8,16},{16,24},{24,0},{1,9},{9,17},{17,25},{25,1},{2,10},{10... | collective-permute-start | bytes 884744 | tf_op jit(solution)/shard_map/ppermute | solution.py:17
  63.2 22.6 %collective-permute-start.5 = (bf16[384,768]{1,0:T(8,128)(2,1)S(1)}, bf16[384,768]{1,0:T(8,128)(2,1)S(1)}, u32[]{:S(2)}, u32[]{:S(2)}) collective-permute-start(bf16[384,768]{1,0:T(8,128)(2,1)S(1)} %bitcast.121), channel_id=1, source_target_pairs={{0,96},{32,0},{64,32},{96,64},{1,97},{33,1},{65,33},{97,65},{2,98}... | collective-permute-start | bytes 1769480 | tf_op jit(solution)/shard_map/ppermute | solution.py:17
  66.1 19.8 %collective-permute-start.6 = (bf16[384,768]{1,0:T(8,128)(2,1)S(1)}, bf16[384,768]{1,0:T(8,128)(2,1)S(1)}, u32[]{:S(2)}, u32[]{:S(2)}) collective-permute-start(bf16[384,768]{1,0:T(8,128)(2,1)S(1)} %bitcast.122), channel_id=1, source_target_pairs={{0,64},{32,96},{64,0},{96,32},{1,65},{33,97},{65,1},{97,33},{2,66}... | collective-permute-start | bytes 1769480 | tf_op jit(solution)/shard_map/ppermute | solution.py:17
  66.9 22.6 %collective-permute-start.7 = (bf16[384,768]{1,0:T(8,128)(2,1)S(1)}, bf16[384,768]{1,0:T(8,128)(2,1)S(1)}, u32[]{:S(2)}, u32[]{:S(2)}) collective-permute-start(bf16[384,768]{1,0:T(8,128)(2,1)S(1)} %bitcast.123), channel_id=1, source_target_pairs={{0,32},{32,64},{64,96},{96,0},{1,33},{33,65},{65,97},{97,1},{2,34}... | collective-permute-start | bytes 1769480 | tf_op jit(solution)/shard_map/ppermute | solution.py:17
  124.6 15.2 %collective-permute-start.10 = (bf16[192,768]{1,0:T(8,128)(2,1)S(1)}, bf16[192,768]{1,0:T(8,128)(2,1)S(1)}, u32[]{:S(2)}, u32[]{:S(2)}) collective-permute-start(bf16[192,768]{1,0:T(8,128)(2,1)S(1)} %get-tuple-element.50), channel_id=1, source_target_pairs={{0,32},{32,64},{64,96},{96,0},{1,33},{33,65},{65,97},{97,1},{2,34}... | collective-permute-start | bytes 884744 | tf_op jit(solution)/shard_map/ppermute | solution.py:17
  126.1 14.1 %collective-permute-start.14 = (bf16[192,768]{1,0:T(8,128)(2,1)S(1)}, bf16[192,768]{1,0:T(8,128)(2,1)S(1)}, u32[]{:S(2)}, u32[]{:S(2)}) collective-permute-start(bf16[192,768]{1,0:T(8,128)(2,1)S(1)} %get-tuple-element.51), channel_id=1, source_target_pairs={{0,96},{32,0},{64,32},{96,64},{1,97},{33,1},{65,33},{97,65},{2,98}... | collective-permute-start | bytes 884744 | tf_op jit(solution)/shard_map/ppermute | solution.py:17
  136.4 3.7 %copy-start.6 = (f32[384,768]{1,0:T(8,128)S(1)}, f32[384,768]{1,0:T(8,128)}, u32[]{:S(2)}) copy-start(f32[384,768]{1,0:T(8,128)} %get-tuple-element.17) | copy-start | bytes 3538948
  137.6 10.0 %collective-permute-start.12 = (bf16[192,768]{1,0:T(8,128)(2,1)S(1)}, bf16[192,768]{1,0:T(8,128)(2,1)S(1)}, u32[]{:S(2)}, u32[]{:S(2)}) collective-permute-start(bf16[192,768]{1,0:T(8,128)(2,1)S(1)} %slice.210), channel_id=1, source_target_pairs={{0,96},{32,0},{64,32},{96,64},{1,97},{33,1},{65,33},{97,65},{2,98}... | collective-permute-start | bytes 884744 | tf_op jit(solution)/shard_map/ppermute | solution.py:17
  139.3 11.2 %collective-permute-start.13 = (bf16[192,768]{1,0:T(8,128)(2,1)S(1)}, bf16[192,768]{1,0:T(8,128)(2,1)S(1)}, u32[]{:S(2)}, u32[]{:S(2)}) collective-permute-start(bf16[192,768]{1,0:T(8,128)(2,1)S(1)} %slice.209), channel_id=1, source_target_pairs={{0,32},{32,64},{64,96},{96,0},{1,33},{33,65},{65,97},{97,1},{2,34}... | collective-permute-start | bytes 884744 | tf_op jit(solution)/shard_map/ppermute | solution.py:17
  139.9 15.3 %collective-permute-start.11 = (bf16[192,768]{1,0:T(8,128)(2,1)S(1)}, bf16[192,768]{1,0:T(8,128)(2,1)S(1)}, u32[]{:S(2)}, u32[]{:S(2)}) collective-permute-start(bf16[192,768]{1,0:T(8,128)(2,1)S(1)} %add_convert_fusion.3), channel_id=1, source_target_pairs={{0,32},{32,64},{64,96},{96,0},{1,33},{33,65},{65,97},{97,1},{2,34}... | collective-permute-start | bytes 884744 | tf_op jit(solution)/shard_map/ppermute | solution.py:17
  140.2 14.9 %collective-permute-start.15 = (bf16[192,768]{1,0:T(8,128)(2,1)S(1)}, bf16[192,768]{1,0:T(8,128)(2,1)S(1)}, u32[]{:S(2)}, u32[]{:S(2)}) collective-permute-start(bf16[192,768]{1,0:T(8,128)(2,1)S(1)} %add_convert_fusion.2), channel_id=1, source_target_pairs={{0,96},{32,0},{64,32},{96,64},{1,97},{33,1},{65,33},{97,65},{2,98}... | collective-permute-start | bytes 884744 | tf_op jit(solution)/shard_map/ppermute | solution.py:17
  155.4 13.8 %collective-permute-start.18 = (bf16[384,768]{1,0:T(8,128)(2,1)S(1)}, bf16[384,768]{1,0:T(8,128)(2,1)S(1)}, u32[]{:S(2)}, u32[]{:S(2)}) collective-permute-start(bf16[384,768]{1,0:T(8,128)(2,1)S(1)} %fusion.1.refs_4_), channel_id=1, source_target_pairs={{0,96},{32,0},{64,32},{96,64},{1,97},{33,1},{65,33},{97,65},{2,98}... | collective-permute-start | bytes 1769480 | tf_op jit(solution)/shard_map/ppermute | solution.py:17
  155.7 16.1 %collective-permute-start.16 = (bf16[384,768]{1,0:T(8,128)(2,1)S(1)}, bf16[384,768]{1,0:T(8,128)(2,1)S(1)}, u32[]{:S(2)}, u32[]{:S(2)}) collective-permute-start(bf16[384,768]{1,0:T(8,128)(2,1)S(1)} %fusion.1.refs_4_), channel_id=1, source_target_pairs={{0,32},{32,64},{64,96},{96,0},{1,33},{33,65},{65,97},{97,1},{2,34}... | collective-permute-start | bytes 1769480 | tf_op jit(solution)/shard_map/ppermute | solution.py:17
  159.0 1.3 collective-permute-start.20
  161.5 21.5 %all-to-all-start = ((f32[64,1,128]{2,1,0:T(1,128)}), f32[64,1,128]{2,1,0:T(1,128)S(1)}, u32[]{:S(2)}, u32[]{:S(2)}) async-start(f32[64,1,128]{2,1,0:T(1,128)} %bitcast.31), calls=%async_computation | async-start | bytes 65536 | tf_op jit(solution)/shard_map/all_to_all | solution.py:205
  169.2 15.0 %collective-permute-start.19 = (bf16[192,768]{1,0:T(8,128)(2,1)S(1)}, bf16[192,768]{1,0:T(8,128)(2,1)S(1)}, u32[]{:S(2)}, u32[]{:S(2)}) collective-permute-start(bf16[192,768]{1,0:T(8,128)(2,1)S(1)} %slice.167), channel_id=1, source_target_pairs={{0,96},{32,0},{64,32},{96,64},{1,97},{33,1},{65,33},{97,65},{2,98}... | collective-permute-start | bytes 884744 | tf_op jit(solution)/shard_map/ppermute | solution.py:17
  171.8 12.4 %collective-permute-start.17 = (bf16[192,768]{1,0:T(8,128)(2,1)S(1)}, bf16[192,768]{1,0:T(8,128)(2,1)S(1)}, u32[]{:S(2)}, u32[]{:S(2)}) collective-permute-start(bf16[192,768]{1,0:T(8,128)(2,1)S(1)} %slice.166), channel_id=1, source_target_pairs={{0,32},{32,64},{64,96},{96,0},{1,33},{33,65},{65,97},{97,1},{2,34}... | collective-permute-start | bytes 884744 | tf_op jit(solution)/shard_map/ppermute | solution.py:17
  198.3 15.6 %collective-permute-start.21 = (bf16[192,768]{1,0:T(8,128)(2,1)S(1)}, bf16[192,768]{1,0:T(8,128)(2,1)S(1)}, u32[]{:S(2)}, u32[]{:S(2)}) collective-permute-start(bf16[192,768]{1,0:T(8,128)(2,1)S(1)} %get-tuple-element.48), channel_id=1, source_target_pairs={{0,32},{32,64},{64,96},{96,0},{1,33},{33,65},{65,97},{97,1},{2,34}... | collective-permute-start | bytes 884744 | tf_op jit(solution)/shard_map/ppermute | solution.py:17
  198.9 15.1 %collective-permute-start.25 = (bf16[192,768]{1,0:T(8,128)(2,1)S(1)}, bf16[192,768]{1,0:T(8,128)(2,1)S(1)}, u32[]{:S(2)}, u32[]{:S(2)}) collective-permute-start(bf16[192,768]{1,0:T(8,128)(2,1)S(1)} %get-tuple-element.49), channel_id=1, source_target_pairs={{0,96},{32,0},{64,32},{96,64},{1,97},{33,1},{65,33},{97,65},{2,98}... | collective-permute-start | bytes 884744 | tf_op jit(solution)/shard_map/ppermute | solution.py:17
  210.5 3.6 %copy-start.5 = (f32[384,768]{1,0:T(8,128)S(1)}, f32[384,768]{1,0:T(8,128)}, u32[]{:S(2)}) copy-start(f32[384,768]{1,0:T(8,128)} %get-tuple-element.22) | copy-start | bytes 3538948
  211.7 10.0 %collective-permute-start.23 = (bf16[192,768]{1,0:T(8,128)(2,1)S(1)}, bf16[192,768]{1,0:T(8,128)(2,1)S(1)}, u32[]{:S(2)}, u32[]{:S(2)}) collective-permute-start(bf16[192,768]{1,0:T(8,128)(2,1)S(1)} %slice.208), channel_id=1, source_target_pairs={{0,96},{32,0},{64,32},{96,64},{1,97},{33,1},{65,33},{97,65},{2,98}... | collective-permute-start | bytes 884744 | tf_op jit(solution)/shard_map/ppermute | solution.py:17
  213.5 11.2 %collective-permute-start.24 = (bf16[192,768]{1,0:T(8,128)(2,1)S(1)}, bf16[192,768]{1,0:T(8,128)(2,1)S(1)}, u32[]{:S(2)}, u32[]{:S(2)}) collective-permute-start(bf16[192,768]{1,0:T(8,128)(2,1)S(1)} %slice.207), channel_id=1, source_target_pairs={{0,32},{32,64},{64,96},{96,0},{1,33},{33,65},{65,97},{97,1},{2,34}... | collective-permute-start | bytes 884744 | tf_op jit(solution)/shard_map/ppermute | solution.py:17
  213.9 14.3 %collective-permute-start.22 = (bf16[192,768]{1,0:T(8,128)(2,1)S(1)}, bf16[192,768]{1,0:T(8,128)(2,1)S(1)}, u32[]{:S(2)}, u32[]{:S(2)}) collective-permute-start(bf16[192,768]{1,0:T(8,128)(2,1)S(1)} %add_convert_fusion.1), channel_id=1, source_target_pairs={{0,32},{32,64},{64,96},{96,0},{1,33},{33,65},{65,97},{97,1},{2,34}... | collective-permute-start | bytes 884744 | tf_op jit(solution)/shard_map/ppermute | solution.py:17
  214.1 14.1 %collective-permute-start.26 = (bf16[192,768]{1,0:T(8,128)(2,1)S(1)}, bf16[192,768]{1,0:T(8,128)(2,1)S(1)}, u32[]{:S(2)}, u32[]{:S(2)}) collective-permute-start(bf16[192,768]{1,0:T(8,128)(2,1)S(1)} %add_convert_fusion), channel_id=1, source_target_pairs={{0,96},{32,0},{64,32},{96,64},{1,97},{33,1},{65,33},{97,65},{2,98}... | collective-permute-start | bytes 884744 | tf_op jit(solution)/shard_map/ppermute | solution.py:17
  230.2 3.0 %collective-permute-start.30 = (f32[64,128]{1,0:T(8,128)S(1)}, f32[64,128]{1,0:T(8,128)S(1)}, u32[]{:S(2)}, u32[]{:S(2)}) collective-permute-start(f32[64,128]{1,0:T(8,128)S(1)} %broadcast_in_dim.7), channel_id=1, source_target_pairs={{0,1},{1,0},{2,3},{3,2},{4,5},{5,4},{6,7},{7,6},{8,9},{9,8},{10,11... | collective-permute-start | bytes 98312 | tf_op jit(solution)/shard_map/ppermute | solution.py:204
  230.4 20.8 %collective-permute-start.27 = (bf16[192,384]{1,0:T(8,128)(2,1)S(1)}, bf16[192,384]{1,0:T(8,128)(2,1)S(1)}, u32[]{:S(2)}, u32[]{:S(2)}) collective-permute-start(bf16[192,384]{1,0:T(8,128)(2,1)S(1)} %get-tuple-element.47), channel_id=1, source_target_pairs={{0,24},{8,0},{16,8},{24,16},{1,25},{9,1},{17,9},{25,17},{2,26},{10... | collective-permute-start | bytes 442376 | tf_op jit(solution)/shard_map/ppermute | solution.py:17
  234.3 15.5 %all-to-all-start.1 = ((f32[64,1,128]{2,1,0:T(1,128)}), f32[64,1,128]{2,1,0:T(1,128)S(1)}, u32[]{:S(2)}, u32[]{:S(2)}) async-start(f32[64,1,128]{2,1,0:T(1,128)} %bitcast.46), calls=%async_computation.1 | async-start | bytes 65536 | tf_op jit(solution)/shard_map/all_to_all | solution.py:205
  240.4 10.8 %collective-permute-start.28 = (bf16[192,384]{1,0:T(8,128)(2,1)S(1)}, bf16[192,384]{1,0:T(8,128)(2,1)S(1)}, u32[]{:S(2)}, u32[]{:S(2)}) collective-permute-start(bf16[192,384]{1,0:T(8,128)(2,1)S(1)} %get-tuple-element.46), channel_id=1, source_target_pairs={{0,16},{8,24},{16,0},{24,8},{1,17},{9,25},{17,1},{25,9},{2,18},{10... | collective-permute-start | bytes 442376 | tf_op jit(solution)/shard_map/ppermute | solution.py:17
  243.5 7.7 %collective-permute-start.29 = (bf16[192,384]{1,0:T(8,128)(2,1)S(1)}, bf16[192,384]{1,0:T(8,128)(2,1)S(1)}, u32[]{:S(2)}, u32[]{:S(2)}) collective-permute-start(bf16[192,384]{1,0:T(8,128)(2,1)S(1)} %get-tuple-element.44), channel_id=1, source_target_pairs={{0,8},{8,16},{16,24},{24,0},{1,9},{9,17},{17,25},{25,1},{2,10},{10... | collective-permute-start | bytes 442376 | tf_op jit(solution)/shard_map/ppermute | solution.py:17
Sparse Core Ops, SparseCore 0:
  9.6 95.4 all-gather.1

commit v4 on v3

--- a/solution.py
+++ b/solution.py
@@ -40,104 +40,154 @@
     )
 
 
-def first_kernel(x_ref, w_ref, t_ref, h_ref, s_ref):
-    hidden = lax.dot_general(w_ref[...], joined(x_ref), NT, preferred_element_type=F32)
-    h_ref[...] = hidden
-    s_ref[...] = slope_of(hidden, t_ref[...])
-
-
-def first_slopes(x, w, t):
+def add_term(s, x, far_ref, total_ref):
+    part = jnp.dot(s, x, preferred_element_type=F32)
+    step = pl.program_id(0)
+
+    @pl.when(step == 0)
+    def _():
+        total_ref[...] = part
+
+    @pl.when(step > 0)
+    def _():
+        total_ref[...] += part
+
+    @pl.when(step == pl.num_programs(0) - 1)
+    def _():
+        far_ref[...] = total_ref[...].astype(BF16)
+
+
+def first_slopes(x, w, t, block):
     blocks, rows, wide = x.shape
     cols = w.shape[0]
     tile = rows // N
-    out = pl.BlockSpec((cols, tile), lambda i: (0, i))
+    per = blocks // N
+    out = pl.BlockSpec((cols, tile), lambda i, which: (0, i))
+
+    def kernel(which_ref, x_ref, w_ref, t_ref, h_ref, s_ref, far_ref, total_ref):
+        hidden = lax.dot_general(w_ref[...], joined(x_ref), NT, preferred_element_type=F32)
+        h_ref[...] = hidden
+        s = slope_of(hidden, t_ref[...])
+        s_ref[...] = s
+        x = jnp.concatenate([x_ref[per * which_ref[0] + k] for k in range(per)], axis=1)
+        add_term(s, x, far_ref, total_ref)
+
     return pl.pallas_call(
-        first_kernel,
-        grid=(N,),
-        in_specs=[
-            pl.BlockSpec((blocks, tile, wide), lambda i: (0, i, 0)),
-            pl.BlockSpec(w.shape, lambda i: (0, 0)),
-            out,
+        kernel,
+        grid_spec=pltpu.PrefetchScalarGridSpec(
+            num_scalar_prefetch=1,
+            grid=(N,),
+            in_specs=[
+                pl.BlockSpec((blocks, tile, wide), lambda i, which: (0, i, 0)),
+                pl.BlockSpec(w.shape, lambda i, which: (0, 0), pipeline_mode=pl.Buffered(1)),
+                out,
+            ],
+            out_specs=[out, out, pl.BlockSpec((cols, per * wide), lambda i, which: (0, 0))],
+            scratch_shapes=[pltpu.VMEM((cols, per * wide), F32)],
+        ),
+        out_shape=[
+            jax.ShapeDtypeStruct((cols, rows), F32),
+            jax.ShapeDtypeStruct((cols, rows), BF16),
+            jax.ShapeDtypeStruct((cols, per * wide), BF16),
         ],
-        out_specs=[out, out],
-        out_shape=[jax.ShapeDtypeStruct((cols, rows), F32), jax.ShapeDtypeStruct((cols, rows), BF16)],
         compiler_params=PARAMS,
-        cost_estimate=cost(cols, blocks * wide, rows, rows * cols),
-    )(x, w, t)
-
-
-def moved_kernel(count, started, last, *refs):
-    refs = list(refs[1:])
-    xs, fs = refs[:count], refs[count : 2 * count]
-    rest = refs[2 * count :]
-    x = jnp.concatenate([x_ref[k] for x_ref in xs for k in range(x_ref.shape[0])], axis=1)
-    f = jnp.concatenate([f_ref[...] for f_ref in fs], axis=1)
-    part = lax.dot_general(f, x, NT, preferred_element_type=F32)
-    if started:
-        part = part + rest.pop(0)[...]
-    if last:
-        scale, hidden, target, out = rest
-        out[...] = slope_of(hidden[...] + scale[0, 0] * part, target[...])
-    else:
-        rest[0][...] = part
-
-
-def moved(x, pieces, which, part=None, last=None):
+        cost_estimate=cost(cols, (blocks + per) * wide, rows, rows * cols),
+    )(jnp.reshape(block, (1,)).astype(jnp.int32), x, w, t)
+
+
+def moved(x, pieces, which):
     blocks, rows, wide = x.shape
     cols, deep = pieces[0].shape
     per = deep // wide
     tile = rows // N
     count = len(pieces)
     at = lambda j: pl.BlockSpec((per, tile, wide), lambda i, which: (which[j], i, 0))
-    out = pl.BlockSpec((cols, tile), lambda i, which: (0, i))
-    specs = [at(j) for j in range(count)] + [pl.BlockSpec((cols, deep), lambda i, which: (0, 0))] * count
-    args = [x] * count + list(pieces)
-    alias = {}
-    if part is not None:
-        if last is None:
-            alias = {1 + len(args): 0}
-        specs.append(out)
-        args.append(part)
-    if last is not None:
-        specs += [pl.BlockSpec(memory_space=pltpu.SMEM), out, out]
-        args += list(last)
-
-    def kernel(*refs):
-        moved_kernel(count, part is not None, last is not None, *refs)
+
+    def kernel(which_ref, *refs):
+        xs, fs = refs[:count], refs[count : 2 * count]
+        x = jnp.concatenate([x_ref[k] for x_ref in xs for k in range(per)], axis=1)
+        f = jnp.concatenate([f_ref[...] for f_ref in fs], axis=1)
+        refs[-1][...] = lax.dot_general(f, x, NT, preferred_element_type=F32)
 
     return pl.pallas_call(
         kernel,
         grid_spec=pltpu.PrefetchScalarGridSpec(
-            num_scalar_prefetch=1, grid=(N,), in_specs=specs, out_specs=out
+            num_scalar_prefetch=1,
+            grid=(N,),
+            in_specs=[at(j) for j in range(count)] + [pl.BlockSpec((cols, deep), lambda i, which: (0, 0))] * count,
+            out_specs=pl.BlockSpec((cols, tile), lambda i, which: (0, i)),
         ),
-        out_shape=jax.ShapeDtypeStruct((cols, rows), F32 if last is None else BF16),
-        input_output_aliases=alias,
+        out_shape=jax.ShapeDtypeStruct((cols, rows), F32),
         compiler_params=PARAMS,
-        cost_estimate=cost(cols, deep * count, rows, 0 if last is None else rows * cols),
-    )(jnp.stack(which).astype(jnp.int32), *args)
-
-
-def terms(x, s, which):
+        cost_estimate=cost(cols, deep * count, rows),
+    )(jnp.stack(which).astype(jnp.int32), *([x] * count), *pieces)
+
+
+def second_slopes(x, piece, block, part, scale, hidden, t):
+    blocks, rows, wide = x.shape
+    cols, deep = piece.shape
+    per = deep // wide
+    tile = rows // N
+    out = pl.BlockSpec((cols, tile), lambda i, which: (0, i))
+    whole = pl.BlockSpec((cols, deep), lambda i, which: (0, 0))
+
+    def kernel(which_ref, scale_ref, x_ref, f_ref, part_ref, h_ref, t_ref, s_ref, far_ref, total_ref):
+        x = joined(x_ref)
+        move = part_ref[...] + lax.dot_general(f_ref[...], x, NT, preferred_element_type=F32)
+        s = slope_of(h_ref[...] + scale_ref[0, 0] * move, t_ref[...])
+        s_ref[...] = s
+        add_term(s, x, far_ref, total_ref)
+
+    return pl.pallas_call(
+        kernel,
+        grid_spec=pltpu.PrefetchScalarGridSpec(
+            num_scalar_prefetch=1,
+            grid=(N,),
+            in_specs=[
+                pl.BlockSpec(memory_space=pltpu.SMEM),
+                pl.BlockSpec((per, tile, wide), lambda i, which: (which[0], i, 0)),
+                whole,
+                out,
+                out,
+                out,
+            ],
+            out_specs=[out, whole],
+            scratch_shapes=[pltpu.VMEM((cols, deep), F32)],
+        ),
+        out_shape=[jax.ShapeDtypeStruct((cols, rows), BF16), jax.ShapeDtypeStruct((cols, deep), BF16)],
+        compiler_params=PARAMS,
+        cost_estimate=cost(cols, 2 * deep, rows, rows * cols),
+    )(jnp.reshape(block, (1,)).astype(jnp.int32), scale, x, piece, part, hidden, t)
+
+
+def terms(x, s, which, cut):
     blocks, rows, wide = x.shape
     cols = s.shape[0]
+    half = cols // 2
     tile = rows // 2
     per = blocks // N
     count = len(which)
     at = lambda j: pl.BlockSpec((per, tile, wide), lambda i, which: (which[j], i, 0))
+    kinds = [F32, BF16, BF16, F32] if cut else [F32] * count
+    tall = half if cut else cols
 
     def kernel(which_ref, *refs):
         s_ref = refs[count]
+        outs, totals = refs[count + 1 : -count], refs[-count:]
         parts = [jnp.dot(s_ref[...], joined(refs[j]), preferred_element_type=F32) for j in range(count)]
 
         @pl.when(pl.program_id(0) == 0)
         def _():
             for j in range(count):
-                refs[count + 1 + j][...] = parts[j]
+                totals[j][...] = parts[j]
 
         @pl.when(pl.program_id(0) > 0)
         def _():
             for j in range(count):
-                refs[count + 1 + j][...] += parts[j]
+                total = totals[j][...] + parts[j]
+                for n in range(cols // tall):
+                    out = outs[j * (cols // tall) + n]
+                    out[...] = total[n * tall : (n + 1) * tall].astype(out.dtype)
 
     return pl.pallas_call(
         kernel,
@@ -145,25 +195,24 @@
             num_scalar_prefetch=1,
             grid=(rows // tile,),
             in_specs=[at(j) for j in range(count)] + [pl.BlockSpec((cols, tile), lambda i, which: (0, i))],
-            out_specs=[pl.BlockSpec((cols, per * wide), lambda i, which: (0, 0))] * count,
+            out_specs=[pl.BlockSpec((tall, per * wide), lambda i, which: (0, 0))] * len(kinds),
+            scratch_shapes=[pltpu.VMEM((cols, per * wide), F32)] * count,
         ),
-        out_shape=[jax.ShapeDtypeStruct((cols, per * wide), F32)] * count,
+        out_shape=[jax.ShapeDtypeStruct((tall, per * wide), kind) for kind in kinds],
         compiler_params=PARAMS,
-        cost_estimate=cost(cols, rows, per * wide * count),
+        cost_estimate=cost(cols * count, rows, per * wide),
     )(jnp.stack(which).astype(jnp.int32), *([x] * count), s)
 
 
-def ring_sum(parts, me):
+def ring_sum(x, s, far, me):
     at = lambda step: lax.rem(me + step, N)
-    far = parts([at(2)])[0].astype(BF16)
     half = far.shape[0] // 2
     far_next, far_prev = shift(far[:half], "x", 1), shift(far[half:], "x", -1)
-    to_next, to_prev = parts([at(1), at(3)])
-    next_low = shift(to_next[half:].astype(BF16), "x", 1)
-    prev_high = shift(to_prev[:half].astype(BF16), "x", -1)
-    next_high = shift((to_next[:half] + far_next.astype(F32)).astype(BF16), "x", 1)
-    prev_low = shift((to_prev[half:] + far_prev.astype(F32)).astype(BF16), "x", -1)
-    own = parts([at(0)])[0]
+    high, to_next, to_prev, low = terms(x, s, [at(1), at(3)], True)
+    next_low, prev_high = shift(to_next, "x", 1), shift(to_prev, "x", -1)
+    next_high = shift((high + far_next.astype(F32)).astype(BF16), "x", 1)
+    prev_low = shift((low + far_prev.astype(F32)).astype(BF16), "x", -1)
+    (own,) = terms(x, s, [at(0)], False)
     high = own[:half] + next_high.astype(F32) + prev_high.astype(F32)
     low = own[half:] + next_low.astype(F32) + prev_low.astype(F32)
     return jnp.concatenate([high, low], axis=0)
@@ -227,15 +276,15 @@
     w_rows = in_order(ring_swap(columns(behind(weight, *first_hop)), "y"), iy).reshape(-1, cols)
     w = in_order(ring_gather(w_rows.T, "x"), ix)
     w = jnp.concatenate([w[k] for k in range(N)], axis=1)
-    hidden, slope = first_slopes(x, w, t)
-    first = ring_sum(lambda bs: terms(x, slope, bs), ix)
+    at = lambda k: lax.rem(ix + k, N)
+    hidden, slope, term = first_slopes(x, w, t, at(2))
+    first = ring_sum(x, slope, term, ix)
     own, after, far, before = ring_gather_halves(first.astype(BF16), "x")
-    at = lambda k: lax.rem(ix + k, N)
     part = moved(x, [own, after, before], [at(0), at(1), at(3)])
     total, part = total_of(first, part)
     scale = 0.5 * math.sqrt(hidden_all) / jnp.sqrt(total + 1e-06)
-    slope = moved(x, [far], [at(2)], part, (scale.reshape(1, 1), hidden, t))
-    second = ring_sum(lambda bs: terms(x, slope, bs), ix)
+    slope, term = second_slopes(x, far, at(2), part, scale.reshape(1, 1), hidden, t)
+    second = ring_sum(x, slope, term, ix)
     total, _ = total_of(second, None)
     factor = jnp.minimum(1.0, math.sqrt(width * hidden_all) / jnp.sqrt(total + 1e-06))
     held = second.astype(BF16).T.reshape(N, -1, cols)

time: 260 us -> 252 us (0.969)
  Pallas kernels: 70 us -> 64.5 us
  local copies, waits for them, and re-layouts: 19.6 us -> 16.2 us
  starting transfers between devices: 57.5 us -> 60.7 us
  waiting for transfers between devices: 81.2 us -> 78.3 us
    pallas_call x1 -> x2, Pallas kernels: 15.1 us -> 29.7 us  [the longest x1 18.7 us: first_slopes(): pl.pallas_call(kernel, grid_spec=pltpu.PrefetchScalarGridSpec(num_scalar_...]
    pallas_call x6 -> x4, Pallas kernels: 34.4 us -> 23.8 us  [terms(): pl.pallas_call(kernel, grid_spec=pltpu.PrefetchScalarGridSpec(num_scalar_...]
    pallas_call x2 -> x1, Pallas kernels: 20.5 us -> 11 us  [moved(): pl.pallas_call(kernel, grid_spec=pltpu.PrefetchScalarGridSpec(num_scalar_...]
    all_gather x1, waiting for transfers between devices: 12.6 us -> 5.3 us  [per_device(): lax.all_gather(tokens, ('z', 'c', 'y'), axis=0, tiled=True)]
    ppermute x29, waiting for transfers between devices: 61 us -> 66 us  [shift(): return lax.ppermute(value, axis, [(i, (i + step) % N) for i in range(N)])]
    ppermute x29, starting transfers between devices: 44.1 us -> 48.1 us  [shift(): return lax.ppermute(value, axis, [(i, (i + step) % N) for i in range(N)])]
    unnamed x43 -> x37, local copies, waits for them, and re-layouts: 7.31 us -> 6.62 us
  transfers between devices with their start and end apart: 34 -> 34, of which waited for: 17 -> 16; matrix products, arithmetic and copies ran while one was open for 12% -> 12% of each run, Pallas kernels for 14% -> 14%
where the time goes in v4:
time: 252 us
  waiting for transfers between devices  78.3 us (31%)
  Pallas kernels  64.5 us (26%)
  starting transfers between devices  60.7 us (24%)
  other arithmetic  16.8 us (7%)
  local copies, waits for them, and re-layouts  16.2 us (6%)
  between operations  15.3 us (6%)
    ppermute x29, waiting for transfers between devices, shift(): return lax.ppermute(value, axis, [(i, (i + step) % N) for i in range(N)])  66 us
    ppermute x29, starting transfers between devices, shift(): return lax.ppermute(value, axis, [(i, (i + step) % N) for i in range(N)])  48.1 us
    pallas_call x4, Pallas kernels, terms(): pl.pallas_call(kernel, grid_spec=pltpu.PrefetchScalarGridSpec(num_scalar_...  23.8 us
    pallas_call x1, Pallas kernels, first_slopes(): pl.pallas_call(kernel, grid_spec=pltpu.PrefetchScalarGridSpec(num_scalar_...  18.7 us
    all_to_all x2, starting transfers between devices, total_of(): lax.all_to_all(total, ('x', 'y', 'z'), split_axis=0, concat_axis=0, tiled...  12.4 us
    pallas_call x1, Pallas kernels, moved(): pl.pallas_call(kernel, grid_spec=pltpu.PrefetchScalarGridSpec(num_scalar_...  11 us
    pallas_call x1, Pallas kernels, second_slopes(): pl.pallas_call(kernel, grid_spec=pltpu.PrefetchScalarGridSpec(num_scalar_...  11 us
    unnamed x37, local copies, waits for them, and re-layouts  6.62 us
  transfers between devices with their start and end apart: 34, of which 16 were waited for; matrix products, arithmetic and copies ran while one was open for 12% of the time, Pallas kernels for 14%

profile of v4, /device:TPU:0, one launch (start us, length us, event | category | flops | bytes accessed | tf_op | source)
XLA Modules:
  0.0 251.8 jit_solution(16305390679108211535)
XLA Ops:
  7.3 1.8 fusion.13
  11.3 1.9 pad_maximum_fusion.5
  13.2 3.1 %collective-permute-start.1 = (bf16[1152,384]{0,1:T(8,128)(2,1)}, bf16[1152,384]{0,1:T(8,128)(2,1)S(1)}, u32[]{:S(2)}, u32[]{:S(2)}) collective-permute-start(bf16[1152,384]{0,1:T(8,128)(2,1)} %pad_maximum_fusion.5), channel_id=1, source_target_pairs={{0,24},{8,0},{16,8},{24,16},{1,25},{9,1},{17,9},{25,17},{2,26},{10... | collective-permute-start | bytes 2654216 | tf_op jit(solution)/shard_map/ppermute | solution.py:17
  16.8 1.0 pad_maximum_fusion.4
  19.1 26.0 %collective-permute-done.1 = bf16[1152,384]{0,1:T(8,128)(2,1)S(1)} collective-permute-done((bf16[1152,384]{0,1:T(8,128)(2,1)}, bf16[1152,384]{0,1:T(8,128)(2,1)S(1)}, u32[]{:S(2)}, u32[]{:S(2)}) %collective-permute-start.1) | collective-permute-done | bytes 884768 | tf_op jit(solution)/shard_map/ppermute | solution.py:17
  45.8 3.6 %collective-permute-start.9 = (bf16[384,384]{0,1:T(8,128)(2,1)}, bf16[384,384]{0,1:T(8,128)(2,1)}, u32[]{:S(2)}, u32[]{:S(2)}) collective-permute-start(bf16[384,384]{0,1:T(8,128)(2,1)} %slice.122), channel_id=1, source_target_pairs={{0,24},{8,0},{16,8},{24,16},{1,25},{9,1},{17,9},{25,17},{2,26},{10... | collective-permute-start | bytes 884744 | tf_op jit(solution)/shard_map/ppermute | solution.py:17
  50.7 4.7 %collective-permute-start.3 = (bf16[192,384]{1,0:T(8,128)(2,1)S(1)}, bf16[192,384]{1,0:T(8,128)(2,1)S(1)}, u32[]{:S(2)}, u32[]{:S(2)}) collective-permute-start(bf16[192,384]{1,0:T(8,128)(2,1)S(1)} %get-tuple-element.67), channel_id=1, source_target_pairs={{0,16},{8,24},{16,0},{24,8},{1,17},{9,25},{17,1},{25,9},{2,18},{10... | collective-permute-start | bytes 442376 | tf_op jit(solution)/shard_map/ppermute | solution.py:17
  56.3 12.1 %collective-permute-done.2 = bf16[192,384]{1,0:T(8,128)(2,1)S(1)} collective-permute-done((bf16[192,384]{1,0:T(8,128)(2,1)S(1)}, bf16[192,384]{1,0:T(8,128)(2,1)S(1)}, u32[]{:S(2)}, u32[]{:S(2)}) %collective-permute-start.2) | collective-permute-done | bytes 147488 | tf_op jit(solution)/shard_map/ppermute | solution.py:17
  68.4 5.3 %collective-permute-done.3 = bf16[192,384]{1,0:T(8,128)(2,1)S(1)} collective-permute-done((bf16[192,384]{1,0:T(8,128)(2,1)S(1)}, bf16[192,384]{1,0:T(8,128)(2,1)S(1)}, u32[]{:S(2)}, u32[]{:S(2)}) %collective-permute-start.3) | collective-permute-done | bytes 147488 | tf_op jit(solution)/shard_map/ppermute | solution.py:17
  74.8 3.2 %collective-permute-start.6 = (bf16[384,768]{1,0:T(8,128)(2,1)S(1)}, bf16[384,768]{1,0:T(8,128)(2,1)S(1)}, u32[]{:S(2)}, u32[]{:S(2)}) collective-permute-start(bf16[384,768]{1,0:T(8,128)(2,1)S(1)} %bitcast.119), channel_id=1, source_target_pairs={{0,64},{32,96},{64,0},{96,32},{1,65},{33,97},{65,1},{97,33},{2,66}... | collective-permute-start | bytes 1769480 | tf_op jit(solution)/shard_map/ppermute | solution.py:17
  78.0 1.1 collective-permute-start.5
  80.1 1.9 fusion.11
  84.6 1.9 fusion.12
  87.4 1.8 dynamic-slice_bitcast_fusion.3
  89.2 8.3 %collective-permute-done.5 = bf16[384,768]{1,0:T(8,128)(2,1)S(1)} collective-permute-done((bf16[384,768]{1,0:T(8,128)(2,1)S(1)}, bf16[384,768]{1,0:T(8,128)(2,1)S(1)}, u32[]{:S(2)}, u32[]{:S(2)}) %collective-permute-start.5) | collective-permute-done | bytes 589856 | tf_op jit(solution)/shard_map/ppermute | solution.py:17
  98.0 2.4 pad_maximum_fusion
  100.4 5.3 %all-gather.2.cloned.1.call-done = bf16[24576,384]{1,0:T(8,128)(2,1)} async-done(((bf16[768,384]{1,0:T(8,128)(2,1)}), bf16[24576,384]{1,0:T(8,128)(2,1)}) %all-gather.2.cloned.1.call-update) | async-done | bytes 18874384 | tf_op jit(solution)/shard_map/all_gather | solution.py:267
  105.7 18.7 %shard_map.37 = (f32[384,3072]{1,0:T(8,128)}, bf16[384,3072]{1,0:T(8,128)(2,1)}, bf16[384,768]{1,0:T(8,128)(2,1)S(1)}) custom-call(s32[1]{0:T(128)} %bitcast.2.which_ref, bf16[8,3072,384]{2,1,0:T(8,128)(2,1)} %bitcast.108, bf16[384,3072]{1,0:T(8,128)(2,1)} %get-tuple-element.69.w_ref, bf16[384,3072]{1,0:T(8,128)(2,1)} %get-tuple-element.70.t_ref), custom_call_target="tpu_custom_call" | custom-call | flops 9059696640 | bytes 31260672 | tf_op jit(solution)/shard_map/pallas_call | solution.py:75
  124.5 1.6 collective-permute-start.10
  126.1 1.7 collective-permute-start.14
  127.8 7.6 %shard_map.39 = (f32[192,768]{1,0:T(8,128)S(1)}, bf16[192,768]{1,0:T(8,128)(2,1)S(1)}, bf16[192,768]{1,0:T(8,128)(2,1)S(1)}, f32[192,768]{1,0:T(8,128)S(1)}) custom-call(s32[2]{0:T(128)S(1)} %pad_add_fusion.which_ref, bf16[8,3072,384]{2,1,0:T(8,128)(2,1)} %bitcast.109, bf16[8,3072,384]{2,1,0:T(8,128)(2,1)} %bitcast.110, ...), custom_call_target="tpu_custom_call" | custom-call | flops 3623878656 | bytes 11796480 | tf_op jit(solution)/shard_map/pallas_call | solution.py:192
  135.4 1.6 collective-permute-start.12
  138.0 3.0 %collective-permute-start.15 = (bf16[192,768]{1,0:T(8,128)(2,1)S(1)}, bf16[192,768]{1,0:T(8,128)(2,1)S(1)}, u32[]{:S(2)}, u32[]{:S(2)}) collective-permute-start(bf16[192,768]{1,0:T(8,128)(2,1)S(1)} %add_convert_fusion.2), channel_id=1, source_target_pairs={{0,96},{32,0},{64,32},{96,64},{1,97},{33,1},{65,33},{97,65},{2,98}... | collective-permute-start | bytes 884744 | tf_op jit(solution)/shard_map/ppermute | solution.py:17
  141.0 4.3 %shard_map.38 = f32[384,768]{1,0:T(8,128)S(1)} custom-call(s32[1]{0:T(128)} %bitcast.which_ref, bf16[8,3072,384]{2,1,0:T(8,128)(2,1)} %bitcast.111, bf16[384,3072]{1,0:T(8,128)(2,1)} %get-tuple-element.22.refs_1_.refs_2_), custom_call_target="tpu_custom_call" | custom-call | flops 1811939328 | bytes 8257536 | tf_op jit(solution)/shard_map/pallas_call | solution.py:192
  145.4 2.8 %collective-permute-done.13 = bf16[192,768]{1,0:T(8,128)(2,1)S(1)} collective-permute-done((bf16[192,768]{1,0:T(8,128)(2,1)S(1)}, bf16[192,768]{1,0:T(8,128)(2,1)S(1)}, u32[]{:S(2)}, u32[]{:S(2)}) %collective-permute-start.13) | collective-permute-done | bytes 294944 | tf_op jit(solution)/shard_map/ppermute | solution.py:17
  148.2 4.7 %collective-permute-done.11 = bf16[192,768]{1,0:T(8,128)(2,1)S(1)} collective-permute-done((bf16[192,768]{1,0:T(8,128)(2,1)S(1)}, bf16[192,768]{1,0:T(8,128)(2,1)S(1)}, u32[]{:S(2)}, u32[]{:S(2)}) %collective-permute-start.11) | collective-permute-done | bytes 294944 | tf_op jit(solution)/shard_map/ppermute | solution.py:17
  153.2 3.2 %collective-permute-start.17 = (bf16[384,768]{1,0:T(8,128)(2,1)S(1)}, bf16[384,768]{1,0:T(8,128)(2,1)S(1)}, u32[]{:S(2)}, u32[]{:S(2)}) collective-permute-start(bf16[384,768]{1,0:T(8,128)(2,1)S(1)} %fusion.1.refs_3_), channel_id=1, source_target_pairs={{0,96},{32,0},{64,32},{96,64},{1,97},{33,1},{65,33},{97,65},{2,98}... | collective-permute-start | bytes 1769480 | tf_op jit(solution)/shard_map/ppermute | solution.py:17
  158.2 1.1 collective-permute-done.16
  159.3 1.3 broadcast_add_fusion.1
  160.6 6.3 %all-to-all-start = ((f32[64,1,128]{2,1,0:T(1,128)}), f32[64,1,128]{2,1,0:T(1,128)S(1)}, u32[]{:S(2)}, u32[]{:S(2)}) async-start(f32[64,1,128]{2,1,0:T(1,128)} %bitcast.31), calls=%async_computation | async-start | bytes 65536 | tf_op jit(solution)/shard_map/all_to_all | solution.py:254
  166.9 1.2 collective-permute-done.18.refs_5_
  168.6 2.9 %collective-permute-start.20 = (bf16[192,768]{1,0:T(8,128)(2,1)S(1)}, bf16[192,768]{1,0:T(8,128)(2,1)S(1)}, u32[]{:S(2)}, u32[]{:S(2)}) collective-permute-start(bf16[192,768]{1,0:T(8,128)(2,1)S(1)} %slice.127), channel_id=1, source_target_pairs={{0,96},{32,0},{64,32},{96,64},{1,97},{33,1},{65,33},{97,65},{2,98}... | collective-permute-start | bytes 884744 | tf_op jit(solution)/shard_map/ppermute | solution.py:17
  171.6 11.0 %shard_map.40.part_ref = f32[384,3072]{1,0:T(8,128)} custom-call(s32[3]{0:T(128)S(1)} %pad_add_fusion.1.which_ref, bf16[8,3072,384]{2,1,0:T(8,128)(2,1)} %bitcast.112, bf16[8,3072,384]{2,1,0:T(8,128)(2,1)} %bitcast.113, bf16[8,3072,384]{2,1,0:T(8,128)(2,1)} %bitcast.114, bf16[384,768]{1,0:T(8,128)(2,1)S(1)} %fusion.1.refs_3_, ...), custom_call_target="tpu_custom_call" | custom-call | flops 5435817984 | bytes 20643840 | tf_op jit(solution)/shard_map/pallas_call | solution.py:112
  183.9 11.0 %shard_map.41 = (bf16[384,3072]{1,0:T(8,128)(2,1)}, bf16[384,768]{1,0:T(8,128)(2,1)S(1)}) custom-call(s32[1]{0:T(128)} %bitcast.2.which_ref, f32[1,1]{1,0:T(1,128)} %bitcast.33.scale_ref, bf16[8,3072,384]{2,1,0:T(8,128)(2,1)} %bitcast.115, bf16[384,768]{1,0:T(8,128)(2,1)S(1)} %pad_maximum_fusion.6.f_ref, f32[384,3072]{1,0:T(8,128)} %shard_map.40.part_ref, ...), custom_call_target="tpu_custom_call" | custom-call | flops 3623878656 | bytes 15335424 | tf_op jit(solution)/shard_map/pallas_call | solution.py:141
  195.1 3.2 %collective-permute-start.25 = (bf16[192,768]{1,0:T(8,128)(2,1)S(1)}, bf16[192,768]{1,0:T(8,128)(2,1)S(1)}, u32[]{:S(2)}, u32[]{:S(2)}) collective-permute-start(bf16[192,768]{1,0:T(8,128)(2,1)S(1)} %get-tuple-element.63), channel_id=1, source_target_pairs={{0,96},{32,0},{64,32},{96,64},{1,97},{33,1},{65,33},{97,65},{2,98}... | collective-permute-start | bytes 884744 | tf_op jit(solution)/shard_map/ppermute | solution.py:17
  198.3 7.5 %shard_map.43 = (f32[192,768]{1,0:T(8,128)S(1)}, bf16[192,768]{1,0:T(8,128)(2,1)S(1)}, bf16[192,768]{1,0:T(8,128)(2,1)S(1)}, f32[192,768]{1,0:T(8,128)S(1)}) custom-call(s32[2]{0:T(128)S(1)} %pad_add_fusion.which_ref, bf16[8,3072,384]{2,1,0:T(8,128)(2,1)} %bitcast.116, bf16[8,3072,384]{2,1,0:T(8,128)(2,1)} %bitcast.117, ...), custom_call_target="tpu_custom_call" | custom-call | flops 3623878656 | bytes 11796480 | tf_op jit(solution)/shard_map/pallas_call | solution.py:192
  206.2 2.0 collective-permute-start.24
  208.4 3.3 %collective-permute-start.26 = (bf16[192,768]{1,0:T(8,128)(2,1)S(1)}, bf16[192,768]{1,0:T(8,128)(2,1)S(1)}, u32[]{:S(2)}, u32[]{:S(2)}) collective-permute-start(bf16[192,768]{1,0:T(8,128)(2,1)S(1)} %add_convert_fusion), channel_id=1, source_target_pairs={{0,96},{32,0},{64,32},{96,64},{1,97},{33,1},{65,33},{97,65},{2,98}... | collective-permute-start | bytes 884744 | tf_op jit(solution)/shard_map/ppermute | solution.py:17
  211.7 4.3 %shard_map.42 = f32[384,768]{1,0:T(8,128)S(1)} custom-call(s32[1]{0:T(128)} %bitcast.which_ref, bf16[8,3072,384]{2,1,0:T(8,128)(2,1)} %bitcast.118, bf16[384,3072]{1,0:T(8,128)(2,1)} %get-tuple-element.31.refs_1_.refs_2_), custom_call_target="tpu_custom_call" | custom-call | flops 1811939328 | bytes 8257536 | tf_op jit(solution)/shard_map/pallas_call | solution.py:192
  216.0 1.1 collective-permute-done.24
  217.1 3.2 %collective-permute-done.22 = bf16[192,768]{1,0:T(8,128)(2,1)S(1)} collective-permute-done((bf16[192,768]{1,0:T(8,128)(2,1)S(1)}, bf16[192,768]{1,0:T(8,128)(2,1)S(1)}, u32[]{:S(2)}, u32[]{:S(2)}) %collective-permute-start.22) | collective-permute-done | bytes 294944 | tf_op jit(solution)/shard_map/ppermute | solution.py:17
  222.4 2.8 %collective-permute-start.27 = (bf16[192,384]{1,0:T(8,128)(2,1)S(1)}, bf16[192,384]{1,0:T(8,128)(2,1)S(1)}, u32[]{:S(2)}, u32[]{:S(2)}) collective-permute-start(bf16[192,384]{1,0:T(8,128)(2,1)S(1)} %get-tuple-element.61), channel_id=1, source_target_pairs={{0,24},{8,0},{16,8},{24,16},{1,25},{9,1},{17,9},{25,17},{2,26},{10... | collective-permute-start | bytes 442376 | tf_op jit(solution)/shard_map/ppermute | solution.py:17
  225.2 1.2 broadcast_add_fusion
  226.3 6.1 %all-to-all-start.1 = ((f32[64,1,128]{2,1,0:T(1,128)}), f32[64,1,128]{2,1,0:T(1,128)S(1)}, u32[]{:S(2)}, u32[]{:S(2)}) async-start(f32[64,1,128]{2,1,0:T(1,128)} %bitcast.46), calls=%async_computation.1 | async-start | bytes 65536 | tf_op jit(solution)/shard_map/all_to_all | solution.py:254
  232.4 1.6 collective-permute-start.29
  234.1 2.7 %collective-permute-start.28 = (bf16[192,384]{1,0:T(8,128)(2,1)S(1)}, bf16[192,384]{1,0:T(8,128)(2,1)S(1)}, u32[]{:S(2)}, u32[]{:S(2)}) collective-permute-start(bf16[192,384]{1,0:T(8,128)(2,1)S(1)} %get-tuple-element.60), channel_id=1, source_target_pairs={{0,16},{8,24},{16,0},{24,8},{1,17},{9,25},{17,1},{25,9},{2,18},{10... | collective-permute-start | bytes 442376 | tf_op jit(solution)/shard_map/ppermute | solution.py:17
  236.8 5.2 %all-to-all-done.1 = f32[64,1,128]{2,1,0:T(1,128)S(1)} async-done(((f32[64,1,128]{2,1,0:T(1,128)}), f32[64,1,128]{2,1,0:T(1,128)S(1)}, u32[]{:S(2)}, u32[]{:S(2)}) %all-to-all-start.1) | async-done | bytes 32800 | tf_op jit(solution)/shard_map/all_to_all | solution.py:254
  243.8 1.1 convert_multiply_fusion
  (111 shorter events, 21.6 us)
Async XLA Ops:
  6.5 3.5 %copy-start = (bf16[768,1536]{1,0:T(8,128)(2,1)S(1)}, bf16[768,1536]{1,0:T(8,128)(2,1)}, u32[]{:S(2)}) copy-start(bf16[768,1536]{1,0:T(8,128)(2,1)} %param.4) | copy-start | bytes 7077892
  6.5 99.2 %all-gather.2.cloned.1.call-start = ((), (), s32[]{:S(2)}) async-start(), calls=%async_computation.2 | async-start | bytes 19464192 | tf_op jit(solution)/shard_map/all_gather | solution.py:267
  11.0 5.3 %copy-start.2 = (bf16[384,384]{1,0:T(8,128)(2,1)S(1)}, bf16[384,384]{1,0:T(8,128)(2,1)}, u32[]{:S(2)}) copy-start(bf16[384,384]{1,0:T(8,128)(2,1)} %get-tuple-element.49) | copy-start | bytes 884740
  13.2 31.8 %collective-permute-start.1 = (bf16[1152,384]{0,1:T(8,128)(2,1)}, bf16[1152,384]{0,1:T(8,128)(2,1)S(1)}, u32[]{:S(2)}, u32[]{:S(2)}) collective-permute-start(bf16[1152,384]{0,1:T(8,128)(2,1)} %pad_maximum_fusion.5), channel_id=1, source_target_pairs={{0,24},{8,0},{16,8},{24,16},{1,25},{9,1},{17,9},{25,17},{2,26},{10... | collective-permute-start | bytes 2654216 | tf_op jit(solution)/shard_map/ppermute | solution.py:17
  16.3 1.5 copy-start.1
  17.8 32.0 %collective-permute-start = (bf16[1152,384]{0,1:T(8,128)(2,1)}, bf16[1152,384]{0,1:T(8,128)(2,1)S(1)}, u32[]{:S(2)}, u32[]{:S(2)}) collective-permute-start(bf16[1152,384]{0,1:T(8,128)(2,1)} %pad_maximum_fusion.4), channel_id=1, source_target_pairs={{0,8},{8,16},{16,24},{24,0},{1,9},{9,17},{17,25},{25,1},{2,10},{10... | collective-permute-start | bytes 2654216 | tf_op jit(solution)/shard_map/ppermute | solution.py:17
  17.8 32.8 %copy-start.3 = (bf16[192,1536]{1,0:T(8,128)(2,1)S(1)}, bf16[192,1536]{1,0:T(8,128)(2,1)}, u32[]{:S(2)}) copy-start(bf16[192,1536]{1,0:T(8,128)(2,1)} %param.5) | copy-start | bytes 1769476
  45.8 34.3 %collective-permute-start.9 = (bf16[384,384]{0,1:T(8,128)(2,1)}, bf16[384,384]{0,1:T(8,128)(2,1)}, u32[]{:S(2)}, u32[]{:S(2)}) collective-permute-start(bf16[384,384]{0,1:T(8,128)(2,1)} %slice.122), channel_id=1, source_target_pairs={{0,24},{8,0},{16,8},{24,16},{1,25},{9,1},{17,9},{25,17},{2,26},{10... | collective-permute-start | bytes 884744 | tf_op jit(solution)/shard_map/ppermute | solution.py:17
  50.6 29.4 %collective-permute-start.8 = (bf16[384,384]{0,1:T(8,128)(2,1)}, bf16[384,384]{0,1:T(8,128)(2,1)}, u32[]{:S(2)}, u32[]{:S(2)}) collective-permute-start(bf16[384,384]{0,1:T(8,128)(2,1)} %slice.121), channel_id=1, source_target_pairs={{0,8},{8,16},{16,24},{24,0},{1,9},{9,17},{17,25},{25,1},{2,10},{10... | collective-permute-start | bytes 884744 | tf_op jit(solution)/shard_map/ppermute | solution.py:17
  50.7 23.6 %collective-permute-start.4 = (bf16[192,384]{1,0:T(8,128)(2,1)S(1)}, bf16[192,384]{1,0:T(8,128)(2,1)S(1)}, u32[]{:S(2)}, u32[]{:S(2)}) collective-permute-start(bf16[192,384]{1,0:T(8,128)(2,1)S(1)} %get-tuple-element.66), channel_id=1, source_target_pairs={{0,8},{8,16},{16,24},{24,0},{1,9},{9,17},{17,25},{25,1},{2,10},{10... | collective-permute-start | bytes 442376 | tf_op jit(solution)/shard_map/ppermute | solution.py:17
  50.7 23.0 %collective-permute-start.3 = (bf16[192,384]{1,0:T(8,128)(2,1)S(1)}, bf16[192,384]{1,0:T(8,128)(2,1)S(1)}, u32[]{:S(2)}, u32[]{:S(2)}) collective-permute-start(bf16[192,384]{1,0:T(8,128)(2,1)S(1)} %get-tuple-element.67), channel_id=1, source_target_pairs={{0,16},{8,24},{16,0},{24,8},{1,17},{9,25},{17,1},{25,9},{2,18},{10... | collective-permute-start | bytes 442376 | tf_op jit(solution)/shard_map/ppermute | solution.py:17
  55.4 12.9 %collective-permute-start.2 = (bf16[192,384]{1,0:T(8,128)(2,1)S(1)}, bf16[192,384]{1,0:T(8,128)(2,1)S(1)}, u32[]{:S(2)}, u32[]{:S(2)}) collective-permute-start(bf16[192,384]{1,0:T(8,128)(2,1)S(1)} %get-tuple-element.68), channel_id=1, source_target_pairs={{0,24},{8,0},{16,8},{24,16},{1,25},{9,1},{17,9},{25,17},{2,26},{10... | collective-permute-start | bytes 442376 | tf_op jit(solution)/shard_map/ppermute | solution.py:17
  74.8 22.7 %collective-permute-start.6 = (bf16[384,768]{1,0:T(8,128)(2,1)S(1)}, bf16[384,768]{1,0:T(8,128)(2,1)S(1)}, u32[]{:S(2)}, u32[]{:S(2)}) collective-permute-start(bf16[384,768]{1,0:T(8,128)(2,1)S(1)} %bitcast.119), channel_id=1, source_target_pairs={{0,64},{32,96},{64,0},{96,32},{1,65},{33,97},{65,1},{97,33},{2,66}... | collective-permute-start | bytes 1769480 | tf_op jit(solution)/shard_map/ppermute | solution.py:17
  78.0 19.5 %collective-permute-start.5 = (bf16[384,768]{1,0:T(8,128)(2,1)S(1)}, bf16[384,768]{1,0:T(8,128)(2,1)S(1)}, u32[]{:S(2)}, u32[]{:S(2)}) collective-permute-start(bf16[384,768]{1,0:T(8,128)(2,1)S(1)} %bitcast.120), channel_id=1, source_target_pairs={{0,96},{32,0},{64,32},{96,64},{1,97},{33,1},{65,33},{97,65},{2,98}... | collective-permute-start | bytes 1769480 | tf_op jit(solution)/shard_map/ppermute | solution.py:17
  79.1 18.5 %collective-permute-start.7 = (bf16[384,768]{1,0:T(8,128)(2,1)S(1)}, bf16[384,768]{1,0:T(8,128)(2,1)S(1)}, u32[]{:S(2)}, u32[]{:S(2)}) collective-permute-start(bf16[384,768]{1,0:T(8,128)(2,1)S(1)} %bitcast.121), channel_id=1, source_target_pairs={{0,32},{32,64},{64,96},{96,0},{1,33},{33,65},{65,97},{97,1},{2,34}... | collective-permute-start | bytes 1769480 | tf_op jit(solution)/shard_map/ppermute | solution.py:17
  124.5 13.0 %collective-permute-start.10 = (bf16[192,768]{1,0:T(8,128)(2,1)S(1)}, bf16[192,768]{1,0:T(8,128)(2,1)S(1)}, u32[]{:S(2)}, u32[]{:S(2)}) collective-permute-start(bf16[192,768]{1,0:T(8,128)(2,1)S(1)} %get-tuple-element.64), channel_id=1, source_target_pairs={{0,32},{32,64},{64,96},{96,0},{1,33},{33,65},{65,97},{97,1},{2,34}... | collective-permute-start | bytes 884744 | tf_op jit(solution)/shard_map/ppermute | solution.py:17
  126.1 11.8 %collective-permute-start.14 = (bf16[192,768]{1,0:T(8,128)(2,1)S(1)}, bf16[192,768]{1,0:T(8,128)(2,1)S(1)}, u32[]{:S(2)}, u32[]{:S(2)}) collective-permute-start(bf16[192,768]{1,0:T(8,128)(2,1)S(1)} %get-tuple-element.65), channel_id=1, source_target_pairs={{0,96},{32,0},{64,32},{96,64},{1,97},{33,1},{65,33},{97,65},{2,98}... | collective-permute-start | bytes 884744 | tf_op jit(solution)/shard_map/ppermute | solution.py:17
  135.4 10.0 %collective-permute-start.12 = (bf16[192,768]{1,0:T(8,128)(2,1)S(1)}, bf16[192,768]{1,0:T(8,128)(2,1)S(1)}, u32[]{:S(2)}, u32[]{:S(2)}) collective-permute-start(bf16[192,768]{1,0:T(8,128)(2,1)S(1)} %get-tuple-element.25), channel_id=1, source_target_pairs={{0,96},{32,0},{64,32},{96,64},{1,97},{33,1},{65,33},{97,65},{2,98}... | collective-permute-start | bytes 884744 | tf_op jit(solution)/shard_map/ppermute | solution.py:17
  137.0 11.2 %collective-permute-start.13 = (bf16[192,768]{1,0:T(8,128)(2,1)S(1)}, bf16[192,768]{1,0:T(8,128)(2,1)S(1)}, u32[]{:S(2)}, u32[]{:S(2)}) collective-permute-start(bf16[192,768]{1,0:T(8,128)(2,1)S(1)} %get-tuple-element.26), channel_id=1, source_target_pairs={{0,32},{32,64},{64,96},{96,0},{1,33},{33,65},{65,97},{97,1},{2,34}... | collective-permute-start | bytes 884744 | tf_op jit(solution)/shard_map/ppermute | solution.py:17
  137.6 15.3 %collective-permute-start.11 = (bf16[192,768]{1,0:T(8,128)(2,1)S(1)}, bf16[192,768]{1,0:T(8,128)(2,1)S(1)}, u32[]{:S(2)}, u32[]{:S(2)}) collective-permute-start(bf16[192,768]{1,0:T(8,128)(2,1)S(1)} %add_convert_fusion.3), channel_id=1, source_target_pairs={{0,32},{32,64},{64,96},{96,0},{1,33},{33,65},{65,97},{97,1},{2,34}... | collective-permute-start | bytes 884744 | tf_op jit(solution)/shard_map/ppermute | solution.py:17
  138.0 14.9 %collective-permute-start.15 = (bf16[192,768]{1,0:T(8,128)(2,1)S(1)}, bf16[192,768]{1,0:T(8,128)(2,1)S(1)}, u32[]{:S(2)}, u32[]{:S(2)}) collective-permute-start(bf16[192,768]{1,0:T(8,128)(2,1)S(1)} %add_convert_fusion.2), channel_id=1, source_target_pairs={{0,96},{32,0},{64,32},{96,64},{1,97},{33,1},{65,33},{97,65},{2,98}... | collective-permute-start | bytes 884744 | tf_op jit(solution)/shard_map/ppermute | solution.py:17
  153.1 15.0 %collective-permute-start.18 = (bf16[384,768]{1,0:T(8,128)(2,1)S(1)}, bf16[384,768]{1,0:T(8,128)(2,1)S(1)}, u32[]{:S(2)}, u32[]{:S(2)}) collective-permute-start(bf16[384,768]{1,0:T(8,128)(2,1)S(1)} %fusion.1.refs_3_), channel_id=1, source_target_pairs={{0,32},{32,64},{64,96},{96,0},{1,33},{33,65},{65,97},{97,1},{2,34}... | collective-permute-start | bytes 1769480 | tf_op jit(solution)/shard_map/ppermute | solution.py:17
  153.2 15.4 %collective-permute-start.17 = (bf16[384,768]{1,0:T(8,128)(2,1)S(1)}, bf16[384,768]{1,0:T(8,128)(2,1)S(1)}, u32[]{:S(2)}, u32[]{:S(2)}) collective-permute-start(bf16[384,768]{1,0:T(8,128)(2,1)S(1)} %fusion.1.refs_3_), channel_id=1, source_target_pairs={{0,96},{32,0},{64,32},{96,64},{1,97},{33,1},{65,33},{97,65},{2,98}... | collective-permute-start | bytes 1769480 | tf_op jit(solution)/shard_map/ppermute | solution.py:17
  158.1 1.3 collective-permute-start.16
  160.6 22.0 %all-to-all-start = ((f32[64,1,128]{2,1,0:T(1,128)}), f32[64,1,128]{2,1,0:T(1,128)S(1)}, u32[]{:S(2)}, u32[]{:S(2)}) async-start(f32[64,1,128]{2,1,0:T(1,128)} %bitcast.31), calls=%async_computation | async-start | bytes 65536 | tf_op jit(solution)/shard_map/all_to_all | solution.py:254
  168.2 15.7 %collective-permute-start.19 = (bf16[192,768]{1,0:T(8,128)(2,1)S(1)}, bf16[192,768]{1,0:T(8,128)(2,1)S(1)}, u32[]{:S(2)}, u32[]{:S(2)}) collective-permute-start(bf16[192,768]{1,0:T(8,128)(2,1)S(1)} %slice.126), channel_id=1, source_target_pairs={{0,32},{32,64},{64,96},{96,0},{1,33},{33,65},{65,97},{97,1},{2,34}... | collective-permute-start | bytes 884744 | tf_op jit(solution)/shard_map/ppermute | solution.py:17
  168.6 15.2 %collective-permute-start.20 = (bf16[192,768]{1,0:T(8,128)(2,1)S(1)}, bf16[192,768]{1,0:T(8,128)(2,1)S(1)}, u32[]{:S(2)}, u32[]{:S(2)}) collective-permute-start(bf16[192,768]{1,0:T(8,128)(2,1)S(1)} %slice.127), channel_id=1, source_target_pairs={{0,96},{32,0},{64,32},{96,64},{1,97},{33,1},{65,33},{97,65},{2,98}... | collective-permute-start | bytes 884744 | tf_op jit(solution)/shard_map/ppermute | solution.py:17
  195.0 13.2 %collective-permute-start.21 = (bf16[192,768]{1,0:T(8,128)(2,1)S(1)}, bf16[192,768]{1,0:T(8,128)(2,1)S(1)}, u32[]{:S(2)}, u32[]{:S(2)}) collective-permute-start(bf16[192,768]{1,0:T(8,128)(2,1)S(1)} %get-tuple-element.62), channel_id=1, source_target_pairs={{0,32},{32,64},{64,96},{96,0},{1,33},{33,65},{65,97},{97,1},{2,34}... | collective-permute-start | bytes 884744 | tf_op jit(solution)/shard_map/ppermute | solution.py:17
  195.1 13.2 %collective-permute-start.25 = (bf16[192,768]{1,0:T(8,128)(2,1)S(1)}, bf16[192,768]{1,0:T(8,128)(2,1)S(1)}, u32[]{:S(2)}, u32[]{:S(2)}) collective-permute-start(bf16[192,768]{1,0:T(8,128)(2,1)S(1)} %get-tuple-element.63), channel_id=1, source_target_pairs={{0,96},{32,0},{64,32},{96,64},{1,97},{33,1},{65,33},{97,65},{2,98}... | collective-permute-start | bytes 884744 | tf_op jit(solution)/shard_map/ppermute | solution.py:17
  205.9 10.1 %collective-permute-start.23 = (bf16[192,768]{1,0:T(8,128)(2,1)S(1)}, bf16[192,768]{1,0:T(8,128)(2,1)S(1)}, u32[]{:S(2)}, u32[]{:S(2)}) collective-permute-start(bf16[192,768]{1,0:T(8,128)(2,1)S(1)} %get-tuple-element.34), channel_id=1, source_target_pairs={{0,96},{32,0},{64,32},{96,64},{1,97},{33,1},{65,33},{97,65},{2,98}... | collective-permute-start | bytes 884744 | tf_op jit(solution)/shard_map/ppermute | solution.py:17
  206.2 10.9 %collective-permute-start.24 = (bf16[192,768]{1,0:T(8,128)(2,1)S(1)}, bf16[192,768]{1,0:T(8,128)(2,1)S(1)}, u32[]{:S(2)}, u32[]{:S(2)}) collective-permute-start(bf16[192,768]{1,0:T(8,128)(2,1)S(1)} %get-tuple-element.35), channel_id=1, source_target_pairs={{0,32},{32,64},{64,96},{96,0},{1,33},{33,65},{65,97},{97,1},{2,34}... | collective-permute-start | bytes 884744 | tf_op jit(solution)/shard_map/ppermute | solution.py:17
  208.2 12.0 %collective-permute-start.22 = (bf16[192,768]{1,0:T(8,128)(2,1)S(1)}, bf16[192,768]{1,0:T(8,128)(2,1)S(1)}, u32[]{:S(2)}, u32[]{:S(2)}) collective-permute-start(bf16[192,768]{1,0:T(8,128)(2,1)S(1)} %add_convert_fusion.1), channel_id=1, source_target_pairs={{0,32},{32,64},{64,96},{96,0},{1,33},{33,65},{65,97},{97,1},{2,34}... | collective-permute-start | bytes 884744 | tf_op jit(solution)/shard_map/ppermute | solution.py:17
  208.4 11.9 %collective-permute-start.26 = (bf16[192,768]{1,0:T(8,128)(2,1)S(1)}, bf16[192,768]{1,0:T(8,128)(2,1)S(1)}, u32[]{:S(2)}, u32[]{:S(2)}) collective-permute-start(bf16[192,768]{1,0:T(8,128)(2,1)S(1)} %add_convert_fusion), channel_id=1, source_target_pairs={{0,96},{32,0},{64,32},{96,64},{1,97},{33,1},{65,33},{97,65},{2,98}... | collective-permute-start | bytes 884744 | tf_op jit(solution)/shard_map/ppermute | solution.py:17
  222.2 2.9 %collective-permute-start.30 = (f32[64,128]{1,0:T(8,128)S(1)}, f32[64,128]{1,0:T(8,128)S(1)}, u32[]{:S(2)}, u32[]{:S(2)}) collective-permute-start(f32[64,128]{1,0:T(8,128)S(1)} %broadcast_in_dim.7), channel_id=1, source_target_pairs={{0,1},{1,0},{2,3},{3,2},{4,5},{5,4},{6,7},{7,6},{8,9},{9,8},{10,11... | collective-permute-start | bytes 98312 | tf_op jit(solution)/shard_map/ppermute | solution.py:253
  222.4 20.8 %collective-permute-start.27 = (bf16[192,384]{1,0:T(8,128)(2,1)S(1)}, bf16[192,384]{1,0:T(8,128)(2,1)S(1)}, u32[]{:S(2)}, u32[]{:S(2)}) collective-permute-start(bf16[192,384]{1,0:T(8,128)(2,1)S(1)} %get-tuple-element.61), channel_id=1, source_target_pairs={{0,24},{8,0},{16,8},{24,16},{1,25},{9,1},{17,9},{25,17},{2,26},{10... | collective-permute-start | bytes 442376 | tf_op jit(solution)/shard_map/ppermute | solution.py:17
  226.3 15.6 %all-to-all-start.1 = ((f32[64,1,128]{2,1,0:T(1,128)}), f32[64,1,128]{2,1,0:T(1,128)S(1)}, u32[]{:S(2)}, u32[]{:S(2)}) async-start(f32[64,1,128]{2,1,0:T(1,128)} %bitcast.46), calls=%async_computation.1 | async-start | bytes 65536 | tf_op jit(solution)/shard_map/all_to_all | solution.py:254
  232.4 11.1 %collective-permute-start.29 = (bf16[192,384]{1,0:T(8,128)(2,1)S(1)}, bf16[192,384]{1,0:T(8,128)(2,1)S(1)}, u32[]{:S(2)}, u32[]{:S(2)}) collective-permute-start(bf16[192,384]{1,0:T(8,128)(2,1)S(1)} %get-tuple-element.58), channel_id=1, source_target_pairs={{0,8},{8,16},{16,24},{24,0},{1,9},{9,17},{17,25},{25,1},{2,10},{10... | collective-permute-start | bytes 442376 | tf_op jit(solution)/shard_map/ppermute | solution.py:17
  234.1 9.4 %collective-permute-start.28 = (bf16[192,384]{1,0:T(8,128)(2,1)S(1)}, bf16[192,384]{1,0:T(8,128)(2,1)S(1)}, u32[]{:S(2)}, u32[]{:S(2)}) collective-permute-start(bf16[192,384]{1,0:T(8,128)(2,1)S(1)} %get-tuple-element.60), channel_id=1, source_target_pairs={{0,16},{8,24},{16,0},{24,8},{1,17},{9,25},{17,1},{25,9},{2,18},{10... | collective-permute-start | bytes 442376 | tf_op jit(solution)/shard_map/ppermute | solution.py:17
Sparse Core Ops, SparseCore 0:
  9.6 96.0 all-gather.1

commit v5 on v4

--- a/solution.py
+++ b/solution.py
@@ -57,42 +57,42 @@
         far_ref[...] = total_ref[...].astype(BF16)
 
 
-def first_slopes(x, w, t, block):
+def first_slopes(x, w, t, which):
     blocks, rows, wide = x.shape
-    cols = w.shape[0]
+    cols, deep = w[0].shape
     tile = rows // N
-    per = blocks // N
+    per = deep // wide
     out = pl.BlockSpec((cols, tile), lambda i, which: (0, i))
-
-    def kernel(which_ref, x_ref, w_ref, t_ref, h_ref, s_ref, far_ref, total_ref):
-        hidden = lax.dot_general(w_ref[...], joined(x_ref), NT, preferred_element_type=F32)
+    whole = pl.BlockSpec((cols, deep), lambda i, which: (0, 0), pipeline_mode=pl.Buffered(1))
+
+    def kernel(which_ref, x_ref, *refs):
+        w_refs, (t_ref, h_ref, s_ref, far_ref, total_ref) = refs[:N], refs[N:]
+        block = lambda j: [x_ref[per * which_ref[j] + k] for k in range(per)]
+        x = jnp.concatenate([part for j in range(N) for part in block(j)], axis=1)
+        w = jnp.concatenate([w_ref[...] for w_ref in w_refs], axis=1)
+        hidden = lax.dot_general(w, x, NT, preferred_element_type=F32)
         h_ref[...] = hidden
         s = slope_of(hidden, t_ref[...])
         s_ref[...] = s
-        x = jnp.concatenate([x_ref[per * which_ref[0] + k] for k in range(per)], axis=1)
-        add_term(s, x, far_ref, total_ref)
+        add_term(s, jnp.concatenate(block(2), axis=1), far_ref, total_ref)
 
     return pl.pallas_call(
         kernel,
         grid_spec=pltpu.PrefetchScalarGridSpec(
             num_scalar_prefetch=1,
             grid=(N,),
-            in_specs=[
-                pl.BlockSpec((blocks, tile, wide), lambda i, which: (0, i, 0)),
-                pl.BlockSpec(w.shape, lambda i, which: (0, 0), pipeline_mode=pl.Buffered(1)),
-                out,
-            ],
-            out_specs=[out, out, pl.BlockSpec((cols, per * wide), lambda i, which: (0, 0))],
-            scratch_shapes=[pltpu.VMEM((cols, per * wide), F32)],
+            in_specs=[pl.BlockSpec((blocks, tile, wide), lambda i, which: (0, i, 0))] + [whole] * N + [out],
+            out_specs=[out, out, pl.BlockSpec((cols, deep), lambda i, which: (0, 0))],
+            scratch_shapes=[pltpu.VMEM((cols, deep), F32)],
         ),
         out_shape=[
             jax.ShapeDtypeStruct((cols, rows), F32),
             jax.ShapeDtypeStruct((cols, rows), BF16),
-            jax.ShapeDtypeStruct((cols, per * wide), BF16),
+            jax.ShapeDtypeStruct((cols, deep), BF16),
         ],
         compiler_params=PARAMS,
         cost_estimate=cost(cols, (blocks + per) * wide, rows, rows * cols),
-    )(jnp.reshape(block, (1,)).astype(jnp.int32), x, w, t)
+    )(jnp.stack(which).astype(jnp.int32), x, *w, t)
 
 
 def moved(x, pieces, which):
@@ -233,14 +233,37 @@
     return [chunk(0), shift(chunk(3), axis, -1), shift(chunk(2), axis, 2), shift(chunk(1), axis, 1)]
 
 
-def ring_swap_halves(chunk, axis):
-    far = chunk(2)
-    half = far.shape[0] // 2
-    rows = 2 * half
-    prev = shift(jnp.concatenate([chunk(1), far[:half]], axis=0), axis, 1)
-    after = shift(jnp.concatenate([chunk(3), far[half:]], axis=0), axis, -1)
+def cut_kernel(which_ref, own, after, far, before, to_next, to_prev, kept):
+    rows = own.shape[0]
+    half = rows // 2
+    to_next[:rows], to_next[rows:] = after[...], far[:half]
+    to_prev[:rows], to_prev[rows:] = before[...], far[half:]
+    kept[...] = own[...]
+
+
+def cut(array, me):
+    rows, cols = array.shape[0], array.shape[1] // N
+    at = lambda k: pl.BlockSpec((rows, cols), lambda i, which: (0, which[k]))
+    tall = [rows + rows // 2, rows + rows // 2, rows]
+    return pl.pallas_call(
+        cut_kernel,
+        grid_spec=pltpu.PrefetchScalarGridSpec(
+            num_scalar_prefetch=1,
+            grid=(1,),
+            in_specs=[at(k) for k in range(N)],
+            out_specs=[pl.BlockSpec((size, cols), lambda i, which: (0, 0)) for size in tall],
+        ),
+        out_shape=[jax.ShapeDtypeStruct((size, cols), array.dtype) for size in tall],
+        compiler_params=PARAMS,
+        cost_estimate=cost(0, 0, 0),
+    )(jnp.stack([lax.rem(me + k, N) for k in range(N)]).astype(jnp.int32), *([array] * N))
+
+
+def ring_swap_halves(to_next, to_prev, kept, axis):
+    rows = kept.shape[0]
+    prev, after = shift(to_next, axis, 1), shift(to_prev, axis, -1)
     high, low = shift(prev[rows:], axis, 1), shift(after[rows:], axis, -1)
-    return [chunk(0), after[:rows], jnp.concatenate([high, low], axis=0), prev[:rows]], (prev, after)
+    return [kept, after[:rows], jnp.concatenate([high, low], axis=0), prev[:rows]]
 
 
 def in_order(pieces, me):
@@ -269,15 +292,15 @@
     def columns(array):
         return lambda k: lax.dynamic_slice_in_dim(array, lax.rem(iy + k, N) * cols, cols, axis=1)
 
-    t_pieces, first_hop = ring_swap_halves(columns(target), "y")
-    t = in_order(t_pieces, iy)
+    to_next, to_prev, kept = cut(target, iy)
+    w_pieces = ring_swap(columns(weight), "y")
+    to_next, to_prev = lax.optimization_barrier((to_next, to_prev, *w_pieces))[:2]
+    t = in_order(ring_swap_halves(to_next, to_prev, kept, "y"), iy)
     t = jnp.concatenate([t[k].T for k in range(N)], axis=1)
-
-    w_rows = in_order(ring_swap(columns(behind(weight, *first_hop)), "y"), iy).reshape(-1, cols)
-    w = in_order(ring_gather(w_rows.T, "x"), ix)
-    w = jnp.concatenate([w[k] for k in range(N)], axis=1)
+    w = ring_gather(in_order(w_pieces, iy).reshape(-1, cols).T, "x")
+
     at = lambda k: lax.rem(ix + k, N)
-    hidden, slope, term = first_slopes(x, w, t, at(2))
+    hidden, slope, term = first_slopes(x, w, t, [at(k) for k in range(N)])
     first = ring_sum(x, slope, term, ix)
     own, after, far, before = ring_gather_halves(first.astype(BF16), "x")
     part = moved(x, [own, after, before], [at(0), at(1), at(3)])

time: 252 us -> 248 us (0.984)
  waiting for transfers between devices: 78.3 us -> 62.3 us
  local copies, waits for them, and re-layouts: 16.2 us -> 27.1 us
  Pallas kernels: 64.5 us -> 68.3 us
  other arithmetic: 16.8 us -> 13.4 us
    ppermute x29, waiting for transfers between devices: 66 us -> 44.3 us  [shift(): return lax.ppermute(value, axis, [(i, (i + step) % N) for i in range(N)])]
    unnamed x37 -> x26, local copies, waits for them, and re-layouts: 6.62 us -> 13.7 us
    all_gather x1, waiting for transfers between devices: 5.3 us -> 11 us  [per_device(): lax.all_gather(tokens, ('z', 'c', 'y'), axis=0, tiled=True)]
    concatenate x3 -> x1, other arithmetic: 5.39 us -> 1.75 us  [per_device(): t = jnp.concatenate([t[k].T for k in range(N)], axis=1)]
    pallas_call x0 -> x1, Pallas kernels: none -> 3.2 us  [cut(): pl.pallas_call(cut_kernel, grid_spec=pltpu.PrefetchScalarGridSpec(num_sca...]
    optimization_barrier x0 -> x2, local copies, waits for them, and re-layouts: none -> 3.07 us  [per_device(): lax.optimization_barrier((to_next, to_prev, *w_pieces))[:2]]
  transfers between devices with their start and end apart: 34 -> 34, of which waited for: 16 -> 14; matrix products, arithmetic and copies ran while one was open for 12% -> 14% of each run, Pallas kernels for 14% -> 15%
where the time goes in v5:
time: 248 us
  Pallas kernels  68.3 us (28%)
  waiting for transfers between devices  62.3 us (25%)
  starting transfers between devices  61.5 us (25%)
  local copies, waits for them, and re-layouts  27.1 us (11%)
  between operations  15.2 us (6%)
  other arithmetic  13.4 us (5%)
    ppermute x29, starting transfers between devices, shift(): return lax.ppermute(value, axis, [(i, (i + step) % N) for i in range(N)])  49.1 us
    ppermute x29, waiting for transfers between devices, shift(): return lax.ppermute(value, axis, [(i, (i + step) % N) for i in range(N)])  44.3 us
    pallas_call x4, Pallas kernels, terms(): pl.pallas_call(kernel, grid_spec=pltpu.PrefetchScalarGridSpec(num_scalar_...  23.8 us
    pallas_call x1, Pallas kernels, first_slopes(): pl.pallas_call(kernel, grid_spec=pltpu.PrefetchScalarGridSpec(num_scalar_...  19.2 us
    unnamed x26, local copies, waits for them, and re-layouts  13.7 us
    all_to_all x2, starting transfers between devices, total_of(): lax.all_to_all(total, ('x', 'y', 'z'), split_axis=0, concat_axis=0, tiled...  12.2 us
    pallas_call x1, Pallas kernels, moved(): pl.pallas_call(kernel, grid_spec=pltpu.PrefetchScalarGridSpec(num_scalar_...  11 us
    pallas_call x1, Pallas kernels, second_slopes(): pl.pallas_call(kernel, grid_spec=pltpu.PrefetchScalarGridSpec(num_scalar_...  11 us
  transfers between devices with their start and end apart: 34, of which 14 were waited for; matrix products, arithmetic and copies ran while one was open for 14% of the time, Pallas kernels for 15%

profile of v5, /device:TPU:0, one launch (start us, length us, event | category | flops | bytes accessed | tf_op | source)
XLA Modules:
  0.0 247.8 jit_solution(1020372847333581826)
XLA Ops:
  7.3 1.8 constant_dynamic-slice_fusion.1
  9.1 1.7 collective-permute-start.2
  10.7 1.6 collective-permute-start
  12.3 2.1 collective-permute-start.1
  14.5 3.2 %shard_map.37 = (bf16[1152,384]{1,0:T(8,128)(2,1)S(1)}, bf16[1152,384]{1,0:T(8,128)(2,1)}, bf16[768,384]{1,0:T(8,128)(2,1)S(1)}) custom-call(s32[4]{0:T(128)S(1)} %pad_add_fusion.1.which_ref, bf16[768,1536]{1,0:T(8,128)(2,1)} %before.1, bf16[768,1536]{1,0:T(8,128)(2,1)} %before.1, bf16[768,1536]{1,0:T(8,128)(2,1)} %before.1, bf16[768,1536]{1,0:T(8,128)(2,1)} %before.1), custom_call_target="tpu_custom_call" | custom-call | tf_op jit(solution)/shard_map/pallas_call | solution.py:248
  18.9 1.6 bitcast_dynamic-update-slice_fusion.14
  20.7 1.6 copy.19
  22.2 1.5 copy.20
  24.7 2.3 collective-permute-start.6
  27.7 1.6 bitcast_dynamic-update-slice_fusion.10
  29.9 1.6 bitcast_dynamic-update-slice_fusion.15
  32.2 1.6 bitcast_dynamic-update-slice_fusion.11
  34.4 20.1 %collective-permute-done.7 = bf16[1152,384]{0,1:T(8,128)(2,1)S(1)} collective-permute-done((bf16[1152,384]{0,1:T(8,128)(2,1)}, bf16[1152,384]{0,1:T(8,128)(2,1)S(1)}, u32[]{:S(2)}, u32[]{:S(2)}) %collective-permute-start.7) | collective-permute-done | bytes 884768 | tf_op jit(solution)/shard_map/ppermute | solution.py:17
  56.1 3.2 %collective-permute-start.9 = (bf16[384,384]{0,1:T(8,128)(2,1)}, bf16[384,384]{0,1:T(8,128)(2,1)}, u32[]{:S(2)}, u32[]{:S(2)}) collective-permute-start(bf16[384,384]{0,1:T(8,128)(2,1)} %slice.98), channel_id=1, source_target_pairs={{0,24},{8,0},{16,8},{24,16},{1,25},{9,1},{17,9},{25,17},{2,26},{10... | collective-permute-start | bytes 884744 | tf_op jit(solution)/shard_map/ppermute | solution.py:17
  60.9 1.5 collective-permute-start.5
  62.4 2.7 %collective-permute-start.4 = (bf16[384,768]{1,0:T(8,128)(2,1)S(1)}, bf16[384,768]{1,0:T(8,128)(2,1)S(1)}, u32[]{:S(2)}, u32[]{:S(2)}) collective-permute-start(bf16[384,768]{1,0:T(8,128)(2,1)S(1)} %bitcast.92), channel_id=1, source_target_pairs={{0,64},{32,96},{64,0},{96,32},{1,65},{33,97},{65,1},{97,33},{2,66}... | collective-permute-start | bytes 1769480 | tf_op jit(solution)/shard_map/ppermute | solution.py:17
  67.4 5.1 %collective-permute-done.8 = bf16[384,384]{0,1:T(8,128)(2,1)} collective-permute-done((bf16[384,384]{0,1:T(8,128)(2,1)}, bf16[384,384]{0,1:T(8,128)(2,1)}, u32[]{:S(2)}, u32[]{:S(2)}) %collective-permute-start.8) | collective-permute-done | bytes 294944 | tf_op jit(solution)/shard_map/ppermute | solution.py:17
  72.7 1.9 fusion.11
  77.3 1.9 fusion.12
  80.0 1.8 dynamic-slice_bitcast_fusion.3
  81.8 1.8 pad_maximum_fusion.refs_4_.t_ref
  83.6 6.1 %collective-permute-done.4.refs_2_ = bf16[384,768]{1,0:T(8,128)(2,1)S(1)} collective-permute-done((bf16[384,768]{1,0:T(8,128)(2,1)S(1)}, bf16[384,768]{1,0:T(8,128)(2,1)S(1)}, u32[]{:S(2)}, u32[]{:S(2)}) %collective-permute-start.4) | collective-permute-done | bytes 589856 | tf_op jit(solution)/shard_map/ppermute | solution.py:17
  90.5 11.0 %all-gather.2.cloned.1.call-done = bf16[24576,384]{1,0:T(8,128)(2,1)} async-done(((bf16[768,384]{1,0:T(8,128)(2,1)}), bf16[24576,384]{1,0:T(8,128)(2,1)}) %all-gather.2.cloned.1.call-update) | async-done | bytes 18874384 | tf_op jit(solution)/shard_map/all_gather | solution.py:290
  101.4 19.2 %shard_map.38 = (f32[384,3072]{1,0:T(8,128)}, bf16[384,3072]{1,0:T(8,128)(2,1)}, bf16[384,768]{1,0:T(8,128)(2,1)S(1)}) custom-call(s32[4]{0:T(128)S(1)} %pad_add_fusion.which_ref, bf16[8,3072,384]{2,1,0:T(8,128)(2,1)} %bitcast.95, bf16[384,768]{1,0:T(8,128)(2,1)S(1)} %bitcast.94, bf16[384,768]{1,0:T(8,128)(2,1)S(1)} %collective-permute-done.3.refs_1_, ...), custom_call_target="tpu_custom_call" | custom-call | flops 9059696640 | bytes 31260672 | tf_op jit(solution)/shard_map/pallas_call | solution.py:79
  120.7 1.5 collective-permute-start.10
  122.2 1.8 collective-permute-start.14
  124.0 7.6 %shard_map.40 = (f32[192,768]{1,0:T(8,128)S(1)}, bf16[192,768]{1,0:T(8,128)(2,1)S(1)}, bf16[192,768]{1,0:T(8,128)(2,1)S(1)}, f32[192,768]{1,0:T(8,128)S(1)}) custom-call(s32[2]{0:T(128)S(1)} %pad_add_fusion.2.which_ref, bf16[8,3072,384]{2,1,0:T(8,128)(2,1)} %bitcast.96, bf16[8,3072,384]{2,1,0:T(8,128)(2,1)} %bitcast.97, ...), custom_call_target="tpu_custom_call" | custom-call | flops 3623878656 | bytes 11796480 | tf_op jit(solution)/shard_map/pallas_call | solution.py:192
  131.6 1.5 collective-permute-start.12
  134.3 3.1 %collective-permute-start.15 = (bf16[192,768]{1,0:T(8,128)(2,1)S(1)}, bf16[192,768]{1,0:T(8,128)(2,1)S(1)}, u32[]{:S(2)}, u32[]{:S(2)}) collective-permute-start(bf16[192,768]{1,0:T(8,128)(2,1)S(1)} %add_convert_fusion.2), channel_id=1, source_target_pairs={{0,96},{32,0},{64,32},{96,64},{1,97},{33,1},{65,33},{97,65},{2,98}... | collective-permute-start | bytes 884744 | tf_op jit(solution)/shard_map/ppermute | solution.py:17
  137.4 4.3 %shard_map.39 = f32[384,768]{1,0:T(8,128)S(1)} custom-call(s32[1]{0:T(128)} %bitcast.which_ref, bf16[8,3072,384]{2,1,0:T(8,128)(2,1)} %bitcast.98, bf16[384,3072]{1,0:T(8,128)(2,1)} %get-tuple-element.30.refs_1_.refs_2_), custom_call_target="tpu_custom_call" | custom-call | flops 1811939328 | bytes 8257536 | tf_op jit(solution)/shard_map/pallas_call | solution.py:192
  141.8 2.5 %collective-permute-done.13 = bf16[192,768]{1,0:T(8,128)(2,1)S(1)} collective-permute-done((bf16[192,768]{1,0:T(8,128)(2,1)S(1)}, bf16[192,768]{1,0:T(8,128)(2,1)S(1)}, u32[]{:S(2)}, u32[]{:S(2)}) %collective-permute-start.13) | collective-permute-done | bytes 294944 | tf_op jit(solution)/shard_map/ppermute | solution.py:17
  144.3 4.7 %collective-permute-done.11 = bf16[192,768]{1,0:T(8,128)(2,1)S(1)} collective-permute-done((bf16[192,768]{1,0:T(8,128)(2,1)S(1)}, bf16[192,768]{1,0:T(8,128)(2,1)S(1)}, u32[]{:S(2)}, u32[]{:S(2)}) %collective-permute-start.11) | collective-permute-done | bytes 294944 | tf_op jit(solution)/shard_map/ppermute | solution.py:17
  149.3 3.2 %collective-permute-start.17 = (bf16[384,768]{1,0:T(8,128)(2,1)S(1)}, bf16[384,768]{1,0:T(8,128)(2,1)S(1)}, u32[]{:S(2)}, u32[]{:S(2)}) collective-permute-start(bf16[384,768]{1,0:T(8,128)(2,1)S(1)} %fusion.1.refs_3_), channel_id=1, source_target_pairs={{0,96},{32,0},{64,32},{96,64},{1,97},{33,1},{65,33},{97,65},{2,98}... | collective-permute-start | bytes 1769480 | tf_op jit(solution)/shard_map/ppermute | solution.py:17
  156.8 6.1 %all-to-all-start = ((f32[64,1,128]{2,1,0:T(1,128)}), f32[64,1,128]{2,1,0:T(1,128)S(1)}, u32[]{:S(2)}, u32[]{:S(2)}) async-start(f32[64,1,128]{2,1,0:T(1,128)} %bitcast.27), calls=%async_computation | async-start | bytes 65536 | tf_op jit(solution)/shard_map/all_to_all | solution.py:277
  164.6 3.0 %collective-permute-start.20 = (bf16[192,768]{1,0:T(8,128)(2,1)S(1)}, bf16[192,768]{1,0:T(8,128)(2,1)S(1)}, u32[]{:S(2)}, u32[]{:S(2)}) collective-permute-start(bf16[192,768]{1,0:T(8,128)(2,1)S(1)} %slice.103), channel_id=1, source_target_pairs={{0,96},{32,0},{64,32},{96,64},{1,97},{33,1},{65,33},{97,65},{2,98}... | collective-permute-start | bytes 884744 | tf_op jit(solution)/shard_map/ppermute | solution.py:17
  167.7 11.0 %shard_map.41.part_ref = f32[384,3072]{1,0:T(8,128)} custom-call(s32[3]{0:T(128)S(1)} %pad_add_fusion.3.which_ref, bf16[8,3072,384]{2,1,0:T(8,128)(2,1)} %bitcast.99, bf16[8,3072,384]{2,1,0:T(8,128)(2,1)} %bitcast.100, bf16[8,3072,384]{2,1,0:T(8,128)(2,1)} %bitcast.101, bf16[384,768]{1,0:T(8,128)(2,1)S(1)} %fusion.1.refs_3_, ...), custom_call_target="tpu_custom_call" | custom-call | flops 5435817984 | bytes 20643840 | tf_op jit(solution)/shard_map/pallas_call | solution.py:112
  180.1 11.0 %shard_map.42 = (bf16[384,3072]{1,0:T(8,128)(2,1)}, bf16[384,768]{1,0:T(8,128)(2,1)S(1)}) custom-call(s32[1]{0:T(128)} %bitcast.2.which_ref, f32[1,1]{1,0:T(1,128)} %bitcast.29.scale_ref, bf16[8,3072,384]{2,1,0:T(8,128)(2,1)} %bitcast.102, bf16[384,768]{1,0:T(8,128)(2,1)S(1)} %pad_maximum_fusion.3.f_ref, f32[384,3072]{1,0:T(8,128)} %shard_map.41.part_ref, ...), custom_call_target="tpu_custom_call" | custom-call | flops 3623878656 | bytes 15335424 | tf_op jit(solution)/shard_map/pallas_call | solution.py:141
  191.2 3.2 %collective-permute-start.25 = (bf16[192,768]{1,0:T(8,128)(2,1)S(1)}, bf16[192,768]{1,0:T(8,128)(2,1)S(1)}, u32[]{:S(2)}, u32[]{:S(2)}) collective-permute-start(bf16[192,768]{1,0:T(8,128)(2,1)S(1)} %get-tuple-element.64), channel_id=1, source_target_pairs={{0,96},{32,0},{64,32},{96,64},{1,97},{33,1},{65,33},{97,65},{2,98}... | collective-permute-start | bytes 884744 | tf_op jit(solution)/shard_map/ppermute | solution.py:17
  194.4 7.6 %shard_map.44 = (f32[192,768]{1,0:T(8,128)S(1)}, bf16[192,768]{1,0:T(8,128)(2,1)S(1)}, bf16[192,768]{1,0:T(8,128)(2,1)S(1)}, f32[192,768]{1,0:T(8,128)S(1)}) custom-call(s32[2]{0:T(128)S(1)} %pad_add_fusion.2.which_ref, bf16[8,3072,384]{2,1,0:T(8,128)(2,1)} %bitcast.103, bf16[8,3072,384]{2,1,0:T(8,128)(2,1)} %bitcast.104, ...), custom_call_target="tpu_custom_call" | custom-call | flops 3623878656 | bytes 11796480 | tf_op jit(solution)/shard_map/pallas_call | solution.py:192
  202.1 2.0 collective-permute-start.24
  204.3 3.5 %collective-permute-start.26 = (bf16[192,768]{1,0:T(8,128)(2,1)S(1)}, bf16[192,768]{1,0:T(8,128)(2,1)S(1)}, u32[]{:S(2)}, u32[]{:S(2)}) collective-permute-start(bf16[192,768]{1,0:T(8,128)(2,1)S(1)} %add_convert_fusion), channel_id=1, source_target_pairs={{0,96},{32,0},{64,32},{96,64},{1,97},{33,1},{65,33},{97,65},{2,98}... | collective-permute-start | bytes 884744 | tf_op jit(solution)/shard_map/ppermute | solution.py:17
  207.8 4.3 %shard_map.43 = f32[384,768]{1,0:T(8,128)S(1)} custom-call(s32[1]{0:T(128)} %bitcast.which_ref, bf16[8,3072,384]{2,1,0:T(8,128)(2,1)} %bitcast.105, bf16[384,3072]{1,0:T(8,128)(2,1)} %get-tuple-element.39.refs_1_.refs_2_), custom_call_target="tpu_custom_call" | custom-call | flops 1811939328 | bytes 8257536 | tf_op jit(solution)/shard_map/pallas_call | solution.py:192
  212.9 3.2 %collective-permute-done.22 = bf16[192,768]{1,0:T(8,128)(2,1)S(1)} collective-permute-done((bf16[192,768]{1,0:T(8,128)(2,1)S(1)}, bf16[192,768]{1,0:T(8,128)(2,1)S(1)}, u32[]{:S(2)}, u32[]{:S(2)}) %collective-permute-start.22) | collective-permute-done | bytes 294944 | tf_op jit(solution)/shard_map/ppermute | solution.py:17
  218.3 2.7 %collective-permute-start.27 = (bf16[192,384]{1,0:T(8,128)(2,1)S(1)}, bf16[192,384]{1,0:T(8,128)(2,1)S(1)}, u32[]{:S(2)}, u32[]{:S(2)}) collective-permute-start(bf16[192,384]{1,0:T(8,128)(2,1)S(1)} %get-tuple-element.62), channel_id=1, source_target_pairs={{0,24},{8,0},{16,8},{24,16},{1,25},{9,1},{17,9},{25,17},{2,26},{10... | collective-permute-start | bytes 442376 | tf_op jit(solution)/shard_map/ppermute | solution.py:17
  222.3 6.1 %all-to-all-start.1 = ((f32[64,1,128]{2,1,0:T(1,128)}), f32[64,1,128]{2,1,0:T(1,128)S(1)}, u32[]{:S(2)}, u32[]{:S(2)}) async-start(f32[64,1,128]{2,1,0:T(1,128)} %bitcast.42), calls=%async_computation.1 | async-start | bytes 65536 | tf_op jit(solution)/shard_map/all_to_all | solution.py:277
  228.4 1.6 collective-permute-start.29
  230.0 2.7 %collective-permute-start.28 = (bf16[192,384]{1,0:T(8,128)(2,1)S(1)}, bf16[192,384]{1,0:T(8,128)(2,1)S(1)}, u32[]{:S(2)}, u32[]{:S(2)}) collective-permute-start(bf16[192,384]{1,0:T(8,128)(2,1)S(1)} %get-tuple-element.61), channel_id=1, source_target_pairs={{0,16},{8,24},{16,0},{24,8},{1,17},{9,25},{17,1},{25,9},{2,18},{10... | collective-permute-start | bytes 442376 | tf_op jit(solution)/shard_map/ppermute | solution.py:17
  232.7 5.2 %all-to-all-done.1 = f32[64,1,128]{2,1,0:T(1,128)S(1)} async-done(((f32[64,1,128]{2,1,0:T(1,128)}), f32[64,1,128]{2,1,0:T(1,128)S(1)}, u32[]{:S(2)}, u32[]{:S(2)}) %all-to-all-start.1) | async-done | bytes 32800 | tf_op jit(solution)/shard_map/all_to_all | solution.py:277
  (99 shorter events, 30.7 us)
Async XLA Ops:
  6.5 94.9 %all-gather.2.cloned.1.call-start = ((), (), s32[]{:S(2)}) async-start(), calls=%async_computation.2 | async-start | bytes 19464192 | tf_op jit(solution)/shard_map/all_gather | solution.py:290
  9.1 11.5 %collective-permute-start.2 = (bf16[192,384]{1,0:T(8,128)(2,1)}, bf16[192,384]{1,0:T(8,128)(2,1)S(1)}, u32[]{:S(2)}, u32[]{:S(2)}) collective-permute-start(bf16[192,384]{1,0:T(8,128)(2,1)} %get-tuple-element.67), channel_id=1, source_target_pairs={{0,8},{8,16},{16,24},{24,0},{1,9},{9,17},{17,25},{25,1},{2,10},{10... | collective-permute-start | bytes 442376 | tf_op jit(solution)/shard_map/ppermute | solution.py:17
  10.7 9.9 %collective-permute-start = (bf16[192,384]{1,0:T(8,128)(2,1)S(1)}, bf16[192,384]{1,0:T(8,128)(2,1)S(1)}, u32[]{:S(2)}, u32[]{:S(2)}) collective-permute-start(bf16[192,384]{1,0:T(8,128)(2,1)S(1)} %get-tuple-element.68), channel_id=1, source_target_pairs={{0,24},{8,0},{16,8},{24,16},{1,25},{9,1},{17,9},{25,17},{2,26},{10... | collective-permute-start | bytes 442376 | tf_op jit(solution)/shard_map/ppermute | solution.py:17
  12.3 8.4 %collective-permute-start.1 = (bf16[192,384]{1,0:T(8,128)(2,1)S(1)}, bf16[192,384]{1,0:T(8,128)(2,1)}, u32[]{:S(2)}, u32[]{:S(2)}) collective-permute-start(bf16[192,384]{1,0:T(8,128)(2,1)S(1)} %get-tuple-element.69), channel_id=1, source_target_pairs={{0,16},{8,24},{16,0},{24,8},{1,17},{9,25},{17,1},{25,9},{2,18},{10... | collective-permute-start | bytes 442376 | tf_op jit(solution)/shard_map/ppermute | solution.py:17
  17.6 3.0 %copy-start = (bf16[1152,384]{1,0:T(8,128)(2,1)S(1)}, bf16[1152,384]{1,0:T(8,128)(2,1)}, u32[]{:S(2)}) copy-start(bf16[1152,384]{1,0:T(8,128)(2,1)} %get-tuple-element.28) | copy-start | bytes 2654212
  22.2 2.5 copy-start.1
  23.7 30.8 %collective-permute-start.7 = (bf16[1152,384]{0,1:T(8,128)(2,1)}, bf16[1152,384]{0,1:T(8,128)(2,1)S(1)}, u32[]{:S(2)}, u32[]{:S(2)}) collective-permute-start(bf16[1152,384]{0,1:T(8,128)(2,1)} %copy.20), channel_id=1, source_target_pairs={{0,8},{8,16},{16,24},{24,0},{1,9},{9,17},{17,25},{25,1},{2,10},{10... | collective-permute-start | bytes 2654216 | tf_op jit(solution)/shard_map/ppermute | solution.py:17
  24.7 30.7 %collective-permute-start.6 = (bf16[1152,384]{0,1:T(8,128)(2,1)S(1)}, bf16[1152,384]{0,1:T(8,128)(2,1)S(1)}, u32[]{:S(2)}, u32[]{:S(2)}) collective-permute-start(bf16[1152,384]{0,1:T(8,128)(2,1)S(1)} %copy-done.1), channel_id=1, source_target_pairs={{0,24},{8,0},{16,8},{24,16},{1,25},{9,1},{17,9},{25,17},{2,26},{10... | collective-permute-start | bytes 2654216 | tf_op jit(solution)/shard_map/ppermute | solution.py:17
  55.4 17.2 %collective-permute-start.8 = (bf16[384,384]{0,1:T(8,128)(2,1)}, bf16[384,384]{0,1:T(8,128)(2,1)}, u32[]{:S(2)}, u32[]{:S(2)}) collective-permute-start(bf16[384,384]{0,1:T(8,128)(2,1)} %slice.97), channel_id=1, source_target_pairs={{0,8},{8,16},{16,24},{24,0},{1,9},{9,17},{17,25},{25,1},{2,10},{10... | collective-permute-start | bytes 884744 | tf_op jit(solution)/shard_map/ppermute | solution.py:17
  56.1 16.6 %collective-permute-start.9 = (bf16[384,384]{0,1:T(8,128)(2,1)}, bf16[384,384]{0,1:T(8,128)(2,1)}, u32[]{:S(2)}, u32[]{:S(2)}) collective-permute-start(bf16[384,384]{0,1:T(8,128)(2,1)} %slice.98), channel_id=1, source_target_pairs={{0,24},{8,0},{16,8},{24,16},{1,25},{9,1},{17,9},{25,17},{2,26},{10... | collective-permute-start | bytes 884744 | tf_op jit(solution)/shard_map/ppermute | solution.py:17
  60.9 22.7 %collective-permute-start.5 = (bf16[384,768]{1,0:T(8,128)(2,1)S(1)}, bf16[384,768]{1,0:T(8,128)(2,1)S(1)}, u32[]{:S(2)}, u32[]{:S(2)}) collective-permute-start(bf16[384,768]{1,0:T(8,128)(2,1)S(1)} %bitcast.91), channel_id=1, source_target_pairs={{0,32},{32,64},{64,96},{96,0},{1,33},{33,65},{65,97},{97,1},{2,34}... | collective-permute-start | bytes 1769480 | tf_op jit(solution)/shard_map/ppermute | solution.py:17
  62.4 27.2 %collective-permute-start.4 = (bf16[384,768]{1,0:T(8,128)(2,1)S(1)}, bf16[384,768]{1,0:T(8,128)(2,1)S(1)}, u32[]{:S(2)}, u32[]{:S(2)}) collective-permute-start(bf16[384,768]{1,0:T(8,128)(2,1)S(1)} %bitcast.92), channel_id=1, source_target_pairs={{0,64},{32,96},{64,0},{96,32},{1,65},{33,97},{65,1},{97,33},{2,66}... | collective-permute-start | bytes 1769480 | tf_op jit(solution)/shard_map/ppermute | solution.py:17
  65.1 25.3 %collective-permute-start.3 = (bf16[384,768]{1,0:T(8,128)(2,1)S(1)}, bf16[384,768]{1,0:T(8,128)(2,1)S(1)}, u32[]{:S(2)}, u32[]{:S(2)}) collective-permute-start(bf16[384,768]{1,0:T(8,128)(2,1)S(1)} %bitcast.93), channel_id=1, source_target_pairs={{0,96},{32,0},{64,32},{96,64},{1,97},{33,1},{65,33},{97,65},{2,98}... | collective-permute-start | bytes 1769480 | tf_op jit(solution)/shard_map/ppermute | solution.py:17
  83.6 6.1 %copy-start.2 = (bf16[384,768]{1,0:T(8,128)(2,1)}, bf16[384,768]{1,0:T(8,128)(2,1)S(1)}, u32[]{:S(2)}) copy-start(bf16[384,768]{1,0:T(8,128)(2,1)S(1)} %collective-permute-done.5.refs_3_) | copy-start | bytes 1769476
  89.6 0.8 copy-start.3
  120.7 13.0 %collective-permute-start.10 = (bf16[192,768]{1,0:T(8,128)(2,1)S(1)}, bf16[192,768]{1,0:T(8,128)(2,1)S(1)}, u32[]{:S(2)}, u32[]{:S(2)}) collective-permute-start(bf16[192,768]{1,0:T(8,128)(2,1)S(1)} %get-tuple-element.65), channel_id=1, source_target_pairs={{0,32},{32,64},{64,96},{96,0},{1,33},{33,65},{65,97},{97,1},{2,34}... | collective-permute-start | bytes 884744 | tf_op jit(solution)/shard_map/ppermute | solution.py:17
  122.2 12.0 %collective-permute-start.14 = (bf16[192,768]{1,0:T(8,128)(2,1)S(1)}, bf16[192,768]{1,0:T(8,128)(2,1)S(1)}, u32[]{:S(2)}, u32[]{:S(2)}) collective-permute-start(bf16[192,768]{1,0:T(8,128)(2,1)S(1)} %get-tuple-element.66), channel_id=1, source_target_pairs={{0,96},{32,0},{64,32},{96,64},{1,97},{33,1},{65,33},{97,65},{2,98}... | collective-permute-start | bytes 884744 | tf_op jit(solution)/shard_map/ppermute | solution.py:17
  131.6 10.1 %collective-permute-start.12 = (bf16[192,768]{1,0:T(8,128)(2,1)S(1)}, bf16[192,768]{1,0:T(8,128)(2,1)S(1)}, u32[]{:S(2)}, u32[]{:S(2)}) collective-permute-start(bf16[192,768]{1,0:T(8,128)(2,1)S(1)} %get-tuple-element.33), channel_id=1, source_target_pairs={{0,96},{32,0},{64,32},{96,64},{1,97},{33,1},{65,33},{97,65},{2,98}... | collective-permute-start | bytes 884744 | tf_op jit(solution)/shard_map/ppermute | solution.py:17
  133.1 11.2 %collective-permute-start.13 = (bf16[192,768]{1,0:T(8,128)(2,1)S(1)}, bf16[192,768]{1,0:T(8,128)(2,1)S(1)}, u32[]{:S(2)}, u32[]{:S(2)}) collective-permute-start(bf16[192,768]{1,0:T(8,128)(2,1)S(1)} %get-tuple-element.34), channel_id=1, source_target_pairs={{0,32},{32,64},{64,96},{96,0},{1,33},{33,65},{65,97},{97,1},{2,34}... | collective-permute-start | bytes 884744 | tf_op jit(solution)/shard_map/ppermute | solution.py:17
  133.8 15.2 %collective-permute-start.11 = (bf16[192,768]{1,0:T(8,128)(2,1)S(1)}, bf16[192,768]{1,0:T(8,128)(2,1)S(1)}, u32[]{:S(2)}, u32[]{:S(2)}) collective-permute-start(bf16[192,768]{1,0:T(8,128)(2,1)S(1)} %add_convert_fusion.3), channel_id=1, source_target_pairs={{0,32},{32,64},{64,96},{96,0},{1,33},{33,65},{65,97},{97,1},{2,34}... | collective-permute-start | bytes 884744 | tf_op jit(solution)/shard_map/ppermute | solution.py:17
  134.3 14.7 %collective-permute-start.15 = (bf16[192,768]{1,0:T(8,128)(2,1)S(1)}, bf16[192,768]{1,0:T(8,128)(2,1)S(1)}, u32[]{:S(2)}, u32[]{:S(2)}) collective-permute-start(bf16[192,768]{1,0:T(8,128)(2,1)S(1)} %add_convert_fusion.2), channel_id=1, source_target_pairs={{0,96},{32,0},{64,32},{96,64},{1,97},{33,1},{65,33},{97,65},{2,98}... | collective-permute-start | bytes 884744 | tf_op jit(solution)/shard_map/ppermute | solution.py:17
  149.2 15.0 %collective-permute-start.18 = (bf16[384,768]{1,0:T(8,128)(2,1)S(1)}, bf16[384,768]{1,0:T(8,128)(2,1)S(1)}, u32[]{:S(2)}, u32[]{:S(2)}) collective-permute-start(bf16[384,768]{1,0:T(8,128)(2,1)S(1)} %fusion.1.refs_3_), channel_id=1, source_target_pairs={{0,32},{32,64},{64,96},{96,0},{1,33},{33,65},{65,97},{97,1},{2,34}... | collective-permute-start | bytes 1769480 | tf_op jit(solution)/shard_map/ppermute | solution.py:17
  149.3 15.3 %collective-permute-start.17 = (bf16[384,768]{1,0:T(8,128)(2,1)S(1)}, bf16[384,768]{1,0:T(8,128)(2,1)S(1)}, u32[]{:S(2)}, u32[]{:S(2)}) collective-permute-start(bf16[384,768]{1,0:T(8,128)(2,1)S(1)} %fusion.1.refs_3_), channel_id=1, source_target_pairs={{0,96},{32,0},{64,32},{96,64},{1,97},{33,1},{65,33},{97,65},{2,98}... | collective-permute-start | bytes 1769480 | tf_op jit(solution)/shard_map/ppermute | solution.py:17
  154.2 1.3 collective-permute-start.16
  156.8 21.9 %all-to-all-start = ((f32[64,1,128]{2,1,0:T(1,128)}), f32[64,1,128]{2,1,0:T(1,128)S(1)}, u32[]{:S(2)}, u32[]{:S(2)}) async-start(f32[64,1,128]{2,1,0:T(1,128)} %bitcast.27), calls=%async_computation | async-start | bytes 65536 | tf_op jit(solution)/shard_map/all_to_all | solution.py:277
  164.3 15.7 %collective-permute-start.19 = (bf16[192,768]{1,0:T(8,128)(2,1)S(1)}, bf16[192,768]{1,0:T(8,128)(2,1)S(1)}, u32[]{:S(2)}, u32[]{:S(2)}) collective-permute-start(bf16[192,768]{1,0:T(8,128)(2,1)S(1)} %slice.102), channel_id=1, source_target_pairs={{0,32},{32,64},{64,96},{96,0},{1,33},{33,65},{65,97},{97,1},{2,34}... | collective-permute-start | bytes 884744 | tf_op jit(solution)/shard_map/ppermute | solution.py:17
  164.6 15.4 %collective-permute-start.20 = (bf16[192,768]{1,0:T(8,128)(2,1)S(1)}, bf16[192,768]{1,0:T(8,128)(2,1)S(1)}, u32[]{:S(2)}, u32[]{:S(2)}) collective-permute-start(bf16[192,768]{1,0:T(8,128)(2,1)S(1)} %slice.103), channel_id=1, source_target_pairs={{0,96},{32,0},{64,32},{96,64},{1,97},{33,1},{65,33},{97,65},{2,98}... | collective-permute-start | bytes 884744 | tf_op jit(solution)/shard_map/ppermute | solution.py:17
  191.1 13.0 %collective-permute-start.21 = (bf16[192,768]{1,0:T(8,128)(2,1)S(1)}, bf16[192,768]{1,0:T(8,128)(2,1)S(1)}, u32[]{:S(2)}, u32[]{:S(2)}) collective-permute-start(bf16[192,768]{1,0:T(8,128)(2,1)S(1)} %get-tuple-element.63), channel_id=1, source_target_pairs={{0,32},{32,64},{64,96},{96,0},{1,33},{33,65},{65,97},{97,1},{2,34}... | collective-permute-start | bytes 884744 | tf_op jit(solution)/shard_map/ppermute | solution.py:17
  191.2 13.0 %collective-permute-start.25 = (bf16[192,768]{1,0:T(8,128)(2,1)S(1)}, bf16[192,768]{1,0:T(8,128)(2,1)S(1)}, u32[]{:S(2)}, u32[]{:S(2)}) collective-permute-start(bf16[192,768]{1,0:T(8,128)(2,1)S(1)} %get-tuple-element.64), channel_id=1, source_target_pairs={{0,96},{32,0},{64,32},{96,64},{1,97},{33,1},{65,33},{97,65},{2,98}... | collective-permute-start | bytes 884744 | tf_op jit(solution)/shard_map/ppermute | solution.py:17
  202.0 10.1 %collective-permute-start.23 = (bf16[192,768]{1,0:T(8,128)(2,1)S(1)}, bf16[192,768]{1,0:T(8,128)(2,1)S(1)}, u32[]{:S(2)}, u32[]{:S(2)}) collective-permute-start(bf16[192,768]{1,0:T(8,128)(2,1)S(1)} %get-tuple-element.42), channel_id=1, source_target_pairs={{0,96},{32,0},{64,32},{96,64},{1,97},{33,1},{65,33},{97,65},{2,98}... | collective-permute-start | bytes 884744 | tf_op jit(solution)/shard_map/ppermute | solution.py:17
  202.1 10.8 %collective-permute-start.24 = (bf16[192,768]{1,0:T(8,128)(2,1)S(1)}, bf16[192,768]{1,0:T(8,128)(2,1)S(1)}, u32[]{:S(2)}, u32[]{:S(2)}) collective-permute-start(bf16[192,768]{1,0:T(8,128)(2,1)S(1)} %get-tuple-element.43), channel_id=1, source_target_pairs={{0,32},{32,64},{64,96},{96,0},{1,33},{33,65},{65,97},{97,1},{2,34}... | collective-permute-start | bytes 884744 | tf_op jit(solution)/shard_map/ppermute | solution.py:17
  204.2 11.9 %collective-permute-start.22 = (bf16[192,768]{1,0:T(8,128)(2,1)S(1)}, bf16[192,768]{1,0:T(8,128)(2,1)S(1)}, u32[]{:S(2)}, u32[]{:S(2)}) collective-permute-start(bf16[192,768]{1,0:T(8,128)(2,1)S(1)} %add_convert_fusion.1), channel_id=1, source_target_pairs={{0,32},{32,64},{64,96},{96,0},{1,33},{33,65},{65,97},{97,1},{2,34}... | collective-permute-start | bytes 884744 | tf_op jit(solution)/shard_map/ppermute | solution.py:17
  204.3 11.7 %collective-permute-start.26 = (bf16[192,768]{1,0:T(8,128)(2,1)S(1)}, bf16[192,768]{1,0:T(8,128)(2,1)S(1)}, u32[]{:S(2)}, u32[]{:S(2)}) collective-permute-start(bf16[192,768]{1,0:T(8,128)(2,1)S(1)} %add_convert_fusion), channel_id=1, source_target_pairs={{0,96},{32,0},{64,32},{96,64},{1,97},{33,1},{65,33},{97,65},{2,98}... | collective-permute-start | bytes 884744 | tf_op jit(solution)/shard_map/ppermute | solution.py:17
  218.2 2.9 %collective-permute-start.30 = (f32[64,128]{1,0:T(8,128)S(1)}, f32[64,128]{1,0:T(8,128)S(1)}, u32[]{:S(2)}, u32[]{:S(2)}) collective-permute-start(f32[64,128]{1,0:T(8,128)S(1)} %broadcast_in_dim.7), channel_id=1, source_target_pairs={{0,1},{1,0},{2,3},{3,2},{4,5},{5,4},{6,7},{7,6},{8,9},{9,8},{10,11... | collective-permute-start | bytes 98312 | tf_op jit(solution)/shard_map/ppermute | solution.py:276
  218.3 20.9 %collective-permute-start.27 = (bf16[192,384]{1,0:T(8,128)(2,1)S(1)}, bf16[192,384]{1,0:T(8,128)(2,1)S(1)}, u32[]{:S(2)}, u32[]{:S(2)}) collective-permute-start(bf16[192,384]{1,0:T(8,128)(2,1)S(1)} %get-tuple-element.62), channel_id=1, source_target_pairs={{0,24},{8,0},{16,8},{24,16},{1,25},{9,1},{17,9},{25,17},{2,26},{10... | collective-permute-start | bytes 442376 | tf_op jit(solution)/shard_map/ppermute | solution.py:17
  222.3 15.6 %all-to-all-start.1 = ((f32[64,1,128]{2,1,0:T(1,128)}), f32[64,1,128]{2,1,0:T(1,128)S(1)}, u32[]{:S(2)}, u32[]{:S(2)}) async-start(f32[64,1,128]{2,1,0:T(1,128)} %bitcast.42), calls=%async_computation.1 | async-start | bytes 65536 | tf_op jit(solution)/shard_map/all_to_all | solution.py:277
  228.4 11.1 %collective-permute-start.29 = (bf16[192,384]{1,0:T(8,128)(2,1)S(1)}, bf16[192,384]{1,0:T(8,128)(2,1)S(1)}, u32[]{:S(2)}, u32[]{:S(2)}) collective-permute-start(bf16[192,384]{1,0:T(8,128)(2,1)S(1)} %get-tuple-element.59), channel_id=1, source_target_pairs={{0,8},{8,16},{16,24},{24,0},{1,9},{9,17},{17,25},{25,1},{2,10},{10... | collective-permute-start | bytes 442376 | tf_op jit(solution)/shard_map/ppermute | solution.py:17
  230.0 9.4 %collective-permute-start.28 = (bf16[192,384]{1,0:T(8,128)(2,1)S(1)}, bf16[192,384]{1,0:T(8,128)(2,1)S(1)}, u32[]{:S(2)}, u32[]{:S(2)}) collective-permute-start(bf16[192,384]{1,0:T(8,128)(2,1)S(1)} %get-tuple-element.61), channel_id=1, source_target_pairs={{0,16},{8,24},{16,0},{24,8},{1,17},{9,25},{17,1},{25,9},{2,18},{10... | collective-permute-start | bytes 442376 | tf_op jit(solution)/shard_map/ppermute | solution.py:17
Sparse Core Ops, SparseCore 0:
  9.6 91.7 all-gather.1

commit v6 on v5

--- a/solution.py
+++ b/solution.py
@@ -72,7 +72,7 @@
         w = jnp.concatenate([w_ref[...] for w_ref in w_refs], axis=1)
         hidden = lax.dot_general(w, x, NT, preferred_element_type=F32)
         h_ref[...] = hidden
-        s = slope_of(hidden, t_ref[...])
+        s = slope_of(hidden, t_ref[0])
         s_ref[...] = s
         add_term(s, jnp.concatenate(block(2), axis=1), far_ref, total_ref)
 
@@ -81,7 +81,9 @@
         grid_spec=pltpu.PrefetchScalarGridSpec(
             num_scalar_prefetch=1,
             grid=(N,),
-            in_specs=[pl.BlockSpec((blocks, tile, wide), lambda i, which: (0, i, 0))] + [whole] * N + [out],
+            in_specs=[pl.BlockSpec((blocks, tile, wide), lambda i, which: (0, i, 0))]
+            + [whole] * N
+            + [pl.BlockSpec((1, cols, tile), lambda i, which: (which[N + i], 0, 0))],
             out_specs=[out, out, pl.BlockSpec((cols, deep), lambda i, which: (0, 0))],
             scratch_shapes=[pltpu.VMEM((cols, deep), F32)],
         ),
@@ -123,7 +125,7 @@
     )(jnp.stack(which).astype(jnp.int32), *([x] * count), *pieces)
 
 
-def second_slopes(x, piece, block, part, scale, hidden, t):
+def second_slopes(x, piece, which, part, scale, hidden, t):
     blocks, rows, wide = x.shape
     cols, deep = piece.shape
     per = deep // wide
@@ -134,7 +136,7 @@
     def kernel(which_ref, scale_ref, x_ref, f_ref, part_ref, h_ref, t_ref, s_ref, far_ref, total_ref):
         x = joined(x_ref)
         move = part_ref[...] + lax.dot_general(f_ref[...], x, NT, preferred_element_type=F32)
-        s = slope_of(h_ref[...] + scale_ref[0, 0] * move, t_ref[...])
+        s = slope_of(h_ref[...] + scale_ref[0, 0] * move, t_ref[0])
         s_ref[...] = s
         add_term(s, x, far_ref, total_ref)
 
@@ -149,7 +151,7 @@
                 whole,
                 out,
                 out,
-                out,
+                pl.BlockSpec((1, cols, tile), lambda i, which: (which[1 + i], 0, 0)),
             ],
             out_specs=[out, whole],
             scratch_shapes=[pltpu.VMEM((cols, deep), F32)],
@@ -157,7 +159,7 @@
         out_shape=[jax.ShapeDtypeStruct((cols, rows), BF16), jax.ShapeDtypeStruct((cols, deep), BF16)],
         compiler_params=PARAMS,
         cost_estimate=cost(cols, 2 * deep, rows, rows * cols),
-    )(jnp.reshape(block, (1,)).astype(jnp.int32), scale, x, piece, part, hidden, t)
+    )(jnp.stack(which).astype(jnp.int32), scale, x, piece, part, hidden, t)
 
 
 def terms(x, s, which, cut):
@@ -236,34 +238,35 @@
 def cut_kernel(which_ref, own, after, far, before, to_next, to_prev, kept):
     rows = own.shape[0]
     half = rows // 2
-    to_next[:rows], to_next[rows:] = after[...], far[:half]
-    to_prev[:rows], to_prev[rows:] = before[...], far[half:]
-    kept[...] = own[...]
+    turned = far[...].T
+    to_next[:, :rows], to_next[:, rows:] = after[...].T, turned[:, :half]
+    to_prev[:, :rows], to_prev[:, rows:] = before[...].T, turned[:, half:]
+    kept[...] = own[...].T
 
 
 def cut(array, me):
     rows, cols = array.shape[0], array.shape[1] // N
     at = lambda k: pl.BlockSpec((rows, cols), lambda i, which: (0, which[k]))
-    tall = [rows + rows // 2, rows + rows // 2, rows]
+    wide = [rows + rows // 2, rows + rows // 2, rows]
     return pl.pallas_call(
         cut_kernel,
         grid_spec=pltpu.PrefetchScalarGridSpec(
             num_scalar_prefetch=1,
             grid=(1,),
             in_specs=[at(k) for k in range(N)],
-            out_specs=[pl.BlockSpec((size, cols), lambda i, which: (0, 0)) for size in tall],
-        ),
-        out_shape=[jax.ShapeDtypeStruct((size, cols), array.dtype) for size in tall],
+            out_specs=[pl.BlockSpec((cols, size), lambda i, which: (0, 0)) for size in wide],
+        ),
+        out_shape=[jax.ShapeDtypeStruct((cols, size), array.dtype) for size in wide],
         compiler_params=PARAMS,
         cost_estimate=cost(0, 0, 0),
     )(jnp.stack([lax.rem(me + k, N) for k in range(N)]).astype(jnp.int32), *([array] * N))
 
 
 def ring_swap_halves(to_next, to_prev, kept, axis):
-    rows = kept.shape[0]
+    size = kept.shape[1]
     prev, after = shift(to_next, axis, 1), shift(to_prev, axis, -1)
-    high, low = shift(prev[rows:], axis, 1), shift(after[rows:], axis, -1)
-    return [kept, after[:rows], jnp.concatenate([high, low], axis=0), prev[:rows]]
+    high, low = shift(prev[:, size:], axis, 1), shift(after[:, size:], axis, -1)
+    return [kept, after[:, :size], jnp.concatenate([high, low], axis=1), prev[:, :size]]
 
 
 def in_order(pieces, me):
@@ -295,18 +298,18 @@
     to_next, to_prev, kept = cut(target, iy)
     w_pieces = ring_swap(columns(weight), "y")
     to_next, to_prev = lax.optimization_barrier((to_next, to_prev, *w_pieces))[:2]
-    t = in_order(ring_swap_halves(to_next, to_prev, kept, "y"), iy)
-    t = jnp.concatenate([t[k].T for k in range(N)], axis=1)
+    t = jnp.stack(ring_swap_halves(to_next, to_prev, kept, "y"))
+    tiles = [lax.rem(k + N - iy, N) for k in range(N)]
     w = ring_gather(in_order(w_pieces, iy).reshape(-1, cols).T, "x")
 
     at = lambda k: lax.rem(ix + k, N)
-    hidden, slope, term = first_slopes(x, w, t, [at(k) for k in range(N)])
+    hidden, slope, term = first_slopes(x, w, t, [at(k) for k in range(N)] + tiles)
     first = ring_sum(x, slope, term, ix)
     own, after, far, before = ring_gather_halves(first.astype(BF16), "x")
     part = moved(x, [own, after, before], [at(0), at(1), at(3)])
     total, part = total_of(first, part)
     scale = 0.5 * math.sqrt(hidden_all) / jnp.sqrt(total + 1e-06)
-    slope, term = second_slopes(x, far, at(2), part, scale.reshape(1, 1), hidden, t)
+    slope, term = second_slopes(x, far, [at(2)] + tiles, part, scale.reshape(1, 1), hidden, t)
     second = ring_sum(x, slope, term, ix)
     total, _ = total_of(second, None)
     factor = jnp.minimum(1.0, math.sqrt(width * hidden_all) / jnp.sqrt(total + 1e-06))

time: 248 us -> 250 us (level)
  waiting for transfers between devices: 62.3 us -> 91.3 us
  local copies, waits for them, and re-layouts: 27.1 us -> 7.74 us
  starting transfers between devices: 61.5 us -> 57 us
  other arithmetic: 13.4 us -> 9.36 us
    all_gather x1, waiting for transfers between devices: 11 us -> 26.9 us  [per_device(): lax.all_gather(tokens, ('z', 'c', 'y'), axis=0, tiled=True)]
    ppermute x29, waiting for transfers between devices: 44.3 us -> 56.9 us  [shift(): return lax.ppermute(value, axis, [(i, (i + step) % N) for i in range(N)])]
    unnamed x26 -> x15, local copies, waits for them, and re-layouts: 13.7 us -> 2.06 us
    ppermute x29, starting transfers between devices: 49.1 us -> 43.8 us  [shift(): return lax.ppermute(value, axis, [(i, (i + step) % N) for i in range(N)])]
    unnamed x2 -> x0, other arithmetic: 3.83 us -> none
    optimization_barrier x2 -> x0, local copies, waits for them, and re-layouts: 3.07 us -> none  [per_device(): lax.optimization_barrier((to_next, to_prev, *w_pieces))[:2]]
  transfers between devices with their start and end apart: 34 -> 34, of which waited for: 14 -> 13; matrix products, arithmetic and copies ran while one was open for 14% -> 5% of each run, Pallas kernels for 15% -> 15%
where the time goes in v6:
time: 250 us
  waiting for transfers between devices  91.3 us (37%)
  Pallas kernels  68.9 us (28%)
  starting transfers between devices  57 us (23%)
  between operations  15.2 us (6%)
  other arithmetic  9.36 us (4%)
  local copies, waits for them, and re-layouts  7.74 us (3%)
    ppermute x29, waiting for transfers between devices, shift(): return lax.ppermute(value, axis, [(i, (i + step) % N) for i in range(N)])  56.9 us
    ppermute x29, starting transfers between devices, shift(): return lax.ppermute(value, axis, [(i, (i + step) % N) for i in range(N)])  43.8 us
    all_gather x1, waiting for transfers between devices, per_device(): lax.all_gather(tokens, ('z', 'c', 'y'), axis=0, tiled=True)  26.9 us
    pallas_call x4, Pallas kernels, terms(): pl.pallas_call(kernel, grid_spec=pltpu.PrefetchScalarGridSpec(num_scalar_...  23.8 us
    pallas_call x1, Pallas kernels, first_slopes(): pl.pallas_call(kernel, grid_spec=pltpu.PrefetchScalarGridSpec(num_scalar_...  19 us
    all_to_all x2, starting transfers between devices, total_of(): lax.all_to_all(total, ('x', 'y', 'z'), split_axis=0, concat_axis=0, tiled...  13.1 us
    pallas_call x1, Pallas kernels, second_slopes(): pl.pallas_call(kernel, grid_spec=pltpu.PrefetchScalarGridSpec(num_scalar_...  11.6 us
    pallas_call x1, Pallas kernels, moved(): pl.pallas_call(kernel, grid_spec=pltpu.PrefetchScalarGridSpec(num_scalar_...  11 us
  transfers between devices with their start and end apart: 34, of which 13 were waited for; matrix products, arithmetic and copies ran while one was open for 5% of the time, Pallas kernels for 15%

profile of v6, /device:TPU:0, one launch (start us, length us, event | category | flops | bytes accessed | tf_op | source)
XLA Modules:
  0.0 249.6 jit_solution(15176896741822203297)
XLA Ops:
  7.3 1.1 constant_dynamic-slice_fusion.1
  8.4 3.2 %collective-permute-start = (bf16[192,384]{1,0:T(8,128)(2,1)S(1)}, bf16[192,384]{1,0:T(8,128)(2,1)S(1)}, u32[]{:S(2)}, u32[]{:S(2)}) collective-permute-start(bf16[192,384]{1,0:T(8,128)(2,1)S(1)} %get-tuple-element.64), channel_id=1, source_target_pairs={{0,24},{8,0},{16,8},{24,16},{1,25},{9,1},{17,9},{25,17},{2,26},{10... | collective-permute-start | bytes 442376 | tf_op jit(solution)/shard_map/ppermute | solution.py:17
  12.2 1.0 collective-permute-start.2
  13.3 3.6 %shard_map.37 = (bf16[384,1152]{1,0:T(8,128)(2,1)S(1)}, bf16[384,1152]{1,0:T(8,128)(2,1)}, bf16[384,768]{1,0:T(8,128)(2,1)S(1)}) custom-call(s32[4]{0:T(128)S(1)} %pad_add_fusion.which_ref, bf16[768,1536]{1,0:T(8,128)(2,1)} %before.1, bf16[768,1536]{1,0:T(8,128)(2,1)} %before.1, bf16[768,1536]{1,0:T(8,128)(2,1)} %before.1, bf16[768,1536]{1,0:T(8,128)(2,1)} %before.1), custom_call_target="tpu_custom_call" | custom-call | tf_op jit(solution)/shard_map/pallas_call | solution.py:251
  17.0 0.9 bitcast_dynamic-update-slice_fusion.12
  17.9 1.9 collective-permute-done.1
  19.9 1.7 collective-permute-done.2
  21.5 3.2 %collective-permute-start.6 = (bf16[384,1152]{1,0:T(8,128)(2,1)}, bf16[384,1152]{1,0:T(8,128)(2,1)}, u32[]{:S(2)}, u32[]{:S(2)}) collective-permute-start(bf16[384,1152]{1,0:T(8,128)(2,1)} %get-tuple-element.28), channel_id=1, source_target_pairs={{0,24},{8,0},{16,8},{24,16},{1,25},{9,1},{17,9},{25,17},{2,26},{10... | collective-permute-start | bytes 2654216 | tf_op jit(solution)/shard_map/ppermute | solution.py:17
  25.4 2.8 %collective-permute-start.3 = (bf16[384,768]{1,0:T(8,128)(2,1)S(1)}, bf16[384,768]{1,0:T(8,128)(2,1)S(1)}, u32[]{:S(2)}, u32[]{:S(2)}) collective-permute-start(bf16[384,768]{1,0:T(8,128)(2,1)S(1)} %bitcast.66), channel_id=1, source_target_pairs={{0,96},{32,0},{64,32},{96,64},{1,97},{33,1},{65,33},{97,65},{2,98}... | collective-permute-start | bytes 1769480 | tf_op jit(solution)/shard_map/ppermute | solution.py:17
  29.9 23.0 %collective-permute-done.6 = bf16[384,1152]{1,0:T(8,128)(2,1)} collective-permute-done((bf16[384,1152]{1,0:T(8,128)(2,1)}, bf16[384,1152]{1,0:T(8,128)(2,1)}, u32[]{:S(2)}, u32[]{:S(2)}) %collective-permute-start.6) | collective-permute-done | bytes 884768 | tf_op jit(solution)/shard_map/ppermute | solution.py:17
  52.9 1.1 slice.82
  54.0 2.1 collective-permute-start.9
  56.3 1.1 slice_bitcast_fusion.1
  57.4 12.2 %collective-permute-done.9 = bf16[384,384]{1,0:T(8,128)(2,1)S(1)} collective-permute-done((bf16[384,384]{1,0:T(8,128)(2,1)S(1)}, bf16[384,384]{1,0:T(8,128)(2,1)S(1)}, u32[]{:S(2)}, u32[]{:S(2)}) %collective-permute-start.9) | collective-permute-done | bytes 294944 | tf_op jit(solution)/shard_map/ppermute | solution.py:17
  69.6 3.5 %collective-permute-done.8 = bf16[384,384]{1,0:T(8,128)(2,1)S(1)} collective-permute-done((bf16[384,384]{1,0:T(8,128)(2,1)S(1)}, bf16[384,384]{1,0:T(8,128)(2,1)S(1)}, u32[]{:S(2)}, u32[]{:S(2)}) %collective-permute-start.8) | collective-permute-done | bytes 294944 | tf_op jit(solution)/shard_map/ppermute | solution.py:17
  73.1 1.7 pad_maximum_fusion.refs_4_.t_ref
  75.7 26.9 %all-gather.2.cloned.1.call-done = bf16[24576,384]{1,0:T(8,128)(2,1)} async-done(((bf16[768,384]{1,0:T(8,128)(2,1)}), bf16[24576,384]{1,0:T(8,128)(2,1)}) %all-gather.2.cloned.1.call-update) | async-done | bytes 18874384 | tf_op jit(solution)/shard_map/all_gather | solution.py:293
  102.6 19.0 %shard_map.38 = (f32[384,3072]{1,0:T(8,128)}, bf16[384,3072]{1,0:T(8,128)(2,1)}, bf16[384,768]{1,0:T(8,128)(2,1)S(1)}) custom-call(s32[8]{0:T(128)S(1)} %stack.126.which_ref, bf16[8,3072,384]{2,1,0:T(8,128)(2,1)} %bitcast.70, bf16[384,768]{1,0:T(8,128)(2,1)S(1)} %bitcast.69, bf16[384,768]{1,0:T(8,128)(2,1)S(1)} %collective-permute-done.3.refs_1_, ...), custom_call_target="tpu_custom_call" | custom-call | flops 9059696640 | bytes 31260672 | tf_op jit(solution)/shard_map/pallas_call | solution.py:79
  121.6 1.5 collective-permute-start.10
  123.2 1.8 collective-permute-start.14
  124.9 7.5 %shard_map.40 = (f32[192,768]{1,0:T(8,128)S(1)}, bf16[192,768]{1,0:T(8,128)(2,1)S(1)}, bf16[192,768]{1,0:T(8,128)(2,1)S(1)}, f32[192,768]{1,0:T(8,128)S(1)}) custom-call(s32[2]{0:T(128)S(1)} %pad_add_fusion.1.which_ref, bf16[8,3072,384]{2,1,0:T(8,128)(2,1)} %bitcast.71, bf16[8,3072,384]{2,1,0:T(8,128)(2,1)} %bitcast.72, ...), custom_call_target="tpu_custom_call" | custom-call | flops 3623878656 | bytes 11796480 | tf_op jit(solution)/shard_map/pallas_call | solution.py:194
  132.5 1.5 collective-permute-start.12
  135.0 3.2 %collective-permute-start.15 = (bf16[192,768]{1,0:T(8,128)(2,1)S(1)}, bf16[192,768]{1,0:T(8,128)(2,1)S(1)}, u32[]{:S(2)}, u32[]{:S(2)}) collective-permute-start(bf16[192,768]{1,0:T(8,128)(2,1)S(1)} %add_convert_fusion.2), channel_id=1, source_target_pairs={{0,96},{32,0},{64,32},{96,64},{1,97},{33,1},{65,33},{97,65},{2,98}... | collective-permute-start | bytes 884744 | tf_op jit(solution)/shard_map/ppermute | solution.py:17
  138.3 4.3 %shard_map.39 = f32[384,768]{1,0:T(8,128)S(1)} custom-call(s32[1]{0:T(128)} %bitcast.which_ref, bf16[8,3072,384]{2,1,0:T(8,128)(2,1)} %bitcast.73, bf16[384,3072]{1,0:T(8,128)(2,1)} %get-tuple-element.30.refs_1_.refs_2_), custom_call_target="tpu_custom_call" | custom-call | flops 1811939328 | bytes 8257536 | tf_op jit(solution)/shard_map/pallas_call | solution.py:194
  142.6 2.6 %collective-permute-done.13 = bf16[192,768]{1,0:T(8,128)(2,1)S(1)} collective-permute-done((bf16[192,768]{1,0:T(8,128)(2,1)S(1)}, bf16[192,768]{1,0:T(8,128)(2,1)S(1)}, u32[]{:S(2)}, u32[]{:S(2)}) %collective-permute-start.13) | collective-permute-done | bytes 294944 | tf_op jit(solution)/shard_map/ppermute | solution.py:17
  145.2 4.7 %collective-permute-done.11 = bf16[192,768]{1,0:T(8,128)(2,1)S(1)} collective-permute-done((bf16[192,768]{1,0:T(8,128)(2,1)S(1)}, bf16[192,768]{1,0:T(8,128)(2,1)S(1)}, u32[]{:S(2)}, u32[]{:S(2)}) %collective-permute-start.11) | collective-permute-done | bytes 294944 | tf_op jit(solution)/shard_map/ppermute | solution.py:17
  150.5 1.8 collective-permute-start.18
  152.2 0.9 multiply_reduce_fusion.1
  154.0 1.0 collective-permute-done.16
  155.0 1.2 broadcast_add_fusion.1
  156.2 7.0 %all-to-all-start = ((f32[64,1,128]{2,1,0:T(1,128)}), f32[64,1,128]{2,1,0:T(1,128)S(1)}, u32[]{:S(2)}, u32[]{:S(2)}) async-start(f32[64,1,128]{2,1,0:T(1,128)} %bitcast.23), calls=%async_computation | async-start | bytes 65536 | tf_op jit(solution)/shard_map/all_to_all | solution.py:280
  164.0 2.3 collective-permute-start.20
  166.4 11.0 %shard_map.41.part_ref = f32[384,3072]{1,0:T(8,128)} custom-call(s32[3]{0:T(128)S(1)} %pad_add_fusion.2.which_ref, bf16[8,3072,384]{2,1,0:T(8,128)(2,1)} %bitcast.74, bf16[8,3072,384]{2,1,0:T(8,128)(2,1)} %bitcast.75, bf16[8,3072,384]{2,1,0:T(8,128)(2,1)} %bitcast.76, bf16[384,768]{1,0:T(8,128)(2,1)S(1)} %fusion.1.refs_3_, ...), custom_call_target="tpu_custom_call" | custom-call | flops 5435817984 | bytes 20643840 | tf_op jit(solution)/shard_map/pallas_call | solution.py:114
  178.8 11.6 %shard_map.42 = (bf16[384,3072]{1,0:T(8,128)(2,1)}, bf16[384,768]{1,0:T(8,128)(2,1)S(1)}) custom-call(s32[5]{0:T(128)S(1)} %stack.123.which_ref, f32[1,1]{1,0:T(1,128)} %bitcast.25.scale_ref, bf16[8,3072,384]{2,1,0:T(8,128)(2,1)} %bitcast.77, bf16[384,768]{1,0:T(8,128)(2,1)S(1)} %pad_maximum_fusion.3.f_ref, f32[384,3072]{1,0:T(8,128)} %shard_map.41.part_ref, ...), custom_call_target="tpu_custom_call" | custom-call | flops 3623878656 | bytes 15335424 | tf_op jit(solution)/shard_map/pallas_call | solution.py:143
  191.1 2.7 %collective-permute-start.25 = (bf16[192,768]{1,0:T(8,128)(2,1)S(1)}, bf16[192,768]{1,0:T(8,128)(2,1)S(1)}, u32[]{:S(2)}, u32[]{:S(2)}) collective-permute-start(bf16[192,768]{1,0:T(8,128)(2,1)S(1)} %get-tuple-element.60), channel_id=1, source_target_pairs={{0,96},{32,0},{64,32},{96,64},{1,97},{33,1},{65,33},{97,65},{2,98}... | collective-permute-start | bytes 884744 | tf_op jit(solution)/shard_map/ppermute | solution.py:17
  193.8 7.6 %shard_map.44 = (f32[192,768]{1,0:T(8,128)S(1)}, bf16[192,768]{1,0:T(8,128)(2,1)S(1)}, bf16[192,768]{1,0:T(8,128)(2,1)S(1)}, f32[192,768]{1,0:T(8,128)S(1)}) custom-call(s32[2]{0:T(128)S(1)} %pad_add_fusion.1.which_ref, bf16[8,3072,384]{2,1,0:T(8,128)(2,1)} %bitcast.78, bf16[8,3072,384]{2,1,0:T(8,128)(2,1)} %bitcast.79, ...), custom_call_target="tpu_custom_call" | custom-call | flops 3623878656 | bytes 11796480 | tf_op jit(solution)/shard_map/pallas_call | solution.py:194
  201.4 2.0 collective-permute-start.23
  203.7 3.5 %collective-permute-start.26 = (bf16[192,768]{1,0:T(8,128)(2,1)S(1)}, bf16[192,768]{1,0:T(8,128)(2,1)S(1)}, u32[]{:S(2)}, u32[]{:S(2)}) collective-permute-start(bf16[192,768]{1,0:T(8,128)(2,1)S(1)} %add_convert_fusion), channel_id=1, source_target_pairs={{0,96},{32,0},{64,32},{96,64},{1,97},{33,1},{65,33},{97,65},{2,98}... | collective-permute-start | bytes 884744 | tf_op jit(solution)/shard_map/ppermute | solution.py:17
  207.2 4.3 %shard_map.43 = f32[384,768]{1,0:T(8,128)S(1)} custom-call(s32[1]{0:T(128)} %bitcast.which_ref, bf16[8,3072,384]{2,1,0:T(8,128)(2,1)} %bitcast.80, bf16[384,3072]{1,0:T(8,128)(2,1)} %get-tuple-element.39.refs_1_.refs_2_), custom_call_target="tpu_custom_call" | custom-call | flops 1811939328 | bytes 8257536 | tf_op jit(solution)/shard_map/pallas_call | solution.py:194
  211.5 3.0 %collective-permute-done.24 = bf16[192,768]{1,0:T(8,128)(2,1)S(1)} collective-permute-done((bf16[192,768]{1,0:T(8,128)(2,1)S(1)}, bf16[192,768]{1,0:T(8,128)(2,1)S(1)}, u32[]{:S(2)}, u32[]{:S(2)}) %collective-permute-start.24) | collective-permute-done | bytes 294944 | tf_op jit(solution)/shard_map/ppermute | solution.py:17
  214.6 3.5 %collective-permute-done.22 = bf16[192,768]{1,0:T(8,128)(2,1)S(1)} collective-permute-done((bf16[192,768]{1,0:T(8,128)(2,1)S(1)}, bf16[192,768]{1,0:T(8,128)(2,1)S(1)}, u32[]{:S(2)}, u32[]{:S(2)}) %collective-permute-start.22) | collective-permute-done | bytes 294944 | tf_op jit(solution)/shard_map/ppermute | solution.py:17
  218.3 1.0 multiply_reduce_fusion
  220.4 2.8 %collective-permute-start.27 = (bf16[192,384]{1,0:T(8,128)(2,1)S(1)}, bf16[192,384]{1,0:T(8,128)(2,1)S(1)}, u32[]{:S(2)}, u32[]{:S(2)}) collective-permute-start(bf16[192,384]{1,0:T(8,128)(2,1)S(1)} %get-tuple-element.58), channel_id=1, source_target_pairs={{0,24},{8,0},{16,8},{24,16},{1,25},{9,1},{17,9},{25,17},{2,26},{10... | collective-permute-start | bytes 442376 | tf_op jit(solution)/shard_map/ppermute | solution.py:17
  223.2 1.2 broadcast_add_fusion
  224.5 6.0 %all-to-all-start.1 = ((f32[64,1,128]{2,1,0:T(1,128)}), f32[64,1,128]{2,1,0:T(1,128)S(1)}, u32[]{:S(2)}, u32[]{:S(2)}) async-start(f32[64,1,128]{2,1,0:T(1,128)} %bitcast.38), calls=%async_computation.1 | async-start | bytes 65536 | tf_op jit(solution)/shard_map/all_to_all | solution.py:280
  230.5 3.2 %collective-permute-start.28 = (bf16[192,384]{1,0:T(8,128)(2,1)S(1)}, bf16[192,384]{1,0:T(8,128)(2,1)S(1)}, u32[]{:S(2)}, u32[]{:S(2)}) collective-permute-start(bf16[192,384]{1,0:T(8,128)(2,1)S(1)} %get-tuple-element.57), channel_id=1, source_target_pairs={{0,16},{8,24},{16,0},{24,8},{1,17},{9,25},{17,1},{25,9},{2,18},{10... | collective-permute-start | bytes 442376 | tf_op jit(solution)/shard_map/ppermute | solution.py:17
  234.2 5.8 %all-to-all-done.1 = f32[64,1,128]{2,1,0:T(1,128)S(1)} async-done(((f32[64,1,128]{2,1,0:T(1,128)}), f32[64,1,128]{2,1,0:T(1,128)S(1)}, u32[]{:S(2)}, u32[]{:S(2)}) %all-to-all-start.1) | async-done | bytes 32800 | tf_op jit(solution)/shard_map/all_to_all | solution.py:280
  241.6 1.1 convert_multiply_fusion
  (85 shorter events, 12.5 us)
Async XLA Ops:
  6.5 96.1 %all-gather.2.cloned.1.call-start = ((), (), s32[]{:S(2)}) async-start(), calls=%async_computation.2 | async-start | bytes 19464192 | tf_op jit(solution)/shard_map/all_gather | solution.py:293
  8.4 9.5 %collective-permute-start = (bf16[192,384]{1,0:T(8,128)(2,1)S(1)}, bf16[192,384]{1,0:T(8,128)(2,1)S(1)}, u32[]{:S(2)}, u32[]{:S(2)}) collective-permute-start(bf16[192,384]{1,0:T(8,128)(2,1)S(1)} %get-tuple-element.64), channel_id=1, source_target_pairs={{0,24},{8,0},{16,8},{24,16},{1,25},{9,1},{17,9},{25,17},{2,26},{10... | collective-permute-start | bytes 442376 | tf_op jit(solution)/shard_map/ppermute | solution.py:17
  11.6 8.3 %collective-permute-start.1 = (bf16[192,384]{1,0:T(8,128)(2,1)S(1)}, bf16[192,384]{1,0:T(8,128)(2,1)S(1)}, u32[]{:S(2)}, u32[]{:S(2)}) collective-permute-start(bf16[192,384]{1,0:T(8,128)(2,1)S(1)} %get-tuple-element.65), channel_id=1, source_target_pairs={{0,16},{8,24},{16,0},{24,8},{1,17},{9,25},{17,1},{25,9},{2,18},{10... | collective-permute-start | bytes 442376 | tf_op jit(solution)/shard_map/ppermute | solution.py:17
  12.2 9.3 %collective-permute-start.2 = (bf16[192,384]{1,0:T(8,128)(2,1)S(1)}, bf16[192,384]{1,0:T(8,128)(2,1)S(1)}, u32[]{:S(2)}, u32[]{:S(2)}) collective-permute-start(bf16[192,384]{1,0:T(8,128)(2,1)S(1)} %get-tuple-element.63), channel_id=1, source_target_pairs={{0,8},{8,16},{16,24},{24,0},{1,9},{9,17},{17,25},{25,1},{2,10},{10... | collective-permute-start | bytes 442376 | tf_op jit(solution)/shard_map/ppermute | solution.py:17
  21.5 34.6 %collective-permute-start.7 = (bf16[384,1152]{1,0:T(8,128)(2,1)S(1)}, bf16[384,1152]{1,0:T(8,128)(2,1)S(1)}, u32[]{:S(2)}, u32[]{:S(2)}) collective-permute-start(bf16[384,1152]{1,0:T(8,128)(2,1)S(1)} %get-tuple-element.29), channel_id=1, source_target_pairs={{0,8},{8,16},{16,24},{24,0},{1,9},{9,17},{17,25},{25,1},{2,10},{10... | collective-permute-start | bytes 2654216 | tf_op jit(solution)/shard_map/ppermute | solution.py:17
  21.5 31.4 %collective-permute-start.6 = (bf16[384,1152]{1,0:T(8,128)(2,1)}, bf16[384,1152]{1,0:T(8,128)(2,1)}, u32[]{:S(2)}, u32[]{:S(2)}) collective-permute-start(bf16[384,1152]{1,0:T(8,128)(2,1)} %get-tuple-element.28), channel_id=1, source_target_pairs={{0,24},{8,0},{16,8},{24,16},{1,25},{9,1},{17,9},{25,17},{2,26},{10... | collective-permute-start | bytes 2654216 | tf_op jit(solution)/shard_map/ppermute | solution.py:17
  25.4 49.5 %collective-permute-start.3 = (bf16[384,768]{1,0:T(8,128)(2,1)S(1)}, bf16[384,768]{1,0:T(8,128)(2,1)S(1)}, u32[]{:S(2)}, u32[]{:S(2)}) collective-permute-start(bf16[384,768]{1,0:T(8,128)(2,1)S(1)} %bitcast.66), channel_id=1, source_target_pairs={{0,96},{32,0},{64,32},{96,64},{1,97},{33,1},{65,33},{97,65},{2,98}... | collective-permute-start | bytes 1769480 | tf_op jit(solution)/shard_map/ppermute | solution.py:17
  28.2 46.7 %collective-permute-start.4 = (bf16[384,768]{1,0:T(8,128)(2,1)S(1)}, bf16[384,768]{1,0:T(8,128)(2,1)S(1)}, u32[]{:S(2)}, u32[]{:S(2)}) collective-permute-start(bf16[384,768]{1,0:T(8,128)(2,1)S(1)} %bitcast.67), channel_id=1, source_target_pairs={{0,64},{32,96},{64,0},{96,32},{1,65},{33,97},{65,1},{97,33},{2,66}... | collective-permute-start | bytes 1769480 | tf_op jit(solution)/shard_map/ppermute | solution.py:17
  29.0 46.7 %collective-permute-start.5 = (bf16[384,768]{1,0:T(8,128)(2,1)S(1)}, bf16[384,768]{1,0:T(8,128)(2,1)}, u32[]{:S(2)}, u32[]{:S(2)}) collective-permute-start(bf16[384,768]{1,0:T(8,128)(2,1)S(1)} %bitcast.68), channel_id=1, source_target_pairs={{0,32},{32,64},{64,96},{96,0},{1,33},{33,65},{65,97},{97,1},{2,34}... | collective-permute-start | bytes 1769480 | tf_op jit(solution)/shard_map/ppermute | solution.py:17
  54.0 15.6 %collective-permute-start.9 = (bf16[384,384]{1,0:T(8,128)(2,1)S(1)}, bf16[384,384]{1,0:T(8,128)(2,1)S(1)}, u32[]{:S(2)}, u32[]{:S(2)}) collective-permute-start(bf16[384,384]{1,0:T(8,128)(2,1)S(1)} %slice.82), channel_id=1, source_target_pairs={{0,24},{8,0},{16,8},{24,16},{1,25},{9,1},{17,9},{25,17},{2,26},{10... | collective-permute-start | bytes 884744 | tf_op jit(solution)/shard_map/ppermute | solution.py:17
  56.2 16.9 %collective-permute-start.8 = (bf16[384,384]{1,0:T(8,128)(2,1)S(1)}, bf16[384,384]{1,0:T(8,128)(2,1)S(1)}, u32[]{:S(2)}, u32[]{:S(2)}) collective-permute-start(bf16[384,384]{1,0:T(8,128)(2,1)S(1)} %slice.81), channel_id=1, source_target_pairs={{0,8},{8,16},{16,24},{24,0},{1,9},{9,17},{17,25},{25,1},{2,10},{10... | collective-permute-start | bytes 884744 | tf_op jit(solution)/shard_map/ppermute | solution.py:17
  74.9 0.8 copy-start
  121.6 13.0 %collective-permute-start.10 = (bf16[192,768]{1,0:T(8,128)(2,1)S(1)}, bf16[192,768]{1,0:T(8,128)(2,1)S(1)}, u32[]{:S(2)}, u32[]{:S(2)}) collective-permute-start(bf16[192,768]{1,0:T(8,128)(2,1)S(1)} %get-tuple-element.61), channel_id=1, source_target_pairs={{0,32},{32,64},{64,96},{96,0},{1,33},{33,65},{65,97},{97,1},{2,34}... | collective-permute-start | bytes 884744 | tf_op jit(solution)/shard_map/ppermute | solution.py:17
  123.2 11.8 %collective-permute-start.14 = (bf16[192,768]{1,0:T(8,128)(2,1)S(1)}, bf16[192,768]{1,0:T(8,128)(2,1)S(1)}, u32[]{:S(2)}, u32[]{:S(2)}) collective-permute-start(bf16[192,768]{1,0:T(8,128)(2,1)S(1)} %get-tuple-element.62), channel_id=1, source_target_pairs={{0,96},{32,0},{64,32},{96,64},{1,97},{33,1},{65,33},{97,65},{2,98}... | collective-permute-start | bytes 884744 | tf_op jit(solution)/shard_map/ppermute | solution.py:17
  132.5 10.1 %collective-permute-start.12 = (bf16[192,768]{1,0:T(8,128)(2,1)S(1)}, bf16[192,768]{1,0:T(8,128)(2,1)S(1)}, u32[]{:S(2)}, u32[]{:S(2)}) collective-permute-start(bf16[192,768]{1,0:T(8,128)(2,1)S(1)} %get-tuple-element.33), channel_id=1, source_target_pairs={{0,96},{32,0},{64,32},{96,64},{1,97},{33,1},{65,33},{97,65},{2,98}... | collective-permute-start | bytes 884744 | tf_op jit(solution)/shard_map/ppermute | solution.py:17
  134.0 11.2 %collective-permute-start.13 = (bf16[192,768]{1,0:T(8,128)(2,1)S(1)}, bf16[192,768]{1,0:T(8,128)(2,1)S(1)}, u32[]{:S(2)}, u32[]{:S(2)}) collective-permute-start(bf16[192,768]{1,0:T(8,128)(2,1)S(1)} %get-tuple-element.34), channel_id=1, source_target_pairs={{0,32},{32,64},{64,96},{96,0},{1,33},{33,65},{65,97},{97,1},{2,34}... | collective-permute-start | bytes 884744 | tf_op jit(solution)/shard_map/ppermute | solution.py:17
  134.7 15.3 %collective-permute-start.11 = (bf16[192,768]{1,0:T(8,128)(2,1)S(1)}, bf16[192,768]{1,0:T(8,128)(2,1)S(1)}, u32[]{:S(2)}, u32[]{:S(2)}) collective-permute-start(bf16[192,768]{1,0:T(8,128)(2,1)S(1)} %add_convert_fusion.3), channel_id=1, source_target_pairs={{0,32},{32,64},{64,96},{96,0},{1,33},{33,65},{65,97},{97,1},{2,34}... | collective-permute-start | bytes 884744 | tf_op jit(solution)/shard_map/ppermute | solution.py:17
  135.0 14.9 %collective-permute-start.15 = (bf16[192,768]{1,0:T(8,128)(2,1)S(1)}, bf16[192,768]{1,0:T(8,128)(2,1)S(1)}, u32[]{:S(2)}, u32[]{:S(2)}) collective-permute-start(bf16[192,768]{1,0:T(8,128)(2,1)S(1)} %add_convert_fusion.2), channel_id=1, source_target_pairs={{0,96},{32,0},{64,32},{96,64},{1,97},{33,1},{65,33},{97,65},{2,98}... | collective-permute-start | bytes 884744 | tf_op jit(solution)/shard_map/ppermute | solution.py:17
  150.1 13.8 %collective-permute-start.17 = (bf16[384,768]{1,0:T(8,128)(2,1)S(1)}, bf16[384,768]{1,0:T(8,128)(2,1)S(1)}, u32[]{:S(2)}, u32[]{:S(2)}) collective-permute-start(bf16[384,768]{1,0:T(8,128)(2,1)S(1)} %fusion.1.refs_3_), channel_id=1, source_target_pairs={{0,96},{32,0},{64,32},{96,64},{1,97},{33,1},{65,33},{97,65},{2,98}... | collective-permute-start | bytes 1769480 | tf_op jit(solution)/shard_map/ppermute | solution.py:17
  150.5 15.8 %collective-permute-start.18 = (bf16[384,768]{1,0:T(8,128)(2,1)S(1)}, bf16[384,768]{1,0:T(8,128)(2,1)S(1)}, u32[]{:S(2)}, u32[]{:S(2)}) collective-permute-start(bf16[384,768]{1,0:T(8,128)(2,1)S(1)} %fusion.1.refs_3_), channel_id=1, source_target_pairs={{0,32},{32,64},{64,96},{96,0},{1,33},{33,65},{65,97},{97,1},{2,34}... | collective-permute-start | bytes 1769480 | tf_op jit(solution)/shard_map/ppermute | solution.py:17
  153.7 1.3 collective-permute-start.16
  156.2 21.2 %all-to-all-start = ((f32[64,1,128]{2,1,0:T(1,128)}), f32[64,1,128]{2,1,0:T(1,128)S(1)}, u32[]{:S(2)}, u32[]{:S(2)}) async-start(f32[64,1,128]{2,1,0:T(1,128)} %bitcast.23), calls=%async_computation | async-start | bytes 65536 | tf_op jit(solution)/shard_map/all_to_all | solution.py:280
  164.0 14.7 %collective-permute-start.20 = (bf16[192,768]{1,0:T(8,128)(2,1)S(1)}, bf16[192,768]{1,0:T(8,128)(2,1)S(1)}, u32[]{:S(2)}, u32[]{:S(2)}) collective-permute-start(bf16[192,768]{1,0:T(8,128)(2,1)S(1)} %slice.87), channel_id=1, source_target_pairs={{0,96},{32,0},{64,32},{96,64},{1,97},{33,1},{65,33},{97,65},{2,98}... | collective-permute-start | bytes 884744 | tf_op jit(solution)/shard_map/ppermute | solution.py:17
  166.3 12.4 %collective-permute-start.19 = (bf16[192,768]{1,0:T(8,128)(2,1)S(1)}, bf16[192,768]{1,0:T(8,128)(2,1)S(1)}, u32[]{:S(2)}, u32[]{:S(2)}) collective-permute-start(bf16[192,768]{1,0:T(8,128)(2,1)S(1)} %slice.86), channel_id=1, source_target_pairs={{0,32},{32,64},{64,96},{96,0},{1,33},{33,65},{65,97},{97,1},{2,34}... | collective-permute-start | bytes 884744 | tf_op jit(solution)/shard_map/ppermute | solution.py:17
  190.5 13.0 %collective-permute-start.21 = (bf16[192,768]{1,0:T(8,128)(2,1)S(1)}, bf16[192,768]{1,0:T(8,128)(2,1)S(1)}, u32[]{:S(2)}, u32[]{:S(2)}) collective-permute-start(bf16[192,768]{1,0:T(8,128)(2,1)S(1)} %get-tuple-element.59), channel_id=1, source_target_pairs={{0,32},{32,64},{64,96},{96,0},{1,33},{33,65},{65,97},{97,1},{2,34}... | collective-permute-start | bytes 884744 | tf_op jit(solution)/shard_map/ppermute | solution.py:17
  191.1 12.5 %collective-permute-start.25 = (bf16[192,768]{1,0:T(8,128)(2,1)S(1)}, bf16[192,768]{1,0:T(8,128)(2,1)S(1)}, u32[]{:S(2)}, u32[]{:S(2)}) collective-permute-start(bf16[192,768]{1,0:T(8,128)(2,1)S(1)} %get-tuple-element.60), channel_id=1, source_target_pairs={{0,96},{32,0},{64,32},{96,64},{1,97},{33,1},{65,33},{97,65},{2,98}... | collective-permute-start | bytes 884744 | tf_op jit(solution)/shard_map/ppermute | solution.py:17
  201.4 10.1 %collective-permute-start.23 = (bf16[192,768]{1,0:T(8,128)(2,1)S(1)}, bf16[192,768]{1,0:T(8,128)(2,1)S(1)}, u32[]{:S(2)}, u32[]{:S(2)}) collective-permute-start(bf16[192,768]{1,0:T(8,128)(2,1)S(1)} %get-tuple-element.42), channel_id=1, source_target_pairs={{0,96},{32,0},{64,32},{96,64},{1,97},{33,1},{65,33},{97,65},{2,98}... | collective-permute-start | bytes 884744 | tf_op jit(solution)/shard_map/ppermute | solution.py:17
  203.4 11.2 %collective-permute-start.24 = (bf16[192,768]{1,0:T(8,128)(2,1)S(1)}, bf16[192,768]{1,0:T(8,128)(2,1)S(1)}, u32[]{:S(2)}, u32[]{:S(2)}) collective-permute-start(bf16[192,768]{1,0:T(8,128)(2,1)S(1)} %get-tuple-element.43), channel_id=1, source_target_pairs={{0,32},{32,64},{64,96},{96,0},{1,33},{33,65},{65,97},{97,1},{2,34}... | collective-permute-start | bytes 884744 | tf_op jit(solution)/shard_map/ppermute | solution.py:17
  203.6 14.5 %collective-permute-start.22 = (bf16[192,768]{1,0:T(8,128)(2,1)S(1)}, bf16[192,768]{1,0:T(8,128)(2,1)S(1)}, u32[]{:S(2)}, u32[]{:S(2)}) collective-permute-start(bf16[192,768]{1,0:T(8,128)(2,1)S(1)} %add_convert_fusion.1), channel_id=1, source_target_pairs={{0,32},{32,64},{64,96},{96,0},{1,33},{33,65},{65,97},{97,1},{2,34}... | collective-permute-start | bytes 884744 | tf_op jit(solution)/shard_map/ppermute | solution.py:17
  203.7 14.3 %collective-permute-start.26 = (bf16[192,768]{1,0:T(8,128)(2,1)S(1)}, bf16[192,768]{1,0:T(8,128)(2,1)S(1)}, u32[]{:S(2)}, u32[]{:S(2)}) collective-permute-start(bf16[192,768]{1,0:T(8,128)(2,1)S(1)} %add_convert_fusion), channel_id=1, source_target_pairs={{0,96},{32,0},{64,32},{96,64},{1,97},{33,1},{65,33},{97,65},{2,98}... | collective-permute-start | bytes 884744 | tf_op jit(solution)/shard_map/ppermute | solution.py:17
  220.2 3.0 %collective-permute-start.30 = (f32[64,128]{1,0:T(8,128)S(1)}, f32[64,128]{1,0:T(8,128)S(1)}, u32[]{:S(2)}, u32[]{:S(2)}) collective-permute-start(f32[64,128]{1,0:T(8,128)S(1)} %broadcast_in_dim.7), channel_id=1, source_target_pairs={{0,1},{1,0},{2,3},{3,2},{4,5},{5,4},{6,7},{7,6},{8,9},{9,8},{10,11... | collective-permute-start | bytes 98312 | tf_op jit(solution)/shard_map/ppermute | solution.py:279
  220.4 20.9 %collective-permute-start.27 = (bf16[192,384]{1,0:T(8,128)(2,1)S(1)}, bf16[192,384]{1,0:T(8,128)(2,1)S(1)}, u32[]{:S(2)}, u32[]{:S(2)}) collective-permute-start(bf16[192,384]{1,0:T(8,128)(2,1)S(1)} %get-tuple-element.58), channel_id=1, source_target_pairs={{0,24},{8,0},{16,8},{24,16},{1,25},{9,1},{17,9},{25,17},{2,26},{10... | collective-permute-start | bytes 442376 | tf_op jit(solution)/shard_map/ppermute | solution.py:17
  224.5 15.5 %all-to-all-start.1 = ((f32[64,1,128]{2,1,0:T(1,128)}), f32[64,1,128]{2,1,0:T(1,128)S(1)}, u32[]{:S(2)}, u32[]{:S(2)}) async-start(f32[64,1,128]{2,1,0:T(1,128)} %bitcast.38), calls=%async_computation.1 | async-start | bytes 65536 | tf_op jit(solution)/shard_map/all_to_all | solution.py:280
  230.5 10.8 %collective-permute-start.28 = (bf16[192,384]{1,0:T(8,128)(2,1)S(1)}, bf16[192,384]{1,0:T(8,128)(2,1)S(1)}, u32[]{:S(2)}, u32[]{:S(2)}) collective-permute-start(bf16[192,384]{1,0:T(8,128)(2,1)S(1)} %get-tuple-element.57), channel_id=1, source_target_pairs={{0,16},{8,24},{16,0},{24,8},{1,17},{9,25},{17,1},{25,9},{2,18},{10... | collective-permute-start | bytes 442376 | tf_op jit(solution)/shard_map/ppermute | solution.py:17
  233.6 7.7 %collective-permute-start.29 = (bf16[192,384]{1,0:T(8,128)(2,1)S(1)}, bf16[192,384]{1,0:T(8,128)(2,1)S(1)}, u32[]{:S(2)}, u32[]{:S(2)}) collective-permute-start(bf16[192,384]{1,0:T(8,128)(2,1)S(1)} %get-tuple-element.55), channel_id=1, source_target_pairs={{0,8},{8,16},{16,24},{24,0},{1,9},{9,17},{17,25},{25,1},{2,10},{10... | collective-permute-start | bytes 442376 | tf_op jit(solution)/shard_map/ppermute | solution.py:17
Sparse Core Ops, SparseCore 0:
  9.6 92.9 all-gather.1

commit v7 on v6

--- a/solution.py
+++ b/solution.py
@@ -10,7 +10,9 @@
 BF16, F32 = jnp.bfloat16, jnp.float32
 N = 4
 NT = (((1,), (1,)), ((), ()))
-PARAMS = pltpu.CompilerParams(vmem_limit_bytes=52 << 20)
+FIRST = pltpu.CompilerParams(vmem_limit_bytes=36 << 20)
+MOVED = pltpu.CompilerParams(vmem_limit_bytes=24 << 20)
+TERMS = pltpu.CompilerParams(vmem_limit_bytes=20 << 20)
 
 
 def shift(value, axis, step):
@@ -92,7 +94,7 @@
             jax.ShapeDtypeStruct((cols, rows), BF16),
             jax.ShapeDtypeStruct((cols, deep), BF16),
         ],
-        compiler_params=PARAMS,
+        compiler_params=FIRST,
         cost_estimate=cost(cols, (blocks + per) * wide, rows, rows * cols),
     )(jnp.stack(which).astype(jnp.int32), x, *w, t)
 
@@ -120,7 +122,7 @@
             out_specs=pl.BlockSpec((cols, tile), lambda i, which: (0, i)),
         ),
         out_shape=jax.ShapeDtypeStruct((cols, rows), F32),
-        compiler_params=PARAMS,
+        compiler_params=MOVED,
         cost_estimate=cost(cols, deep * count, rows),
     )(jnp.stack(which).astype(jnp.int32), *([x] * count), *pieces)
 
@@ -157,7 +159,7 @@
             scratch_shapes=[pltpu.VMEM((cols, deep), F32)],
         ),
         out_shape=[jax.ShapeDtypeStruct((cols, rows), BF16), jax.ShapeDtypeStruct((cols, deep), BF16)],
-        compiler_params=PARAMS,
+        compiler_params=MOVED,
         cost_estimate=cost(cols, 2 * deep, rows, rows * cols),
     )(jnp.stack(which).astype(jnp.int32), scale, x, piece, part, hidden, t)
 
@@ -201,7 +203,7 @@
             scratch_shapes=[pltpu.VMEM((cols, per * wide), F32)] * count,
         ),
         out_shape=[jax.ShapeDtypeStruct((tall, per * wide), kind) for kind in kinds],
-        compiler_params=PARAMS,
+        compiler_params=TERMS,
         cost_estimate=cost(cols * count, rows, per * wide),
     )(jnp.stack(which).astype(jnp.int32), *([x] * count), s)
 
@@ -257,7 +259,7 @@
             out_specs=[pl.BlockSpec((cols, size), lambda i, which: (0, 0)) for size in wide],
         ),
         out_shape=[jax.ShapeDtypeStruct((cols, size), array.dtype) for size in wide],
-        compiler_params=PARAMS,
+        compiler_params=FIRST,
         cost_estimate=cost(0, 0, 0),
     )(jnp.stack([lax.rem(me + k, N) for k in range(N)]).astype(jnp.int32), *([array] * N))
 
@@ -303,6 +305,7 @@
     w = ring_gather(in_order(w_pieces, iy).reshape(-1, cols).T, "x")
 
     at = lambda k: lax.rem(ix + k, N)
+    x = pltpu.with_memory_space_constraint(x, pltpu.HBM)
     hidden, slope, term = first_slopes(x, w, t, [at(k) for k in range(N)] + tiles)
     first = ring_sum(x, slope, term, ix)
     own, after, far, before = ring_gather_halves(first.astype(BF16), "x")

time: 250 us -> 263 us (1.052)
  local copies, waits for them, and re-layouts: 7.74 us -> 28 us
  Pallas kernels: 68.9 us -> 61 us
  waiting for transfers between devices: 91.3 us -> 87.1 us
  other arithmetic: 9.36 us -> 13.1 us
    unnamed x15 -> x39, local copies, waits for them, and re-layouts: 2.06 us -> 15.4 us
    ppermute x29, waiting for transfers between devices: 56.9 us -> 53.4 us  [shift(): return lax.ppermute(value, axis, [(i, (i + step) % N) for i in range(N)])]
  transfers between devices with their start and end apart: 34 -> 34, of which waited for: 13 -> 14; matrix products, arithmetic and copies ran while one was open for 5% -> 8% of each run, Pallas kernels for 15% -> 13%
where the time goes in v7:
time: 263 us; the launch traced here: 262 us
  waiting for transfers between devices  87.1 us (33%)
  Pallas kernels  61 us (23%)
  starting transfers between devices  57.6 us (22%)
  local copies, waits for them, and re-layouts  28 us (11%)
  between operations  15.2 us (6%)
  other arithmetic  13.1 us (5%)
    ppermute x29, waiting for transfers between devices, shift(): return lax.ppermute(value, axis, [(i, (i + step) % N) for i in range(N)])  53.4 us
    ppermute x29, starting transfers between devices, shift(): return lax.ppermute(value, axis, [(i, (i + step) % N) for i in range(N)])  44.2 us
    all_gather x1, waiting for transfers between devices, per_device(): lax.all_gather(tokens, ('z', 'c', 'y'), axis=0, tiled=True)  25.8 us
    pallas_call x4, Pallas kernels, terms(): pl.pallas_call(kernel, grid_spec=pltpu.PrefetchScalarGridSpec(num_scalar_...  22.5 us
    pallas_call x1, Pallas kernels, first_slopes(): pl.pallas_call(kernel, grid_spec=pltpu.PrefetchScalarGridSpec(num_scalar_...  17.8 us
    unnamed x39, local copies, waits for them, and re-layouts  15.4 us
    all_to_all x2, starting transfers between devices, total_of(): lax.all_to_all(total, ('x', 'y', 'z'), split_axis=0, concat_axis=0, tiled...  13.4 us
    pallas_call x1, Pallas kernels, moved(): pl.pallas_call(kernel, grid_spec=pltpu.PrefetchScalarGridSpec(num_scalar_...  9.84 us
  transfers between devices with their start and end apart: 34, of which 14 were waited for; matrix products, arithmetic and copies ran while one was open for 8% of the time, Pallas kernels for 13%

profile of v7, /device:TPU:0, one launch (start us, length us, event | category | flops | bytes accessed | tf_op | source)
XLA Modules:
  0.0 262.1 jit_solution(6397973474466129240)
XLA Ops:
  8.4 3.2 %collective-permute-start = (bf16[192,384]{1,0:T(8,128)(2,1)S(1)}, bf16[192,384]{1,0:T(8,128)(2,1)S(1)}, u32[]{:S(2)}, u32[]{:S(2)}) collective-permute-start(bf16[192,384]{1,0:T(8,128)(2,1)S(1)} %get-tuple-element.64), channel_id=1, source_target_pairs={{0,24},{8,0},{16,8},{24,16},{1,25},{9,1},{17,9},{25,17},{2,26},{10... | collective-permute-start | bytes 442376 | tf_op jit(solution)/shard_map/ppermute | solution.py:19
  13.3 1.7 copy-done
  15.0 1.2 shard_map.37
  17.8 2.0 collective-permute-done.1
  19.9 1.7 collective-permute-done.2
  21.5 3.2 %collective-permute-start.6 = (bf16[384,1152]{1,0:T(8,128)(2,1)S(1)}, bf16[384,1152]{1,0:T(8,128)(2,1)}, u32[]{:S(2)}, u32[]{:S(2)}) collective-permute-start(bf16[384,1152]{1,0:T(8,128)(2,1)S(1)} %get-tuple-element.28), channel_id=1, source_target_pairs={{0,24},{8,0},{16,8},{24,16},{1,25},{9,1},{17,9},{25,17},{2,26},{10... | collective-permute-start | bytes 2654216 | tf_op jit(solution)/shard_map/ppermute | solution.py:19
  25.9 1.3 copy.11
  27.2 2.8 %collective-permute-start.3 = (bf16[384,768]{1,0:T(8,128)(2,1)S(1)}, bf16[384,768]{1,0:T(8,128)(2,1)S(1)}, u32[]{:S(2)}, u32[]{:S(2)}) collective-permute-start(bf16[384,768]{1,0:T(8,128)(2,1)S(1)} %bitcast.66), channel_id=1, source_target_pairs={{0,96},{32,0},{64,32},{96,64},{1,97},{33,1},{65,33},{97,65},{2,98}... | collective-permute-start | bytes 1769480 | tf_op jit(solution)/shard_map/ppermute | solution.py:19
  31.7 21.0 %collective-permute-done.6 = bf16[384,1152]{1,0:T(8,128)(2,1)} collective-permute-done((bf16[384,1152]{1,0:T(8,128)(2,1)S(1)}, bf16[384,1152]{1,0:T(8,128)(2,1)}, u32[]{:S(2)}, u32[]{:S(2)}) %collective-permute-start.6) | collective-permute-done | bytes 884768 | tf_op jit(solution)/shard_map/ppermute | solution.py:19
  53.8 2.4 collective-permute-start.9
  59.4 10.0 %collective-permute-done.9 = bf16[384,384]{1,0:T(8,128)(2,1)S(1)} collective-permute-done((bf16[384,384]{1,0:T(8,128)(2,1)S(1)}, bf16[384,384]{1,0:T(8,128)(2,1)S(1)}, u32[]{:S(2)}, u32[]{:S(2)}) %collective-permute-start.9) | collective-permute-done | bytes 294944 | tf_op jit(solution)/shard_map/ppermute | solution.py:19
  69.4 4.7 %collective-permute-done.8 = bf16[384,384]{1,0:T(8,128)(2,1)S(1)} collective-permute-done((bf16[384,384]{1,0:T(8,128)(2,1)S(1)}, bf16[384,384]{1,0:T(8,128)(2,1)S(1)}, u32[]{:S(2)}, u32[]{:S(2)}) %collective-permute-start.8) | collective-permute-done | bytes 294944 | tf_op jit(solution)/shard_map/ppermute | solution.py:19
  76.9 25.8 %all-gather.2.cloned.1.call-done = bf16[24576,384]{1,0:T(8,128)(2,1)} async-done(((bf16[768,384]{1,0:T(8,128)(2,1)}), bf16[24576,384]{1,0:T(8,128)(2,1)}) %all-gather.2.cloned.1.call-update) | async-done | bytes 18874384 | tf_op jit(solution)/shard_map/all_gather | solution.py:295
  105.9 17.8 %shard_map.38 = (f32[384,3072]{1,0:T(8,128)S(1)}, bf16[384,3072]{1,0:T(8,128)(2,1)S(1)}, bf16[384,768]{1,0:T(8,128)(2,1)S(1)}) custom-call(s32[8]{0:T(128)S(1)} %stack.126.which_ref, bf16[8,3072,384]{2,1,0:T(8,128)(2,1)} %bitcast.70, bf16[384,768]{1,0:T(8,128)(2,1)S(1)} %bitcast.69, bf16[384,768]{1,0:T(8,128)(2,1)S(1)} %copy-done.8, ...), custom_call_target="tpu_custom_call" | custom-call | flops 9059696640 | bytes 31260672 | tf_op jit(solution)/shard_map/pallas_call | solution.py:81
  123.7 1.5 collective-permute-start.10
  125.3 1.8 collective-permute-start.14
  127.0 7.2 %shard_map.40 = (f32[192,768]{1,0:T(8,128)S(1)}, bf16[192,768]{1,0:T(8,128)(2,1)S(1)}, bf16[192,768]{1,0:T(8,128)(2,1)S(1)}, f32[192,768]{1,0:T(8,128)S(1)}) custom-call(s32[2]{0:T(128)S(1)} %pad_add_fusion.1.which_ref, bf16[8,3072,384]{2,1,0:T(8,128)(2,1)} %bitcast.71, bf16[8,3072,384]{2,1,0:T(8,128)(2,1)} %bitcast.72, ...), custom_call_target="tpu_custom_call" | custom-call | flops 3623878656 | bytes 11796480 | tf_op jit(solution)/shard_map/pallas_call | solution.py:196
  134.3 1.6 collective-permute-start.12
  136.8 3.2 %collective-permute-start.15 = (bf16[192,768]{1,0:T(8,128)(2,1)S(1)}, bf16[192,768]{1,0:T(8,128)(2,1)S(1)}, u32[]{:S(2)}, u32[]{:S(2)}) collective-permute-start(bf16[192,768]{1,0:T(8,128)(2,1)S(1)} %add_convert_fusion.2), channel_id=1, source_target_pairs={{0,96},{32,0},{64,32},{96,64},{1,97},{33,1},{65,33},{97,65},{2,98}... | collective-permute-start | bytes 884744 | tf_op jit(solution)/shard_map/ppermute | solution.py:19
  140.1 4.0 %shard_map.39 = f32[384,768]{1,0:T(8,128)S(1)} custom-call(s32[1]{0:T(128)} %bitcast.which_ref, bf16[8,3072,384]{2,1,0:T(8,128)(2,1)} %bitcast.73, bf16[384,3072]{1,0:T(8,128)(2,1)S(1)} %get-tuple-element.30.refs_1_.refs_2_), custom_call_target="tpu_custom_call" | custom-call | flops 1811939328 | bytes 8257536 | tf_op jit(solution)/shard_map/pallas_call | solution.py:196
  144.3 2.7 %collective-permute-done.13 = bf16[192,768]{1,0:T(8,128)(2,1)S(1)} collective-permute-done((bf16[192,768]{1,0:T(8,128)(2,1)S(1)}, bf16[192,768]{1,0:T(8,128)(2,1)S(1)}, u32[]{:S(2)}, u32[]{:S(2)}) %collective-permute-start.13) | collective-permute-done | bytes 294944 | tf_op jit(solution)/shard_map/ppermute | solution.py:19
  147.0 4.7 %collective-permute-done.11 = bf16[192,768]{1,0:T(8,128)(2,1)S(1)} collective-permute-done((bf16[192,768]{1,0:T(8,128)(2,1)S(1)}, bf16[192,768]{1,0:T(8,128)(2,1)S(1)}, u32[]{:S(2)}, u32[]{:S(2)}) %collective-permute-start.11) | collective-permute-done | bytes 294944 | tf_op jit(solution)/shard_map/ppermute | solution.py:19
  152.3 1.8 collective-permute-start.18
  155.0 1.2 broadcast_in_dim.6
  156.4 1.4 collective-permute-done.16
  157.7 2.0 broadcast_add_fusion.1
  159.7 7.3 %all-to-all-start = ((f32[64,1,128]{2,1,0:T(1,128)}), f32[64,1,128]{2,1,0:T(1,128)}, u32[]{:S(2)}, u32[]{:S(2)}) async-start(f32[64,1,128]{2,1,0:T(1,128)} %bitcast.84), calls=%async_computation | async-start | bytes 65536 | tf_op jit(solution)/shard_map/all_to_all | solution.py:282
  167.8 2.9 %collective-permute-start.20 = (bf16[192,768]{1,0:T(8,128)(2,1)}, bf16[192,768]{1,0:T(8,128)(2,1)}, u32[]{:S(2)}, u32[]{:S(2)}) collective-permute-start(bf16[192,768]{1,0:T(8,128)(2,1)} %slice.87), channel_id=1, source_target_pairs={{0,96},{32,0},{64,32},{96,64},{1,97},{33,1},{65,33},{97,65},{2,98}... | collective-permute-start | bytes 884744 | tf_op jit(solution)/shard_map/ppermute | solution.py:19
  170.7 1.7 slice.86
  172.4 9.8 %shard_map.41.part_ref = f32[384,3072]{1,0:T(8,128)S(1)} custom-call(s32[3]{0:T(128)S(1)} %pad_add_fusion.2.which_ref, bf16[8,3072,384]{2,1,0:T(8,128)(2,1)} %bitcast.74, bf16[8,3072,384]{2,1,0:T(8,128)(2,1)} %bitcast.75, bf16[8,3072,384]{2,1,0:T(8,128)(2,1)} %bitcast.76, bf16[384,768]{1,0:T(8,128)(2,1)S(1)} %fusion.1.refs_3_, ...), custom_call_target="tpu_custom_call" | custom-call | flops 5435817984 | bytes 20643840 | tf_op jit(solution)/shard_map/pallas_call | solution.py:116
  182.3 2.1 copy-done.1
  184.4 1.4 slice_reduce_fusion.1
  187.6 2.3 copy-done.2
  189.9 2.3 copy-done.6
  192.3 9.7 %shard_map.42 = (bf16[384,3072]{1,0:T(8,128)(2,1)S(1)}, bf16[384,768]{1,0:T(8,128)(2,1)S(1)}) custom-call(s32[5]{0:T(128)S(1)} %stack.123.which_ref, f32[1,1]{1,0:T(1,128)} %bitcast.25.scale_ref, bf16[8,3072,384]{2,1,0:T(8,128)(2,1)} %bitcast.77, bf16[384,768]{1,0:T(8,128)(2,1)S(1)} %pad_maximum_fusion.3.f_ref, f32[384,3072]{1,0:T(8,128)S(1)} %copy-done.2, ...), custom_call_target="tpu_custom_call" | custom-call | flops 3623878656 | bytes 15335424 | tf_op jit(solution)/shard_map/pallas_call | solution.py:145
  202.7 2.7 %collective-permute-start.25 = (bf16[192,768]{1,0:T(8,128)(2,1)S(1)}, bf16[192,768]{1,0:T(8,128)(2,1)S(1)}, u32[]{:S(2)}, u32[]{:S(2)}) collective-permute-start(bf16[192,768]{1,0:T(8,128)(2,1)S(1)} %get-tuple-element.60), channel_id=1, source_target_pairs={{0,96},{32,0},{64,32},{96,64},{1,97},{33,1},{65,33},{97,65},{2,98}... | collective-permute-start | bytes 884744 | tf_op jit(solution)/shard_map/ppermute | solution.py:19
  205.4 7.2 %shard_map.44 = (f32[192,768]{1,0:T(8,128)S(1)}, bf16[192,768]{1,0:T(8,128)(2,1)S(1)}, bf16[192,768]{1,0:T(8,128)(2,1)S(1)}, f32[192,768]{1,0:T(8,128)S(1)}) custom-call(s32[2]{0:T(128)S(1)} %pad_add_fusion.1.which_ref, bf16[8,3072,384]{2,1,0:T(8,128)(2,1)} %bitcast.78, bf16[8,3072,384]{2,1,0:T(8,128)(2,1)} %bitcast.79, ...), custom_call_target="tpu_custom_call" | custom-call | flops 3623878656 | bytes 11796480 | tf_op jit(solution)/shard_map/pallas_call | solution.py:196
  212.7 2.0 collective-permute-start.23
  216.3 3.2 %collective-permute-start.26 = (bf16[192,768]{1,0:T(8,128)(2,1)}, bf16[192,768]{1,0:T(8,128)(2,1)}, u32[]{:S(2)}, u32[]{:S(2)}) collective-permute-start(bf16[192,768]{1,0:T(8,128)(2,1)} %add_convert_fusion), channel_id=1, source_target_pairs={{0,96},{32,0},{64,32},{96,64},{1,97},{33,1},{65,33},{97,65},{2,98}... | collective-permute-start | bytes 884744 | tf_op jit(solution)/shard_map/ppermute | solution.py:19
  219.5 4.0 %shard_map.43 = f32[384,768]{1,0:T(8,128)S(1)} custom-call(s32[1]{0:T(128)} %bitcast.which_ref, bf16[8,3072,384]{2,1,0:T(8,128)(2,1)} %bitcast.80, bf16[384,3072]{1,0:T(8,128)(2,1)S(1)} %copy-done.4), custom_call_target="tpu_custom_call" | custom-call | flops 1811939328 | bytes 8257536 | tf_op jit(solution)/shard_map/pallas_call | solution.py:196
  223.6 2.3 collective-permute-done.24
  225.8 3.6 %collective-permute-done.22 = bf16[192,768]{1,0:T(8,128)(2,1)} collective-permute-done((bf16[192,768]{1,0:T(8,128)(2,1)}, bf16[192,768]{1,0:T(8,128)(2,1)}, u32[]{:S(2)}, u32[]{:S(2)}) %collective-permute-start.22) | collective-permute-done | bytes 294944 | tf_op jit(solution)/shard_map/ppermute | solution.py:19
  229.4 1.3 fusion.4
  232.8 2.8 %collective-permute-start.27 = (bf16[192,384]{1,0:T(8,128)(2,1)S(1)}, bf16[192,384]{1,0:T(8,128)(2,1)S(1)}, u32[]{:S(2)}, u32[]{:S(2)}) collective-permute-start(bf16[192,384]{1,0:T(8,128)(2,1)S(1)} %get-tuple-element.58), channel_id=1, source_target_pairs={{0,24},{8,0},{16,8},{24,16},{1,25},{9,1},{17,9},{25,17},{2,26},{10... | collective-permute-start | bytes 442376 | tf_op jit(solution)/shard_map/ppermute | solution.py:19
  235.7 1.2 broadcast_add_fusion
  236.9 6.0 %all-to-all-start.1 = ((f32[64,1,128]{2,1,0:T(1,128)}), f32[64,1,128]{2,1,0:T(1,128)S(1)}, u32[]{:S(2)}, u32[]{:S(2)}) async-start(f32[64,1,128]{2,1,0:T(1,128)} %bitcast.38), calls=%async_computation.1 | async-start | bytes 65536 | tf_op jit(solution)/shard_map/all_to_all | solution.py:282
  242.9 3.2 %collective-permute-start.28 = (bf16[192,384]{1,0:T(8,128)(2,1)S(1)}, bf16[192,384]{1,0:T(8,128)(2,1)S(1)}, u32[]{:S(2)}, u32[]{:S(2)}) collective-permute-start(bf16[192,384]{1,0:T(8,128)(2,1)S(1)} %get-tuple-element.57), channel_id=1, source_target_pairs={{0,16},{8,24},{16,0},{24,8},{1,17},{9,25},{17,1},{25,9},{2,18},{10... | collective-permute-start | bytes 442376 | tf_op jit(solution)/shard_map/ppermute | solution.py:19
  246.7 5.8 %all-to-all-done.1 = f32[64,1,128]{2,1,0:T(1,128)S(1)} async-done(((f32[64,1,128]{2,1,0:T(1,128)}), f32[64,1,128]{2,1,0:T(1,128)S(1)}, u32[]{:S(2)}, u32[]{:S(2)}) %all-to-all-start.1) | async-done | bytes 32800 | tf_op jit(solution)/shard_map/all_to_all | solution.py:282
  (109 shorter events, 30.1 us)
Async XLA Ops:
  6.5 96.2 %all-gather.2.cloned.1.call-start = ((), (), s32[]{:S(2)}) async-start(), calls=%async_computation.2 | async-start | bytes 19464192 | tf_op jit(solution)/shard_map/all_gather | solution.py:295
  8.4 9.4 %collective-permute-start = (bf16[192,384]{1,0:T(8,128)(2,1)S(1)}, bf16[192,384]{1,0:T(8,128)(2,1)S(1)}, u32[]{:S(2)}, u32[]{:S(2)}) collective-permute-start(bf16[192,384]{1,0:T(8,128)(2,1)S(1)} %get-tuple-element.64), channel_id=1, source_target_pairs={{0,24},{8,0},{16,8},{24,16},{1,25},{9,1},{17,9},{25,17},{2,26},{10... | collective-permute-start | bytes 442376 | tf_op jit(solution)/shard_map/ppermute | solution.py:19
  11.6 8.3 %collective-permute-start.1 = (bf16[192,384]{1,0:T(8,128)(2,1)S(1)}, bf16[192,384]{1,0:T(8,128)(2,1)S(1)}, u32[]{:S(2)}, u32[]{:S(2)}) collective-permute-start(bf16[192,384]{1,0:T(8,128)(2,1)S(1)} %get-tuple-element.65), channel_id=1, source_target_pairs={{0,16},{8,24},{16,0},{24,8},{1,17},{9,25},{17,1},{25,9},{2,18},{10... | collective-permute-start | bytes 442376 | tf_op jit(solution)/shard_map/ppermute | solution.py:19
  12.2 9.3 %collective-permute-start.2 = (bf16[192,384]{1,0:T(8,128)(2,1)S(1)}, bf16[192,384]{1,0:T(8,128)(2,1)S(1)}, u32[]{:S(2)}, u32[]{:S(2)}) collective-permute-start(bf16[192,384]{1,0:T(8,128)(2,1)S(1)} %get-tuple-element.63), channel_id=1, source_target_pairs={{0,8},{8,16},{16,24},{24,0},{1,9},{9,17},{17,25},{25,1},{2,10},{10... | collective-permute-start | bytes 442376 | tf_op jit(solution)/shard_map/ppermute | solution.py:19
  13.3 1.7 copy-start
  21.5 34.6 %collective-permute-start.7 = (bf16[384,1152]{1,0:T(8,128)(2,1)S(1)}, bf16[384,1152]{1,0:T(8,128)(2,1)}, u32[]{:S(2)}, u32[]{:S(2)}) collective-permute-start(bf16[384,1152]{1,0:T(8,128)(2,1)S(1)} %get-tuple-element.29), channel_id=1, source_target_pairs={{0,8},{8,16},{16,24},{24,0},{1,9},{9,17},{17,25},{25,1},{2,10},{10... | collective-permute-start | bytes 2654216 | tf_op jit(solution)/shard_map/ppermute | solution.py:19
  21.5 31.2 %collective-permute-start.6 = (bf16[384,1152]{1,0:T(8,128)(2,1)S(1)}, bf16[384,1152]{1,0:T(8,128)(2,1)}, u32[]{:S(2)}, u32[]{:S(2)}) collective-permute-start(bf16[384,1152]{1,0:T(8,128)(2,1)S(1)} %get-tuple-element.28), channel_id=1, source_target_pairs={{0,24},{8,0},{16,8},{24,16},{1,25},{9,1},{17,9},{25,17},{2,26},{10... | collective-permute-start | bytes 2654216 | tf_op jit(solution)/shard_map/ppermute | solution.py:19
  27.2 47.2 %collective-permute-start.3 = (bf16[384,768]{1,0:T(8,128)(2,1)S(1)}, bf16[384,768]{1,0:T(8,128)(2,1)S(1)}, u32[]{:S(2)}, u32[]{:S(2)}) collective-permute-start(bf16[384,768]{1,0:T(8,128)(2,1)S(1)} %bitcast.66), channel_id=1, source_target_pairs={{0,96},{32,0},{64,32},{96,64},{1,97},{33,1},{65,33},{97,65},{2,98}... | collective-permute-start | bytes 1769480 | tf_op jit(solution)/shard_map/ppermute | solution.py:19
  30.0 45.2 %collective-permute-start.4 = (bf16[384,768]{1,0:T(8,128)(2,1)S(1)}, bf16[384,768]{1,0:T(8,128)(2,1)S(1)}, u32[]{:S(2)}, u32[]{:S(2)}) collective-permute-start(bf16[384,768]{1,0:T(8,128)(2,1)S(1)} %bitcast.67), channel_id=1, source_target_pairs={{0,64},{32,96},{64,0},{96,32},{1,65},{33,97},{65,1},{97,33},{2,66}... | collective-permute-start | bytes 1769480 | tf_op jit(solution)/shard_map/ppermute | solution.py:19
  30.8 45.2 %collective-permute-start.5 = (bf16[384,768]{1,0:T(8,128)(2,1)S(1)}, bf16[384,768]{1,0:T(8,128)(2,1)S(1)}, u32[]{:S(2)}, u32[]{:S(2)}) collective-permute-start(bf16[384,768]{1,0:T(8,128)(2,1)S(1)} %bitcast.68), channel_id=1, source_target_pairs={{0,32},{32,64},{64,96},{96,0},{1,33},{33,65},{65,97},{97,1},{2,34}... | collective-permute-start | bytes 1769480 | tf_op jit(solution)/shard_map/ppermute | solution.py:19
  53.8 15.6 %collective-permute-start.9 = (bf16[384,384]{1,0:T(8,128)(2,1)S(1)}, bf16[384,384]{1,0:T(8,128)(2,1)S(1)}, u32[]{:S(2)}, u32[]{:S(2)}) collective-permute-start(bf16[384,384]{1,0:T(8,128)(2,1)S(1)} %slice.82), channel_id=1, source_target_pairs={{0,24},{8,0},{16,8},{24,16},{1,25},{9,1},{17,9},{25,17},{2,26},{10... | collective-permute-start | bytes 884744 | tf_op jit(solution)/shard_map/ppermute | solution.py:19
  57.1 16.9 %collective-permute-start.8 = (bf16[384,384]{1,0:T(8,128)(2,1)S(1)}, bf16[384,384]{1,0:T(8,128)(2,1)S(1)}, u32[]{:S(2)}, u32[]{:S(2)}) collective-permute-start(bf16[384,384]{1,0:T(8,128)(2,1)S(1)} %slice.81), channel_id=1, source_target_pairs={{0,8},{8,16},{16,24},{24,0},{1,9},{9,17},{17,25},{25,1},{2,10},{10... | collective-permute-start | bytes 884744 | tf_op jit(solution)/shard_map/ppermute | solution.py:19
  74.4 0.8 copy-start.7
  75.2 0.8 copy-start.9
  76.1 0.8 copy-start.11
  102.7 1.1 copy-start.8
  103.8 1.1 copy-start.10
  104.8 1.1 copy-start.12
  123.7 10.6 %copy-start.5 = (f32[384,3072]{1,0:T(8,128)}, f32[384,3072]{1,0:T(8,128)S(1)}, u32[]{:S(2)}) copy-start(f32[384,3072]{1,0:T(8,128)S(1)} %get-tuple-element.38.h_ref) | copy-start | bytes 14155780
  123.7 12.7 %collective-permute-start.10 = (bf16[192,768]{1,0:T(8,128)(2,1)S(1)}, bf16[192,768]{1,0:T(8,128)(2,1)S(1)}, u32[]{:S(2)}, u32[]{:S(2)}) collective-permute-start(bf16[192,768]{1,0:T(8,128)(2,1)S(1)} %get-tuple-element.61), channel_id=1, source_target_pairs={{0,32},{32,64},{64,96},{96,0},{1,33},{33,65},{65,97},{97,1},{2,34}... | collective-permute-start | bytes 884744 | tf_op jit(solution)/shard_map/ppermute | solution.py:19
  125.3 11.5 %collective-permute-start.14 = (bf16[192,768]{1,0:T(8,128)(2,1)S(1)}, bf16[192,768]{1,0:T(8,128)(2,1)S(1)}, u32[]{:S(2)}, u32[]{:S(2)}) collective-permute-start(bf16[192,768]{1,0:T(8,128)(2,1)S(1)} %get-tuple-element.62), channel_id=1, source_target_pairs={{0,96},{32,0},{64,32},{96,64},{1,97},{33,1},{65,33},{97,65},{2,98}... | collective-permute-start | bytes 884744 | tf_op jit(solution)/shard_map/ppermute | solution.py:19
  134.3 10.0 %collective-permute-start.12 = (bf16[192,768]{1,0:T(8,128)(2,1)S(1)}, bf16[192,768]{1,0:T(8,128)(2,1)S(1)}, u32[]{:S(2)}, u32[]{:S(2)}) collective-permute-start(bf16[192,768]{1,0:T(8,128)(2,1)S(1)} %get-tuple-element.33), channel_id=1, source_target_pairs={{0,96},{32,0},{64,32},{96,64},{1,97},{33,1},{65,33},{97,65},{2,98}... | collective-permute-start | bytes 884744 | tf_op jit(solution)/shard_map/ppermute | solution.py:19
  135.8 11.2 %collective-permute-start.13 = (bf16[192,768]{1,0:T(8,128)(2,1)S(1)}, bf16[192,768]{1,0:T(8,128)(2,1)S(1)}, u32[]{:S(2)}, u32[]{:S(2)}) collective-permute-start(bf16[192,768]{1,0:T(8,128)(2,1)S(1)} %get-tuple-element.34), channel_id=1, source_target_pairs={{0,32},{32,64},{64,96},{96,0},{1,33},{33,65},{65,97},{97,1},{2,34}... | collective-permute-start | bytes 884744 | tf_op jit(solution)/shard_map/ppermute | solution.py:19
  136.4 15.2 %collective-permute-start.11 = (bf16[192,768]{1,0:T(8,128)(2,1)S(1)}, bf16[192,768]{1,0:T(8,128)(2,1)S(1)}, u32[]{:S(2)}, u32[]{:S(2)}) collective-permute-start(bf16[192,768]{1,0:T(8,128)(2,1)S(1)} %add_convert_fusion.3), channel_id=1, source_target_pairs={{0,32},{32,64},{64,96},{96,0},{1,33},{33,65},{65,97},{97,1},{2,34}... | collective-permute-start | bytes 884744 | tf_op jit(solution)/shard_map/ppermute | solution.py:19
  136.8 14.9 %collective-permute-start.15 = (bf16[192,768]{1,0:T(8,128)(2,1)S(1)}, bf16[192,768]{1,0:T(8,128)(2,1)S(1)}, u32[]{:S(2)}, u32[]{:S(2)}) collective-permute-start(bf16[192,768]{1,0:T(8,128)(2,1)S(1)} %add_convert_fusion.2), channel_id=1, source_target_pairs={{0,96},{32,0},{64,32},{96,64},{1,97},{33,1},{65,33},{97,65},{2,98}... | collective-permute-start | bytes 884744 | tf_op jit(solution)/shard_map/ppermute | solution.py:19
  152.0 15.1 %collective-permute-start.17 = (bf16[384,768]{1,0:T(8,128)(2,1)S(1)}, bf16[384,768]{1,0:T(8,128)(2,1)S(1)}, u32[]{:S(2)}, u32[]{:S(2)}) collective-permute-start(bf16[384,768]{1,0:T(8,128)(2,1)S(1)} %fusion.1.refs_3_), channel_id=1, source_target_pairs={{0,96},{32,0},{64,32},{96,64},{1,97},{33,1},{65,33},{97,65},{2,98}... | collective-permute-start | bytes 1769480 | tf_op jit(solution)/shard_map/ppermute | solution.py:19
  152.3 18.4 %collective-permute-start.18 = (bf16[384,768]{1,0:T(8,128)(2,1)S(1)}, bf16[384,768]{1,0:T(8,128)(2,1)}, u32[]{:S(2)}, u32[]{:S(2)}) collective-permute-start(bf16[384,768]{1,0:T(8,128)(2,1)S(1)} %fusion.1.refs_3_), channel_id=1, source_target_pairs={{0,32},{32,64},{64,96},{96,0},{1,33},{33,65},{65,97},{97,1},{2,34}... | collective-permute-start | bytes 1769480 | tf_op jit(solution)/shard_map/ppermute | solution.py:19
  156.2 1.6 collective-permute-start.16
  159.7 24.7 %all-to-all-start = ((f32[64,1,128]{2,1,0:T(1,128)}), f32[64,1,128]{2,1,0:T(1,128)}, u32[]{:S(2)}, u32[]{:S(2)}) async-start(f32[64,1,128]{2,1,0:T(1,128)} %bitcast.84), calls=%async_computation | async-start | bytes 65536 | tf_op jit(solution)/shard_map/all_to_all | solution.py:282
  167.8 18.7 %collective-permute-start.20 = (bf16[192,768]{1,0:T(8,128)(2,1)}, bf16[192,768]{1,0:T(8,128)(2,1)}, u32[]{:S(2)}, u32[]{:S(2)}) collective-permute-start(bf16[192,768]{1,0:T(8,128)(2,1)} %slice.87), channel_id=1, source_target_pairs={{0,96},{32,0},{64,32},{96,64},{1,97},{33,1},{65,33},{97,65},{2,98}... | collective-permute-start | bytes 884744 | tf_op jit(solution)/shard_map/ppermute | solution.py:19
  172.4 14.1 %collective-permute-start.19 = (bf16[192,768]{1,0:T(8,128)(2,1)}, bf16[192,768]{1,0:T(8,128)(2,1)}, u32[]{:S(2)}, u32[]{:S(2)}) collective-permute-start(bf16[192,768]{1,0:T(8,128)(2,1)} %slice.86), channel_id=1, source_target_pairs={{0,32},{32,64},{64,96},{96,0},{1,33},{33,65},{65,97},{97,1},{2,34}... | collective-permute-start | bytes 884744 | tf_op jit(solution)/shard_map/ppermute | solution.py:19
  182.3 2.1 copy-start.1
  187.6 2.3 copy-start.2
  189.9 2.3 copy-start.6
  202.0 10.7 %copy-start.3 = (bf16[384,3072]{1,0:T(8,128)(2,1)}, bf16[384,3072]{1,0:T(8,128)(2,1)S(1)}, u32[]{:S(2)}) copy-start(bf16[384,3072]{1,0:T(8,128)(2,1)S(1)} %get-tuple-element.39.refs_1_.refs_2_) | copy-start | bytes 7077892
  202.0 12.7 %collective-permute-start.21 = (bf16[192,768]{1,0:T(8,128)(2,1)S(1)}, bf16[192,768]{1,0:T(8,128)(2,1)S(1)}, u32[]{:S(2)}, u32[]{:S(2)}) collective-permute-start(bf16[192,768]{1,0:T(8,128)(2,1)S(1)} %get-tuple-element.59), channel_id=1, source_target_pairs={{0,32},{32,64},{64,96},{96,0},{1,33},{33,65},{65,97},{97,1},{2,34}... | collective-permute-start | bytes 884744 | tf_op jit(solution)/shard_map/ppermute | solution.py:19
  202.7 12.8 %collective-permute-start.25 = (bf16[192,768]{1,0:T(8,128)(2,1)S(1)}, bf16[192,768]{1,0:T(8,128)(2,1)S(1)}, u32[]{:S(2)}, u32[]{:S(2)}) collective-permute-start(bf16[192,768]{1,0:T(8,128)(2,1)S(1)} %get-tuple-element.60), channel_id=1, source_target_pairs={{0,96},{32,0},{64,32},{96,64},{1,97},{33,1},{65,33},{97,65},{2,98}... | collective-permute-start | bytes 884744 | tf_op jit(solution)/shard_map/ppermute | solution.py:19
  212.7 10.9 %collective-permute-start.23 = (bf16[192,768]{1,0:T(8,128)(2,1)S(1)}, bf16[192,768]{1,0:T(8,128)(2,1)S(1)}, u32[]{:S(2)}, u32[]{:S(2)}) collective-permute-start(bf16[192,768]{1,0:T(8,128)(2,1)S(1)} %get-tuple-element.42), channel_id=1, source_target_pairs={{0,96},{32,0},{64,32},{96,64},{1,97},{33,1},{65,33},{97,65},{2,98}... | collective-permute-start | bytes 884744 | tf_op jit(solution)/shard_map/ppermute | solution.py:19
  214.7 11.2 %collective-permute-start.24 = (bf16[192,768]{1,0:T(8,128)(2,1)S(1)}, bf16[192,768]{1,0:T(8,128)(2,1)S(1)}, u32[]{:S(2)}, u32[]{:S(2)}) collective-permute-start(bf16[192,768]{1,0:T(8,128)(2,1)S(1)} %get-tuple-element.43), channel_id=1, source_target_pairs={{0,32},{32,64},{64,96},{96,0},{1,33},{33,65},{65,97},{97,1},{2,34}... | collective-permute-start | bytes 884744 | tf_op jit(solution)/shard_map/ppermute | solution.py:19
  214.8 4.8 %copy-start.4 = (bf16[384,3072]{1,0:T(8,128)(2,1)S(1)}, bf16[384,3072]{1,0:T(8,128)(2,1)}, u32[]{:S(2)}) copy-start(bf16[384,3072]{1,0:T(8,128)(2,1)} %copy-done.3) | copy-start | bytes 7077892
  215.5 13.9 %collective-permute-start.22 = (bf16[192,768]{1,0:T(8,128)(2,1)}, bf16[192,768]{1,0:T(8,128)(2,1)}, u32[]{:S(2)}, u32[]{:S(2)}) collective-permute-start(bf16[192,768]{1,0:T(8,128)(2,1)} %add_convert_fusion.1), channel_id=1, source_target_pairs={{0,32},{32,64},{64,96},{96,0},{1,33},{33,65},{65,97},{97,1},{2,34}... | collective-permute-start | bytes 884744 | tf_op jit(solution)/shard_map/ppermute | solution.py:19
  216.3 13.1 %collective-permute-start.26 = (bf16[192,768]{1,0:T(8,128)(2,1)}, bf16[192,768]{1,0:T(8,128)(2,1)}, u32[]{:S(2)}, u32[]{:S(2)}) collective-permute-start(bf16[192,768]{1,0:T(8,128)(2,1)} %add_convert_fusion), channel_id=1, source_target_pairs={{0,96},{32,0},{64,32},{96,64},{1,97},{33,1},{65,33},{97,65},{2,98}... | collective-permute-start | bytes 884744 | tf_op jit(solution)/shard_map/ppermute | solution.py:19
  232.7 3.0 %collective-permute-start.30 = (f32[64,128]{1,0:T(8,128)S(1)}, f32[64,128]{1,0:T(8,128)S(1)}, u32[]{:S(2)}, u32[]{:S(2)}) collective-permute-start(f32[64,128]{1,0:T(8,128)S(1)} %broadcast_in_dim.7), channel_id=1, source_target_pairs={{0,1},{1,0},{2,3},{3,2},{4,5},{5,4},{6,7},{7,6},{8,9},{9,8},{10,11... | collective-permute-start | bytes 98312 | tf_op jit(solution)/shard_map/ppermute | solution.py:281
  232.8 20.9 %collective-permute-start.27 = (bf16[192,384]{1,0:T(8,128)(2,1)S(1)}, bf16[192,384]{1,0:T(8,128)(2,1)S(1)}, u32[]{:S(2)}, u32[]{:S(2)}) collective-permute-start(bf16[192,384]{1,0:T(8,128)(2,1)S(1)} %get-tuple-element.58), channel_id=1, source_target_pairs={{0,24},{8,0},{16,8},{24,16},{1,25},{9,1},{17,9},{25,17},{2,26},{10... | collective-permute-start | bytes 442376 | tf_op jit(solution)/shard_map/ppermute | solution.py:19
  236.9 15.5 %all-to-all-start.1 = ((f32[64,1,128]{2,1,0:T(1,128)}), f32[64,1,128]{2,1,0:T(1,128)S(1)}, u32[]{:S(2)}, u32[]{:S(2)}) async-start(f32[64,1,128]{2,1,0:T(1,128)} %bitcast.38), calls=%async_computation.1 | async-start | bytes 65536 | tf_op jit(solution)/shard_map/all_to_all | solution.py:282
  242.9 10.8 %collective-permute-start.28 = (bf16[192,384]{1,0:T(8,128)(2,1)S(1)}, bf16[192,384]{1,0:T(8,128)(2,1)S(1)}, u32[]{:S(2)}, u32[]{:S(2)}) collective-permute-start(bf16[192,384]{1,0:T(8,128)(2,1)S(1)} %get-tuple-element.57), channel_id=1, source_target_pairs={{0,16},{8,24},{16,0},{24,8},{1,17},{9,25},{17,1},{25,9},{2,18},{10... | collective-permute-start | bytes 442376 | tf_op jit(solution)/shard_map/ppermute | solution.py:19
  246.1 7.7 %collective-permute-start.29 = (bf16[192,384]{1,0:T(8,128)(2,1)S(1)}, bf16[192,384]{1,0:T(8,128)(2,1)S(1)}, u32[]{:S(2)}, u32[]{:S(2)}) collective-permute-start(bf16[192,384]{1,0:T(8,128)(2,1)S(1)} %get-tuple-element.55), channel_id=1, source_target_pairs={{0,8},{8,16},{16,24},{24,0},{1,9},{9,17},{17,25},{25,1},{2,10},{10... | collective-permute-start | bytes 442376 | tf_op jit(solution)/shard_map/ppermute | solution.py:19
Sparse Core Ops, SparseCore 0:
  9.6 93.0 all-gather.1

commit v8 on v6

--- a/solution.py
+++ b/solution.py
@@ -31,7 +31,10 @@
 
 
 def joined(x_ref):
-    return jnp.concatenate([x_ref[k] for k in range(x_ref.shape[0])], axis=1)
+    groups = [
+        jnp.concatenate([x_ref[g, k] for k in range(x_ref.shape[1])], axis=1) for g in range(x_ref.shape[0])
+    ]
+    return groups[0] if len(groups) == 1 else jnp.concatenate(groups, axis=0)
 
 
 def cost(rows, deep, cols, exps=0):
@@ -58,16 +61,16 @@
 
 
 def first_slopes(x, w, t, which):
-    blocks, rows, wide = x.shape
+    groups, blocks, tile, wide = x.shape
+    rows = groups * tile
     cols, deep = w[0].shape
-    tile = rows // N
     per = deep // wide
     out = pl.BlockSpec((cols, tile), lambda i, which: (0, i))
     whole = pl.BlockSpec((cols, deep), lambda i, which: (0, 0), pipeline_mode=pl.Buffered(1))
 
     def kernel(which_ref, x_ref, *refs):
         w_refs, (t_ref, h_ref, s_ref, far_ref, total_ref) = refs[:N], refs[N:]
-        block = lambda j: [x_ref[per * which_ref[j] + k] for k in range(per)]
+        block = lambda j: [x_ref[0, per * which_ref[j] + k] for k in range(per)]
         x = jnp.concatenate([part for j in range(N) for part in block(j)], axis=1)
         w = jnp.concatenate([w_ref[...] for w_ref in w_refs], axis=1)
         hidden = lax.dot_general(w, x, NT, preferred_element_type=F32)
@@ -81,7 +84,7 @@
         grid_spec=pltpu.PrefetchScalarGridSpec(
             num_scalar_prefetch=1,
             grid=(N,),
-            in_specs=[pl.BlockSpec((blocks, tile, wide), lambda i, which: (0, i, 0))]
+            in_specs=[pl.BlockSpec((1, blocks, tile, wide), lambda i, which: (i, 0, 0, 0))]
             + [whole] * N
             + [pl.BlockSpec((1, cols, tile), lambda i, which: (which[N + i], 0, 0))],
             out_specs=[out, out, pl.BlockSpec((cols, deep), lambda i, which: (0, 0))],
@@ -98,16 +101,16 @@
 
 
 def moved(x, pieces, which):
-    blocks, rows, wide = x.shape
+    groups, blocks, tile, wide = x.shape
+    rows = groups * tile
     cols, deep = pieces[0].shape
     per = deep // wide
-    tile = rows // N
     count = len(pieces)
-    at = lambda j: pl.BlockSpec((per, tile, wide), lambda i, which: (which[j], i, 0))
+    at = lambda j: pl.BlockSpec((1, per, tile, wide), lambda i, which: (i, which[j], 0, 0))
 
     def kernel(which_ref, *refs):
         xs, fs = refs[:count], refs[count : 2 * count]
-        x = jnp.concatenate([x_ref[k] for x_ref in xs for k in range(per)], axis=1)
+        x = jnp.concatenate([x_ref[0, k] for x_ref in xs for k in range(per)], axis=1)
         f = jnp.concatenate([f_ref[...] for f_ref in fs], axis=1)
         refs[-1][...] = lax.dot_general(f, x, NT, preferred_element_type=F32)
 
@@ -126,10 +129,10 @@
 
 
 def second_slopes(x, piece, which, part, scale, hidden, t):
-    blocks, rows, wide = x.shape
+    groups, blocks, tile, wide = x.shape
+    rows = groups * tile
     cols, deep = piece.shape
     per = deep // wide
-    tile = rows // N
     out = pl.BlockSpec((cols, tile), lambda i, which: (0, i))
     whole = pl.BlockSpec((cols, deep), lambda i, which: (0, 0))
 
@@ -147,7 +150,7 @@
             grid=(N,),
             in_specs=[
                 pl.BlockSpec(memory_space=pltpu.SMEM),
-                pl.BlockSpec((per, tile, wide), lambda i, which: (which[0], i, 0)),
+                pl.BlockSpec((1, per, tile, wide), lambda i, which: (i, which[0], 0, 0)),
                 whole,
                 out,
                 out,
@@ -163,13 +166,14 @@
 
 
 def terms(x, s, which, cut):
-    blocks, rows, wide = x.shape
+    groups, blocks, size, wide = x.shape
+    rows = groups * size
     cols = s.shape[0]
     half = cols // 2
     tile = rows // 2
     per = blocks // N
     count = len(which)
-    at = lambda j: pl.BlockSpec((per, tile, wide), lambda i, which: (which[j], i, 0))
+    at = lambda j: pl.BlockSpec((groups // 2, per, size, wide), lambda i, which: (i, which[j], 0, 0))
     kinds = [F32, BF16, BF16, F32] if cut else [F32] * count
     tall = half if cut else cols
 
@@ -290,7 +294,7 @@
     width = wide * 2 * N
     hidden_all = weight.shape[1] * 2 * N
 
-    x = lax.all_gather(tokens, ("z", "c", "y"), axis=0, tiled=True).reshape(2 * N, N * rows, wide)
+    x = lax.all_gather(tokens, ("y", "z", "c"), axis=0, tiled=True).reshape(N, 2 * N, rows, wide)
 
     def columns(array):
         return lambda k: lax.dynamic_slice_in_dim(array, lax.rem(iy + k, N) * cols, cols, axis=1)

time: 250 us -> 250 us (level)
  no operation moved by 1% of the time
where the time goes in v8:
time: 250 us
  waiting for transfers between devices  91.3 us (37%)
  Pallas kernels  68.9 us (28%)
  starting transfers between devices  57 us (23%)
  between operations  15.2 us (6%)
  other arithmetic  9.36 us (4%)
  local copies, waits for them, and re-layouts  7.74 us (3%)
    ppermute x29, waiting for transfers between devices, shift(): return lax.ppermute(value, axis, [(i, (i + step) % N) for i in range(N)])  56.9 us
    ppermute x29, starting transfers between devices, shift(): return lax.ppermute(value, axis, [(i, (i + step) % N) for i in range(N)])  43.8 us
    all_gather x1, waiting for transfers between devices, per_device(): lax.all_gather(tokens, ('y', 'z', 'c'), axis=0, tiled=True)  26.9 us
    pallas_call x4, Pallas kernels, terms(): pl.pallas_call(kernel, grid_spec=pltpu.PrefetchScalarGridSpec(num_scalar_...  23.8 us
    pallas_call x1, Pallas kernels, first_slopes(): pl.pallas_call(kernel, grid_spec=pltpu.PrefetchScalarGridSpec(num_scalar_...  19 us
    all_to_all x2, starting transfers between devices, total_of(): lax.all_to_all(total, ('x', 'y', 'z'), split_axis=0, concat_axis=0, tiled...  13.1 us
    pallas_call x1, Pallas kernels, second_slopes(): pl.pallas_call(kernel, grid_spec=pltpu.PrefetchScalarGridSpec(num_scalar_...  11.6 us
    pallas_call x1, Pallas kernels, moved(): pl.pallas_call(kernel, grid_spec=pltpu.PrefetchScalarGridSpec(num_scalar_...  11 us
  transfers between devices with their start and end apart: 34, of which 13 were waited for; matrix products, arithmetic and copies ran while one was open for 5% of the time, Pallas kernels for 15%

profile of v8, /device:TPU:0, one launch (start us, length us, event | category | flops | bytes accessed | tf_op | source)
XLA Modules:
  0.0 249.5 jit_solution(3813973997781138435)
XLA Ops:
  7.3 1.1 constant_dynamic-slice_fusion.1
  8.4 3.2 %collective-permute-start = (bf16[192,384]{1,0:T(8,128)(2,1)S(1)}, bf16[192,384]{1,0:T(8,128)(2,1)S(1)}, u32[]{:S(2)}, u32[]{:S(2)}) collective-permute-start(bf16[192,384]{1,0:T(8,128)(2,1)S(1)} %get-tuple-element.64), channel_id=1, source_target_pairs={{0,24},{8,0},{16,8},{24,16},{1,25},{9,1},{17,9},{25,17},{2,26},{10... | collective-permute-start | bytes 442376 | tf_op jit(solution)/shard_map/ppermute | solution.py:17
  12.2 1.0 collective-permute-start.2
  13.3 3.6 %shard_map.37 = (bf16[384,1152]{1,0:T(8,128)(2,1)S(1)}, bf16[384,1152]{1,0:T(8,128)(2,1)}, bf16[384,768]{1,0:T(8,128)(2,1)S(1)}) custom-call(s32[4]{0:T(128)S(1)} %pad_add_fusion.which_ref, bf16[768,1536]{1,0:T(8,128)(2,1)} %before.1, bf16[768,1536]{1,0:T(8,128)(2,1)} %before.1, bf16[768,1536]{1,0:T(8,128)(2,1)} %before.1, bf16[768,1536]{1,0:T(8,128)(2,1)} %before.1), custom_call_target="tpu_custom_call" | custom-call | tf_op jit(solution)/shard_map/pallas_call | solution.py:255
  17.0 0.9 bitcast_dynamic-update-slice_fusion.12
  17.9 1.9 collective-permute-done.1
  19.9 1.7 collective-permute-done.2
  21.5 3.2 %collective-permute-start.6 = (bf16[384,1152]{1,0:T(8,128)(2,1)}, bf16[384,1152]{1,0:T(8,128)(2,1)}, u32[]{:S(2)}, u32[]{:S(2)}) collective-permute-start(bf16[384,1152]{1,0:T(8,128)(2,1)} %get-tuple-element.28), channel_id=1, source_target_pairs={{0,24},{8,0},{16,8},{24,16},{1,25},{9,1},{17,9},{25,17},{2,26},{10... | collective-permute-start | bytes 2654216 | tf_op jit(solution)/shard_map/ppermute | solution.py:17
  25.4 2.8 %collective-permute-start.3 = (bf16[384,768]{1,0:T(8,128)(2,1)S(1)}, bf16[384,768]{1,0:T(8,128)(2,1)S(1)}, u32[]{:S(2)}, u32[]{:S(2)}) collective-permute-start(bf16[384,768]{1,0:T(8,128)(2,1)S(1)} %bitcast.66), channel_id=1, source_target_pairs={{0,96},{32,0},{64,32},{96,64},{1,97},{33,1},{65,33},{97,65},{2,98}... | collective-permute-start | bytes 1769480 | tf_op jit(solution)/shard_map/ppermute | solution.py:17
  29.9 23.0 %collective-permute-done.6 = bf16[384,1152]{1,0:T(8,128)(2,1)} collective-permute-done((bf16[384,1152]{1,0:T(8,128)(2,1)}, bf16[384,1152]{1,0:T(8,128)(2,1)}, u32[]{:S(2)}, u32[]{:S(2)}) %collective-permute-start.6) | collective-permute-done | bytes 884768 | tf_op jit(solution)/shard_map/ppermute | solution.py:17
  52.9 1.1 slice.82
  54.0 2.2 collective-permute-start.9
  56.3 1.1 slice_bitcast_fusion.1
  57.4 12.2 %collective-permute-done.9 = bf16[384,384]{1,0:T(8,128)(2,1)S(1)} collective-permute-done((bf16[384,384]{1,0:T(8,128)(2,1)S(1)}, bf16[384,384]{1,0:T(8,128)(2,1)S(1)}, u32[]{:S(2)}, u32[]{:S(2)}) %collective-permute-start.9) | collective-permute-done | bytes 294944 | tf_op jit(solution)/shard_map/ppermute | solution.py:17
  69.6 3.5 %collective-permute-done.8 = bf16[384,384]{1,0:T(8,128)(2,1)S(1)} collective-permute-done((bf16[384,384]{1,0:T(8,128)(2,1)S(1)}, bf16[384,384]{1,0:T(8,128)(2,1)S(1)}, u32[]{:S(2)}, u32[]{:S(2)}) %collective-permute-start.8) | collective-permute-done | bytes 294944 | tf_op jit(solution)/shard_map/ppermute | solution.py:17
  73.2 1.7 pad_maximum_fusion.refs_4_.t_ref
  75.7 26.9 %all-gather.2.cloned.1.call-done = bf16[24576,384]{1,0:T(8,128)(2,1)} async-done(((bf16[768,384]{1,0:T(8,128)(2,1)}), bf16[24576,384]{1,0:T(8,128)(2,1)}) %all-gather.2.cloned.1.call-update) | async-done | bytes 18874384 | tf_op jit(solution)/shard_map/all_gather | solution.py:297
  102.6 19.0 %shard_map.38 = (f32[384,3072]{1,0:T(8,128)}, bf16[384,3072]{1,0:T(8,128)(2,1)}, bf16[384,768]{1,0:T(8,128)(2,1)S(1)}) custom-call(s32[8]{0:T(128)S(1)} %stack.126.which_ref, bf16[4,8,768,384]{3,2,1,0:T(8,128)(2,1)} %bitcast.70, bf16[384,768]{1,0:T(8,128)(2,1)S(1)} %bitcast.69, bf16[384,768]{1,0:T(8,128)(2,1)S(1)} %collective-permute-done.3.refs_1_, ...), custom_call_target="tpu_custom_call" | custom-call | flops 9059696640 | bytes 31260672 | tf_op jit(solution)/shard_map/pallas_call | solution.py:82
  121.6 1.6 collective-permute-start.10
  123.1 1.8 collective-permute-start.14
  124.9 7.5 %shard_map.40 = (f32[192,768]{1,0:T(8,128)S(1)}, bf16[192,768]{1,0:T(8,128)(2,1)S(1)}, bf16[192,768]{1,0:T(8,128)(2,1)S(1)}, f32[192,768]{1,0:T(8,128)S(1)}) custom-call(s32[2]{0:T(128)S(1)} %pad_add_fusion.1.which_ref, bf16[4,8,768,384]{3,2,1,0:T(8,128)(2,1)} %bitcast.71, bf16[4,8,768,384]{3,2,1,0:T(8,128)(2,1)} %bitcast.72, ...), custom_call_target="tpu_custom_call" | custom-call | flops 3623878656 | bytes 11796480 | tf_op jit(solution)/shard_map/pallas_call | solution.py:198
  132.5 1.6 collective-permute-start.12
  135.0 3.2 %collective-permute-start.15 = (bf16[192,768]{1,0:T(8,128)(2,1)S(1)}, bf16[192,768]{1,0:T(8,128)(2,1)S(1)}, u32[]{:S(2)}, u32[]{:S(2)}) collective-permute-start(bf16[192,768]{1,0:T(8,128)(2,1)S(1)} %add_convert_fusion.2), channel_id=1, source_target_pairs={{0,96},{32,0},{64,32},{96,64},{1,97},{33,1},{65,33},{97,65},{2,98}... | collective-permute-start | bytes 884744 | tf_op jit(solution)/shard_map/ppermute | solution.py:17
  138.2 4.3 %shard_map.39 = f32[384,768]{1,0:T(8,128)S(1)} custom-call(s32[1]{0:T(128)} %bitcast.which_ref, bf16[4,8,768,384]{3,2,1,0:T(8,128)(2,1)} %bitcast.73, bf16[384,3072]{1,0:T(8,128)(2,1)} %get-tuple-element.30.refs_1_.refs_2_), custom_call_target="tpu_custom_call" | custom-call | flops 1811939328 | bytes 8257536 | tf_op jit(solution)/shard_map/pallas_call | solution.py:198
  142.6 2.6 %collective-permute-done.13 = bf16[192,768]{1,0:T(8,128)(2,1)S(1)} collective-permute-done((bf16[192,768]{1,0:T(8,128)(2,1)S(1)}, bf16[192,768]{1,0:T(8,128)(2,1)S(1)}, u32[]{:S(2)}, u32[]{:S(2)}) %collective-permute-start.13) | collective-permute-done | bytes 294944 | tf_op jit(solution)/shard_map/ppermute | solution.py:17
  145.2 4.7 %collective-permute-done.11 = bf16[192,768]{1,0:T(8,128)(2,1)S(1)} collective-permute-done((bf16[192,768]{1,0:T(8,128)(2,1)S(1)}, bf16[192,768]{1,0:T(8,128)(2,1)S(1)}, u32[]{:S(2)}, u32[]{:S(2)}) %collective-permute-start.11) | collective-permute-done | bytes 294944 | tf_op jit(solution)/shard_map/ppermute | solution.py:17
  150.5 1.8 collective-permute-start.18
  152.2 0.9 multiply_reduce_fusion.1
  153.9 1.0 collective-permute-done.16
  155.0 1.2 broadcast_add_fusion.1
  156.1 7.1 %all-to-all-start = ((f32[64,1,128]{2,1,0:T(1,128)}), f32[64,1,128]{2,1,0:T(1,128)S(1)}, u32[]{:S(2)}, u32[]{:S(2)}) async-start(f32[64,1,128]{2,1,0:T(1,128)} %bitcast.23), calls=%async_computation | async-start | bytes 65536 | tf_op jit(solution)/shard_map/all_to_all | solution.py:284
  163.9 2.4 collective-permute-start.20
  166.4 11.0 %shard_map.41.part_ref = f32[384,3072]{1,0:T(8,128)} custom-call(s32[3]{0:T(128)S(1)} %pad_add_fusion.2.which_ref, bf16[4,8,768,384]{3,2,1,0:T(8,128)(2,1)} %bitcast.74, bf16[4,8,768,384]{3,2,1,0:T(8,128)(2,1)} %bitcast.75, bf16[4,8,768,384]{3,2,1,0:T(8,128)(2,1)} %bitcast.76, bf16[384,768]{1,0:T(8,128)(2,1)S(1)} %fusion.1.refs_3_, ...), custom_call_target="tpu_custom_call" | custom-call | flops 5435817984 | bytes 20643840 | tf_op jit(solution)/shard_map/pallas_call | solution.py:117
  178.8 11.6 %shard_map.42 = (bf16[384,3072]{1,0:T(8,128)(2,1)}, bf16[384,768]{1,0:T(8,128)(2,1)S(1)}) custom-call(s32[5]{0:T(128)S(1)} %stack.123.which_ref, f32[1,1]{1,0:T(1,128)} %bitcast.25.scale_ref, bf16[4,8,768,384]{3,2,1,0:T(8,128)(2,1)} %bitcast.77, bf16[384,768]{1,0:T(8,128)(2,1)S(1)} %pad_maximum_fusion.3.f_ref, f32[384,3072]{1,0:T(8,128)} %shard_map.41.part_ref, ...), custom_call_target="tpu_custom_call" | custom-call | flops 3623878656 | bytes 15335424 | tf_op jit(solution)/shard_map/pallas_call | solution.py:146
  191.1 2.7 %collective-permute-start.25 = (bf16[192,768]{1,0:T(8,128)(2,1)S(1)}, bf16[192,768]{1,0:T(8,128)(2,1)S(1)}, u32[]{:S(2)}, u32[]{:S(2)}) collective-permute-start(bf16[192,768]{1,0:T(8,128)(2,1)S(1)} %get-tuple-element.60), channel_id=1, source_target_pairs={{0,96},{32,0},{64,32},{96,64},{1,97},{33,1},{65,33},{97,65},{2,98}... | collective-permute-start | bytes 884744 | tf_op jit(solution)/shard_map/ppermute | solution.py:17
  193.8 7.5 %shard_map.44 = (f32[192,768]{1,0:T(8,128)S(1)}, bf16[192,768]{1,0:T(8,128)(2,1)S(1)}, bf16[192,768]{1,0:T(8,128)(2,1)S(1)}, f32[192,768]{1,0:T(8,128)S(1)}) custom-call(s32[2]{0:T(128)S(1)} %pad_add_fusion.1.which_ref, bf16[4,8,768,384]{3,2,1,0:T(8,128)(2,1)} %bitcast.78, bf16[4,8,768,384]{3,2,1,0:T(8,128)(2,1)} %bitcast.79, ...), custom_call_target="tpu_custom_call" | custom-call | flops 3623878656 | bytes 11796480 | tf_op jit(solution)/shard_map/pallas_call | solution.py:198
  201.3 2.0 collective-permute-start.23
  203.6 3.5 %collective-permute-start.26 = (bf16[192,768]{1,0:T(8,128)(2,1)S(1)}, bf16[192,768]{1,0:T(8,128)(2,1)S(1)}, u32[]{:S(2)}, u32[]{:S(2)}) collective-permute-start(bf16[192,768]{1,0:T(8,128)(2,1)S(1)} %add_convert_fusion), channel_id=1, source_target_pairs={{0,96},{32,0},{64,32},{96,64},{1,97},{33,1},{65,33},{97,65},{2,98}... | collective-permute-start | bytes 884744 | tf_op jit(solution)/shard_map/ppermute | solution.py:17
  207.1 4.3 %shard_map.43 = f32[384,768]{1,0:T(8,128)S(1)} custom-call(s32[1]{0:T(128)} %bitcast.which_ref, bf16[4,8,768,384]{3,2,1,0:T(8,128)(2,1)} %bitcast.80, bf16[384,3072]{1,0:T(8,128)(2,1)} %get-tuple-element.39.refs_1_.refs_2_), custom_call_target="tpu_custom_call" | custom-call | flops 1811939328 | bytes 8257536 | tf_op jit(solution)/shard_map/pallas_call | solution.py:198
  211.5 3.0 %collective-permute-done.24 = bf16[192,768]{1,0:T(8,128)(2,1)S(1)} collective-permute-done((bf16[192,768]{1,0:T(8,128)(2,1)S(1)}, bf16[192,768]{1,0:T(8,128)(2,1)S(1)}, u32[]{:S(2)}, u32[]{:S(2)}) %collective-permute-start.24) | collective-permute-done | bytes 294944 | tf_op jit(solution)/shard_map/ppermute | solution.py:17
  214.5 3.5 %collective-permute-done.22 = bf16[192,768]{1,0:T(8,128)(2,1)S(1)} collective-permute-done((bf16[192,768]{1,0:T(8,128)(2,1)S(1)}, bf16[192,768]{1,0:T(8,128)(2,1)S(1)}, u32[]{:S(2)}, u32[]{:S(2)}) %collective-permute-start.22) | collective-permute-done | bytes 294944 | tf_op jit(solution)/shard_map/ppermute | solution.py:17
  218.3 1.0 multiply_reduce_fusion
  220.3 2.8 %collective-permute-start.27 = (bf16[192,384]{1,0:T(8,128)(2,1)S(1)}, bf16[192,384]{1,0:T(8,128)(2,1)S(1)}, u32[]{:S(2)}, u32[]{:S(2)}) collective-permute-start(bf16[192,384]{1,0:T(8,128)(2,1)S(1)} %get-tuple-element.58), channel_id=1, source_target_pairs={{0,24},{8,0},{16,8},{24,16},{1,25},{9,1},{17,9},{25,17},{2,26},{10... | collective-permute-start | bytes 442376 | tf_op jit(solution)/shard_map/ppermute | solution.py:17
  223.2 1.2 broadcast_add_fusion
  224.4 6.0 %all-to-all-start.1 = ((f32[64,1,128]{2,1,0:T(1,128)}), f32[64,1,128]{2,1,0:T(1,128)S(1)}, u32[]{:S(2)}, u32[]{:S(2)}) async-start(f32[64,1,128]{2,1,0:T(1,128)} %bitcast.38), calls=%async_computation.1 | async-start | bytes 65536 | tf_op jit(solution)/shard_map/all_to_all | solution.py:284
  230.4 3.2 %collective-permute-start.28 = (bf16[192,384]{1,0:T(8,128)(2,1)S(1)}, bf16[192,384]{1,0:T(8,128)(2,1)S(1)}, u32[]{:S(2)}, u32[]{:S(2)}) collective-permute-start(bf16[192,384]{1,0:T(8,128)(2,1)S(1)} %get-tuple-element.57), channel_id=1, source_target_pairs={{0,16},{8,24},{16,0},{24,8},{1,17},{9,25},{17,1},{25,9},{2,18},{10... | collective-permute-start | bytes 442376 | tf_op jit(solution)/shard_map/ppermute | solution.py:17
  234.1 5.8 %all-to-all-done.1 = f32[64,1,128]{2,1,0:T(1,128)S(1)} async-done(((f32[64,1,128]{2,1,0:T(1,128)}), f32[64,1,128]{2,1,0:T(1,128)S(1)}, u32[]{:S(2)}, u32[]{:S(2)}) %all-to-all-start.1) | async-done | bytes 32800 | tf_op jit(solution)/shard_map/all_to_all | solution.py:284
  241.5 1.1 convert_multiply_fusion
  (85 shorter events, 12.4 us)
Async XLA Ops:
  6.5 96.1 %all-gather.2.cloned.1.call-start = ((), (), s32[]{:S(2)}) async-start(), calls=%async_computation.2 | async-start | bytes 19464192 | tf_op jit(solution)/shard_map/all_gather | solution.py:297
  8.4 9.5 %collective-permute-start = (bf16[192,384]{1,0:T(8,128)(2,1)S(1)}, bf16[192,384]{1,0:T(8,128)(2,1)S(1)}, u32[]{:S(2)}, u32[]{:S(2)}) collective-permute-start(bf16[192,384]{1,0:T(8,128)(2,1)S(1)} %get-tuple-element.64), channel_id=1, source_target_pairs={{0,24},{8,0},{16,8},{24,16},{1,25},{9,1},{17,9},{25,17},{2,26},{10... | collective-permute-start | bytes 442376 | tf_op jit(solution)/shard_map/ppermute | solution.py:17
  11.6 8.3 %collective-permute-start.1 = (bf16[192,384]{1,0:T(8,128)(2,1)S(1)}, bf16[192,384]{1,0:T(8,128)(2,1)S(1)}, u32[]{:S(2)}, u32[]{:S(2)}) collective-permute-start(bf16[192,384]{1,0:T(8,128)(2,1)S(1)} %get-tuple-element.65), channel_id=1, source_target_pairs={{0,16},{8,24},{16,0},{24,8},{1,17},{9,25},{17,1},{25,9},{2,18},{10... | collective-permute-start | bytes 442376 | tf_op jit(solution)/shard_map/ppermute | solution.py:17
  12.2 9.3 %collective-permute-start.2 = (bf16[192,384]{1,0:T(8,128)(2,1)S(1)}, bf16[192,384]{1,0:T(8,128)(2,1)S(1)}, u32[]{:S(2)}, u32[]{:S(2)}) collective-permute-start(bf16[192,384]{1,0:T(8,128)(2,1)S(1)} %get-tuple-element.63), channel_id=1, source_target_pairs={{0,8},{8,16},{16,24},{24,0},{1,9},{9,17},{17,25},{25,1},{2,10},{10... | collective-permute-start | bytes 442376 | tf_op jit(solution)/shard_map/ppermute | solution.py:17
  21.5 34.6 %collective-permute-start.7 = (bf16[384,1152]{1,0:T(8,128)(2,1)S(1)}, bf16[384,1152]{1,0:T(8,128)(2,1)S(1)}, u32[]{:S(2)}, u32[]{:S(2)}) collective-permute-start(bf16[384,1152]{1,0:T(8,128)(2,1)S(1)} %get-tuple-element.29), channel_id=1, source_target_pairs={{0,8},{8,16},{16,24},{24,0},{1,9},{9,17},{17,25},{25,1},{2,10},{10... | collective-permute-start | bytes 2654216 | tf_op jit(solution)/shard_map/ppermute | solution.py:17
  21.5 31.4 %collective-permute-start.6 = (bf16[384,1152]{1,0:T(8,128)(2,1)}, bf16[384,1152]{1,0:T(8,128)(2,1)}, u32[]{:S(2)}, u32[]{:S(2)}) collective-permute-start(bf16[384,1152]{1,0:T(8,128)(2,1)} %get-tuple-element.28), channel_id=1, source_target_pairs={{0,24},{8,0},{16,8},{24,16},{1,25},{9,1},{17,9},{25,17},{2,26},{10... | collective-permute-start | bytes 2654216 | tf_op jit(solution)/shard_map/ppermute | solution.py:17
  25.4 49.5 %collective-permute-start.3 = (bf16[384,768]{1,0:T(8,128)(2,1)S(1)}, bf16[384,768]{1,0:T(8,128)(2,1)S(1)}, u32[]{:S(2)}, u32[]{:S(2)}) collective-permute-start(bf16[384,768]{1,0:T(8,128)(2,1)S(1)} %bitcast.66), channel_id=1, source_target_pairs={{0,96},{32,0},{64,32},{96,64},{1,97},{33,1},{65,33},{97,65},{2,98}... | collective-permute-start | bytes 1769480 | tf_op jit(solution)/shard_map/ppermute | solution.py:17
  28.2 46.7 %collective-permute-start.4 = (bf16[384,768]{1,0:T(8,128)(2,1)S(1)}, bf16[384,768]{1,0:T(8,128)(2,1)S(1)}, u32[]{:S(2)}, u32[]{:S(2)}) collective-permute-start(bf16[384,768]{1,0:T(8,128)(2,1)S(1)} %bitcast.67), channel_id=1, source_target_pairs={{0,64},{32,96},{64,0},{96,32},{1,65},{33,97},{65,1},{97,33},{2,66}... | collective-permute-start | bytes 1769480 | tf_op jit(solution)/shard_map/ppermute | solution.py:17
  29.0 46.7 %collective-permute-start.5 = (bf16[384,768]{1,0:T(8,128)(2,1)S(1)}, bf16[384,768]{1,0:T(8,128)(2,1)}, u32[]{:S(2)}, u32[]{:S(2)}) collective-permute-start(bf16[384,768]{1,0:T(8,128)(2,1)S(1)} %bitcast.68), channel_id=1, source_target_pairs={{0,32},{32,64},{64,96},{96,0},{1,33},{33,65},{65,97},{97,1},{2,34}... | collective-permute-start | bytes 1769480 | tf_op jit(solution)/shard_map/ppermute | solution.py:17
  54.0 15.6 %collective-permute-start.9 = (bf16[384,384]{1,0:T(8,128)(2,1)S(1)}, bf16[384,384]{1,0:T(8,128)(2,1)S(1)}, u32[]{:S(2)}, u32[]{:S(2)}) collective-permute-start(bf16[384,384]{1,0:T(8,128)(2,1)S(1)} %slice.82), channel_id=1, source_target_pairs={{0,24},{8,0},{16,8},{24,16},{1,25},{9,1},{17,9},{25,17},{2,26},{10... | collective-permute-start | bytes 884744 | tf_op jit(solution)/shard_map/ppermute | solution.py:17
  56.2 16.9 %collective-permute-start.8 = (bf16[384,384]{1,0:T(8,128)(2,1)S(1)}, bf16[384,384]{1,0:T(8,128)(2,1)S(1)}, u32[]{:S(2)}, u32[]{:S(2)}) collective-permute-start(bf16[384,384]{1,0:T(8,128)(2,1)S(1)} %slice.81), channel_id=1, source_target_pairs={{0,8},{8,16},{16,24},{24,0},{1,9},{9,17},{17,25},{25,1},{2,10},{10... | collective-permute-start | bytes 884744 | tf_op jit(solution)/shard_map/ppermute | solution.py:17
  74.9 0.8 copy-start
  121.6 13.0 %collective-permute-start.10 = (bf16[192,768]{1,0:T(8,128)(2,1)S(1)}, bf16[192,768]{1,0:T(8,128)(2,1)S(1)}, u32[]{:S(2)}, u32[]{:S(2)}) collective-permute-start(bf16[192,768]{1,0:T(8,128)(2,1)S(1)} %get-tuple-element.61), channel_id=1, source_target_pairs={{0,32},{32,64},{64,96},{96,0},{1,33},{33,65},{65,97},{97,1},{2,34}... | collective-permute-start | bytes 884744 | tf_op jit(solution)/shard_map/ppermute | solution.py:17
  123.1 11.8 %collective-permute-start.14 = (bf16[192,768]{1,0:T(8,128)(2,1)S(1)}, bf16[192,768]{1,0:T(8,128)(2,1)S(1)}, u32[]{:S(2)}, u32[]{:S(2)}) collective-permute-start(bf16[192,768]{1,0:T(8,128)(2,1)S(1)} %get-tuple-element.62), channel_id=1, source_target_pairs={{0,96},{32,0},{64,32},{96,64},{1,97},{33,1},{65,33},{97,65},{2,98}... | collective-permute-start | bytes 884744 | tf_op jit(solution)/shard_map/ppermute | solution.py:17
  132.5 10.1 %collective-permute-start.12 = (bf16[192,768]{1,0:T(8,128)(2,1)S(1)}, bf16[192,768]{1,0:T(8,128)(2,1)S(1)}, u32[]{:S(2)}, u32[]{:S(2)}) collective-permute-start(bf16[192,768]{1,0:T(8,128)(2,1)S(1)} %get-tuple-element.33), channel_id=1, source_target_pairs={{0,96},{32,0},{64,32},{96,64},{1,97},{33,1},{65,33},{97,65},{2,98}... | collective-permute-start | bytes 884744 | tf_op jit(solution)/shard_map/ppermute | solution.py:17
  134.0 11.2 %collective-permute-start.13 = (bf16[192,768]{1,0:T(8,128)(2,1)S(1)}, bf16[192,768]{1,0:T(8,128)(2,1)S(1)}, u32[]{:S(2)}, u32[]{:S(2)}) collective-permute-start(bf16[192,768]{1,0:T(8,128)(2,1)S(1)} %get-tuple-element.34), channel_id=1, source_target_pairs={{0,32},{32,64},{64,96},{96,0},{1,33},{33,65},{65,97},{97,1},{2,34}... | collective-permute-start | bytes 884744 | tf_op jit(solution)/shard_map/ppermute | solution.py:17
  134.6 15.3 %collective-permute-start.11 = (bf16[192,768]{1,0:T(8,128)(2,1)S(1)}, bf16[192,768]{1,0:T(8,128)(2,1)S(1)}, u32[]{:S(2)}, u32[]{:S(2)}) collective-permute-start(bf16[192,768]{1,0:T(8,128)(2,1)S(1)} %add_convert_fusion.3), channel_id=1, source_target_pairs={{0,32},{32,64},{64,96},{96,0},{1,33},{33,65},{65,97},{97,1},{2,34}... | collective-permute-start | bytes 884744 | tf_op jit(solution)/shard_map/ppermute | solution.py:17
  135.0 14.9 %collective-permute-start.15 = (bf16[192,768]{1,0:T(8,128)(2,1)S(1)}, bf16[192,768]{1,0:T(8,128)(2,1)S(1)}, u32[]{:S(2)}, u32[]{:S(2)}) collective-permute-start(bf16[192,768]{1,0:T(8,128)(2,1)S(1)} %add_convert_fusion.2), channel_id=1, source_target_pairs={{0,96},{32,0},{64,32},{96,64},{1,97},{33,1},{65,33},{97,65},{2,98}... | collective-permute-start | bytes 884744 | tf_op jit(solution)/shard_map/ppermute | solution.py:17
  150.1 13.8 %collective-permute-start.17 = (bf16[384,768]{1,0:T(8,128)(2,1)S(1)}, bf16[384,768]{1,0:T(8,128)(2,1)S(1)}, u32[]{:S(2)}, u32[]{:S(2)}) collective-permute-start(bf16[384,768]{1,0:T(8,128)(2,1)S(1)} %fusion.1.refs_3_), channel_id=1, source_target_pairs={{0,96},{32,0},{64,32},{96,64},{1,97},{33,1},{65,33},{97,65},{2,98}... | collective-permute-start | bytes 1769480 | tf_op jit(solution)/shard_map/ppermute | solution.py:17
  150.5 15.8 %collective-permute-start.18 = (bf16[384,768]{1,0:T(8,128)(2,1)S(1)}, bf16[384,768]{1,0:T(8,128)(2,1)S(1)}, u32[]{:S(2)}, u32[]{:S(2)}) collective-permute-start(bf16[384,768]{1,0:T(8,128)(2,1)S(1)} %fusion.1.refs_3_), channel_id=1, source_target_pairs={{0,32},{32,64},{64,96},{96,0},{1,33},{33,65},{65,97},{97,1},{2,34}... | collective-permute-start | bytes 1769480 | tf_op jit(solution)/shard_map/ppermute | solution.py:17
  153.7 1.3 collective-permute-start.16
  156.1 21.3 %all-to-all-start = ((f32[64,1,128]{2,1,0:T(1,128)}), f32[64,1,128]{2,1,0:T(1,128)S(1)}, u32[]{:S(2)}, u32[]{:S(2)}) async-start(f32[64,1,128]{2,1,0:T(1,128)} %bitcast.23), calls=%async_computation | async-start | bytes 65536 | tf_op jit(solution)/shard_map/all_to_all | solution.py:284
  163.9 14.8 %collective-permute-start.20 = (bf16[192,768]{1,0:T(8,128)(2,1)S(1)}, bf16[192,768]{1,0:T(8,128)(2,1)S(1)}, u32[]{:S(2)}, u32[]{:S(2)}) collective-permute-start(bf16[192,768]{1,0:T(8,128)(2,1)S(1)} %slice.87), channel_id=1, source_target_pairs={{0,96},{32,0},{64,32},{96,64},{1,97},{33,1},{65,33},{97,65},{2,98}... | collective-permute-start | bytes 884744 | tf_op jit(solution)/shard_map/ppermute | solution.py:17
  166.3 12.4 %collective-permute-start.19 = (bf16[192,768]{1,0:T(8,128)(2,1)S(1)}, bf16[192,768]{1,0:T(8,128)(2,1)S(1)}, u32[]{:S(2)}, u32[]{:S(2)}) collective-permute-start(bf16[192,768]{1,0:T(8,128)(2,1)S(1)} %slice.86), channel_id=1, source_target_pairs={{0,32},{32,64},{64,96},{96,0},{1,33},{33,65},{65,97},{97,1},{2,34}... | collective-permute-start | bytes 884744 | tf_op jit(solution)/shard_map/ppermute | solution.py:17
  190.4 13.0 %collective-permute-start.21 = (bf16[192,768]{1,0:T(8,128)(2,1)S(1)}, bf16[192,768]{1,0:T(8,128)(2,1)S(1)}, u32[]{:S(2)}, u32[]{:S(2)}) collective-permute-start(bf16[192,768]{1,0:T(8,128)(2,1)S(1)} %get-tuple-element.59), channel_id=1, source_target_pairs={{0,32},{32,64},{64,96},{96,0},{1,33},{33,65},{65,97},{97,1},{2,34}... | collective-permute-start | bytes 884744 | tf_op jit(solution)/shard_map/ppermute | solution.py:17
  191.1 12.5 %collective-permute-start.25 = (bf16[192,768]{1,0:T(8,128)(2,1)S(1)}, bf16[192,768]{1,0:T(8,128)(2,1)S(1)}, u32[]{:S(2)}, u32[]{:S(2)}) collective-permute-start(bf16[192,768]{1,0:T(8,128)(2,1)S(1)} %get-tuple-element.60), channel_id=1, source_target_pairs={{0,96},{32,0},{64,32},{96,64},{1,97},{33,1},{65,33},{97,65},{2,98}... | collective-permute-start | bytes 884744 | tf_op jit(solution)/shard_map/ppermute | solution.py:17
  201.3 10.1 %collective-permute-start.23 = (bf16[192,768]{1,0:T(8,128)(2,1)S(1)}, bf16[192,768]{1,0:T(8,128)(2,1)S(1)}, u32[]{:S(2)}, u32[]{:S(2)}) collective-permute-start(bf16[192,768]{1,0:T(8,128)(2,1)S(1)} %get-tuple-element.42), channel_id=1, source_target_pairs={{0,96},{32,0},{64,32},{96,64},{1,97},{33,1},{65,33},{97,65},{2,98}... | collective-permute-start | bytes 884744 | tf_op jit(solution)/shard_map/ppermute | solution.py:17
  203.3 11.2 %collective-permute-start.24 = (bf16[192,768]{1,0:T(8,128)(2,1)S(1)}, bf16[192,768]{1,0:T(8,128)(2,1)S(1)}, u32[]{:S(2)}, u32[]{:S(2)}) collective-permute-start(bf16[192,768]{1,0:T(8,128)(2,1)S(1)} %get-tuple-element.43), channel_id=1, source_target_pairs={{0,32},{32,64},{64,96},{96,0},{1,33},{33,65},{65,97},{97,1},{2,34}... | collective-permute-start | bytes 884744 | tf_op jit(solution)/shard_map/ppermute | solution.py:17
  203.5 14.5 %collective-permute-start.22 = (bf16[192,768]{1,0:T(8,128)(2,1)S(1)}, bf16[192,768]{1,0:T(8,128)(2,1)S(1)}, u32[]{:S(2)}, u32[]{:S(2)}) collective-permute-start(bf16[192,768]{1,0:T(8,128)(2,1)S(1)} %add_convert_fusion.1), channel_id=1, source_target_pairs={{0,32},{32,64},{64,96},{96,0},{1,33},{33,65},{65,97},{97,1},{2,34}... | collective-permute-start | bytes 884744 | tf_op jit(solution)/shard_map/ppermute | solution.py:17
  203.6 14.4 %collective-permute-start.26 = (bf16[192,768]{1,0:T(8,128)(2,1)S(1)}, bf16[192,768]{1,0:T(8,128)(2,1)S(1)}, u32[]{:S(2)}, u32[]{:S(2)}) collective-permute-start(bf16[192,768]{1,0:T(8,128)(2,1)S(1)} %add_convert_fusion), channel_id=1, source_target_pairs={{0,96},{32,0},{64,32},{96,64},{1,97},{33,1},{65,33},{97,65},{2,98}... | collective-permute-start | bytes 884744 | tf_op jit(solution)/shard_map/ppermute | solution.py:17
  220.2 3.0 %collective-permute-start.30 = (f32[64,128]{1,0:T(8,128)S(1)}, f32[64,128]{1,0:T(8,128)S(1)}, u32[]{:S(2)}, u32[]{:S(2)}) collective-permute-start(f32[64,128]{1,0:T(8,128)S(1)} %broadcast_in_dim.7), channel_id=1, source_target_pairs={{0,1},{1,0},{2,3},{3,2},{4,5},{5,4},{6,7},{7,6},{8,9},{9,8},{10,11... | collective-permute-start | bytes 98312 | tf_op jit(solution)/shard_map/ppermute | solution.py:283
  220.3 20.9 %collective-permute-start.27 = (bf16[192,384]{1,0:T(8,128)(2,1)S(1)}, bf16[192,384]{1,0:T(8,128)(2,1)S(1)}, u32[]{:S(2)}, u32[]{:S(2)}) collective-permute-start(bf16[192,384]{1,0:T(8,128)(2,1)S(1)} %get-tuple-element.58), channel_id=1, source_target_pairs={{0,24},{8,0},{16,8},{24,16},{1,25},{9,1},{17,9},{25,17},{2,26},{10... | collective-permute-start | bytes 442376 | tf_op jit(solution)/shard_map/ppermute | solution.py:17
  224.4 15.5 %all-to-all-start.1 = ((f32[64,1,128]{2,1,0:T(1,128)}), f32[64,1,128]{2,1,0:T(1,128)S(1)}, u32[]{:S(2)}, u32[]{:S(2)}) async-start(f32[64,1,128]{2,1,0:T(1,128)} %bitcast.38), calls=%async_computation.1 | async-start | bytes 65536 | tf_op jit(solution)/shard_map/all_to_all | solution.py:284
  230.4 10.8 %collective-permute-start.28 = (bf16[192,384]{1,0:T(8,128)(2,1)S(1)}, bf16[192,384]{1,0:T(8,128)(2,1)S(1)}, u32[]{:S(2)}, u32[]{:S(2)}) collective-permute-start(bf16[192,384]{1,0:T(8,128)(2,1)S(1)} %get-tuple-element.57), channel_id=1, source_target_pairs={{0,16},{8,24},{16,0},{24,8},{1,17},{9,25},{17,1},{25,9},{2,18},{10... | collective-permute-start | bytes 442376 | tf_op jit(solution)/shard_map/ppermute | solution.py:17
  233.6 7.7 %collective-permute-start.29 = (bf16[192,384]{1,0:T(8,128)(2,1)S(1)}, bf16[192,384]{1,0:T(8,128)(2,1)S(1)}, u32[]{:S(2)}, u32[]{:S(2)}) collective-permute-start(bf16[192,384]{1,0:T(8,128)(2,1)S(1)} %get-tuple-element.55), channel_id=1, source_target_pairs={{0,8},{8,16},{16,24},{24,0},{1,9},{9,17},{17,25},{25,1},{2,10},{10... | collective-permute-start | bytes 442376 | tf_op jit(solution)/shard_map/ppermute | solution.py:17
Sparse Core Ops, SparseCore 0:
  9.6 92.9 all-gather.1

commit v9 on v8

--- a/solution.py
+++ b/solution.py
@@ -278,13 +278,23 @@
     return lax.dynamic_slice_in_dim(twice, lax.rem(N - me, N), N, axis=0)
 
 
-def total_of(value, beside):
-    total = jnp.full((N * N * N, 128), jnp.sum(value * value), F32)
-    total = total + lax.ppermute(total, "c", [(0, 1), (1, 0)])
-    each = lax.all_to_all(total, ("x", "y", "z"), split_axis=0, concat_axis=0, tiled=True)
-    if beside is not None:
-        each, beside = lax.optimization_barrier((each, beside))
+def both(value):
+    return value + lax.ppermute(value, "c", [(0, 1), (1, 0)])
+
+
+def spread(value):
+    return lax.all_to_all(value, ("x", "y", "z"), split_axis=0, concat_axis=0, tiled=True)
+
+
+def total_beside(value, beside):
+    part = jnp.full((N * N * N, 128), jnp.sum(value * value), F32)
+    each, beside = lax.optimization_barrier((spread(both(part)), beside))
     return jnp.sum(each[:, 0]), beside
+
+
+def total_of(value):
+    each = spread(jnp.full((N * N * N, 128), jnp.sum(value * value), F32))
+    return both(jnp.full((8, 128), jnp.sum(each[:, 0]), F32))[0, 0]
 
 
 def per_device(tokens, target, weight):
@@ -311,11 +321,11 @@
     first = ring_sum(x, slope, term, ix)
     own, after, far, before = ring_gather_halves(first.astype(BF16), "x")
     part = moved(x, [own, after, before], [at(0), at(1), at(3)])
-    total, part = total_of(first, part)
+    total, part = total_beside(first, part)
     scale = 0.5 * math.sqrt(hidden_all) / jnp.sqrt(total + 1e-06)
     slope, term = second_slopes(x, far, [at(2)] + tiles, part, scale.reshape(1, 1), hidden, t)
     second = ring_sum(x, slope, term, ix)
-    total, _ = total_of(second, None)
+    total = total_of(second)
     factor = jnp.minimum(1.0, math.sqrt(width * hidden_all) / jnp.sqrt(total + 1e-06))
     held = second.astype(BF16).T.reshape(N, -1, cols)
     parts = in_order(ring_swap(lambda k: lax.dynamic_index_in_dim(held, lax.rem(iy + k, N), 0, keepdims=False), "y"), iy)

time: 250 us -> 261 us (1.044)
  waiting for transfers between devices: 91.3 us -> 102 us
    ppermute x29, waiting for transfers between devices: 56.9 us -> 64.3 us  [shift(): return lax.ppermute(value, axis, [(i, (i + step) % N) for i in range(N)])]
    ppermute x29, starting transfers between devices: 43.8 us -> 39.8 us  [shift(): return lax.ppermute(value, axis, [(i, (i + step) % N) for i in range(N)])]
    all_to_all x2, waiting for transfers between devices: 5.76 us -> 9.1 us  [spread(): lax.all_to_all(value, ('x', 'y', 'z'), split_axis=0, concat_axis=0, tiled...]
  transfers between devices with their start and end apart: 34 -> 34, of which waited for: 13 -> 17; matrix products, arithmetic and copies ran while one was open for 5% -> 5% of each run, Pallas kernels for 15% -> 15%
where the time goes in v9:
time: 261 us; the launch traced here: 259 us
  waiting for transfers between devices  102 us (39%)
  Pallas kernels  68.9 us (26%)
  starting transfers between devices  54.9 us (21%)
  between operations  15.2 us (6%)
  local copies, waits for them, and re-layouts  9.52 us (4%)
  other arithmetic  8.77 us (3%)
    ppermute x29, waiting for transfers between devices, shift(): return lax.ppermute(value, axis, [(i, (i + step) % N) for i in range(N)])  64.3 us
    ppermute x29, starting transfers between devices, shift(): return lax.ppermute(value, axis, [(i, (i + step) % N) for i in range(N)])  39.8 us
    all_gather x1, waiting for transfers between devices, per_device(): lax.all_gather(tokens, ('y', 'z', 'c'), axis=0, tiled=True)  26.9 us
    pallas_call x4, Pallas kernels, terms(): pl.pallas_call(kernel, grid_spec=pltpu.PrefetchScalarGridSpec(num_scalar_...  23.8 us
    pallas_call x1, Pallas kernels, first_slopes(): pl.pallas_call(kernel, grid_spec=pltpu.PrefetchScalarGridSpec(num_scalar_...  19 us
    all_to_all x2, starting transfers between devices, spread(): lax.all_to_all(value, ('x', 'y', 'z'), split_axis=0, concat_axis=0, tiled...  15 us
    pallas_call x1, Pallas kernels, second_slopes(): pl.pallas_call(kernel, grid_spec=pltpu.PrefetchScalarGridSpec(num_scalar_...  11.6 us
    pallas_call x1, Pallas kernels, moved(): pl.pallas_call(kernel, grid_spec=pltpu.PrefetchScalarGridSpec(num_scalar_...  11 us
  transfers between devices with their start and end apart: 34, of which 17 were waited for; matrix products, arithmetic and copies ran while one was open for 5% of the time, Pallas kernels for 15%

profile of v9, /device:TPU:0, one launch (start us, length us, event | category | flops | bytes accessed | tf_op | source)
XLA Modules:
  0.0 259.3 jit_solution(2362018456131271065)
XLA Ops:
  7.3 1.1 constant_dynamic-slice_fusion.1
  8.4 3.2 %collective-permute-start = (bf16[192,384]{1,0:T(8,128)(2,1)S(1)}, bf16[192,384]{1,0:T(8,128)(2,1)S(1)}, u32[]{:S(2)}, u32[]{:S(2)}) collective-permute-start(bf16[192,384]{1,0:T(8,128)(2,1)S(1)} %get-tuple-element.64), channel_id=1, source_target_pairs={{0,24},{8,0},{16,8},{24,16},{1,25},{9,1},{17,9},{25,17},{2,26},{10... | collective-permute-start | bytes 442376 | tf_op jit(solution)/shard_map/ppermute | solution.py:17
  12.2 1.0 collective-permute-start.2
  13.3 3.6 %shard_map.37 = (bf16[384,1152]{1,0:T(8,128)(2,1)S(1)}, bf16[384,1152]{1,0:T(8,128)(2,1)}, bf16[384,768]{1,0:T(8,128)(2,1)S(1)}) custom-call(s32[4]{0:T(128)S(1)} %pad_add_fusion.which_ref, bf16[768,1536]{1,0:T(8,128)(2,1)} %before.1, bf16[768,1536]{1,0:T(8,128)(2,1)} %before.1, bf16[768,1536]{1,0:T(8,128)(2,1)} %before.1, bf16[768,1536]{1,0:T(8,128)(2,1)} %before.1), custom_call_target="tpu_custom_call" | custom-call | tf_op jit(solution)/shard_map/pallas_call | solution.py:255
  17.9 1.9 collective-permute-done.1
  19.9 1.7 collective-permute-done.2
  21.5 3.2 %collective-permute-start.6 = (bf16[384,1152]{1,0:T(8,128)(2,1)}, bf16[384,1152]{1,0:T(8,128)(2,1)}, u32[]{:S(2)}, u32[]{:S(2)}) collective-permute-start(bf16[384,1152]{1,0:T(8,128)(2,1)} %get-tuple-element.28), channel_id=1, source_target_pairs={{0,24},{8,0},{16,8},{24,16},{1,25},{9,1},{17,9},{25,17},{2,26},{10... | collective-permute-start | bytes 2654216 | tf_op jit(solution)/shard_map/ppermute | solution.py:17
  25.4 2.8 %collective-permute-start.3 = (bf16[384,768]{1,0:T(8,128)(2,1)S(1)}, bf16[384,768]{1,0:T(8,128)(2,1)S(1)}, u32[]{:S(2)}, u32[]{:S(2)}) collective-permute-start(bf16[384,768]{1,0:T(8,128)(2,1)S(1)} %bitcast.66), channel_id=1, source_target_pairs={{0,96},{32,0},{64,32},{96,64},{1,97},{33,1},{65,33},{97,65},{2,98}... | collective-permute-start | bytes 1769480 | tf_op jit(solution)/shard_map/ppermute | solution.py:17
  29.9 23.0 %collective-permute-done.6 = bf16[384,1152]{1,0:T(8,128)(2,1)} collective-permute-done((bf16[384,1152]{1,0:T(8,128)(2,1)}, bf16[384,1152]{1,0:T(8,128)(2,1)}, u32[]{:S(2)}, u32[]{:S(2)}) %collective-permute-start.6) | collective-permute-done | bytes 884768 | tf_op jit(solution)/shard_map/ppermute | solution.py:17
  52.9 1.1 slice.86
  54.0 2.2 collective-permute-start.9
  56.3 1.1 slice_bitcast_fusion.1
  57.4 12.2 %collective-permute-done.9 = bf16[384,384]{1,0:T(8,128)(2,1)S(1)} collective-permute-done((bf16[384,384]{1,0:T(8,128)(2,1)S(1)}, bf16[384,384]{1,0:T(8,128)(2,1)S(1)}, u32[]{:S(2)}, u32[]{:S(2)}) %collective-permute-start.9) | collective-permute-done | bytes 294944 | tf_op jit(solution)/shard_map/ppermute | solution.py:17
  69.6 3.5 %collective-permute-done.8 = bf16[384,384]{1,0:T(8,128)(2,1)S(1)} collective-permute-done((bf16[384,384]{1,0:T(8,128)(2,1)S(1)}, bf16[384,384]{1,0:T(8,128)(2,1)S(1)}, u32[]{:S(2)}, u32[]{:S(2)}) %collective-permute-start.8) | collective-permute-done | bytes 294944 | tf_op jit(solution)/shard_map/ppermute | solution.py:17
  73.2 1.7 pad_maximum_fusion.refs_4_.t_ref
  75.7 26.9 %all-gather.2.cloned.1.call-done = bf16[24576,384]{1,0:T(8,128)(2,1)} async-done(((bf16[768,384]{1,0:T(8,128)(2,1)}), bf16[24576,384]{1,0:T(8,128)(2,1)}) %all-gather.2.cloned.1.call-update) | async-done | bytes 18874384 | tf_op jit(solution)/shard_map/all_gather | solution.py:307
  102.6 19.0 %shard_map.38 = (f32[384,3072]{1,0:T(8,128)}, bf16[384,3072]{1,0:T(8,128)(2,1)}, bf16[384,768]{1,0:T(8,128)(2,1)S(1)}) custom-call(s32[8]{0:T(128)S(1)} %stack.126.which_ref, bf16[4,8,768,384]{3,2,1,0:T(8,128)(2,1)} %bitcast.70, bf16[384,768]{1,0:T(8,128)(2,1)S(1)} %bitcast.69, bf16[384,768]{1,0:T(8,128)(2,1)S(1)} %collective-permute-done.3.refs_1_, ...), custom_call_target="tpu_custom_call" | custom-call | flops 9059696640 | bytes 31260672 | tf_op jit(solution)/shard_map/pallas_call | solution.py:82
  121.6 1.6 collective-permute-start.10
  123.1 1.8 collective-permute-start.14
  124.9 7.5 %shard_map.40 = (f32[192,768]{1,0:T(8,128)S(1)}, bf16[192,768]{1,0:T(8,128)(2,1)S(1)}, bf16[192,768]{1,0:T(8,128)(2,1)S(1)}, f32[192,768]{1,0:T(8,128)S(1)}) custom-call(s32[2]{0:T(128)S(1)} %pad_add_fusion.1.which_ref, bf16[4,8,768,384]{3,2,1,0:T(8,128)(2,1)} %bitcast.71, bf16[4,8,768,384]{3,2,1,0:T(8,128)(2,1)} %bitcast.72, ...), custom_call_target="tpu_custom_call" | custom-call | flops 3623878656 | bytes 11796480 | tf_op jit(solution)/shard_map/pallas_call | solution.py:198
  132.5 1.6 collective-permute-start.12
  135.0 3.2 %collective-permute-start.15 = (bf16[192,768]{1,0:T(8,128)(2,1)S(1)}, bf16[192,768]{1,0:T(8,128)(2,1)S(1)}, u32[]{:S(2)}, u32[]{:S(2)}) collective-permute-start(bf16[192,768]{1,0:T(8,128)(2,1)S(1)} %add_convert_fusion.2), channel_id=1, source_target_pairs={{0,96},{32,0},{64,32},{96,64},{1,97},{33,1},{65,33},{97,65},{2,98}... | collective-permute-start | bytes 884744 | tf_op jit(solution)/shard_map/ppermute | solution.py:17
  138.2 4.3 %shard_map.39 = f32[384,768]{1,0:T(8,128)S(1)} custom-call(s32[1]{0:T(128)} %bitcast.which_ref, bf16[4,8,768,384]{3,2,1,0:T(8,128)(2,1)} %bitcast.73, bf16[384,3072]{1,0:T(8,128)(2,1)} %get-tuple-element.30.refs_1_.refs_2_), custom_call_target="tpu_custom_call" | custom-call | flops 1811939328 | bytes 8257536 | tf_op jit(solution)/shard_map/pallas_call | solution.py:198
  142.6 2.6 %collective-permute-done.13 = bf16[192,768]{1,0:T(8,128)(2,1)S(1)} collective-permute-done((bf16[192,768]{1,0:T(8,128)(2,1)S(1)}, bf16[192,768]{1,0:T(8,128)(2,1)S(1)}, u32[]{:S(2)}, u32[]{:S(2)}) %collective-permute-start.13) | collective-permute-done | bytes 294944 | tf_op jit(solution)/shard_map/ppermute | solution.py:17
  145.2 4.7 %collective-permute-done.11 = bf16[192,768]{1,0:T(8,128)(2,1)S(1)} collective-permute-done((bf16[192,768]{1,0:T(8,128)(2,1)S(1)}, bf16[192,768]{1,0:T(8,128)(2,1)S(1)}, u32[]{:S(2)}, u32[]{:S(2)}) %collective-permute-start.11) | collective-permute-done | bytes 294944 | tf_op jit(solution)/shard_map/ppermute | solution.py:17
  150.5 1.8 collective-permute-start.18
  153.9 1.0 collective-permute-done.16
  155.0 1.2 broadcast_add_fusion
  156.1 7.1 %all-to-all-start = ((f32[64,1,128]{2,1,0:T(1,128)}), f32[64,1,128]{2,1,0:T(1,128)S(1)}, u32[]{:S(2)}, u32[]{:S(2)}) async-start(f32[64,1,128]{2,1,0:T(1,128)} %bitcast.23), calls=%async_computation | async-start | bytes 65536 | tf_op jit(solution)/shard_map/all_to_all | solution.py:286
  163.9 2.4 collective-permute-start.20
  166.4 11.0 %shard_map.41.part_ref = f32[384,3072]{1,0:T(8,128)} custom-call(s32[3]{0:T(128)S(1)} %pad_add_fusion.2.which_ref, bf16[4,8,768,384]{3,2,1,0:T(8,128)(2,1)} %bitcast.74, bf16[4,8,768,384]{3,2,1,0:T(8,128)(2,1)} %bitcast.75, bf16[4,8,768,384]{3,2,1,0:T(8,128)(2,1)} %bitcast.76, bf16[384,768]{1,0:T(8,128)(2,1)S(1)} %fusion.1.refs_3_, ...), custom_call_target="tpu_custom_call" | custom-call | flops 5435817984 | bytes 20643840 | tf_op jit(solution)/shard_map/pallas_call | solution.py:117
  178.8 11.6 %shard_map.42 = (bf16[384,3072]{1,0:T(8,128)(2,1)}, bf16[384,768]{1,0:T(8,128)(2,1)S(1)}) custom-call(s32[5]{0:T(128)S(1)} %stack.123.which_ref, f32[1,1]{1,0:T(1,128)} %bitcast.25.scale_ref, bf16[4,8,768,384]{3,2,1,0:T(8,128)(2,1)} %bitcast.77, bf16[384,768]{1,0:T(8,128)(2,1)S(1)} %pad_maximum_fusion.3.f_ref, f32[384,3072]{1,0:T(8,128)} %shard_map.41.part_ref, ...), custom_call_target="tpu_custom_call" | custom-call | flops 3623878656 | bytes 15335424 | tf_op jit(solution)/shard_map/pallas_call | solution.py:146
  191.1 2.7 %collective-permute-start.25 = (bf16[192,768]{1,0:T(8,128)(2,1)S(1)}, bf16[192,768]{1,0:T(8,128)(2,1)S(1)}, u32[]{:S(2)}, u32[]{:S(2)}) collective-permute-start(bf16[192,768]{1,0:T(8,128)(2,1)S(1)} %get-tuple-element.60), channel_id=1, source_target_pairs={{0,96},{32,0},{64,32},{96,64},{1,97},{33,1},{65,33},{97,65},{2,98}... | collective-permute-start | bytes 884744 | tf_op jit(solution)/shard_map/ppermute | solution.py:17
  193.8 7.5 %shard_map.44 = (f32[192,768]{1,0:T(8,128)S(1)}, bf16[192,768]{1,0:T(8,128)(2,1)S(1)}, bf16[192,768]{1,0:T(8,128)(2,1)S(1)}, f32[192,768]{1,0:T(8,128)S(1)}) custom-call(s32[2]{0:T(128)S(1)} %pad_add_fusion.1.which_ref, bf16[4,8,768,384]{3,2,1,0:T(8,128)(2,1)} %bitcast.78, bf16[4,8,768,384]{3,2,1,0:T(8,128)(2,1)} %bitcast.79, ...), custom_call_target="tpu_custom_call" | custom-call | flops 3623878656 | bytes 11796480 | tf_op jit(solution)/shard_map/pallas_call | solution.py:198
  201.3 2.0 collective-permute-start.23
  203.6 3.3 %collective-permute-start.26 = (bf16[192,768]{1,0:T(8,128)(2,1)S(1)}, bf16[192,768]{1,0:T(8,128)(2,1)S(1)}, u32[]{:S(2)}, u32[]{:S(2)}) collective-permute-start(bf16[192,768]{1,0:T(8,128)(2,1)S(1)} %add_convert_fusion), channel_id=1, source_target_pairs={{0,96},{32,0},{64,32},{96,64},{1,97},{33,1},{65,33},{97,65},{2,98}... | collective-permute-start | bytes 884744 | tf_op jit(solution)/shard_map/ppermute | solution.py:17
  206.9 4.3 %shard_map.43 = f32[384,768]{1,0:T(8,128)S(1)} custom-call(s32[1]{0:T(128)} %bitcast.which_ref, bf16[4,8,768,384]{3,2,1,0:T(8,128)(2,1)} %bitcast.80, bf16[384,3072]{1,0:T(8,128)(2,1)} %get-tuple-element.39.refs_1_.refs_2_), custom_call_target="tpu_custom_call" | custom-call | flops 1811939328 | bytes 8257536 | tf_op jit(solution)/shard_map/pallas_call | solution.py:198
  211.3 3.2 %collective-permute-done.24 = bf16[192,768]{1,0:T(8,128)(2,1)S(1)} collective-permute-done((bf16[192,768]{1,0:T(8,128)(2,1)S(1)}, bf16[192,768]{1,0:T(8,128)(2,1)S(1)}, u32[]{:S(2)}, u32[]{:S(2)}) %collective-permute-start.24) | collective-permute-done | bytes 294944 | tf_op jit(solution)/shard_map/ppermute | solution.py:17
  214.5 3.5 %collective-permute-done.22 = bf16[192,768]{1,0:T(8,128)(2,1)S(1)} collective-permute-done((bf16[192,768]{1,0:T(8,128)(2,1)S(1)}, bf16[192,768]{1,0:T(8,128)(2,1)S(1)}, u32[]{:S(2)}, u32[]{:S(2)}) %collective-permute-start.22) | collective-permute-done | bytes 294944 | tf_op jit(solution)/shard_map/ppermute | solution.py:17
  219.1 1.3 broadcast_in_dim.10
  220.4 7.9 %all-to-all-start.1 = ((f32[64,1,128]{2,1,0:T(1,128)}), f32[64,1,128]{2,1,0:T(1,128)S(1)}, u32[]{:S(2)}, u32[]{:S(2)}) async-start(f32[64,1,128]{2,1,0:T(1,128)} %broadcast_in_dim.10), calls=%async_computation.1 | async-start | bytes 65536 | tf_op jit(solution)/shard_map/all_to_all | solution.py:286
  228.7 9.1 %all-to-all-done.1 = f32[64,1,128]{2,1,0:T(1,128)S(1)} async-done(((f32[64,1,128]{2,1,0:T(1,128)}), f32[64,1,128]{2,1,0:T(1,128)S(1)}, u32[]{:S(2)}, u32[]{:S(2)}) %all-to-all-start.1) | async-done | bytes 32800 | tf_op jit(solution)/shard_map/all_to_all | solution.py:286
  239.3 1.2 collective-permute-start.27
  240.4 1.6 collective-permute-start.28
  243.9 2.1 collective-permute-done.27
  246.0 2.6 %collective-permute-done.28 = bf16[192,384]{1,0:T(8,128)(2,1)S(1)} collective-permute-done((bf16[192,384]{1,0:T(8,128)(2,1)S(1)}, bf16[192,384]{1,0:T(8,128)(2,1)S(1)}, u32[]{:S(2)}, u32[]{:S(2)}) %collective-permute-start.28) | collective-permute-done | bytes 147488 | tf_op jit(solution)/shard_map/ppermute | solution.py:17
  248.6 2.4 collective-permute-done.29
  251.3 1.1 convert_multiply_fusion
  (87 shorter events, 15.9 us)
Async XLA Ops:
  6.5 96.1 %all-gather.2.cloned.1.call-start = ((), (), s32[]{:S(2)}) async-start(), calls=%async_computation.2 | async-start | bytes 19464192 | tf_op jit(solution)/shard_map/all_gather | solution.py:307
  8.4 9.5 %collective-permute-start = (bf16[192,384]{1,0:T(8,128)(2,1)S(1)}, bf16[192,384]{1,0:T(8,128)(2,1)S(1)}, u32[]{:S(2)}, u32[]{:S(2)}) collective-permute-start(bf16[192,384]{1,0:T(8,128)(2,1)S(1)} %get-tuple-element.64), channel_id=1, source_target_pairs={{0,24},{8,0},{16,8},{24,16},{1,25},{9,1},{17,9},{25,17},{2,26},{10... | collective-permute-start | bytes 442376 | tf_op jit(solution)/shard_map/ppermute | solution.py:17
  11.6 8.3 %collective-permute-start.1 = (bf16[192,384]{1,0:T(8,128)(2,1)S(1)}, bf16[192,384]{1,0:T(8,128)(2,1)S(1)}, u32[]{:S(2)}, u32[]{:S(2)}) collective-permute-start(bf16[192,384]{1,0:T(8,128)(2,1)S(1)} %get-tuple-element.65), channel_id=1, source_target_pairs={{0,16},{8,24},{16,0},{24,8},{1,17},{9,25},{17,1},{25,9},{2,18},{10... | collective-permute-start | bytes 442376 | tf_op jit(solution)/shard_map/ppermute | solution.py:17
  12.2 9.3 %collective-permute-start.2 = (bf16[192,384]{1,0:T(8,128)(2,1)S(1)}, bf16[192,384]{1,0:T(8,128)(2,1)S(1)}, u32[]{:S(2)}, u32[]{:S(2)}) collective-permute-start(bf16[192,384]{1,0:T(8,128)(2,1)S(1)} %get-tuple-element.63), channel_id=1, source_target_pairs={{0,8},{8,16},{16,24},{24,0},{1,9},{9,17},{17,25},{25,1},{2,10},{10... | collective-permute-start | bytes 442376 | tf_op jit(solution)/shard_map/ppermute | solution.py:17
  21.5 34.6 %collective-permute-start.7 = (bf16[384,1152]{1,0:T(8,128)(2,1)S(1)}, bf16[384,1152]{1,0:T(8,128)(2,1)S(1)}, u32[]{:S(2)}, u32[]{:S(2)}) collective-permute-start(bf16[384,1152]{1,0:T(8,128)(2,1)S(1)} %get-tuple-element.29), channel_id=1, source_target_pairs={{0,8},{8,16},{16,24},{24,0},{1,9},{9,17},{17,25},{25,1},{2,10},{10... | collective-permute-start | bytes 2654216 | tf_op jit(solution)/shard_map/ppermute | solution.py:17
  21.5 31.4 %collective-permute-start.6 = (bf16[384,1152]{1,0:T(8,128)(2,1)}, bf16[384,1152]{1,0:T(8,128)(2,1)}, u32[]{:S(2)}, u32[]{:S(2)}) collective-permute-start(bf16[384,1152]{1,0:T(8,128)(2,1)} %get-tuple-element.28), channel_id=1, source_target_pairs={{0,24},{8,0},{16,8},{24,16},{1,25},{9,1},{17,9},{25,17},{2,26},{10... | collective-permute-start | bytes 2654216 | tf_op jit(solution)/shard_map/ppermute | solution.py:17
  25.4 49.5 %collective-permute-start.3 = (bf16[384,768]{1,0:T(8,128)(2,1)S(1)}, bf16[384,768]{1,0:T(8,128)(2,1)S(1)}, u32[]{:S(2)}, u32[]{:S(2)}) collective-permute-start(bf16[384,768]{1,0:T(8,128)(2,1)S(1)} %bitcast.66), channel_id=1, source_target_pairs={{0,96},{32,0},{64,32},{96,64},{1,97},{33,1},{65,33},{97,65},{2,98}... | collective-permute-start | bytes 1769480 | tf_op jit(solution)/shard_map/ppermute | solution.py:17
  28.2 46.7 %collective-permute-start.4 = (bf16[384,768]{1,0:T(8,128)(2,1)S(1)}, bf16[384,768]{1,0:T(8,128)(2,1)S(1)}, u32[]{:S(2)}, u32[]{:S(2)}) collective-permute-start(bf16[384,768]{1,0:T(8,128)(2,1)S(1)} %bitcast.67), channel_id=1, source_target_pairs={{0,64},{32,96},{64,0},{96,32},{1,65},{33,97},{65,1},{97,33},{2,66}... | collective-permute-start | bytes 1769480 | tf_op jit(solution)/shard_map/ppermute | solution.py:17
  29.0 46.7 %collective-permute-start.5 = (bf16[384,768]{1,0:T(8,128)(2,1)S(1)}, bf16[384,768]{1,0:T(8,128)(2,1)}, u32[]{:S(2)}, u32[]{:S(2)}) collective-permute-start(bf16[384,768]{1,0:T(8,128)(2,1)S(1)} %bitcast.68), channel_id=1, source_target_pairs={{0,32},{32,64},{64,96},{96,0},{1,33},{33,65},{65,97},{97,1},{2,34}... | collective-permute-start | bytes 1769480 | tf_op jit(solution)/shard_map/ppermute | solution.py:17
  54.0 15.6 %collective-permute-start.9 = (bf16[384,384]{1,0:T(8,128)(2,1)S(1)}, bf16[384,384]{1,0:T(8,128)(2,1)S(1)}, u32[]{:S(2)}, u32[]{:S(2)}) collective-permute-start(bf16[384,384]{1,0:T(8,128)(2,1)S(1)} %slice.86), channel_id=1, source_target_pairs={{0,24},{8,0},{16,8},{24,16},{1,25},{9,1},{17,9},{25,17},{2,26},{10... | collective-permute-start | bytes 884744 | tf_op jit(solution)/shard_map/ppermute | solution.py:17
  56.2 16.9 %collective-permute-start.8 = (bf16[384,384]{1,0:T(8,128)(2,1)S(1)}, bf16[384,384]{1,0:T(8,128)(2,1)S(1)}, u32[]{:S(2)}, u32[]{:S(2)}) collective-permute-start(bf16[384,384]{1,0:T(8,128)(2,1)S(1)} %slice.85), channel_id=1, source_target_pairs={{0,8},{8,16},{16,24},{24,0},{1,9},{9,17},{17,25},{25,1},{2,10},{10... | collective-permute-start | bytes 884744 | tf_op jit(solution)/shard_map/ppermute | solution.py:17
  74.9 0.8 copy-start
  121.6 13.0 %collective-permute-start.10 = (bf16[192,768]{1,0:T(8,128)(2,1)S(1)}, bf16[192,768]{1,0:T(8,128)(2,1)S(1)}, u32[]{:S(2)}, u32[]{:S(2)}) collective-permute-start(bf16[192,768]{1,0:T(8,128)(2,1)S(1)} %get-tuple-element.61), channel_id=1, source_target_pairs={{0,32},{32,64},{64,96},{96,0},{1,33},{33,65},{65,97},{97,1},{2,34}... | collective-permute-start | bytes 884744 | tf_op jit(solution)/shard_map/ppermute | solution.py:17
  123.1 11.8 %collective-permute-start.14 = (bf16[192,768]{1,0:T(8,128)(2,1)S(1)}, bf16[192,768]{1,0:T(8,128)(2,1)S(1)}, u32[]{:S(2)}, u32[]{:S(2)}) collective-permute-start(bf16[192,768]{1,0:T(8,128)(2,1)S(1)} %get-tuple-element.62), channel_id=1, source_target_pairs={{0,96},{32,0},{64,32},{96,64},{1,97},{33,1},{65,33},{97,65},{2,98}... | collective-permute-start | bytes 884744 | tf_op jit(solution)/shard_map/ppermute | solution.py:17
  132.5 10.1 %collective-permute-start.12 = (bf16[192,768]{1,0:T(8,128)(2,1)S(1)}, bf16[192,768]{1,0:T(8,128)(2,1)S(1)}, u32[]{:S(2)}, u32[]{:S(2)}) collective-permute-start(bf16[192,768]{1,0:T(8,128)(2,1)S(1)} %get-tuple-element.33), channel_id=1, source_target_pairs={{0,96},{32,0},{64,32},{96,64},{1,97},{33,1},{65,33},{97,65},{2,98}... | collective-permute-start | bytes 884744 | tf_op jit(solution)/shard_map/ppermute | solution.py:17
  134.0 11.2 %collective-permute-start.13 = (bf16[192,768]{1,0:T(8,128)(2,1)S(1)}, bf16[192,768]{1,0:T(8,128)(2,1)S(1)}, u32[]{:S(2)}, u32[]{:S(2)}) collective-permute-start(bf16[192,768]{1,0:T(8,128)(2,1)S(1)} %get-tuple-element.34), channel_id=1, source_target_pairs={{0,32},{32,64},{64,96},{96,0},{1,33},{33,65},{65,97},{97,1},{2,34}... | collective-permute-start | bytes 884744 | tf_op jit(solution)/shard_map/ppermute | solution.py:17
  134.6 15.3 %collective-permute-start.11 = (bf16[192,768]{1,0:T(8,128)(2,1)S(1)}, bf16[192,768]{1,0:T(8,128)(2,1)S(1)}, u32[]{:S(2)}, u32[]{:S(2)}) collective-permute-start(bf16[192,768]{1,0:T(8,128)(2,1)S(1)} %add_convert_fusion.3), channel_id=1, source_target_pairs={{0,32},{32,64},{64,96},{96,0},{1,33},{33,65},{65,97},{97,1},{2,34}... | collective-permute-start | bytes 884744 | tf_op jit(solution)/shard_map/ppermute | solution.py:17
  135.0 14.9 %collective-permute-start.15 = (bf16[192,768]{1,0:T(8,128)(2,1)S(1)}, bf16[192,768]{1,0:T(8,128)(2,1)S(1)}, u32[]{:S(2)}, u32[]{:S(2)}) collective-permute-start(bf16[192,768]{1,0:T(8,128)(2,1)S(1)} %add_convert_fusion.2), channel_id=1, source_target_pairs={{0,96},{32,0},{64,32},{96,64},{1,97},{33,1},{65,33},{97,65},{2,98}... | collective-permute-start | bytes 884744 | tf_op jit(solution)/shard_map/ppermute | solution.py:17
  150.1 13.8 %collective-permute-start.17 = (bf16[384,768]{1,0:T(8,128)(2,1)S(1)}, bf16[384,768]{1,0:T(8,128)(2,1)S(1)}, u32[]{:S(2)}, u32[]{:S(2)}) collective-permute-start(bf16[384,768]{1,0:T(8,128)(2,1)S(1)} %fusion.1.refs_3_), channel_id=1, source_target_pairs={{0,96},{32,0},{64,32},{96,64},{1,97},{33,1},{65,33},{97,65},{2,98}... | collective-permute-start | bytes 1769480 | tf_op jit(solution)/shard_map/ppermute | solution.py:17
  150.5 15.8 %collective-permute-start.18 = (bf16[384,768]{1,0:T(8,128)(2,1)S(1)}, bf16[384,768]{1,0:T(8,128)(2,1)S(1)}, u32[]{:S(2)}, u32[]{:S(2)}) collective-permute-start(bf16[384,768]{1,0:T(8,128)(2,1)S(1)} %fusion.1.refs_3_), channel_id=1, source_target_pairs={{0,32},{32,64},{64,96},{96,0},{1,33},{33,65},{65,97},{97,1},{2,34}... | collective-permute-start | bytes 1769480 | tf_op jit(solution)/shard_map/ppermute | solution.py:17
  153.7 1.3 collective-permute-start.16
  156.1 21.3 %all-to-all-start = ((f32[64,1,128]{2,1,0:T(1,128)}), f32[64,1,128]{2,1,0:T(1,128)S(1)}, u32[]{:S(2)}, u32[]{:S(2)}) async-start(f32[64,1,128]{2,1,0:T(1,128)} %bitcast.23), calls=%async_computation | async-start | bytes 65536 | tf_op jit(solution)/shard_map/all_to_all | solution.py:286
  163.9 14.8 %collective-permute-start.20 = (bf16[192,768]{1,0:T(8,128)(2,1)S(1)}, bf16[192,768]{1,0:T(8,128)(2,1)S(1)}, u32[]{:S(2)}, u32[]{:S(2)}) collective-permute-start(bf16[192,768]{1,0:T(8,128)(2,1)S(1)} %slice.91), channel_id=1, source_target_pairs={{0,96},{32,0},{64,32},{96,64},{1,97},{33,1},{65,33},{97,65},{2,98}... | collective-permute-start | bytes 884744 | tf_op jit(solution)/shard_map/ppermute | solution.py:17
  166.3 12.4 %collective-permute-start.19 = (bf16[192,768]{1,0:T(8,128)(2,1)S(1)}, bf16[192,768]{1,0:T(8,128)(2,1)S(1)}, u32[]{:S(2)}, u32[]{:S(2)}) collective-permute-start(bf16[192,768]{1,0:T(8,128)(2,1)S(1)} %slice.90), channel_id=1, source_target_pairs={{0,32},{32,64},{64,96},{96,0},{1,33},{33,65},{65,97},{97,1},{2,34}... | collective-permute-start | bytes 884744 | tf_op jit(solution)/shard_map/ppermute | solution.py:17
  190.4 13.0 %collective-permute-start.21 = (bf16[192,768]{1,0:T(8,128)(2,1)S(1)}, bf16[192,768]{1,0:T(8,128)(2,1)S(1)}, u32[]{:S(2)}, u32[]{:S(2)}) collective-permute-start(bf16[192,768]{1,0:T(8,128)(2,1)S(1)} %get-tuple-element.59), channel_id=1, source_target_pairs={{0,32},{32,64},{64,96},{96,0},{1,33},{33,65},{65,97},{97,1},{2,34}... | collective-permute-start | bytes 884744 | tf_op jit(solution)/shard_map/ppermute | solution.py:17
  191.1 12.5 %collective-permute-start.25 = (bf16[192,768]{1,0:T(8,128)(2,1)S(1)}, bf16[192,768]{1,0:T(8,128)(2,1)S(1)}, u32[]{:S(2)}, u32[]{:S(2)}) collective-permute-start(bf16[192,768]{1,0:T(8,128)(2,1)S(1)} %get-tuple-element.60), channel_id=1, source_target_pairs={{0,96},{32,0},{64,32},{96,64},{1,97},{33,1},{65,33},{97,65},{2,98}... | collective-permute-start | bytes 884744 | tf_op jit(solution)/shard_map/ppermute | solution.py:17
  201.3 10.0 %collective-permute-start.23 = (bf16[192,768]{1,0:T(8,128)(2,1)S(1)}, bf16[192,768]{1,0:T(8,128)(2,1)S(1)}, u32[]{:S(2)}, u32[]{:S(2)}) collective-permute-start(bf16[192,768]{1,0:T(8,128)(2,1)S(1)} %get-tuple-element.42), channel_id=1, source_target_pairs={{0,96},{32,0},{64,32},{96,64},{1,97},{33,1},{65,33},{97,65},{2,98}... | collective-permute-start | bytes 884744 | tf_op jit(solution)/shard_map/ppermute | solution.py:17
  203.3 11.2 %collective-permute-start.24 = (bf16[192,768]{1,0:T(8,128)(2,1)S(1)}, bf16[192,768]{1,0:T(8,128)(2,1)S(1)}, u32[]{:S(2)}, u32[]{:S(2)}) collective-permute-start(bf16[192,768]{1,0:T(8,128)(2,1)S(1)} %get-tuple-element.43), channel_id=1, source_target_pairs={{0,32},{32,64},{64,96},{96,0},{1,33},{33,65},{65,97},{97,1},{2,34}... | collective-permute-start | bytes 884744 | tf_op jit(solution)/shard_map/ppermute | solution.py:17
  203.5 14.5 %collective-permute-start.22 = (bf16[192,768]{1,0:T(8,128)(2,1)S(1)}, bf16[192,768]{1,0:T(8,128)(2,1)S(1)}, u32[]{:S(2)}, u32[]{:S(2)}) collective-permute-start(bf16[192,768]{1,0:T(8,128)(2,1)S(1)} %add_convert_fusion.1), channel_id=1, source_target_pairs={{0,32},{32,64},{64,96},{96,0},{1,33},{33,65},{65,97},{97,1},{2,34}... | collective-permute-start | bytes 884744 | tf_op jit(solution)/shard_map/ppermute | solution.py:17
  203.6 14.4 %collective-permute-start.26 = (bf16[192,768]{1,0:T(8,128)(2,1)S(1)}, bf16[192,768]{1,0:T(8,128)(2,1)S(1)}, u32[]{:S(2)}, u32[]{:S(2)}) collective-permute-start(bf16[192,768]{1,0:T(8,128)(2,1)S(1)} %add_convert_fusion), channel_id=1, source_target_pairs={{0,96},{32,0},{64,32},{96,64},{1,97},{33,1},{65,33},{97,65},{2,98}... | collective-permute-start | bytes 884744 | tf_op jit(solution)/shard_map/ppermute | solution.py:17
  220.4 17.4 %all-to-all-start.1 = ((f32[64,1,128]{2,1,0:T(1,128)}), f32[64,1,128]{2,1,0:T(1,128)S(1)}, u32[]{:S(2)}, u32[]{:S(2)}) async-start(f32[64,1,128]{2,1,0:T(1,128)} %broadcast_in_dim.10), calls=%async_computation.1 | async-start | bytes 65536 | tf_op jit(solution)/shard_map/all_to_all | solution.py:286
  239.1 2.9 %collective-permute-start.30 = (f32[8,128]{1,0:T(8,128)S(1)}, f32[8,128]{1,0:T(8,128)S(1)}, u32[]{:S(2)}, u32[]{:S(2)}) collective-permute-start(f32[8,128]{1,0:T(8,128)S(1)} %broadcast_in_dim.11), channel_id=1, source_target_pairs={{0,1},{1,0},{2,3},{3,2},{4,5},{5,4},{6,7},{7,6},{8,9},{9,8},{10,11... | collective-permute-start | bytes 12296 | tf_op jit(solution)/shard_map/ppermute | solution.py:282
  239.3 6.7 %collective-permute-start.27 = (bf16[192,384]{1,0:T(8,128)(2,1)S(1)}, bf16[192,384]{1,0:T(8,128)(2,1)S(1)}, u32[]{:S(2)}, u32[]{:S(2)}) collective-permute-start(bf16[192,384]{1,0:T(8,128)(2,1)S(1)} %get-tuple-element.58), channel_id=1, source_target_pairs={{0,24},{8,0},{16,8},{24,16},{1,25},{9,1},{17,9},{25,17},{2,26},{10... | collective-permute-start | bytes 442376 | tf_op jit(solution)/shard_map/ppermute | solution.py:17
  240.4 8.2 %collective-permute-start.28 = (bf16[192,384]{1,0:T(8,128)(2,1)S(1)}, bf16[192,384]{1,0:T(8,128)(2,1)S(1)}, u32[]{:S(2)}, u32[]{:S(2)}) collective-permute-start(bf16[192,384]{1,0:T(8,128)(2,1)S(1)} %get-tuple-element.57), channel_id=1, source_target_pairs={{0,16},{8,24},{16,0},{24,8},{1,17},{9,25},{17,1},{25,9},{2,18},{10... | collective-permute-start | bytes 442376 | tf_op jit(solution)/shard_map/ppermute | solution.py:17
  242.0 9.1 %collective-permute-start.29 = (bf16[192,384]{1,0:T(8,128)(2,1)S(1)}, bf16[192,384]{1,0:T(8,128)(2,1)S(1)}, u32[]{:S(2)}, u32[]{:S(2)}) collective-permute-start(bf16[192,384]{1,0:T(8,128)(2,1)S(1)} %get-tuple-element.55), channel_id=1, source_target_pairs={{0,8},{8,16},{16,24},{24,0},{1,9},{9,17},{17,25},{25,1},{2,10},{10... | collective-permute-start | bytes 442376 | tf_op jit(solution)/shard_map/ppermute | solution.py:17
Sparse Core Ops, SparseCore 0:
  9.6 92.9 all-gather.1

commit v10 on v8

--- a/solution.py
+++ b/solution.py
@@ -278,13 +278,13 @@
     return lax.dynamic_slice_in_dim(twice, lax.rem(N - me, N), N, axis=0)
 
 
-def total_of(value, beside):
-    total = jnp.full((N * N * N, 128), jnp.sum(value * value), F32)
-    total = total + lax.ppermute(total, "c", [(0, 1), (1, 0)])
-    each = lax.all_to_all(total, ("x", "y", "z"), split_axis=0, concat_axis=0, tiled=True)
-    if beside is not None:
-        each, beside = lax.optimization_barrier((each, beside))
-    return jnp.sum(each[:, 0]), beside
+def part_of(value):
+    part = jnp.full((N * N * N, 128), jnp.sum(value * value), F32)
+    return part + lax.ppermute(part, "c", [(0, 1), (1, 0)])
+
+
+def spread(part):
+    return lax.all_to_all(part, ("x", "y", "z"), split_axis=0, concat_axis=0, tiled=True)
 
 
 def per_device(tokens, target, weight):
@@ -311,13 +311,14 @@
     first = ring_sum(x, slope, term, ix)
     own, after, far, before = ring_gather_halves(first.astype(BF16), "x")
     part = moved(x, [own, after, before], [at(0), at(1), at(3)])
-    total, part = total_of(first, part)
-    scale = 0.5 * math.sqrt(hidden_all) / jnp.sqrt(total + 1e-06)
+    each, part = lax.optimization_barrier((spread(part_of(first)), part))
+    scale = 0.5 * math.sqrt(hidden_all) / jnp.sqrt(jnp.sum(each[:, 0]) + 1e-06)
     slope, term = second_slopes(x, far, [at(2)] + tiles, part, scale.reshape(1, 1), hidden, t)
     second = ring_sum(x, slope, term, ix)
-    total, _ = total_of(second, None)
+    share, second = lax.optimization_barrier((part_of(second), second.astype(BF16)))
+    total = jnp.sum(spread(share)[:, 0])
     factor = jnp.minimum(1.0, math.sqrt(width * hidden_all) / jnp.sqrt(total + 1e-06))
-    held = second.astype(BF16).T.reshape(N, -1, cols)
+    held = second.T.reshape(N, -1, cols)
     parts = in_order(ring_swap(lambda k: lax.dynamic_index_in_dim(held, lax.rem(iy + k, N), 0, keepdims=False), "y"), iy)
     whole = jnp.concatenate([parts[k] for k in range(N)], axis=1)
     return whole.astype(F32) * factor

time: 250 us -> 251 us (level)
  transfers between devices with their start and end apart: 34 -> 34, of which waited for: 13 -> 15; matrix products, arithmetic and copies ran while one was open for 5% -> 4% of each run, Pallas kernels for 15% -> 15%
where the time goes in v10:
time: 251 us; the launch traced here: 250 us
  waiting for transfers between devices  92.6 us (37%)
  Pallas kernels  68.9 us (27%)
  starting transfers between devices  56.6 us (23%)
  between operations  15.2 us (6%)
  other arithmetic  9.36 us (4%)
  local copies, waits for them, and re-layouts  7.74 us (3%)
    ppermute x29, waiting for transfers between devices, shift(): return lax.ppermute(value, axis, [(i, (i + step) % N) for i in range(N)])  57.1 us
    ppermute x29, starting transfers between devices, shift(): return lax.ppermute(value, axis, [(i, (i + step) % N) for i in range(N)])  43.6 us
    all_gather x1, waiting for transfers between devices, per_device(): lax.all_gather(tokens, ('y', 'z', 'c'), axis=0, tiled=True)  26.9 us
    pallas_call x4, Pallas kernels, terms(): pl.pallas_call(kernel, grid_spec=pltpu.PrefetchScalarGridSpec(num_scalar_...  23.8 us
    pallas_call x1, Pallas kernels, first_slopes(): pl.pallas_call(kernel, grid_spec=pltpu.PrefetchScalarGridSpec(num_scalar_...  19 us
    all_to_all x2, starting transfers between devices, spread(): lax.all_to_all(part, ('x', 'y', 'z'), split_axis=0, concat_axis=0, tiled=...  12.6 us
    pallas_call x1, Pallas kernels, second_slopes(): pl.pallas_call(kernel, grid_spec=pltpu.PrefetchScalarGridSpec(num_scalar_...  11.6 us
    pallas_call x1, Pallas kernels, moved(): pl.pallas_call(kernel, grid_spec=pltpu.PrefetchScalarGridSpec(num_scalar_...  11 us
  transfers between devices with their start and end apart: 34, of which 15 were waited for; matrix products, arithmetic and copies ran while one was open for 4% of the time, Pallas kernels for 15%

profile of v10, /device:TPU:0, one launch (start us, length us, event | category | flops | bytes accessed | tf_op | source)
XLA Modules:
  0.0 250.4 jit_solution(12642110162524467235)
XLA Ops:
  7.3 1.1 constant_dynamic-slice_fusion.1
  8.4 3.2 %collective-permute-start = (bf16[192,384]{1,0:T(8,128)(2,1)S(1)}, bf16[192,384]{1,0:T(8,128)(2,1)S(1)}, u32[]{:S(2)}, u32[]{:S(2)}) collective-permute-start(bf16[192,384]{1,0:T(8,128)(2,1)S(1)} %get-tuple-element.68), channel_id=1, source_target_pairs={{0,24},{8,0},{16,8},{24,16},{1,25},{9,1},{17,9},{25,17},{2,26},{10... | collective-permute-start | bytes 442376 | tf_op jit(solution)/shard_map/ppermute | solution.py:17
  12.2 1.0 collective-permute-start.2
  13.3 3.6 %shard_map.37 = (bf16[384,1152]{1,0:T(8,128)(2,1)S(1)}, bf16[384,1152]{1,0:T(8,128)(2,1)}, bf16[384,768]{1,0:T(8,128)(2,1)S(1)}) custom-call(s32[4]{0:T(128)S(1)} %pad_add_fusion.which_ref, bf16[768,1536]{1,0:T(8,128)(2,1)} %before.1, bf16[768,1536]{1,0:T(8,128)(2,1)} %before.1, bf16[768,1536]{1,0:T(8,128)(2,1)} %before.1, bf16[768,1536]{1,0:T(8,128)(2,1)} %before.1), custom_call_target="tpu_custom_call" | custom-call | tf_op jit(solution)/shard_map/pallas_call | solution.py:255
  17.0 0.9 bitcast_dynamic-update-slice_fusion.12
  17.9 1.9 collective-permute-done.1
  19.9 1.7 collective-permute-done.2
  21.5 3.2 %collective-permute-start.6 = (bf16[384,1152]{1,0:T(8,128)(2,1)}, bf16[384,1152]{1,0:T(8,128)(2,1)}, u32[]{:S(2)}, u32[]{:S(2)}) collective-permute-start(bf16[384,1152]{1,0:T(8,128)(2,1)} %get-tuple-element.30), channel_id=1, source_target_pairs={{0,24},{8,0},{16,8},{24,16},{1,25},{9,1},{17,9},{25,17},{2,26},{10... | collective-permute-start | bytes 2654216 | tf_op jit(solution)/shard_map/ppermute | solution.py:17
  25.4 2.8 %collective-permute-start.3 = (bf16[384,768]{1,0:T(8,128)(2,1)S(1)}, bf16[384,768]{1,0:T(8,128)(2,1)S(1)}, u32[]{:S(2)}, u32[]{:S(2)}) collective-permute-start(bf16[384,768]{1,0:T(8,128)(2,1)S(1)} %bitcast.65), channel_id=1, source_target_pairs={{0,96},{32,0},{64,32},{96,64},{1,97},{33,1},{65,33},{97,65},{2,98}... | collective-permute-start | bytes 1769480 | tf_op jit(solution)/shard_map/ppermute | solution.py:17
  29.9 23.0 %collective-permute-done.6 = bf16[384,1152]{1,0:T(8,128)(2,1)} collective-permute-done((bf16[384,1152]{1,0:T(8,128)(2,1)}, bf16[384,1152]{1,0:T(8,128)(2,1)}, u32[]{:S(2)}, u32[]{:S(2)}) %collective-permute-start.6) | collective-permute-done | bytes 884768 | tf_op jit(solution)/shard_map/ppermute | solution.py:17
  52.9 1.1 slice.82
  54.0 2.2 collective-permute-start.9
  56.3 1.1 slice_bitcast_fusion.1
  57.4 12.2 %collective-permute-done.9 = bf16[384,384]{1,0:T(8,128)(2,1)S(1)} collective-permute-done((bf16[384,384]{1,0:T(8,128)(2,1)S(1)}, bf16[384,384]{1,0:T(8,128)(2,1)S(1)}, u32[]{:S(2)}, u32[]{:S(2)}) %collective-permute-start.9) | collective-permute-done | bytes 294944 | tf_op jit(solution)/shard_map/ppermute | solution.py:17
  69.6 3.5 %collective-permute-done.8 = bf16[384,384]{1,0:T(8,128)(2,1)S(1)} collective-permute-done((bf16[384,384]{1,0:T(8,128)(2,1)S(1)}, bf16[384,384]{1,0:T(8,128)(2,1)S(1)}, u32[]{:S(2)}, u32[]{:S(2)}) %collective-permute-start.8) | collective-permute-done | bytes 294944 | tf_op jit(solution)/shard_map/ppermute | solution.py:17
  73.2 1.7 pad_maximum_fusion.refs_4_.t_ref
  75.7 26.9 %all-gather.2.cloned.1.call-done = bf16[24576,384]{1,0:T(8,128)(2,1)} async-done(((bf16[768,384]{1,0:T(8,128)(2,1)}), bf16[24576,384]{1,0:T(8,128)(2,1)}) %all-gather.2.cloned.1.call-update) | async-done | bytes 18874384 | tf_op jit(solution)/shard_map/all_gather | solution.py:297
  102.6 19.0 %shard_map.38 = (f32[384,3072]{1,0:T(8,128)}, bf16[384,3072]{1,0:T(8,128)(2,1)}, bf16[384,768]{1,0:T(8,128)(2,1)S(1)}) custom-call(s32[8]{0:T(128)S(1)} %stack.126.which_ref, bf16[4,8,768,384]{3,2,1,0:T(8,128)(2,1)} %bitcast.69, bf16[384,768]{1,0:T(8,128)(2,1)S(1)} %bitcast.68, bf16[384,768]{1,0:T(8,128)(2,1)S(1)} %collective-permute-done.3.refs_1_, ...), custom_call_target="tpu_custom_call" | custom-call | flops 9059696640 | bytes 31260672 | tf_op jit(solution)/shard_map/pallas_call | solution.py:82
  121.6 1.6 collective-permute-start.10
  123.1 1.8 collective-permute-start.14
  124.9 7.5 %shard_map.40 = (f32[192,768]{1,0:T(8,128)S(1)}, bf16[192,768]{1,0:T(8,128)(2,1)S(1)}, bf16[192,768]{1,0:T(8,128)(2,1)S(1)}, f32[192,768]{1,0:T(8,128)S(1)}) custom-call(s32[2]{0:T(128)S(1)} %pad_add_fusion.1.which_ref, bf16[4,8,768,384]{3,2,1,0:T(8,128)(2,1)} %bitcast.70, bf16[4,8,768,384]{3,2,1,0:T(8,128)(2,1)} %bitcast.71, ...), custom_call_target="tpu_custom_call" | custom-call | flops 3623878656 | bytes 11796480 | tf_op jit(solution)/shard_map/pallas_call | solution.py:198
  132.5 1.6 collective-permute-start.12
  135.0 3.2 %collective-permute-start.15 = (bf16[192,768]{1,0:T(8,128)(2,1)S(1)}, bf16[192,768]{1,0:T(8,128)(2,1)S(1)}, u32[]{:S(2)}, u32[]{:S(2)}) collective-permute-start(bf16[192,768]{1,0:T(8,128)(2,1)S(1)} %add_convert_fusion.2), channel_id=1, source_target_pairs={{0,96},{32,0},{64,32},{96,64},{1,97},{33,1},{65,33},{97,65},{2,98}... | collective-permute-start | bytes 884744 | tf_op jit(solution)/shard_map/ppermute | solution.py:17
  138.2 4.3 %shard_map.39 = f32[384,768]{1,0:T(8,128)S(1)} custom-call(s32[1]{0:T(128)} %bitcast.which_ref, bf16[4,8,768,384]{3,2,1,0:T(8,128)(2,1)} %bitcast.72, bf16[384,3072]{1,0:T(8,128)(2,1)} %get-tuple-element.32.refs_1_.refs_2_), custom_call_target="tpu_custom_call" | custom-call | flops 1811939328 | bytes 8257536 | tf_op jit(solution)/shard_map/pallas_call | solution.py:198
  142.6 2.6 %collective-permute-done.13 = bf16[192,768]{1,0:T(8,128)(2,1)S(1)} collective-permute-done((bf16[192,768]{1,0:T(8,128)(2,1)S(1)}, bf16[192,768]{1,0:T(8,128)(2,1)S(1)}, u32[]{:S(2)}, u32[]{:S(2)}) %collective-permute-start.13) | collective-permute-done | bytes 294944 | tf_op jit(solution)/shard_map/ppermute | solution.py:17
  145.2 4.7 %collective-permute-done.11 = bf16[192,768]{1,0:T(8,128)(2,1)S(1)} collective-permute-done((bf16[192,768]{1,0:T(8,128)(2,1)S(1)}, bf16[192,768]{1,0:T(8,128)(2,1)S(1)}, u32[]{:S(2)}, u32[]{:S(2)}) %collective-permute-start.11) | collective-permute-done | bytes 294944 | tf_op jit(solution)/shard_map/ppermute | solution.py:17
  150.5 1.8 collective-permute-start.18
  153.9 1.0 collective-permute-done.16
  155.0 1.2 broadcast_add_fusion.1
  156.1 7.1 %all-to-all-start = ((f32[64,1,128]{2,1,0:T(1,128)}), f32[64,1,128]{2,1,0:T(1,128)S(1)}, u32[]{:S(2)}, u32[]{:S(2)}) async-start(f32[64,1,128]{2,1,0:T(1,128)} %bitcast.23), calls=%async_computation | async-start | bytes 65536 | tf_op jit(solution)/shard_map/all_to_all | solution.py:287
  163.9 2.4 collective-permute-start.20
  166.4 11.0 %shard_map.41.part_ref = f32[384,3072]{1,0:T(8,128)} custom-call(s32[3]{0:T(128)S(1)} %pad_add_fusion.2.which_ref, bf16[4,8,768,384]{3,2,1,0:T(8,128)(2,1)} %bitcast.73, bf16[4,8,768,384]{3,2,1,0:T(8,128)(2,1)} %bitcast.74, bf16[4,8,768,384]{3,2,1,0:T(8,128)(2,1)} %bitcast.75, bf16[384,768]{1,0:T(8,128)(2,1)S(1)} %fusion.1.refs_3_, ...), custom_call_target="tpu_custom_call" | custom-call | flops 5435817984 | bytes 20643840 | tf_op jit(solution)/shard_map/pallas_call | solution.py:117
  178.8 11.6 %shard_map.42 = (bf16[384,3072]{1,0:T(8,128)(2,1)}, bf16[384,768]{1,0:T(8,128)(2,1)S(1)}) custom-call(s32[5]{0:T(128)S(1)} %stack.123.which_ref, f32[1,1]{1,0:T(1,128)} %bitcast.25.scale_ref, bf16[4,8,768,384]{3,2,1,0:T(8,128)(2,1)} %bitcast.76, bf16[384,768]{1,0:T(8,128)(2,1)S(1)} %pad_maximum_fusion.3.f_ref, f32[384,3072]{1,0:T(8,128)} %shard_map.41.part_ref, ...), custom_call_target="tpu_custom_call" | custom-call | flops 3623878656 | bytes 15335424 | tf_op jit(solution)/shard_map/pallas_call | solution.py:146
  191.1 2.7 %collective-permute-start.25 = (bf16[192,768]{1,0:T(8,128)(2,1)S(1)}, bf16[192,768]{1,0:T(8,128)(2,1)S(1)}, u32[]{:S(2)}, u32[]{:S(2)}) collective-permute-start(bf16[192,768]{1,0:T(8,128)(2,1)S(1)} %get-tuple-element.64), channel_id=1, source_target_pairs={{0,96},{32,0},{64,32},{96,64},{1,97},{33,1},{65,33},{97,65},{2,98}... | collective-permute-start | bytes 884744 | tf_op jit(solution)/shard_map/ppermute | solution.py:17
  193.8 7.5 %shard_map.44 = (f32[192,768]{1,0:T(8,128)S(1)}, bf16[192,768]{1,0:T(8,128)(2,1)S(1)}, bf16[192,768]{1,0:T(8,128)(2,1)S(1)}, f32[192,768]{1,0:T(8,128)S(1)}) custom-call(s32[2]{0:T(128)S(1)} %pad_add_fusion.1.which_ref, bf16[4,8,768,384]{3,2,1,0:T(8,128)(2,1)} %bitcast.77, bf16[4,8,768,384]{3,2,1,0:T(8,128)(2,1)} %bitcast.78, ...), custom_call_target="tpu_custom_call" | custom-call | flops 3623878656 | bytes 11796480 | tf_op jit(solution)/shard_map/pallas_call | solution.py:198
  201.3 2.0 collective-permute-start.23
  203.6 3.3 %collective-permute-start.26 = (bf16[192,768]{1,0:T(8,128)(2,1)S(1)}, bf16[192,768]{1,0:T(8,128)(2,1)S(1)}, u32[]{:S(2)}, u32[]{:S(2)}) collective-permute-start(bf16[192,768]{1,0:T(8,128)(2,1)S(1)} %add_convert_fusion), channel_id=1, source_target_pairs={{0,96},{32,0},{64,32},{96,64},{1,97},{33,1},{65,33},{97,65},{2,98}... | collective-permute-start | bytes 884744 | tf_op jit(solution)/shard_map/ppermute | solution.py:17
  206.9 4.3 %shard_map.43 = f32[384,768]{1,0:T(8,128)S(1)} custom-call(s32[1]{0:T(128)} %bitcast.which_ref, bf16[4,8,768,384]{3,2,1,0:T(8,128)(2,1)} %bitcast.79, bf16[384,3072]{1,0:T(8,128)(2,1)} %get-tuple-element.41.refs_1_.refs_2_), custom_call_target="tpu_custom_call" | custom-call | flops 1811939328 | bytes 8257536 | tf_op jit(solution)/shard_map/pallas_call | solution.py:198
  211.3 3.2 %collective-permute-done.24 = bf16[192,768]{1,0:T(8,128)(2,1)S(1)} collective-permute-done((bf16[192,768]{1,0:T(8,128)(2,1)S(1)}, bf16[192,768]{1,0:T(8,128)(2,1)S(1)}, u32[]{:S(2)}, u32[]{:S(2)}) %collective-permute-start.24) | collective-permute-done | bytes 294944 | tf_op jit(solution)/shard_map/ppermute | solution.py:17
  214.5 3.5 %collective-permute-done.22 = bf16[192,768]{1,0:T(8,128)(2,1)S(1)} collective-permute-done((bf16[192,768]{1,0:T(8,128)(2,1)S(1)}, bf16[192,768]{1,0:T(8,128)(2,1)S(1)}, u32[]{:S(2)}, u32[]{:S(2)}) %collective-permute-start.22) | collective-permute-done | bytes 294944 | tf_op jit(solution)/shard_map/ppermute | solution.py:17
  218.2 1.0 multiply_reduce_fusion
  220.2 1.1 collective-permute-done.27
  221.3 1.2 broadcast_add_fusion
  222.9 2.8 %collective-permute-start.28 = (bf16[192,384]{1,0:T(8,128)(2,1)S(1)}, bf16[192,384]{1,0:T(8,128)(2,1)S(1)}, u32[]{:S(2)}, u32[]{:S(2)}) collective-permute-start(bf16[192,384]{1,0:T(8,128)(2,1)S(1)} %get-tuple-element.62), channel_id=1, source_target_pairs={{0,24},{8,0},{16,8},{24,16},{1,25},{9,1},{17,9},{25,17},{2,26},{10... | collective-permute-start | bytes 442376 | tf_op jit(solution)/shard_map/ppermute | solution.py:17
  225.7 5.5 %all-to-all-start.1 = ((f32[64,1,128]{2,1,0:T(1,128)}), f32[64,1,128]{2,1,0:T(1,128)S(1)}, u32[]{:S(2)}, u32[]{:S(2)}) async-start(f32[64,1,128]{2,1,0:T(1,128)} %bitcast.38), calls=%async_computation.1 | async-start | bytes 65536 | tf_op jit(solution)/shard_map/all_to_all | solution.py:287
  231.3 3.2 %collective-permute-start.29 = (bf16[192,384]{1,0:T(8,128)(2,1)S(1)}, bf16[192,384]{1,0:T(8,128)(2,1)S(1)}, u32[]{:S(2)}, u32[]{:S(2)}) collective-permute-start(bf16[192,384]{1,0:T(8,128)(2,1)S(1)} %get-tuple-element.61), channel_id=1, source_target_pairs={{0,16},{8,24},{16,0},{24,8},{1,17},{9,25},{17,1},{25,9},{2,18},{10... | collective-permute-start | bytes 442376 | tf_op jit(solution)/shard_map/ppermute | solution.py:17
  235.0 5.8 %all-to-all-done.1 = f32[64,1,128]{2,1,0:T(1,128)S(1)} async-done(((f32[64,1,128]{2,1,0:T(1,128)}), f32[64,1,128]{2,1,0:T(1,128)S(1)}, u32[]{:S(2)}, u32[]{:S(2)}) %all-to-all-start.1) | async-done | bytes 32800 | tf_op jit(solution)/shard_map/all_to_all | solution.py:287
  242.4 1.1 convert_multiply_fusion
  (85 shorter events, 13.6 us)
Async XLA Ops:
  6.5 96.1 %all-gather.2.cloned.1.call-start = ((), (), s32[]{:S(2)}) async-start(), calls=%async_computation.2 | async-start | bytes 19464192 | tf_op jit(solution)/shard_map/all_gather | solution.py:297
  8.4 9.5 %collective-permute-start = (bf16[192,384]{1,0:T(8,128)(2,1)S(1)}, bf16[192,384]{1,0:T(8,128)(2,1)S(1)}, u32[]{:S(2)}, u32[]{:S(2)}) collective-permute-start(bf16[192,384]{1,0:T(8,128)(2,1)S(1)} %get-tuple-element.68), channel_id=1, source_target_pairs={{0,24},{8,0},{16,8},{24,16},{1,25},{9,1},{17,9},{25,17},{2,26},{10... | collective-permute-start | bytes 442376 | tf_op jit(solution)/shard_map/ppermute | solution.py:17
  11.6 8.3 %collective-permute-start.1 = (bf16[192,384]{1,0:T(8,128)(2,1)S(1)}, bf16[192,384]{1,0:T(8,128)(2,1)S(1)}, u32[]{:S(2)}, u32[]{:S(2)}) collective-permute-start(bf16[192,384]{1,0:T(8,128)(2,1)S(1)} %get-tuple-element.69), channel_id=1, source_target_pairs={{0,16},{8,24},{16,0},{24,8},{1,17},{9,25},{17,1},{25,9},{2,18},{10... | collective-permute-start | bytes 442376 | tf_op jit(solution)/shard_map/ppermute | solution.py:17
  12.2 9.3 %collective-permute-start.2 = (bf16[192,384]{1,0:T(8,128)(2,1)S(1)}, bf16[192,384]{1,0:T(8,128)(2,1)S(1)}, u32[]{:S(2)}, u32[]{:S(2)}) collective-permute-start(bf16[192,384]{1,0:T(8,128)(2,1)S(1)} %get-tuple-element.67), channel_id=1, source_target_pairs={{0,8},{8,16},{16,24},{24,0},{1,9},{9,17},{17,25},{25,1},{2,10},{10... | collective-permute-start | bytes 442376 | tf_op jit(solution)/shard_map/ppermute | solution.py:17
  21.5 34.6 %collective-permute-start.7 = (bf16[384,1152]{1,0:T(8,128)(2,1)S(1)}, bf16[384,1152]{1,0:T(8,128)(2,1)S(1)}, u32[]{:S(2)}, u32[]{:S(2)}) collective-permute-start(bf16[384,1152]{1,0:T(8,128)(2,1)S(1)} %get-tuple-element.31), channel_id=1, source_target_pairs={{0,8},{8,16},{16,24},{24,0},{1,9},{9,17},{17,25},{25,1},{2,10},{10... | collective-permute-start | bytes 2654216 | tf_op jit(solution)/shard_map/ppermute | solution.py:17
  21.5 31.4 %collective-permute-start.6 = (bf16[384,1152]{1,0:T(8,128)(2,1)}, bf16[384,1152]{1,0:T(8,128)(2,1)}, u32[]{:S(2)}, u32[]{:S(2)}) collective-permute-start(bf16[384,1152]{1,0:T(8,128)(2,1)} %get-tuple-element.30), channel_id=1, source_target_pairs={{0,24},{8,0},{16,8},{24,16},{1,25},{9,1},{17,9},{25,17},{2,26},{10... | collective-permute-start | bytes 2654216 | tf_op jit(solution)/shard_map/ppermute | solution.py:17
  25.4 49.5 %collective-permute-start.3 = (bf16[384,768]{1,0:T(8,128)(2,1)S(1)}, bf16[384,768]{1,0:T(8,128)(2,1)S(1)}, u32[]{:S(2)}, u32[]{:S(2)}) collective-permute-start(bf16[384,768]{1,0:T(8,128)(2,1)S(1)} %bitcast.65), channel_id=1, source_target_pairs={{0,96},{32,0},{64,32},{96,64},{1,97},{33,1},{65,33},{97,65},{2,98}... | collective-permute-start | bytes 1769480 | tf_op jit(solution)/shard_map/ppermute | solution.py:17
  28.2 46.7 %collective-permute-start.4 = (bf16[384,768]{1,0:T(8,128)(2,1)S(1)}, bf16[384,768]{1,0:T(8,128)(2,1)S(1)}, u32[]{:S(2)}, u32[]{:S(2)}) collective-permute-start(bf16[384,768]{1,0:T(8,128)(2,1)S(1)} %bitcast.66), channel_id=1, source_target_pairs={{0,64},{32,96},{64,0},{96,32},{1,65},{33,97},{65,1},{97,33},{2,66}... | collective-permute-start | bytes 1769480 | tf_op jit(solution)/shard_map/ppermute | solution.py:17
  29.0 46.7 %collective-permute-start.5 = (bf16[384,768]{1,0:T(8,128)(2,1)S(1)}, bf16[384,768]{1,0:T(8,128)(2,1)}, u32[]{:S(2)}, u32[]{:S(2)}) collective-permute-start(bf16[384,768]{1,0:T(8,128)(2,1)S(1)} %bitcast.67), channel_id=1, source_target_pairs={{0,32},{32,64},{64,96},{96,0},{1,33},{33,65},{65,97},{97,1},{2,34}... | collective-permute-start | bytes 1769480 | tf_op jit(solution)/shard_map/ppermute | solution.py:17
  54.0 15.6 %collective-permute-start.9 = (bf16[384,384]{1,0:T(8,128)(2,1)S(1)}, bf16[384,384]{1,0:T(8,128)(2,1)S(1)}, u32[]{:S(2)}, u32[]{:S(2)}) collective-permute-start(bf16[384,384]{1,0:T(8,128)(2,1)S(1)} %slice.82), channel_id=1, source_target_pairs={{0,24},{8,0},{16,8},{24,16},{1,25},{9,1},{17,9},{25,17},{2,26},{10... | collective-permute-start | bytes 884744 | tf_op jit(solution)/shard_map/ppermute | solution.py:17
  56.2 16.9 %collective-permute-start.8 = (bf16[384,384]{1,0:T(8,128)(2,1)S(1)}, bf16[384,384]{1,0:T(8,128)(2,1)S(1)}, u32[]{:S(2)}, u32[]{:S(2)}) collective-permute-start(bf16[384,384]{1,0:T(8,128)(2,1)S(1)} %slice.81), channel_id=1, source_target_pairs={{0,8},{8,16},{16,24},{24,0},{1,9},{9,17},{17,25},{25,1},{2,10},{10... | collective-permute-start | bytes 884744 | tf_op jit(solution)/shard_map/ppermute | solution.py:17
  74.9 0.8 copy-start
  121.6 13.0 %collective-permute-start.10 = (bf16[192,768]{1,0:T(8,128)(2,1)S(1)}, bf16[192,768]{1,0:T(8,128)(2,1)S(1)}, u32[]{:S(2)}, u32[]{:S(2)}) collective-permute-start(bf16[192,768]{1,0:T(8,128)(2,1)S(1)} %get-tuple-element.65), channel_id=1, source_target_pairs={{0,32},{32,64},{64,96},{96,0},{1,33},{33,65},{65,97},{97,1},{2,34}... | collective-permute-start | bytes 884744 | tf_op jit(solution)/shard_map/ppermute | solution.py:17
  123.1 11.8 %collective-permute-start.14 = (bf16[192,768]{1,0:T(8,128)(2,1)S(1)}, bf16[192,768]{1,0:T(8,128)(2,1)S(1)}, u32[]{:S(2)}, u32[]{:S(2)}) collective-permute-start(bf16[192,768]{1,0:T(8,128)(2,1)S(1)} %get-tuple-element.66), channel_id=1, source_target_pairs={{0,96},{32,0},{64,32},{96,64},{1,97},{33,1},{65,33},{97,65},{2,98}... | collective-permute-start | bytes 884744 | tf_op jit(solution)/shard_map/ppermute | solution.py:17
  132.5 10.1 %collective-permute-start.12 = (bf16[192,768]{1,0:T(8,128)(2,1)S(1)}, bf16[192,768]{1,0:T(8,128)(2,1)S(1)}, u32[]{:S(2)}, u32[]{:S(2)}) collective-permute-start(bf16[192,768]{1,0:T(8,128)(2,1)S(1)} %get-tuple-element.35), channel_id=1, source_target_pairs={{0,96},{32,0},{64,32},{96,64},{1,97},{33,1},{65,33},{97,65},{2,98}... | collective-permute-start | bytes 884744 | tf_op jit(solution)/shard_map/ppermute | solution.py:17
  134.0 11.2 %collective-permute-start.13 = (bf16[192,768]{1,0:T(8,128)(2,1)S(1)}, bf16[192,768]{1,0:T(8,128)(2,1)S(1)}, u32[]{:S(2)}, u32[]{:S(2)}) collective-permute-start(bf16[192,768]{1,0:T(8,128)(2,1)S(1)} %get-tuple-element.36), channel_id=1, source_target_pairs={{0,32},{32,64},{64,96},{96,0},{1,33},{33,65},{65,97},{97,1},{2,34}... | collective-permute-start | bytes 884744 | tf_op jit(solution)/shard_map/ppermute | solution.py:17
  134.6 15.3 %collective-permute-start.11 = (bf16[192,768]{1,0:T(8,128)(2,1)S(1)}, bf16[192,768]{1,0:T(8,128)(2,1)S(1)}, u32[]{:S(2)}, u32[]{:S(2)}) collective-permute-start(bf16[192,768]{1,0:T(8,128)(2,1)S(1)} %add_convert_fusion.3), channel_id=1, source_target_pairs={{0,32},{32,64},{64,96},{96,0},{1,33},{33,65},{65,97},{97,1},{2,34}... | collective-permute-start | bytes 884744 | tf_op jit(solution)/shard_map/ppermute | solution.py:17
  135.0 14.9 %collective-permute-start.15 = (bf16[192,768]{1,0:T(8,128)(2,1)S(1)}, bf16[192,768]{1,0:T(8,128)(2,1)S(1)}, u32[]{:S(2)}, u32[]{:S(2)}) collective-permute-start(bf16[192,768]{1,0:T(8,128)(2,1)S(1)} %add_convert_fusion.2), channel_id=1, source_target_pairs={{0,96},{32,0},{64,32},{96,64},{1,97},{33,1},{65,33},{97,65},{2,98}... | collective-permute-start | bytes 884744 | tf_op jit(solution)/shard_map/ppermute | solution.py:17
  150.1 13.8 %collective-permute-start.17 = (bf16[384,768]{1,0:T(8,128)(2,1)S(1)}, bf16[384,768]{1,0:T(8,128)(2,1)S(1)}, u32[]{:S(2)}, u32[]{:S(2)}) collective-permute-start(bf16[384,768]{1,0:T(8,128)(2,1)S(1)} %fusion.1.refs_3_), channel_id=1, source_target_pairs={{0,96},{32,0},{64,32},{96,64},{1,97},{33,1},{65,33},{97,65},{2,98}... | collective-permute-start | bytes 1769480 | tf_op jit(solution)/shard_map/ppermute | solution.py:17
  150.5 15.8 %collective-permute-start.18 = (bf16[384,768]{1,0:T(8,128)(2,1)S(1)}, bf16[384,768]{1,0:T(8,128)(2,1)S(1)}, u32[]{:S(2)}, u32[]{:S(2)}) collective-permute-start(bf16[384,768]{1,0:T(8,128)(2,1)S(1)} %fusion.1.refs_3_), channel_id=1, source_target_pairs={{0,32},{32,64},{64,96},{96,0},{1,33},{33,65},{65,97},{97,1},{2,34}... | collective-permute-start | bytes 1769480 | tf_op jit(solution)/shard_map/ppermute | solution.py:17
  153.7 1.3 collective-permute-start.16
  156.1 21.3 %all-to-all-start = ((f32[64,1,128]{2,1,0:T(1,128)}), f32[64,1,128]{2,1,0:T(1,128)S(1)}, u32[]{:S(2)}, u32[]{:S(2)}) async-start(f32[64,1,128]{2,1,0:T(1,128)} %bitcast.23), calls=%async_computation | async-start | bytes 65536 | tf_op jit(solution)/shard_map/all_to_all | solution.py:287
  163.9 14.8 %collective-permute-start.20 = (bf16[192,768]{1,0:T(8,128)(2,1)S(1)}, bf16[192,768]{1,0:T(8,128)(2,1)S(1)}, u32[]{:S(2)}, u32[]{:S(2)}) collective-permute-start(bf16[192,768]{1,0:T(8,128)(2,1)S(1)} %slice.87), channel_id=1, source_target_pairs={{0,96},{32,0},{64,32},{96,64},{1,97},{33,1},{65,33},{97,65},{2,98}... | collective-permute-start | bytes 884744 | tf_op jit(solution)/shard_map/ppermute | solution.py:17
  166.3 12.4 %collective-permute-start.19 = (bf16[192,768]{1,0:T(8,128)(2,1)S(1)}, bf16[192,768]{1,0:T(8,128)(2,1)S(1)}, u32[]{:S(2)}, u32[]{:S(2)}) collective-permute-start(bf16[192,768]{1,0:T(8,128)(2,1)S(1)} %slice.86), channel_id=1, source_target_pairs={{0,32},{32,64},{64,96},{96,0},{1,33},{33,65},{65,97},{97,1},{2,34}... | collective-permute-start | bytes 884744 | tf_op jit(solution)/shard_map/ppermute | solution.py:17
  190.4 13.0 %collective-permute-start.21 = (bf16[192,768]{1,0:T(8,128)(2,1)S(1)}, bf16[192,768]{1,0:T(8,128)(2,1)S(1)}, u32[]{:S(2)}, u32[]{:S(2)}) collective-permute-start(bf16[192,768]{1,0:T(8,128)(2,1)S(1)} %get-tuple-element.63), channel_id=1, source_target_pairs={{0,32},{32,64},{64,96},{96,0},{1,33},{33,65},{65,97},{97,1},{2,34}... | collective-permute-start | bytes 884744 | tf_op jit(solution)/shard_map/ppermute | solution.py:17
  191.1 12.5 %collective-permute-start.25 = (bf16[192,768]{1,0:T(8,128)(2,1)S(1)}, bf16[192,768]{1,0:T(8,128)(2,1)S(1)}, u32[]{:S(2)}, u32[]{:S(2)}) collective-permute-start(bf16[192,768]{1,0:T(8,128)(2,1)S(1)} %get-tuple-element.64), channel_id=1, source_target_pairs={{0,96},{32,0},{64,32},{96,64},{1,97},{33,1},{65,33},{97,65},{2,98}... | collective-permute-start | bytes 884744 | tf_op jit(solution)/shard_map/ppermute | solution.py:17
  201.3 10.0 %collective-permute-start.23 = (bf16[192,768]{1,0:T(8,128)(2,1)S(1)}, bf16[192,768]{1,0:T(8,128)(2,1)S(1)}, u32[]{:S(2)}, u32[]{:S(2)}) collective-permute-start(bf16[192,768]{1,0:T(8,128)(2,1)S(1)} %get-tuple-element.44), channel_id=1, source_target_pairs={{0,96},{32,0},{64,32},{96,64},{1,97},{33,1},{65,33},{97,65},{2,98}... | collective-permute-start | bytes 884744 | tf_op jit(solution)/shard_map/ppermute | solution.py:17
  203.3 11.2 %collective-permute-start.24 = (bf16[192,768]{1,0:T(8,128)(2,1)S(1)}, bf16[192,768]{1,0:T(8,128)(2,1)S(1)}, u32[]{:S(2)}, u32[]{:S(2)}) collective-permute-start(bf16[192,768]{1,0:T(8,128)(2,1)S(1)} %get-tuple-element.45), channel_id=1, source_target_pairs={{0,32},{32,64},{64,96},{96,0},{1,33},{33,65},{65,97},{97,1},{2,34}... | collective-permute-start | bytes 884744 | tf_op jit(solution)/shard_map/ppermute | solution.py:17
  203.5 14.5 %collective-permute-start.22 = (bf16[192,768]{1,0:T(8,128)(2,1)S(1)}, bf16[192,768]{1,0:T(8,128)(2,1)S(1)}, u32[]{:S(2)}, u32[]{:S(2)}) collective-permute-start(bf16[192,768]{1,0:T(8,128)(2,1)S(1)} %add_convert_fusion.1), channel_id=1, source_target_pairs={{0,32},{32,64},{64,96},{96,0},{1,33},{33,65},{65,97},{97,1},{2,34}... | collective-permute-start | bytes 884744 | tf_op jit(solution)/shard_map/ppermute | solution.py:17
  203.6 14.4 %collective-permute-start.26 = (bf16[192,768]{1,0:T(8,128)(2,1)S(1)}, bf16[192,768]{1,0:T(8,128)(2,1)S(1)}, u32[]{:S(2)}, u32[]{:S(2)}) collective-permute-start(bf16[192,768]{1,0:T(8,128)(2,1)S(1)} %add_convert_fusion), channel_id=1, source_target_pairs={{0,96},{32,0},{64,32},{96,64},{1,97},{33,1},{65,33},{97,65},{2,98}... | collective-permute-start | bytes 884744 | tf_op jit(solution)/shard_map/ppermute | solution.py:17
  219.8 1.5 collective-permute-start.27
  222.9 19.1 %collective-permute-start.28 = (bf16[192,384]{1,0:T(8,128)(2,1)S(1)}, bf16[192,384]{1,0:T(8,128)(2,1)S(1)}, u32[]{:S(2)}, u32[]{:S(2)}) collective-permute-start(bf16[192,384]{1,0:T(8,128)(2,1)S(1)} %get-tuple-element.62), channel_id=1, source_target_pairs={{0,24},{8,0},{16,8},{24,16},{1,25},{9,1},{17,9},{25,17},{2,26},{10... | collective-permute-start | bytes 442376 | tf_op jit(solution)/shard_map/ppermute | solution.py:17
  225.7 15.0 %all-to-all-start.1 = ((f32[64,1,128]{2,1,0:T(1,128)}), f32[64,1,128]{2,1,0:T(1,128)S(1)}, u32[]{:S(2)}, u32[]{:S(2)}) async-start(f32[64,1,128]{2,1,0:T(1,128)} %bitcast.38), calls=%async_computation.1 | async-start | bytes 65536 | tf_op jit(solution)/shard_map/all_to_all | solution.py:287
  231.3 10.8 %collective-permute-start.29 = (bf16[192,384]{1,0:T(8,128)(2,1)S(1)}, bf16[192,384]{1,0:T(8,128)(2,1)S(1)}, u32[]{:S(2)}, u32[]{:S(2)}) collective-permute-start(bf16[192,384]{1,0:T(8,128)(2,1)S(1)} %get-tuple-element.61), channel_id=1, source_target_pairs={{0,16},{8,24},{16,0},{24,8},{1,17},{9,25},{17,1},{25,9},{2,18},{10... | collective-permute-start | bytes 442376 | tf_op jit(solution)/shard_map/ppermute | solution.py:17
  234.4 7.7 %collective-permute-start.30 = (bf16[192,384]{1,0:T(8,128)(2,1)S(1)}, bf16[192,384]{1,0:T(8,128)(2,1)S(1)}, u32[]{:S(2)}, u32[]{:S(2)}) collective-permute-start(bf16[192,384]{1,0:T(8,128)(2,1)S(1)} %get-tuple-element.59), channel_id=1, source_target_pairs={{0,8},{8,16},{16,24},{24,0},{1,9},{9,17},{17,25},{25,1},{2,10},{10... | collective-permute-start | bytes 442376 | tf_op jit(solution)/shard_map/ppermute | solution.py:17
Sparse Core Ops, SparseCore 0:
  9.6 92.9 all-gather.1

commit v11 on v10

--- a/solution.py
+++ b/solution.py
@@ -269,8 +269,9 @@
 def ring_swap_halves(to_next, to_prev, kept, axis):
     size = kept.shape[1]
     prev, after = shift(to_next, axis, 1), shift(to_prev, axis, -1)
-    high, low = shift(prev[:, size:], axis, 1), shift(after[:, size:], axis, -1)
-    return [kept, after[:, :size], jnp.concatenate([high, low], axis=1), prev[:, :size]]
+    sent_on = prev[:, size:], after[:, size:]
+    high, low = shift(sent_on[0], axis, 1), shift(sent_on[1], axis, -1)
+    return [kept, after[:, :size], jnp.concatenate([high, low], axis=1), prev[:, :size]], sent_on
 
 
 def in_order(pieces, me):
@@ -300,9 +301,9 @@
         return lambda k: lax.dynamic_slice_in_dim(array, lax.rem(iy + k, N) * cols, cols, axis=1)
 
     to_next, to_prev, kept = cut(target, iy)
-    w_pieces = ring_swap(columns(weight), "y")
-    to_next, to_prev = lax.optimization_barrier((to_next, to_prev, *w_pieces))[:2]
-    t = jnp.stack(ring_swap_halves(to_next, to_prev, kept, "y"))
+    t_pieces, sent_on = ring_swap_halves(to_next, to_prev, kept, "y")
+    t = jnp.stack(t_pieces)
+    w_pieces = ring_swap(columns(behind(weight, *sent_on)), "y")
     tiles = [lax.rem(k + N - iy, N) for k in range(N)]
     w = ring_gather(in_order(w_pieces, iy).reshape(-1, cols).T, "x")
 

time: 251 us -> 252 us (level)
    all_gather x1, waiting for transfers between devices: 26.9 us -> 8.26 us  [per_device(): lax.all_gather(tokens, ('y', 'z', 'c'), axis=0, tiled=True)]
    ppermute x29, waiting for transfers between devices: 57.1 us -> 74.6 us  [shift(): return lax.ppermute(value, axis, [(i, (i + step) % N) for i in range(N)])]
  transfers between devices with their start and end apart: 34 -> 34, of which waited for: 15 -> 15; matrix products, arithmetic and copies ran while one was open for 4% -> 5% of each run, Pallas kernels for 15% -> 15%
where the time goes in v11:
time: 252 us
  waiting for transfers between devices  91.5 us (36%)
  Pallas kernels  68.9 us (27%)
  starting transfers between devices  58.6 us (23%)
  between operations  15.2 us (6%)
  other arithmetic  10.5 us (4%)
  local copies, waits for them, and re-layouts  7.28 us (3%)
    ppermute x29, waiting for transfers between devices, shift(): return lax.ppermute(value, axis, [(i, (i + step) % N) for i in range(N)])  74.6 us
    ppermute x29, starting transfers between devices, shift(): return lax.ppermute(value, axis, [(i, (i + step) % N) for i in range(N)])  44.9 us
    pallas_call x4, Pallas kernels, terms(): pl.pallas_call(kernel, grid_spec=pltpu.PrefetchScalarGridSpec(num_scalar_...  23.8 us
    pallas_call x1, Pallas kernels, first_slopes(): pl.pallas_call(kernel, grid_spec=pltpu.PrefetchScalarGridSpec(num_scalar_...  19 us
    all_to_all x2, starting transfers between devices, spread(): lax.all_to_all(part, ('x', 'y', 'z'), split_axis=0, concat_axis=0, tiled=...  13.3 us
    pallas_call x1, Pallas kernels, second_slopes(): pl.pallas_call(kernel, grid_spec=pltpu.PrefetchScalarGridSpec(num_scalar_...  11.6 us
    pallas_call x1, Pallas kernels, moved(): pl.pallas_call(kernel, grid_spec=pltpu.PrefetchScalarGridSpec(num_scalar_...  11 us
    all_gather x1, waiting for transfers between devices, per_device(): lax.all_gather(tokens, ('y', 'z', 'c'), axis=0, tiled=True)  8.26 us
  transfers between devices with their start and end apart: 34, of which 15 were waited for; matrix products, arithmetic and copies ran while one was open for 5% of the time, Pallas kernels for 15%

profile of v11, /device:TPU:0, one launch (start us, length us, event | category | flops | bytes accessed | tf_op | source)
XLA Modules:
  0.0 252.0 jit_solution(7071037947265764335)
XLA Ops:
  7.3 3.6 %shard_map.37 = (bf16[384,1152]{1,0:T(8,128)(2,1)S(1)}, bf16[384,1152]{1,0:T(8,128)(2,1)}, bf16[384,768]{1,0:T(8,128)(2,1)S(1)}) custom-call(s32[4]{0:T(128)S(1)} %pad_add_fusion.which_ref, bf16[768,1536]{1,0:T(8,128)(2,1)} %before.1, bf16[768,1536]{1,0:T(8,128)(2,1)} %before.1, bf16[768,1536]{1,0:T(8,128)(2,1)} %before.1, bf16[768,1536]{1,0:T(8,128)(2,1)} %before.1), custom_call_target="tpu_custom_call" | custom-call | tf_op jit(solution)/shard_map/pallas_call | solution.py:255
  10.9 3.1 %collective-permute-start.1 = (bf16[384,1152]{1,0:T(8,128)(2,1)}, bf16[384,1152]{1,0:T(8,128)(2,1)S(1)}, u32[]{:S(2)}, u32[]{:S(2)}) collective-permute-start(bf16[384,1152]{1,0:T(8,128)(2,1)} %get-tuple-element.27), channel_id=1, source_target_pairs={{0,24},{8,0},{16,8},{24,16},{1,25},{9,1},{17,9},{25,17},{2,26},{10... | collective-permute-start | bytes 2654216 | tf_op jit(solution)/shard_map/ppermute | solution.py:17
  14.2 28.5 %collective-permute-done.1 = bf16[384,1152]{1,0:T(8,128)(2,1)S(1)} collective-permute-done((bf16[384,1152]{1,0:T(8,128)(2,1)}, bf16[384,1152]{1,0:T(8,128)(2,1)S(1)}, u32[]{:S(2)}, u32[]{:S(2)}) %collective-permute-start.1) | collective-permute-done | bytes 884768 | tf_op jit(solution)/shard_map/ppermute | solution.py:17
  43.5 3.6 %collective-permute-start.9 = (bf16[384,384]{1,0:T(8,128)(2,1)}, bf16[384,384]{1,0:T(8,128)(2,1)}, u32[]{:S(2)}, u32[]{:S(2)}) collective-permute-start(bf16[384,384]{1,0:T(8,128)(2,1)} %slice.81), channel_id=1, source_target_pairs={{0,24},{8,0},{16,8},{24,16},{1,25},{9,1},{17,9},{25,17},{2,26},{10... | collective-permute-start | bytes 884744 | tf_op jit(solution)/shard_map/ppermute | solution.py:17
  47.1 1.7 slice.80
  48.8 3.3 %collective-permute-start.2 = (bf16[192,384]{1,0:T(8,128)(2,1)S(1)}, bf16[192,384]{1,0:T(8,128)(2,1)S(1)}, u32[]{:S(2)}, u32[]{:S(2)}) collective-permute-start(bf16[192,384]{1,0:T(8,128)(2,1)S(1)} %get-tuple-element.65), channel_id=1, source_target_pairs={{0,24},{8,0},{16,8},{24,16},{1,25},{9,1},{17,9},{25,17},{2,26},{10... | collective-permute-start | bytes 442376 | tf_op jit(solution)/shard_map/ppermute | solution.py:17
  52.1 0.9 collective-permute-start.4
  53.1 1.3 slice_bitcast_fusion
  54.4 9.5 %collective-permute-done.2 = bf16[192,384]{1,0:T(8,128)(2,1)S(1)} collective-permute-done((bf16[192,384]{1,0:T(8,128)(2,1)S(1)}, bf16[192,384]{1,0:T(8,128)(2,1)S(1)}, u32[]{:S(2)}, u32[]{:S(2)}) %collective-permute-start.2) | collective-permute-done | bytes 147488 | tf_op jit(solution)/shard_map/ppermute | solution.py:17
  63.9 2.0 collective-permute-done.3
  65.9 6.1 %collective-permute-done.4 = bf16[192,384]{1,0:T(8,128)(2,1)S(1)} collective-permute-done((bf16[192,384]{1,0:T(8,128)(2,1)S(1)}, bf16[192,384]{1,0:T(8,128)(2,1)S(1)}, u32[]{:S(2)}, u32[]{:S(2)}) %collective-permute-start.4) | collective-permute-done | bytes 147488 | tf_op jit(solution)/shard_map/ppermute | solution.py:17
  72.5 2.8 %collective-permute-start.5 = (bf16[384,768]{1,0:T(8,128)(2,1)S(1)}, bf16[384,768]{1,0:T(8,128)(2,1)S(1)}, u32[]{:S(2)}, u32[]{:S(2)}) collective-permute-start(bf16[384,768]{1,0:T(8,128)(2,1)S(1)} %bitcast.65), channel_id=1, source_target_pairs={{0,96},{32,0},{64,32},{96,64},{1,97},{33,1},{65,33},{97,65},{2,98}... | collective-permute-start | bytes 1769480 | tf_op jit(solution)/shard_map/ppermute | solution.py:17
  77.0 1.2 maximum_bitcast_fusion
  78.2 1.7 pad_maximum_fusion.refs_4_.t_ref
  80.0 11.6 %collective-permute-done.5.refs_1_ = bf16[384,768]{1,0:T(8,128)(2,1)S(1)} collective-permute-done((bf16[384,768]{1,0:T(8,128)(2,1)S(1)}, bf16[384,768]{1,0:T(8,128)(2,1)S(1)}, u32[]{:S(2)}, u32[]{:S(2)}) %collective-permute-start.5) | collective-permute-done | bytes 589856 | tf_op jit(solution)/shard_map/ppermute | solution.py:17
  92.4 2.9 %collective-permute-done.7.refs_3_ = bf16[384,768]{1,0:T(8,128)(2,1)} collective-permute-done((bf16[384,768]{1,0:T(8,128)(2,1)S(1)}, bf16[384,768]{1,0:T(8,128)(2,1)}, u32[]{:S(2)}, u32[]{:S(2)}) %collective-permute-start.7) | collective-permute-done | bytes 589856 | tf_op jit(solution)/shard_map/ppermute | solution.py:17
  95.3 8.3 %all-gather.2.cloned.1.call-done = bf16[24576,384]{1,0:T(8,128)(2,1)} async-done(((bf16[768,384]{1,0:T(8,128)(2,1)}), bf16[24576,384]{1,0:T(8,128)(2,1)}) %all-gather.2.cloned.1.call-update) | async-done | bytes 18874384 | tf_op jit(solution)/shard_map/all_gather | solution.py:298
  103.6 19.0 %shard_map.38 = (f32[384,3072]{1,0:T(8,128)}, bf16[384,3072]{1,0:T(8,128)(2,1)}, bf16[384,768]{1,0:T(8,128)(2,1)S(1)}) custom-call(s32[8]{0:T(128)S(1)} %stack.126.which_ref, bf16[4,8,768,384]{3,2,1,0:T(8,128)(2,1)} %bitcast.69, bf16[384,768]{1,0:T(8,128)(2,1)S(1)} %bitcast.68, bf16[384,768]{1,0:T(8,128)(2,1)S(1)} %collective-permute-done.5.refs_1_, ...), custom_call_target="tpu_custom_call" | custom-call | flops 9059696640 | bytes 31260672 | tf_op jit(solution)/shard_map/pallas_call | solution.py:82
  122.6 1.3 collective-permute-start.10
  123.9 2.0 collective-permute-start.14
  125.9 7.5 %shard_map.40 = (f32[192,768]{1,0:T(8,128)S(1)}, bf16[192,768]{1,0:T(8,128)(2,1)S(1)}, bf16[192,768]{1,0:T(8,128)(2,1)S(1)}, f32[192,768]{1,0:T(8,128)S(1)}) custom-call(s32[2]{0:T(128)S(1)} %pad_add_fusion.1.which_ref, bf16[4,8,768,384]{3,2,1,0:T(8,128)(2,1)} %bitcast.70, bf16[4,8,768,384]{3,2,1,0:T(8,128)(2,1)} %bitcast.71, ...), custom_call_target="tpu_custom_call" | custom-call | flops 3623878656 | bytes 11796480 | tf_op jit(solution)/shard_map/pallas_call | solution.py:198
  133.5 1.4 collective-permute-start.12
  135.8 3.4 %collective-permute-start.15 = (bf16[192,768]{1,0:T(8,128)(2,1)S(1)}, bf16[192,768]{1,0:T(8,128)(2,1)S(1)}, u32[]{:S(2)}, u32[]{:S(2)}) collective-permute-start(bf16[192,768]{1,0:T(8,128)(2,1)S(1)} %add_convert_fusion.2), channel_id=1, source_target_pairs={{0,96},{32,0},{64,32},{96,64},{1,97},{33,1},{65,33},{97,65},{2,98}... | collective-permute-start | bytes 884744 | tf_op jit(solution)/shard_map/ppermute | solution.py:17
  139.2 4.3 %shard_map.39 = f32[384,768]{1,0:T(8,128)S(1)} custom-call(s32[1]{0:T(128)} %bitcast.which_ref, bf16[4,8,768,384]{3,2,1,0:T(8,128)(2,1)} %bitcast.72, bf16[384,3072]{1,0:T(8,128)(2,1)} %get-tuple-element.30.refs_1_.refs_2_), custom_call_target="tpu_custom_call" | custom-call | flops 1811939328 | bytes 8257536 | tf_op jit(solution)/shard_map/pallas_call | solution.py:198
  143.6 2.5 collective-permute-done.13
  146.1 4.7 %collective-permute-done.11 = bf16[192,768]{1,0:T(8,128)(2,1)S(1)} collective-permute-done((bf16[192,768]{1,0:T(8,128)(2,1)S(1)}, bf16[192,768]{1,0:T(8,128)(2,1)S(1)}, u32[]{:S(2)}, u32[]{:S(2)}) %collective-permute-start.11) | collective-permute-done | bytes 294944 | tf_op jit(solution)/shard_map/ppermute | solution.py:17
  151.3 1.8 collective-permute-start.18
  154.8 1.0 collective-permute-done.16
  155.8 1.2 broadcast_add_fusion.1
  157.0 7.8 %all-to-all-start = ((f32[64,1,128]{2,1,0:T(1,128)}), f32[64,1,128]{2,1,0:T(1,128)S(1)}, u32[]{:S(2)}, u32[]{:S(2)}) async-start(f32[64,1,128]{2,1,0:T(1,128)} %bitcast.23), calls=%async_computation | async-start | bytes 65536 | tf_op jit(solution)/shard_map/all_to_all | solution.py:288
  164.8 3.1 %collective-permute-start.20 = (bf16[192,768]{1,0:T(8,128)(2,1)S(1)}, bf16[192,768]{1,0:T(8,128)(2,1)S(1)}, u32[]{:S(2)}, u32[]{:S(2)}) collective-permute-start(bf16[192,768]{1,0:T(8,128)(2,1)S(1)} %slice.87), channel_id=1, source_target_pairs={{0,96},{32,0},{64,32},{96,64},{1,97},{33,1},{65,33},{97,65},{2,98}... | collective-permute-start | bytes 884744 | tf_op jit(solution)/shard_map/ppermute | solution.py:17
  168.0 11.0 %shard_map.41.part_ref = f32[384,3072]{1,0:T(8,128)} custom-call(s32[3]{0:T(128)S(1)} %pad_add_fusion.2.which_ref, bf16[4,8,768,384]{3,2,1,0:T(8,128)(2,1)} %bitcast.73, bf16[4,8,768,384]{3,2,1,0:T(8,128)(2,1)} %bitcast.74, bf16[4,8,768,384]{3,2,1,0:T(8,128)(2,1)} %bitcast.75, bf16[384,768]{1,0:T(8,128)(2,1)S(1)} %fusion.1.refs_3_, ...), custom_call_target="tpu_custom_call" | custom-call | flops 5435817984 | bytes 20643840 | tf_op jit(solution)/shard_map/pallas_call | solution.py:117
  180.4 11.6 %shard_map.42 = (bf16[384,3072]{1,0:T(8,128)(2,1)}, bf16[384,768]{1,0:T(8,128)(2,1)S(1)}) custom-call(s32[5]{0:T(128)S(1)} %stack.123.which_ref, f32[1,1]{1,0:T(1,128)} %bitcast.25.scale_ref, bf16[4,8,768,384]{3,2,1,0:T(8,128)(2,1)} %bitcast.76, bf16[384,768]{1,0:T(8,128)(2,1)S(1)} %pad_maximum_fusion.3.f_ref, f32[384,3072]{1,0:T(8,128)} %shard_map.41.part_ref, ...), custom_call_target="tpu_custom_call" | custom-call | flops 3623878656 | bytes 15335424 | tf_op jit(solution)/shard_map/pallas_call | solution.py:146
  192.7 2.7 %collective-permute-start.25 = (bf16[192,768]{1,0:T(8,128)(2,1)S(1)}, bf16[192,768]{1,0:T(8,128)(2,1)S(1)}, u32[]{:S(2)}, u32[]{:S(2)}) collective-permute-start(bf16[192,768]{1,0:T(8,128)(2,1)S(1)} %get-tuple-element.60), channel_id=1, source_target_pairs={{0,96},{32,0},{64,32},{96,64},{1,97},{33,1},{65,33},{97,65},{2,98}... | collective-permute-start | bytes 884744 | tf_op jit(solution)/shard_map/ppermute | solution.py:17
  195.4 7.6 %shard_map.44 = (f32[192,768]{1,0:T(8,128)S(1)}, bf16[192,768]{1,0:T(8,128)(2,1)S(1)}, bf16[192,768]{1,0:T(8,128)(2,1)S(1)}, f32[192,768]{1,0:T(8,128)S(1)}) custom-call(s32[2]{0:T(128)S(1)} %pad_add_fusion.1.which_ref, bf16[4,8,768,384]{3,2,1,0:T(8,128)(2,1)} %bitcast.77, bf16[4,8,768,384]{3,2,1,0:T(8,128)(2,1)} %bitcast.78, ...), custom_call_target="tpu_custom_call" | custom-call | flops 3623878656 | bytes 11796480 | tf_op jit(solution)/shard_map/pallas_call | solution.py:198
  202.9 2.0 collective-permute-start.23
  205.2 3.3 %collective-permute-start.26 = (bf16[192,768]{1,0:T(8,128)(2,1)S(1)}, bf16[192,768]{1,0:T(8,128)(2,1)S(1)}, u32[]{:S(2)}, u32[]{:S(2)}) collective-permute-start(bf16[192,768]{1,0:T(8,128)(2,1)S(1)} %add_convert_fusion), channel_id=1, source_target_pairs={{0,96},{32,0},{64,32},{96,64},{1,97},{33,1},{65,33},{97,65},{2,98}... | collective-permute-start | bytes 884744 | tf_op jit(solution)/shard_map/ppermute | solution.py:17
  208.5 4.3 %shard_map.43 = f32[384,768]{1,0:T(8,128)S(1)} custom-call(s32[1]{0:T(128)} %bitcast.which_ref, bf16[4,8,768,384]{3,2,1,0:T(8,128)(2,1)} %bitcast.79, bf16[384,3072]{1,0:T(8,128)(2,1)} %get-tuple-element.39.refs_1_.refs_2_), custom_call_target="tpu_custom_call" | custom-call | flops 1811939328 | bytes 8257536 | tf_op jit(solution)/shard_map/pallas_call | solution.py:198
  212.9 3.2 %collective-permute-done.24 = bf16[192,768]{1,0:T(8,128)(2,1)S(1)} collective-permute-done((bf16[192,768]{1,0:T(8,128)(2,1)S(1)}, bf16[192,768]{1,0:T(8,128)(2,1)S(1)}, u32[]{:S(2)}, u32[]{:S(2)}) %collective-permute-start.24) | collective-permute-done | bytes 294944 | tf_op jit(solution)/shard_map/ppermute | solution.py:17
  216.1 3.5 %collective-permute-done.22 = bf16[192,768]{1,0:T(8,128)(2,1)S(1)} collective-permute-done((bf16[192,768]{1,0:T(8,128)(2,1)S(1)}, bf16[192,768]{1,0:T(8,128)(2,1)S(1)}, u32[]{:S(2)}, u32[]{:S(2)}) %collective-permute-start.22) | collective-permute-done | bytes 294944 | tf_op jit(solution)/shard_map/ppermute | solution.py:17
  219.8 1.0 multiply_reduce_fusion
  221.8 1.1 collective-permute-done.27
  222.9 1.2 broadcast_add_fusion
  224.5 2.8 %collective-permute-start.28 = (bf16[192,384]{1,0:T(8,128)(2,1)S(1)}, bf16[192,384]{1,0:T(8,128)(2,1)S(1)}, u32[]{:S(2)}, u32[]{:S(2)}) collective-permute-start(bf16[192,384]{1,0:T(8,128)(2,1)S(1)} %get-tuple-element.58), channel_id=1, source_target_pairs={{0,24},{8,0},{16,8},{24,16},{1,25},{9,1},{17,9},{25,17},{2,26},{10... | collective-permute-start | bytes 442376 | tf_op jit(solution)/shard_map/ppermute | solution.py:17
  227.3 5.5 %all-to-all-start.1 = ((f32[64,1,128]{2,1,0:T(1,128)}), f32[64,1,128]{2,1,0:T(1,128)S(1)}, u32[]{:S(2)}, u32[]{:S(2)}) async-start(f32[64,1,128]{2,1,0:T(1,128)} %bitcast.38), calls=%async_computation.1 | async-start | bytes 65536 | tf_op jit(solution)/shard_map/all_to_all | solution.py:288
  232.9 3.2 %collective-permute-start.29 = (bf16[192,384]{1,0:T(8,128)(2,1)S(1)}, bf16[192,384]{1,0:T(8,128)(2,1)S(1)}, u32[]{:S(2)}, u32[]{:S(2)}) collective-permute-start(bf16[192,384]{1,0:T(8,128)(2,1)S(1)} %get-tuple-element.57), channel_id=1, source_target_pairs={{0,16},{8,24},{16,0},{24,8},{1,17},{9,25},{17,1},{25,9},{2,18},{10... | collective-permute-start | bytes 442376 | tf_op jit(solution)/shard_map/ppermute | solution.py:17
  236.6 5.8 %all-to-all-done.1 = f32[64,1,128]{2,1,0:T(1,128)S(1)} async-done(((f32[64,1,128]{2,1,0:T(1,128)}), f32[64,1,128]{2,1,0:T(1,128)S(1)}, u32[]{:S(2)}, u32[]{:S(2)}) %all-to-all-start.1) | async-done | bytes 32800 | tf_op jit(solution)/shard_map/all_to_all | solution.py:288
  244.0 1.1 convert_multiply_fusion
  (87 shorter events, 12.9 us)
Async XLA Ops:
  6.5 97.0 %all-gather.2.cloned.1.call-start = ((), (), s32[]{:S(2)}) async-start(), calls=%async_computation.2 | async-start | bytes 19464192 | tf_op jit(solution)/shard_map/all_gather | solution.py:298
  10.9 37.8 %copy-start = (bf16[192,1536]{1,0:T(8,128)(2,1)S(1)}, bf16[192,1536]{1,0:T(8,128)(2,1)}, u32[]{:S(2)}) copy-start(bf16[192,1536]{1,0:T(8,128)(2,1)} %param.5) | copy-start | bytes 1769476
  10.9 31.8 %collective-permute-start.1 = (bf16[384,1152]{1,0:T(8,128)(2,1)}, bf16[384,1152]{1,0:T(8,128)(2,1)S(1)}, u32[]{:S(2)}, u32[]{:S(2)}) collective-permute-start(bf16[384,1152]{1,0:T(8,128)(2,1)} %get-tuple-element.27), channel_id=1, source_target_pairs={{0,24},{8,0},{16,8},{24,16},{1,25},{9,1},{17,9},{25,17},{2,26},{10... | collective-permute-start | bytes 2654216 | tf_op jit(solution)/shard_map/ppermute | solution.py:17
  14.0 33.0 %collective-permute-start = (bf16[384,1152]{1,0:T(8,128)(2,1)S(1)}, bf16[384,1152]{1,0:T(8,128)(2,1)}, u32[]{:S(2)}, u32[]{:S(2)}) collective-permute-start(bf16[384,1152]{1,0:T(8,128)(2,1)S(1)} %get-tuple-element.26), channel_id=1, source_target_pairs={{0,8},{8,16},{16,24},{24,0},{1,9},{9,17},{17,25},{25,1},{2,10},{10... | collective-permute-start | bytes 2654216 | tf_op jit(solution)/shard_map/ppermute | solution.py:17
  43.5 33.5 %collective-permute-start.9 = (bf16[384,384]{1,0:T(8,128)(2,1)}, bf16[384,384]{1,0:T(8,128)(2,1)}, u32[]{:S(2)}, u32[]{:S(2)}) collective-permute-start(bf16[384,384]{1,0:T(8,128)(2,1)} %slice.81), channel_id=1, source_target_pairs={{0,24},{8,0},{16,8},{24,16},{1,25},{9,1},{17,9},{25,17},{2,26},{10... | collective-permute-start | bytes 884744 | tf_op jit(solution)/shard_map/ppermute | solution.py:17
  48.8 28.3 %collective-permute-start.8 = (bf16[384,384]{1,0:T(8,128)(2,1)}, bf16[384,384]{1,0:T(8,128)(2,1)}, u32[]{:S(2)}, u32[]{:S(2)}) collective-permute-start(bf16[384,384]{1,0:T(8,128)(2,1)} %slice.80), channel_id=1, source_target_pairs={{0,8},{8,16},{16,24},{24,0},{1,9},{9,17},{17,25},{25,1},{2,10},{10... | collective-permute-start | bytes 884744 | tf_op jit(solution)/shard_map/ppermute | solution.py:17
  48.8 15.0 %collective-permute-start.2 = (bf16[192,384]{1,0:T(8,128)(2,1)S(1)}, bf16[192,384]{1,0:T(8,128)(2,1)S(1)}, u32[]{:S(2)}, u32[]{:S(2)}) collective-permute-start(bf16[192,384]{1,0:T(8,128)(2,1)S(1)} %get-tuple-element.65), channel_id=1, source_target_pairs={{0,24},{8,0},{16,8},{24,16},{1,25},{9,1},{17,9},{25,17},{2,26},{10... | collective-permute-start | bytes 442376 | tf_op jit(solution)/shard_map/ppermute | solution.py:17
  52.1 13.8 %collective-permute-start.3 = (bf16[192,384]{1,0:T(8,128)(2,1)S(1)}, bf16[192,384]{1,0:T(8,128)(2,1)S(1)}, u32[]{:S(2)}, u32[]{:S(2)}) collective-permute-start(bf16[192,384]{1,0:T(8,128)(2,1)S(1)} %get-tuple-element.64), channel_id=1, source_target_pairs={{0,16},{8,24},{16,0},{24,8},{1,17},{9,25},{17,1},{25,9},{2,18},{10... | collective-permute-start | bytes 442376 | tf_op jit(solution)/shard_map/ppermute | solution.py:17
  52.1 19.9 %collective-permute-start.4 = (bf16[192,384]{1,0:T(8,128)(2,1)S(1)}, bf16[192,384]{1,0:T(8,128)(2,1)S(1)}, u32[]{:S(2)}, u32[]{:S(2)}) collective-permute-start(bf16[192,384]{1,0:T(8,128)(2,1)S(1)} %get-tuple-element.63), channel_id=1, source_target_pairs={{0,8},{8,16},{16,24},{24,0},{1,9},{9,17},{17,25},{25,1},{2,10},{10... | collective-permute-start | bytes 442376 | tf_op jit(solution)/shard_map/ppermute | solution.py:17
  72.5 19.1 %collective-permute-start.5 = (bf16[384,768]{1,0:T(8,128)(2,1)S(1)}, bf16[384,768]{1,0:T(8,128)(2,1)S(1)}, u32[]{:S(2)}, u32[]{:S(2)}) collective-permute-start(bf16[384,768]{1,0:T(8,128)(2,1)S(1)} %bitcast.65), channel_id=1, source_target_pairs={{0,96},{32,0},{64,32},{96,64},{1,97},{33,1},{65,33},{97,65},{2,98}... | collective-permute-start | bytes 1769480 | tf_op jit(solution)/shard_map/ppermute | solution.py:17
  75.3 16.3 %collective-permute-start.6 = (bf16[384,768]{1,0:T(8,128)(2,1)S(1)}, bf16[384,768]{1,0:T(8,128)(2,1)S(1)}, u32[]{:S(2)}, u32[]{:S(2)}) collective-permute-start(bf16[384,768]{1,0:T(8,128)(2,1)S(1)} %bitcast.66), channel_id=1, source_target_pairs={{0,64},{32,96},{64,0},{96,32},{1,65},{33,97},{65,1},{97,33},{2,66}... | collective-permute-start | bytes 1769480 | tf_op jit(solution)/shard_map/ppermute | solution.py:17
  76.1 19.3 %collective-permute-start.7 = (bf16[384,768]{1,0:T(8,128)(2,1)S(1)}, bf16[384,768]{1,0:T(8,128)(2,1)}, u32[]{:S(2)}, u32[]{:S(2)}) collective-permute-start(bf16[384,768]{1,0:T(8,128)(2,1)S(1)} %bitcast.67), channel_id=1, source_target_pairs={{0,32},{32,64},{64,96},{96,0},{1,33},{33,65},{65,97},{97,1},{2,34}... | collective-permute-start | bytes 1769480 | tf_op jit(solution)/shard_map/ppermute | solution.py:17
  91.6 0.8 copy-start.1
  122.6 13.0 %collective-permute-start.10 = (bf16[192,768]{1,0:T(8,128)(2,1)S(1)}, bf16[192,768]{1,0:T(8,128)(2,1)S(1)}, u32[]{:S(2)}, u32[]{:S(2)}) collective-permute-start(bf16[192,768]{1,0:T(8,128)(2,1)S(1)} %get-tuple-element.61), channel_id=1, source_target_pairs={{0,32},{32,64},{64,96},{96,0},{1,33},{33,65},{65,97},{97,1},{2,34}... | collective-permute-start | bytes 884744 | tf_op jit(solution)/shard_map/ppermute | solution.py:17
  123.9 11.8 %collective-permute-start.14 = (bf16[192,768]{1,0:T(8,128)(2,1)S(1)}, bf16[192,768]{1,0:T(8,128)(2,1)S(1)}, u32[]{:S(2)}, u32[]{:S(2)}) collective-permute-start(bf16[192,768]{1,0:T(8,128)(2,1)S(1)} %get-tuple-element.62), channel_id=1, source_target_pairs={{0,96},{32,0},{64,32},{96,64},{1,97},{33,1},{65,33},{97,65},{2,98}... | collective-permute-start | bytes 884744 | tf_op jit(solution)/shard_map/ppermute | solution.py:17
  133.5 10.1 %collective-permute-start.12 = (bf16[192,768]{1,0:T(8,128)(2,1)S(1)}, bf16[192,768]{1,0:T(8,128)(2,1)S(1)}, u32[]{:S(2)}, u32[]{:S(2)}) collective-permute-start(bf16[192,768]{1,0:T(8,128)(2,1)S(1)} %get-tuple-element.33), channel_id=1, source_target_pairs={{0,96},{32,0},{64,32},{96,64},{1,97},{33,1},{65,33},{97,65},{2,98}... | collective-permute-start | bytes 884744 | tf_op jit(solution)/shard_map/ppermute | solution.py:17
  134.9 11.2 %collective-permute-start.13 = (bf16[192,768]{1,0:T(8,128)(2,1)S(1)}, bf16[192,768]{1,0:T(8,128)(2,1)S(1)}, u32[]{:S(2)}, u32[]{:S(2)}) collective-permute-start(bf16[192,768]{1,0:T(8,128)(2,1)S(1)} %get-tuple-element.34), channel_id=1, source_target_pairs={{0,32},{32,64},{64,96},{96,0},{1,33},{33,65},{65,97},{97,1},{2,34}... | collective-permute-start | bytes 884744 | tf_op jit(solution)/shard_map/ppermute | solution.py:17
  135.6 15.1 %collective-permute-start.11 = (bf16[192,768]{1,0:T(8,128)(2,1)S(1)}, bf16[192,768]{1,0:T(8,128)(2,1)S(1)}, u32[]{:S(2)}, u32[]{:S(2)}) collective-permute-start(bf16[192,768]{1,0:T(8,128)(2,1)S(1)} %add_convert_fusion.3), channel_id=1, source_target_pairs={{0,32},{32,64},{64,96},{96,0},{1,33},{33,65},{65,97},{97,1},{2,34}... | collective-permute-start | bytes 884744 | tf_op jit(solution)/shard_map/ppermute | solution.py:17
  135.8 15.0 %collective-permute-start.15 = (bf16[192,768]{1,0:T(8,128)(2,1)S(1)}, bf16[192,768]{1,0:T(8,128)(2,1)S(1)}, u32[]{:S(2)}, u32[]{:S(2)}) collective-permute-start(bf16[192,768]{1,0:T(8,128)(2,1)S(1)} %add_convert_fusion.2), channel_id=1, source_target_pairs={{0,96},{32,0},{64,32},{96,64},{1,97},{33,1},{65,33},{97,65},{2,98}... | collective-permute-start | bytes 884744 | tf_op jit(solution)/shard_map/ppermute | solution.py:17
  151.0 13.8 %collective-permute-start.17 = (bf16[384,768]{1,0:T(8,128)(2,1)S(1)}, bf16[384,768]{1,0:T(8,128)(2,1)S(1)}, u32[]{:S(2)}, u32[]{:S(2)}) collective-permute-start(bf16[384,768]{1,0:T(8,128)(2,1)S(1)} %fusion.1.refs_3_), channel_id=1, source_target_pairs={{0,96},{32,0},{64,32},{96,64},{1,97},{33,1},{65,33},{97,65},{2,98}... | collective-permute-start | bytes 1769480 | tf_op jit(solution)/shard_map/ppermute | solution.py:17
  151.3 16.6 %collective-permute-start.18 = (bf16[384,768]{1,0:T(8,128)(2,1)S(1)}, bf16[384,768]{1,0:T(8,128)(2,1)S(1)}, u32[]{:S(2)}, u32[]{:S(2)}) collective-permute-start(bf16[384,768]{1,0:T(8,128)(2,1)S(1)} %fusion.1.refs_3_), channel_id=1, source_target_pairs={{0,32},{32,64},{64,96},{96,0},{1,33},{33,65},{65,97},{97,1},{2,34}... | collective-permute-start | bytes 1769480 | tf_op jit(solution)/shard_map/ppermute | solution.py:17
  154.6 1.3 collective-permute-start.16
  157.0 22.0 %all-to-all-start = ((f32[64,1,128]{2,1,0:T(1,128)}), f32[64,1,128]{2,1,0:T(1,128)S(1)}, u32[]{:S(2)}, u32[]{:S(2)}) async-start(f32[64,1,128]{2,1,0:T(1,128)} %bitcast.23), calls=%async_computation | async-start | bytes 65536 | tf_op jit(solution)/shard_map/all_to_all | solution.py:288
  164.8 15.4 %collective-permute-start.20 = (bf16[192,768]{1,0:T(8,128)(2,1)S(1)}, bf16[192,768]{1,0:T(8,128)(2,1)S(1)}, u32[]{:S(2)}, u32[]{:S(2)}) collective-permute-start(bf16[192,768]{1,0:T(8,128)(2,1)S(1)} %slice.87), channel_id=1, source_target_pairs={{0,96},{32,0},{64,32},{96,64},{1,97},{33,1},{65,33},{97,65},{2,98}... | collective-permute-start | bytes 884744 | tf_op jit(solution)/shard_map/ppermute | solution.py:17
  167.9 12.4 %collective-permute-start.19 = (bf16[192,768]{1,0:T(8,128)(2,1)S(1)}, bf16[192,768]{1,0:T(8,128)(2,1)S(1)}, u32[]{:S(2)}, u32[]{:S(2)}) collective-permute-start(bf16[192,768]{1,0:T(8,128)(2,1)S(1)} %slice.86), channel_id=1, source_target_pairs={{0,32},{32,64},{64,96},{96,0},{1,33},{33,65},{65,97},{97,1},{2,34}... | collective-permute-start | bytes 884744 | tf_op jit(solution)/shard_map/ppermute | solution.py:17
  192.0 13.0 %collective-permute-start.21 = (bf16[192,768]{1,0:T(8,128)(2,1)S(1)}, bf16[192,768]{1,0:T(8,128)(2,1)S(1)}, u32[]{:S(2)}, u32[]{:S(2)}) collective-permute-start(bf16[192,768]{1,0:T(8,128)(2,1)S(1)} %get-tuple-element.59), channel_id=1, source_target_pairs={{0,32},{32,64},{64,96},{96,0},{1,33},{33,65},{65,97},{97,1},{2,34}... | collective-permute-start | bytes 884744 | tf_op jit(solution)/shard_map/ppermute | solution.py:17
  192.7 12.5 %collective-permute-start.25 = (bf16[192,768]{1,0:T(8,128)(2,1)S(1)}, bf16[192,768]{1,0:T(8,128)(2,1)S(1)}, u32[]{:S(2)}, u32[]{:S(2)}) collective-permute-start(bf16[192,768]{1,0:T(8,128)(2,1)S(1)} %get-tuple-element.60), channel_id=1, source_target_pairs={{0,96},{32,0},{64,32},{96,64},{1,97},{33,1},{65,33},{97,65},{2,98}... | collective-permute-start | bytes 884744 | tf_op jit(solution)/shard_map/ppermute | solution.py:17
  202.9 10.0 %collective-permute-start.23 = (bf16[192,768]{1,0:T(8,128)(2,1)S(1)}, bf16[192,768]{1,0:T(8,128)(2,1)S(1)}, u32[]{:S(2)}, u32[]{:S(2)}) collective-permute-start(bf16[192,768]{1,0:T(8,128)(2,1)S(1)} %get-tuple-element.42), channel_id=1, source_target_pairs={{0,96},{32,0},{64,32},{96,64},{1,97},{33,1},{65,33},{97,65},{2,98}... | collective-permute-start | bytes 884744 | tf_op jit(solution)/shard_map/ppermute | solution.py:17
  204.9 11.2 %collective-permute-start.24 = (bf16[192,768]{1,0:T(8,128)(2,1)S(1)}, bf16[192,768]{1,0:T(8,128)(2,1)S(1)}, u32[]{:S(2)}, u32[]{:S(2)}) collective-permute-start(bf16[192,768]{1,0:T(8,128)(2,1)S(1)} %get-tuple-element.43), channel_id=1, source_target_pairs={{0,32},{32,64},{64,96},{96,0},{1,33},{33,65},{65,97},{97,1},{2,34}... | collective-permute-start | bytes 884744 | tf_op jit(solution)/shard_map/ppermute | solution.py:17
  205.1 14.5 %collective-permute-start.22 = (bf16[192,768]{1,0:T(8,128)(2,1)S(1)}, bf16[192,768]{1,0:T(8,128)(2,1)S(1)}, u32[]{:S(2)}, u32[]{:S(2)}) collective-permute-start(bf16[192,768]{1,0:T(8,128)(2,1)S(1)} %add_convert_fusion.1), channel_id=1, source_target_pairs={{0,32},{32,64},{64,96},{96,0},{1,33},{33,65},{65,97},{97,1},{2,34}... | collective-permute-start | bytes 884744 | tf_op jit(solution)/shard_map/ppermute | solution.py:17
  205.2 14.4 %collective-permute-start.26 = (bf16[192,768]{1,0:T(8,128)(2,1)S(1)}, bf16[192,768]{1,0:T(8,128)(2,1)S(1)}, u32[]{:S(2)}, u32[]{:S(2)}) collective-permute-start(bf16[192,768]{1,0:T(8,128)(2,1)S(1)} %add_convert_fusion), channel_id=1, source_target_pairs={{0,96},{32,0},{64,32},{96,64},{1,97},{33,1},{65,33},{97,65},{2,98}... | collective-permute-start | bytes 884744 | tf_op jit(solution)/shard_map/ppermute | solution.py:17
  221.4 1.5 collective-permute-start.27
  224.5 19.2 %collective-permute-start.28 = (bf16[192,384]{1,0:T(8,128)(2,1)S(1)}, bf16[192,384]{1,0:T(8,128)(2,1)S(1)}, u32[]{:S(2)}, u32[]{:S(2)}) collective-permute-start(bf16[192,384]{1,0:T(8,128)(2,1)S(1)} %get-tuple-element.58), channel_id=1, source_target_pairs={{0,24},{8,0},{16,8},{24,16},{1,25},{9,1},{17,9},{25,17},{2,26},{10... | collective-permute-start | bytes 442376 | tf_op jit(solution)/shard_map/ppermute | solution.py:17
  227.3 15.0 %all-to-all-start.1 = ((f32[64,1,128]{2,1,0:T(1,128)}), f32[64,1,128]{2,1,0:T(1,128)S(1)}, u32[]{:S(2)}, u32[]{:S(2)}) async-start(f32[64,1,128]{2,1,0:T(1,128)} %bitcast.38), calls=%async_computation.1 | async-start | bytes 65536 | tf_op jit(solution)/shard_map/all_to_all | solution.py:288
  232.9 10.8 %collective-permute-start.29 = (bf16[192,384]{1,0:T(8,128)(2,1)S(1)}, bf16[192,384]{1,0:T(8,128)(2,1)S(1)}, u32[]{:S(2)}, u32[]{:S(2)}) collective-permute-start(bf16[192,384]{1,0:T(8,128)(2,1)S(1)} %get-tuple-element.57), channel_id=1, source_target_pairs={{0,16},{8,24},{16,0},{24,8},{1,17},{9,25},{17,1},{25,9},{2,18},{10... | collective-permute-start | bytes 442376 | tf_op jit(solution)/shard_map/ppermute | solution.py:17
  236.0 7.7 %collective-permute-start.30 = (bf16[192,384]{1,0:T(8,128)(2,1)S(1)}, bf16[192,384]{1,0:T(8,128)(2,1)S(1)}, u32[]{:S(2)}, u32[]{:S(2)}) collective-permute-start(bf16[192,384]{1,0:T(8,128)(2,1)S(1)} %get-tuple-element.55), channel_id=1, source_target_pairs={{0,8},{8,16},{16,24},{24,0},{1,9},{9,17},{17,25},{25,1},{2,10},{10... | collective-permute-start | bytes 442376 | tf_op jit(solution)/shard_map/ppermute | solution.py:17
Sparse Core Ops, SparseCore 0:
  9.6 93.9 all-gather.1

commit v12 on v5

--- a/solution.py
+++ b/solution.py
@@ -10,7 +10,7 @@
 BF16, F32 = jnp.bfloat16, jnp.float32
 N = 4
 NT = (((1,), (1,)), ((), ()))
-PARAMS = pltpu.CompilerParams(vmem_limit_bytes=52 << 20)
+PARAMS = pltpu.CompilerParams(vmem_limit_bytes=46 << 20)
 
 
 def shift(value, axis, step):

time: 248 us -> 255 us (1.028)
  local copies, waits for them, and re-layouts: 27.1 us -> 35.6 us
  Pallas kernels: 68.3 us -> 61.6 us
  other arithmetic: 13.4 us -> 16.2 us
    unnamed x26 -> x38, local copies, waits for them, and re-layouts: 13.7 us -> 20.7 us
    ppermute x29, waiting for transfers between devices: 44.3 us -> 46.9 us  [shift(): return lax.ppermute(value, axis, [(i, (i + step) % N) for i in range(N)])]
  transfers between devices with their start and end apart: 34 -> 34, of which waited for: 14 -> 15; matrix products, arithmetic and copies ran while one was open for 14% -> 15% of each run, Pallas kernels for 15% -> 13%
where the time goes in v12:
time: 255 us; the launch traced here: 254 us
  waiting for transfers between devices  64.5 us (25%)
  Pallas kernels  61.6 us (24%)
  starting transfers between devices  61.2 us (24%)
  local copies, waits for them, and re-layouts  35.6 us (14%)
  other arithmetic  16.2 us (6%)
  between operations  15.2 us (6%)
    ppermute x29, starting transfers between devices, shift(): return lax.ppermute(value, axis, [(i, (i + step) % N) for i in range(N)])  48.6 us
    ppermute x29, waiting for transfers between devices, shift(): return lax.ppermute(value, axis, [(i, (i + step) % N) for i in range(N)])  46.9 us
    pallas_call x4, Pallas kernels, terms(): pl.pallas_call(kernel, grid_spec=pltpu.PrefetchScalarGridSpec(num_scalar_...  22.5 us
    unnamed x38, local copies, waits for them, and re-layouts  20.7 us
    pallas_call x1, Pallas kernels, first_slopes(): pl.pallas_call(kernel, grid_spec=pltpu.PrefetchScalarGridSpec(num_scalar_...  18.6 us
    all_to_all x2, starting transfers between devices, total_of(): lax.all_to_all(total, ('x', 'y', 'z'), split_axis=0, concat_axis=0, tiled...  12.5 us
    all_gather x1, waiting for transfers between devices, per_device(): lax.all_gather(tokens, ('z', 'c', 'y'), axis=0, tiled=True)  10.6 us
    pallas_call x1, Pallas kernels, moved(): pl.pallas_call(kernel, grid_spec=pltpu.PrefetchScalarGridSpec(num_scalar_...  9.82 us
  transfers between devices with their start and end apart: 34, of which 15 were waited for; matrix products, arithmetic and copies ran while one was open for 15% of the time, Pallas kernels for 13%

profile of v12, /device:TPU:0, one launch (start us, length us, event | category | flops | bytes accessed | tf_op | source)
XLA Modules:
  0.0 254.3 jit_solution(12927246087085236006)
XLA Ops:
  7.3 1.8 constant_dynamic-slice_fusion.1
  9.0 1.7 collective-permute-start.2
  10.7 1.6 collective-permute-start
  12.3 2.1 collective-permute-start.1
  14.4 1.7 copy-done
  18.5 1.6 bitcast_dynamic-update-slice_fusion.14
  21.5 1.5 copy.20
  24.0 2.3 collective-permute-start.6
  27.0 1.6 bitcast_dynamic-update-slice_fusion.10
  29.2 1.6 bitcast_dynamic-update-slice_fusion.15
  31.5 1.6 bitcast_dynamic-update-slice_fusion.11
  33.7 20.7 %collective-permute-done.7 = bf16[1152,384]{0,1:T(8,128)(2,1)S(1)} collective-permute-done((bf16[1152,384]{0,1:T(8,128)(2,1)}, bf16[1152,384]{0,1:T(8,128)(2,1)S(1)}, u32[]{:S(2)}, u32[]{:S(2)}) %collective-permute-start.7) | collective-permute-done | bytes 884768 | tf_op jit(solution)/shard_map/ppermute | solution.py:17
  56.0 3.2 %collective-permute-start.9 = (bf16[384,384]{0,1:T(8,128)(2,1)}, bf16[384,384]{0,1:T(8,128)(2,1)}, u32[]{:S(2)}, u32[]{:S(2)}) collective-permute-start(bf16[384,384]{0,1:T(8,128)(2,1)} %slice.98), channel_id=1, source_target_pairs={{0,24},{8,0},{16,8},{24,16},{1,25},{9,1},{17,9},{25,17},{2,26},{10... | collective-permute-start | bytes 884744 | tf_op jit(solution)/shard_map/ppermute | solution.py:17
  60.7 1.6 collective-permute-start.5
  62.2 2.7 %collective-permute-start.4 = (bf16[384,768]{1,0:T(8,128)(2,1)S(1)}, bf16[384,768]{1,0:T(8,128)(2,1)S(1)}, u32[]{:S(2)}, u32[]{:S(2)}) collective-permute-start(bf16[384,768]{1,0:T(8,128)(2,1)S(1)} %bitcast.92), channel_id=1, source_target_pairs={{0,64},{32,96},{64,0},{96,32},{1,65},{33,97},{65,1},{97,33},{2,66}... | collective-permute-start | bytes 1769480 | tf_op jit(solution)/shard_map/ppermute | solution.py:17
  67.3 5.2 %collective-permute-done.8 = bf16[384,384]{0,1:T(8,128)(2,1)} collective-permute-done((bf16[384,384]{0,1:T(8,128)(2,1)}, bf16[384,384]{0,1:T(8,128)(2,1)}, u32[]{:S(2)}, u32[]{:S(2)}) %collective-permute-start.8) | collective-permute-done | bytes 294944 | tf_op jit(solution)/shard_map/ppermute | solution.py:17
  72.7 1.9 fusion.11
  77.2 1.9 fusion.12
  80.0 1.8 dynamic-slice_bitcast_fusion.3
  82.1 7.6 %collective-permute-done.4.refs_2_ = bf16[384,768]{1,0:T(8,128)(2,1)S(1)} collective-permute-done((bf16[384,768]{1,0:T(8,128)(2,1)S(1)}, bf16[384,768]{1,0:T(8,128)(2,1)S(1)}, u32[]{:S(2)}, u32[]{:S(2)}) %collective-permute-start.4) | collective-permute-done | bytes 589856 | tf_op jit(solution)/shard_map/ppermute | solution.py:17
  91.3 10.6 %all-gather.2.cloned.1.call-done = bf16[24576,384]{1,0:T(8,128)(2,1)} async-done(((bf16[768,384]{1,0:T(8,128)(2,1)}), bf16[24576,384]{1,0:T(8,128)(2,1)}) %all-gather.2.cloned.1.call-update) | async-done | bytes 18874384 | tf_op jit(solution)/shard_map/all_gather | solution.py:290
  104.1 18.6 %shard_map.38 = (f32[384,3072]{1,0:T(8,128)}, bf16[384,3072]{1,0:T(8,128)(2,1)S(1)}, bf16[384,768]{1,0:T(8,128)(2,1)S(1)}) custom-call(s32[4]{0:T(128)S(1)} %pad_add_fusion.which_ref, bf16[8,3072,384]{2,1,0:T(8,128)(2,1)} %bitcast.95, bf16[384,768]{1,0:T(8,128)(2,1)S(1)} %bitcast.94, bf16[384,768]{1,0:T(8,128)(2,1)S(1)} %copy-done.7, ...), custom_call_target="tpu_custom_call" | custom-call | flops 9059696640 | bytes 31260672 | tf_op jit(solution)/shard_map/pallas_call | solution.py:79
  122.7 1.5 collective-permute-start.10
  124.3 1.8 collective-permute-start.14
  126.0 7.2 %shard_map.40 = (f32[192,768]{1,0:T(8,128)S(1)}, bf16[192,768]{1,0:T(8,128)(2,1)S(1)}, bf16[192,768]{1,0:T(8,128)(2,1)S(1)}, f32[192,768]{1,0:T(8,128)S(1)}) custom-call(s32[2]{0:T(128)S(1)} %pad_add_fusion.2.which_ref, bf16[8,3072,384]{2,1,0:T(8,128)(2,1)} %bitcast.96, bf16[8,3072,384]{2,1,0:T(8,128)(2,1)} %bitcast.97, ...), custom_call_target="tpu_custom_call" | custom-call | flops 3623878656 | bytes 11796480 | tf_op jit(solution)/shard_map/pallas_call | solution.py:192
  133.3 1.7 collective-permute-start.12
  136.0 3.1 %collective-permute-start.15 = (bf16[192,768]{1,0:T(8,128)(2,1)S(1)}, bf16[192,768]{1,0:T(8,128)(2,1)S(1)}, u32[]{:S(2)}, u32[]{:S(2)}) collective-permute-start(bf16[192,768]{1,0:T(8,128)(2,1)S(1)} %add_convert_fusion.2), channel_id=1, source_target_pairs={{0,96},{32,0},{64,32},{96,64},{1,97},{33,1},{65,33},{97,65},{2,98}... | collective-permute-start | bytes 884744 | tf_op jit(solution)/shard_map/ppermute | solution.py:17
  139.0 4.0 %shard_map.39 = f32[384,768]{1,0:T(8,128)S(1)} custom-call(s32[1]{0:T(128)} %bitcast.which_ref, bf16[8,3072,384]{2,1,0:T(8,128)(2,1)} %bitcast.98, bf16[384,3072]{1,0:T(8,128)(2,1)S(1)} %get-tuple-element.30.refs_1_.refs_2_), custom_call_target="tpu_custom_call" | custom-call | flops 1811939328 | bytes 8257536 | tf_op jit(solution)/shard_map/pallas_call | solution.py:192
  143.4 2.7 %collective-permute-done.13 = bf16[192,768]{1,0:T(8,128)(2,1)S(1)} collective-permute-done((bf16[192,768]{1,0:T(8,128)(2,1)S(1)}, bf16[192,768]{1,0:T(8,128)(2,1)S(1)}, u32[]{:S(2)}, u32[]{:S(2)}) %collective-permute-start.13) | collective-permute-done | bytes 294944 | tf_op jit(solution)/shard_map/ppermute | solution.py:17
  146.2 4.7 %collective-permute-done.11 = bf16[192,768]{1,0:T(8,128)(2,1)S(1)} collective-permute-done((bf16[192,768]{1,0:T(8,128)(2,1)S(1)}, bf16[192,768]{1,0:T(8,128)(2,1)S(1)}, u32[]{:S(2)}, u32[]{:S(2)}) %collective-permute-start.11) | collective-permute-done | bytes 294944 | tf_op jit(solution)/shard_map/ppermute | solution.py:17
  151.2 3.2 %collective-permute-start.17 = (bf16[384,768]{1,0:T(8,128)(2,1)S(1)}, bf16[384,768]{1,0:T(8,128)(2,1)}, u32[]{:S(2)}, u32[]{:S(2)}) collective-permute-start(bf16[384,768]{1,0:T(8,128)(2,1)S(1)} %fusion.1.refs_3_), channel_id=1, source_target_pairs={{0,96},{32,0},{64,32},{96,64},{1,97},{33,1},{65,33},{97,65},{2,98}... | collective-permute-start | bytes 1769480 | tf_op jit(solution)/shard_map/ppermute | solution.py:17
  158.5 6.4 %all-to-all-start = ((f32[64,1,128]{2,1,0:T(1,128)}), f32[64,1,128]{2,1,0:T(1,128)}, u32[]{:S(2)}, u32[]{:S(2)}) async-start(f32[64,1,128]{2,1,0:T(1,128)} %bitcast.109), calls=%async_computation | async-start | bytes 65536 | tf_op jit(solution)/shard_map/all_to_all | solution.py:277
  167.2 1.7 slice.103
  168.9 2.9 %collective-permute-start.20 = (bf16[192,768]{1,0:T(8,128)(2,1)}, bf16[192,768]{1,0:T(8,128)(2,1)}, u32[]{:S(2)}, u32[]{:S(2)}) collective-permute-start(bf16[192,768]{1,0:T(8,128)(2,1)} %slice.103), channel_id=1, source_target_pairs={{0,96},{32,0},{64,32},{96,64},{1,97},{33,1},{65,33},{97,65},{2,98}... | collective-permute-start | bytes 884744 | tf_op jit(solution)/shard_map/ppermute | solution.py:17
  171.8 9.8 %shard_map.41.part_ref = f32[384,3072]{1,0:T(8,128)S(1)} custom-call(s32[3]{0:T(128)S(1)} %pad_add_fusion.3.which_ref, bf16[8,3072,384]{2,1,0:T(8,128)(2,1)} %bitcast.99, bf16[8,3072,384]{2,1,0:T(8,128)(2,1)} %bitcast.100, bf16[8,3072,384]{2,1,0:T(8,128)(2,1)} %bitcast.101, bf16[384,768]{1,0:T(8,128)(2,1)S(1)} %fusion.1.refs_3_, ...), custom_call_target="tpu_custom_call" | custom-call | flops 5435817984 | bytes 20643840 | tf_op jit(solution)/shard_map/pallas_call | solution.py:112
  181.6 2.1 copy-done.1
  187.0 9.7 %shard_map.42 = (bf16[384,3072]{1,0:T(8,128)(2,1)S(1)}, bf16[384,768]{1,0:T(8,128)(2,1)S(1)}) custom-call(s32[1]{0:T(128)} %bitcast.2.which_ref, f32[1,1]{1,0:T(1,128)} %bitcast.29.scale_ref, bf16[8,3072,384]{2,1,0:T(8,128)(2,1)} %bitcast.102, bf16[384,768]{1,0:T(8,128)(2,1)S(1)} %pad_maximum_fusion.3.f_ref, f32[384,3072]{1,0:T(8,128)} %copy-done.1, ...), custom_call_target="tpu_custom_call" | custom-call | flops 3623878656 | bytes 15335424 | tf_op jit(solution)/shard_map/pallas_call | solution.py:141
  196.8 3.2 %collective-permute-start.25 = (bf16[192,768]{1,0:T(8,128)(2,1)S(1)}, bf16[192,768]{1,0:T(8,128)(2,1)S(1)}, u32[]{:S(2)}, u32[]{:S(2)}) collective-permute-start(bf16[192,768]{1,0:T(8,128)(2,1)S(1)} %get-tuple-element.64), channel_id=1, source_target_pairs={{0,96},{32,0},{64,32},{96,64},{1,97},{33,1},{65,33},{97,65},{2,98}... | collective-permute-start | bytes 884744 | tf_op jit(solution)/shard_map/ppermute | solution.py:17
  200.0 7.2 %shard_map.44 = (f32[192,768]{1,0:T(8,128)S(1)}, bf16[192,768]{1,0:T(8,128)(2,1)S(1)}, bf16[192,768]{1,0:T(8,128)(2,1)S(1)}, f32[192,768]{1,0:T(8,128)S(1)}) custom-call(s32[2]{0:T(128)S(1)} %pad_add_fusion.2.which_ref, bf16[8,3072,384]{2,1,0:T(8,128)(2,1)} %bitcast.103, bf16[8,3072,384]{2,1,0:T(8,128)(2,1)} %bitcast.104, ...), custom_call_target="tpu_custom_call" | custom-call | flops 3623878656 | bytes 11796480 | tf_op jit(solution)/shard_map/pallas_call | solution.py:192
  207.3 2.0 collective-permute-start.24
  210.9 3.2 %collective-permute-start.26 = (bf16[192,768]{1,0:T(8,128)(2,1)}, bf16[192,768]{1,0:T(8,128)(2,1)}, u32[]{:S(2)}, u32[]{:S(2)}) collective-permute-start(bf16[192,768]{1,0:T(8,128)(2,1)} %add_convert_fusion), channel_id=1, source_target_pairs={{0,96},{32,0},{64,32},{96,64},{1,97},{33,1},{65,33},{97,65},{2,98}... | collective-permute-start | bytes 884744 | tf_op jit(solution)/shard_map/ppermute | solution.py:17
  214.1 4.0 %shard_map.43 = f32[384,768]{1,0:T(8,128)S(1)} custom-call(s32[1]{0:T(128)} %bitcast.which_ref, bf16[8,3072,384]{2,1,0:T(8,128)(2,1)} %bitcast.105, bf16[384,3072]{1,0:T(8,128)(2,1)S(1)} %copy-done.3), custom_call_target="tpu_custom_call" | custom-call | flops 1811939328 | bytes 8257536 | tf_op jit(solution)/shard_map/pallas_call | solution.py:192
  218.3 3.3 %collective-permute-done.22 = bf16[192,768]{1,0:T(8,128)(2,1)} collective-permute-done((bf16[192,768]{1,0:T(8,128)(2,1)}, bf16[192,768]{1,0:T(8,128)(2,1)}, u32[]{:S(2)}, u32[]{:S(2)}) %collective-permute-start.22) | collective-permute-done | bytes 294944 | tf_op jit(solution)/shard_map/ppermute | solution.py:17
  224.9 2.7 %collective-permute-start.27 = (bf16[192,384]{1,0:T(8,128)(2,1)S(1)}, bf16[192,384]{1,0:T(8,128)(2,1)S(1)}, u32[]{:S(2)}, u32[]{:S(2)}) collective-permute-start(bf16[192,384]{1,0:T(8,128)(2,1)S(1)} %get-tuple-element.62), channel_id=1, source_target_pairs={{0,24},{8,0},{16,8},{24,16},{1,25},{9,1},{17,9},{25,17},{2,26},{10... | collective-permute-start | bytes 442376 | tf_op jit(solution)/shard_map/ppermute | solution.py:17
  228.9 6.1 %all-to-all-start.1 = ((f32[64,1,128]{2,1,0:T(1,128)}), f32[64,1,128]{2,1,0:T(1,128)S(1)}, u32[]{:S(2)}, u32[]{:S(2)}) async-start(f32[64,1,128]{2,1,0:T(1,128)} %bitcast.42), calls=%async_computation.1 | async-start | bytes 65536 | tf_op jit(solution)/shard_map/all_to_all | solution.py:277
  234.9 1.6 collective-permute-start.29
  236.6 2.7 %collective-permute-start.28 = (bf16[192,384]{1,0:T(8,128)(2,1)S(1)}, bf16[192,384]{1,0:T(8,128)(2,1)S(1)}, u32[]{:S(2)}, u32[]{:S(2)}) collective-permute-start(bf16[192,384]{1,0:T(8,128)(2,1)S(1)} %get-tuple-element.61), channel_id=1, source_target_pairs={{0,16},{8,24},{16,0},{24,8},{1,17},{9,25},{17,1},{25,9},{2,18},{10... | collective-permute-start | bytes 442376 | tf_op jit(solution)/shard_map/ppermute | solution.py:17
  239.3 5.2 %all-to-all-done.1 = f32[64,1,128]{2,1,0:T(1,128)S(1)} async-done(((f32[64,1,128]{2,1,0:T(1,128)}), f32[64,1,128]{2,1,0:T(1,128)S(1)}, u32[]{:S(2)}, u32[]{:S(2)}) %all-to-all-start.1) | async-done | bytes 32800 | tf_op jit(solution)/shard_map/all_to_all | solution.py:277
  (111 shorter events, 40.5 us)
Async XLA Ops:
  6.5 95.4 %all-gather.2.cloned.1.call-start = ((), (), s32[]{:S(2)}) async-start(), calls=%async_computation.2 | async-start | bytes 19464192 | tf_op jit(solution)/shard_map/all_gather | solution.py:290
  9.0 11.1 %collective-permute-start.2 = (bf16[192,384]{1,0:T(8,128)(2,1)}, bf16[192,384]{1,0:T(8,128)(2,1)S(1)}, u32[]{:S(2)}, u32[]{:S(2)}) collective-permute-start(bf16[192,384]{1,0:T(8,128)(2,1)} %get-tuple-element.67), channel_id=1, source_target_pairs={{0,8},{8,16},{16,24},{24,0},{1,9},{9,17},{17,25},{25,1},{2,10},{10... | collective-permute-start | bytes 442376 | tf_op jit(solution)/shard_map/ppermute | solution.py:17
  10.7 9.5 %collective-permute-start = (bf16[192,384]{1,0:T(8,128)(2,1)S(1)}, bf16[192,384]{1,0:T(8,128)(2,1)S(1)}, u32[]{:S(2)}, u32[]{:S(2)}) collective-permute-start(bf16[192,384]{1,0:T(8,128)(2,1)S(1)} %get-tuple-element.68), channel_id=1, source_target_pairs={{0,24},{8,0},{16,8},{24,16},{1,25},{9,1},{17,9},{25,17},{2,26},{10... | collective-permute-start | bytes 442376 | tf_op jit(solution)/shard_map/ppermute | solution.py:17
  12.3 8.4 %collective-permute-start.1 = (bf16[192,384]{1,0:T(8,128)(2,1)S(1)}, bf16[192,384]{1,0:T(8,128)(2,1)}, u32[]{:S(2)}, u32[]{:S(2)}) collective-permute-start(bf16[192,384]{1,0:T(8,128)(2,1)S(1)} %get-tuple-element.69), channel_id=1, source_target_pairs={{0,16},{8,24},{16,0},{24,8},{1,17},{9,25},{17,1},{25,9},{2,18},{10... | collective-permute-start | bytes 442376 | tf_op jit(solution)/shard_map/ppermute | solution.py:17
  14.4 1.7 copy-start
  17.4 4.2 %copy-start.8 = (bf16[768,384]{0,1:T(8,128)(2,1)}, bf16[768,384]{0,1:T(8,128)(2,1)S(1)}, u32[]{:S(2)}) copy-start(bf16[768,384]{0,1:T(8,128)(2,1)S(1)} %copy.18) | copy-start | bytes 1769476
  23.0 31.4 %collective-permute-start.7 = (bf16[1152,384]{0,1:T(8,128)(2,1)}, bf16[1152,384]{0,1:T(8,128)(2,1)S(1)}, u32[]{:S(2)}, u32[]{:S(2)}) collective-permute-start(bf16[1152,384]{0,1:T(8,128)(2,1)} %copy.20), channel_id=1, source_target_pairs={{0,8},{8,16},{16,24},{24,0},{1,9},{9,17},{17,25},{25,1},{2,10},{10... | collective-permute-start | bytes 2654216 | tf_op jit(solution)/shard_map/ppermute | solution.py:17
  24.0 31.3 %collective-permute-start.6 = (bf16[1152,384]{0,1:T(8,128)(2,1)S(1)}, bf16[1152,384]{0,1:T(8,128)(2,1)S(1)}, u32[]{:S(2)}, u32[]{:S(2)}) collective-permute-start(bf16[1152,384]{0,1:T(8,128)(2,1)S(1)} %copy.19), channel_id=1, source_target_pairs={{0,24},{8,0},{16,8},{24,16},{1,25},{9,1},{17,9},{25,17},{2,26},{10... | collective-permute-start | bytes 2654216 | tf_op jit(solution)/shard_map/ppermute | solution.py:17
  55.3 17.2 %collective-permute-start.8 = (bf16[384,384]{0,1:T(8,128)(2,1)}, bf16[384,384]{0,1:T(8,128)(2,1)}, u32[]{:S(2)}, u32[]{:S(2)}) collective-permute-start(bf16[384,384]{0,1:T(8,128)(2,1)} %slice.97), channel_id=1, source_target_pairs={{0,8},{8,16},{16,24},{24,0},{1,9},{9,17},{17,25},{25,1},{2,10},{10... | collective-permute-start | bytes 884744 | tf_op jit(solution)/shard_map/ppermute | solution.py:17
  56.0 16.6 %collective-permute-start.9 = (bf16[384,384]{0,1:T(8,128)(2,1)}, bf16[384,384]{0,1:T(8,128)(2,1)}, u32[]{:S(2)}, u32[]{:S(2)}) collective-permute-start(bf16[384,384]{0,1:T(8,128)(2,1)} %slice.98), channel_id=1, source_target_pairs={{0,24},{8,0},{16,8},{24,16},{1,25},{9,1},{17,9},{25,17},{2,26},{10... | collective-permute-start | bytes 884744 | tf_op jit(solution)/shard_map/ppermute | solution.py:17
  60.7 21.4 %collective-permute-start.5 = (bf16[384,768]{1,0:T(8,128)(2,1)S(1)}, bf16[384,768]{1,0:T(8,128)(2,1)S(1)}, u32[]{:S(2)}, u32[]{:S(2)}) collective-permute-start(bf16[384,768]{1,0:T(8,128)(2,1)S(1)} %bitcast.91), channel_id=1, source_target_pairs={{0,32},{32,64},{64,96},{96,0},{1,33},{33,65},{65,97},{97,1},{2,34}... | collective-permute-start | bytes 1769480 | tf_op jit(solution)/shard_map/ppermute | solution.py:17
  62.2 27.5 %collective-permute-start.4 = (bf16[384,768]{1,0:T(8,128)(2,1)S(1)}, bf16[384,768]{1,0:T(8,128)(2,1)S(1)}, u32[]{:S(2)}, u32[]{:S(2)}) collective-permute-start(bf16[384,768]{1,0:T(8,128)(2,1)S(1)} %bitcast.92), channel_id=1, source_target_pairs={{0,64},{32,96},{64,0},{96,32},{1,65},{33,97},{65,1},{97,33},{2,66}... | collective-permute-start | bytes 1769480 | tf_op jit(solution)/shard_map/ppermute | solution.py:17
  65.0 25.6 %collective-permute-start.3 = (bf16[384,768]{1,0:T(8,128)(2,1)S(1)}, bf16[384,768]{1,0:T(8,128)(2,1)S(1)}, u32[]{:S(2)}, u32[]{:S(2)}) collective-permute-start(bf16[384,768]{1,0:T(8,128)(2,1)S(1)} %bitcast.93), channel_id=1, source_target_pairs={{0,96},{32,0},{64,32},{96,64},{1,97},{33,1},{65,33},{97,65},{2,98}... | collective-permute-start | bytes 1769480 | tf_op jit(solution)/shard_map/ppermute | solution.py:17
  67.2 8.2 %copy-start.9 = (bf16[768,384]{0,1:T(8,128)(2,1)S(1)}, bf16[768,384]{0,1:T(8,128)(2,1)}, u32[]{:S(2)}) copy-start(bf16[768,384]{0,1:T(8,128)(2,1)} %copy-done.8) | copy-start | bytes 1769476
  89.7 0.8 copy-start.4
  90.5 0.8 copy-start.6
  102.0 1.1 copy-start.5
  103.0 1.1 copy-start.7
  122.7 12.8 %collective-permute-start.10 = (bf16[192,768]{1,0:T(8,128)(2,1)S(1)}, bf16[192,768]{1,0:T(8,128)(2,1)S(1)}, u32[]{:S(2)}, u32[]{:S(2)}) collective-permute-start(bf16[192,768]{1,0:T(8,128)(2,1)S(1)} %get-tuple-element.65), channel_id=1, source_target_pairs={{0,32},{32,64},{64,96},{96,0},{1,33},{33,65},{65,97},{97,1},{2,34}... | collective-permute-start | bytes 884744 | tf_op jit(solution)/shard_map/ppermute | solution.py:17
  124.3 11.7 %collective-permute-start.14 = (bf16[192,768]{1,0:T(8,128)(2,1)S(1)}, bf16[192,768]{1,0:T(8,128)(2,1)S(1)}, u32[]{:S(2)}, u32[]{:S(2)}) collective-permute-start(bf16[192,768]{1,0:T(8,128)(2,1)S(1)} %get-tuple-element.66), channel_id=1, source_target_pairs={{0,96},{32,0},{64,32},{96,64},{1,97},{33,1},{65,33},{97,65},{2,98}... | collective-permute-start | bytes 884744 | tf_op jit(solution)/shard_map/ppermute | solution.py:17
  133.3 10.2 %collective-permute-start.12 = (bf16[192,768]{1,0:T(8,128)(2,1)S(1)}, bf16[192,768]{1,0:T(8,128)(2,1)S(1)}, u32[]{:S(2)}, u32[]{:S(2)}) collective-permute-start(bf16[192,768]{1,0:T(8,128)(2,1)S(1)} %get-tuple-element.33), channel_id=1, source_target_pairs={{0,96},{32,0},{64,32},{96,64},{1,97},{33,1},{65,33},{97,65},{2,98}... | collective-permute-start | bytes 884744 | tf_op jit(solution)/shard_map/ppermute | solution.py:17
  135.0 11.2 %collective-permute-start.13 = (bf16[192,768]{1,0:T(8,128)(2,1)S(1)}, bf16[192,768]{1,0:T(8,128)(2,1)S(1)}, u32[]{:S(2)}, u32[]{:S(2)}) collective-permute-start(bf16[192,768]{1,0:T(8,128)(2,1)S(1)} %get-tuple-element.34), channel_id=1, source_target_pairs={{0,32},{32,64},{64,96},{96,0},{1,33},{33,65},{65,97},{97,1},{2,34}... | collective-permute-start | bytes 884744 | tf_op jit(solution)/shard_map/ppermute | solution.py:17
  135.6 15.3 %collective-permute-start.11 = (bf16[192,768]{1,0:T(8,128)(2,1)S(1)}, bf16[192,768]{1,0:T(8,128)(2,1)S(1)}, u32[]{:S(2)}, u32[]{:S(2)}) collective-permute-start(bf16[192,768]{1,0:T(8,128)(2,1)S(1)} %add_convert_fusion.3), channel_id=1, source_target_pairs={{0,32},{32,64},{64,96},{96,0},{1,33},{33,65},{65,97},{97,1},{2,34}... | collective-permute-start | bytes 884744 | tf_op jit(solution)/shard_map/ppermute | solution.py:17
  136.0 14.9 %collective-permute-start.15 = (bf16[192,768]{1,0:T(8,128)(2,1)S(1)}, bf16[192,768]{1,0:T(8,128)(2,1)S(1)}, u32[]{:S(2)}, u32[]{:S(2)}) collective-permute-start(bf16[192,768]{1,0:T(8,128)(2,1)S(1)} %add_convert_fusion.2), channel_id=1, source_target_pairs={{0,96},{32,0},{64,32},{96,64},{1,97},{33,1},{65,33},{97,65},{2,98}... | collective-permute-start | bytes 884744 | tf_op jit(solution)/shard_map/ppermute | solution.py:17
  151.1 15.0 %collective-permute-start.18 = (bf16[384,768]{1,0:T(8,128)(2,1)S(1)}, bf16[384,768]{1,0:T(8,128)(2,1)S(1)}, u32[]{:S(2)}, u32[]{:S(2)}) collective-permute-start(bf16[384,768]{1,0:T(8,128)(2,1)S(1)} %fusion.1.refs_3_), channel_id=1, source_target_pairs={{0,32},{32,64},{64,96},{96,0},{1,33},{33,65},{65,97},{97,1},{2,34}... | collective-permute-start | bytes 1769480 | tf_op jit(solution)/shard_map/ppermute | solution.py:17
  151.2 16.0 %collective-permute-start.17 = (bf16[384,768]{1,0:T(8,128)(2,1)S(1)}, bf16[384,768]{1,0:T(8,128)(2,1)}, u32[]{:S(2)}, u32[]{:S(2)}) collective-permute-start(bf16[384,768]{1,0:T(8,128)(2,1)S(1)} %fusion.1.refs_3_), channel_id=1, source_target_pairs={{0,96},{32,0},{64,32},{96,64},{1,97},{33,1},{65,33},{97,65},{2,98}... | collective-permute-start | bytes 1769480 | tf_op jit(solution)/shard_map/ppermute | solution.py:17
  156.0 1.3 collective-permute-start.16
  158.5 25.3 %all-to-all-start = ((f32[64,1,128]{2,1,0:T(1,128)}), f32[64,1,128]{2,1,0:T(1,128)}, u32[]{:S(2)}, u32[]{:S(2)}) async-start(f32[64,1,128]{2,1,0:T(1,128)} %bitcast.109), calls=%async_computation | async-start | bytes 65536 | tf_op jit(solution)/shard_map/all_to_all | solution.py:277
  166.9 19.0 %collective-permute-start.19 = (bf16[192,768]{1,0:T(8,128)(2,1)}, bf16[192,768]{1,0:T(8,128)(2,1)}, u32[]{:S(2)}, u32[]{:S(2)}) collective-permute-start(bf16[192,768]{1,0:T(8,128)(2,1)} %slice.102), channel_id=1, source_target_pairs={{0,32},{32,64},{64,96},{96,0},{1,33},{33,65},{65,97},{97,1},{2,34}... | collective-permute-start | bytes 884744 | tf_op jit(solution)/shard_map/ppermute | solution.py:17
  168.9 17.0 %collective-permute-start.20 = (bf16[192,768]{1,0:T(8,128)(2,1)}, bf16[192,768]{1,0:T(8,128)(2,1)}, u32[]{:S(2)}, u32[]{:S(2)}) collective-permute-start(bf16[192,768]{1,0:T(8,128)(2,1)} %slice.103), channel_id=1, source_target_pairs={{0,96},{32,0},{64,32},{96,64},{1,97},{33,1},{65,33},{97,65},{2,98}... | collective-permute-start | bytes 884744 | tf_op jit(solution)/shard_map/ppermute | solution.py:17
  181.6 2.2 copy-start.1
  196.6 10.6 %copy-start.2 = (bf16[384,3072]{1,0:T(8,128)(2,1)}, bf16[384,3072]{1,0:T(8,128)(2,1)S(1)}, u32[]{:S(2)}) copy-start(bf16[384,3072]{1,0:T(8,128)(2,1)S(1)} %get-tuple-element.39.refs_1_.refs_2_) | copy-start | bytes 7077892
  196.7 12.7 %collective-permute-start.21 = (bf16[192,768]{1,0:T(8,128)(2,1)S(1)}, bf16[192,768]{1,0:T(8,128)(2,1)S(1)}, u32[]{:S(2)}, u32[]{:S(2)}) collective-permute-start(bf16[192,768]{1,0:T(8,128)(2,1)S(1)} %get-tuple-element.63), channel_id=1, source_target_pairs={{0,32},{32,64},{64,96},{96,0},{1,33},{33,65},{65,97},{97,1},{2,34}... | collective-permute-start | bytes 884744 | tf_op jit(solution)/shard_map/ppermute | solution.py:17
  196.8 13.3 %collective-permute-start.25 = (bf16[192,768]{1,0:T(8,128)(2,1)S(1)}, bf16[192,768]{1,0:T(8,128)(2,1)S(1)}, u32[]{:S(2)}, u32[]{:S(2)}) collective-permute-start(bf16[192,768]{1,0:T(8,128)(2,1)S(1)} %get-tuple-element.64), channel_id=1, source_target_pairs={{0,96},{32,0},{64,32},{96,64},{1,97},{33,1},{65,33},{97,65},{2,98}... | collective-permute-start | bytes 884744 | tf_op jit(solution)/shard_map/ppermute | solution.py:17
  207.3 10.9 %collective-permute-start.23 = (bf16[192,768]{1,0:T(8,128)(2,1)S(1)}, bf16[192,768]{1,0:T(8,128)(2,1)S(1)}, u32[]{:S(2)}, u32[]{:S(2)}) collective-permute-start(bf16[192,768]{1,0:T(8,128)(2,1)S(1)} %get-tuple-element.42), channel_id=1, source_target_pairs={{0,96},{32,0},{64,32},{96,64},{1,97},{33,1},{65,33},{97,65},{2,98}... | collective-permute-start | bytes 884744 | tf_op jit(solution)/shard_map/ppermute | solution.py:17
  207.3 10.9 %collective-permute-start.24 = (bf16[192,768]{1,0:T(8,128)(2,1)S(1)}, bf16[192,768]{1,0:T(8,128)(2,1)S(1)}, u32[]{:S(2)}, u32[]{:S(2)}) collective-permute-start(bf16[192,768]{1,0:T(8,128)(2,1)S(1)} %get-tuple-element.43), channel_id=1, source_target_pairs={{0,32},{32,64},{64,96},{96,0},{1,33},{33,65},{65,97},{97,1},{2,34}... | collective-permute-start | bytes 884744 | tf_op jit(solution)/shard_map/ppermute | solution.py:17
  209.4 4.8 %copy-start.3 = (bf16[384,3072]{1,0:T(8,128)(2,1)S(1)}, bf16[384,3072]{1,0:T(8,128)(2,1)}, u32[]{:S(2)}) copy-start(bf16[384,3072]{1,0:T(8,128)(2,1)} %copy-done.2) | copy-start | bytes 7077892
  210.1 11.4 %collective-permute-start.22 = (bf16[192,768]{1,0:T(8,128)(2,1)}, bf16[192,768]{1,0:T(8,128)(2,1)}, u32[]{:S(2)}, u32[]{:S(2)}) collective-permute-start(bf16[192,768]{1,0:T(8,128)(2,1)} %add_convert_fusion.1), channel_id=1, source_target_pairs={{0,32},{32,64},{64,96},{96,0},{1,33},{33,65},{65,97},{97,1},{2,34}... | collective-permute-start | bytes 884744 | tf_op jit(solution)/shard_map/ppermute | solution.py:17
  210.9 10.6 %collective-permute-start.26 = (bf16[192,768]{1,0:T(8,128)(2,1)}, bf16[192,768]{1,0:T(8,128)(2,1)}, u32[]{:S(2)}, u32[]{:S(2)}) collective-permute-start(bf16[192,768]{1,0:T(8,128)(2,1)} %add_convert_fusion), channel_id=1, source_target_pairs={{0,96},{32,0},{64,32},{96,64},{1,97},{33,1},{65,33},{97,65},{2,98}... | collective-permute-start | bytes 884744 | tf_op jit(solution)/shard_map/ppermute | solution.py:17
  224.8 2.9 %collective-permute-start.30 = (f32[64,128]{1,0:T(8,128)S(1)}, f32[64,128]{1,0:T(8,128)S(1)}, u32[]{:S(2)}, u32[]{:S(2)}) collective-permute-start(f32[64,128]{1,0:T(8,128)S(1)} %broadcast_in_dim.7), channel_id=1, source_target_pairs={{0,1},{1,0},{2,3},{3,2},{4,5},{5,4},{6,7},{7,6},{8,9},{9,8},{10,11... | collective-permute-start | bytes 98312 | tf_op jit(solution)/shard_map/ppermute | solution.py:276
  224.9 20.8 %collective-permute-start.27 = (bf16[192,384]{1,0:T(8,128)(2,1)S(1)}, bf16[192,384]{1,0:T(8,128)(2,1)S(1)}, u32[]{:S(2)}, u32[]{:S(2)}) collective-permute-start(bf16[192,384]{1,0:T(8,128)(2,1)S(1)} %get-tuple-element.62), channel_id=1, source_target_pairs={{0,24},{8,0},{16,8},{24,16},{1,25},{9,1},{17,9},{25,17},{2,26},{10... | collective-permute-start | bytes 442376 | tf_op jit(solution)/shard_map/ppermute | solution.py:17
  228.9 15.6 %all-to-all-start.1 = ((f32[64,1,128]{2,1,0:T(1,128)}), f32[64,1,128]{2,1,0:T(1,128)S(1)}, u32[]{:S(2)}, u32[]{:S(2)}) async-start(f32[64,1,128]{2,1,0:T(1,128)} %bitcast.42), calls=%async_computation.1 | async-start | bytes 65536 | tf_op jit(solution)/shard_map/all_to_all | solution.py:277
  234.9 11.1 %collective-permute-start.29 = (bf16[192,384]{1,0:T(8,128)(2,1)S(1)}, bf16[192,384]{1,0:T(8,128)(2,1)S(1)}, u32[]{:S(2)}, u32[]{:S(2)}) collective-permute-start(bf16[192,384]{1,0:T(8,128)(2,1)S(1)} %get-tuple-element.59), channel_id=1, source_target_pairs={{0,8},{8,16},{16,24},{24,0},{1,9},{9,17},{17,25},{25,1},{2,10},{10... | collective-permute-start | bytes 442376 | tf_op jit(solution)/shard_map/ppermute | solution.py:17
  236.6 9.4 %collective-permute-start.28 = (bf16[192,384]{1,0:T(8,128)(2,1)S(1)}, bf16[192,384]{1,0:T(8,128)(2,1)S(1)}, u32[]{:S(2)}, u32[]{:S(2)}) collective-permute-start(bf16[192,384]{1,0:T(8,128)(2,1)S(1)} %get-tuple-element.61), channel_id=1, source_target_pairs={{0,16},{8,24},{16,0},{24,8},{1,17},{9,25},{17,1},{25,9},{2,18},{10... | collective-permute-start | bytes 442376 | tf_op jit(solution)/shard_map/ppermute | solution.py:17
Sparse Core Ops, SparseCore 0:
  9.6 92.3 all-gather.1

commit v13 on v12

--- a/solution.py
+++ b/solution.py
@@ -10,6 +10,7 @@
 BF16, F32 = jnp.bfloat16, jnp.float32
 N = 4
 NT = (((1,), (1,)), ((), ()))
+WIDE = pltpu.CompilerParams(vmem_limit_bytes=52 << 20)
 PARAMS = pltpu.CompilerParams(vmem_limit_bytes=46 << 20)
 
 
@@ -90,7 +91,7 @@
             jax.ShapeDtypeStruct((cols, rows), BF16),
             jax.ShapeDtypeStruct((cols, deep), BF16),
         ],
-        compiler_params=PARAMS,
+        compiler_params=WIDE,
         cost_estimate=cost(cols, (blocks + per) * wide, rows, rows * cols),
     )(jnp.stack(which).astype(jnp.int32), x, *w, t)
 
@@ -118,7 +119,7 @@
             out_specs=pl.BlockSpec((cols, tile), lambda i, which: (0, i)),
         ),
         out_shape=jax.ShapeDtypeStruct((cols, rows), F32),
-        compiler_params=PARAMS,
+        compiler_params=WIDE,
         cost_estimate=cost(cols, deep * count, rows),
     )(jnp.stack(which).astype(jnp.int32), *([x] * count), *pieces)
 
@@ -254,7 +255,7 @@
             out_specs=[pl.BlockSpec((size, cols), lambda i, which: (0, 0)) for size in tall],
         ),
         out_shape=[jax.ShapeDtypeStruct((size, cols), array.dtype) for size in tall],
-        compiler_params=PARAMS,
+        compiler_params=WIDE,
         cost_estimate=cost(0, 0, 0),
     )(jnp.stack([lax.rem(me + k, N) for k in range(N)]).astype(jnp.int32), *([array] * N))
 

time: 255 us -> 253 us (level)
  local copies, waits for them, and re-layouts: 35.6 us -> 31 us
  Pallas kernels: 61.6 us -> 65.5 us
    unnamed x38 -> x36, local copies, waits for them, and re-layouts: 20.7 us -> 16 us
  transfers between devices with their start and end apart: 34 -> 34, of which waited for: 15 -> 14; matrix products, arithmetic and copies ran while one was open for 15% -> 15% of each run, Pallas kernels for 13% -> 15%
where the time goes in v13:
time: 253 us
  Pallas kernels  65.5 us (26%)
  waiting for transfers between devices  64.3 us (25%)
  starting transfers between devices  61.1 us (24%)
  local copies, waits for them, and re-layouts  31 us (12%)
  other arithmetic  15.5 us (6%)
  between operations  15.2 us (6%)
    ppermute x29, starting transfers between devices, shift(): return lax.ppermute(value, axis, [(i, (i + step) % N) for i in range(N)])  48.4 us
    ppermute x29, waiting for transfers between devices, shift(): return lax.ppermute(value, axis, [(i, (i + step) % N) for i in range(N)])  47.1 us
    pallas_call x4, Pallas kernels, terms(): pl.pallas_call(kernel, grid_spec=pltpu.PrefetchScalarGridSpec(num_scalar_...  22.5 us
    pallas_call x1, Pallas kernels, first_slopes(): pl.pallas_call(kernel, grid_spec=pltpu.PrefetchScalarGridSpec(num_scalar_...  19 us
    unnamed x36, local copies, waits for them, and re-layouts  16 us
    all_to_all x2, starting transfers between devices, total_of(): lax.all_to_all(total, ('x', 'y', 'z'), split_axis=0, concat_axis=0, tiled...  12.4 us
    pallas_call x1, Pallas kernels, moved(): pl.pallas_call(kernel, grid_spec=pltpu.PrefetchScalarGridSpec(num_scalar_...  11.1 us
    all_gather x1, waiting for transfers between devices, per_device(): lax.all_gather(tokens, ('z', 'c', 'y'), axis=0, tiled=True)  10.2 us
  transfers between devices with their start and end apart: 34, of which 14 were waited for; matrix products, arithmetic and copies ran while one was open for 15% of the time, Pallas kernels for 15%

profile of v13, /device:TPU:0, one launch (start us, length us, event | category | flops | bytes accessed | tf_op | source)
XLA Modules:
  0.0 252.6 jit_solution(12801844433967055816)
XLA Ops:
  7.3 1.9 constant_dynamic-slice_fusion.1
  9.2 1.7 collective-permute-start.2
  10.8 1.6 collective-permute-start
  12.4 2.1 collective-permute-start.1
  14.5 3.2 %shard_map.37 = (bf16[1152,384]{1,0:T(8,128)(2,1)S(1)}, bf16[1152,384]{1,0:T(8,128)(2,1)}, bf16[768,384]{1,0:T(8,128)(2,1)S(1)}) custom-call(s32[4]{0:T(128)S(1)} %pad_add_fusion.1.which_ref, bf16[768,1536]{1,0:T(8,128)(2,1)} %before.1, bf16[768,1536]{1,0:T(8,128)(2,1)} %before.1, bf16[768,1536]{1,0:T(8,128)(2,1)} %before.1, bf16[768,1536]{1,0:T(8,128)(2,1)} %before.1), custom_call_target="tpu_custom_call" | custom-call | tf_op jit(solution)/shard_map/pallas_call | solution.py:249
  19.0 1.6 bitcast_dynamic-update-slice_fusion.14
  20.7 1.5 copy.19
  22.2 1.6 copy.20
  24.9 2.1 collective-permute-start.6
  31.7 22.8 %collective-permute-done.7 = bf16[1152,384]{0,1:T(8,128)(2,1)S(1)} collective-permute-done((bf16[1152,384]{0,1:T(8,128)(2,1)}, bf16[1152,384]{0,1:T(8,128)(2,1)S(1)}, u32[]{:S(2)}, u32[]{:S(2)}) %collective-permute-start.7) | collective-permute-done | bytes 884768 | tf_op jit(solution)/shard_map/ppermute | solution.py:18
  54.7 1.7 slice.98
  56.4 3.2 %collective-permute-start.9 = (bf16[384,384]{0,1:T(8,128)(2,1)}, bf16[384,384]{0,1:T(8,128)(2,1)S(1)}, u32[]{:S(2)}, u32[]{:S(2)}) collective-permute-start(bf16[384,384]{0,1:T(8,128)(2,1)} %slice.98), channel_id=1, source_target_pairs={{0,24},{8,0},{16,8},{24,16},{1,25},{9,1},{17,9},{25,17},{2,26},{10... | collective-permute-start | bytes 884744 | tf_op jit(solution)/shard_map/ppermute | solution.py:18
  61.1 1.5 collective-permute-start.5
  62.6 2.7 %collective-permute-start.4 = (bf16[384,768]{1,0:T(8,128)(2,1)S(1)}, bf16[384,768]{1,0:T(8,128)(2,1)S(1)}, u32[]{:S(2)}, u32[]{:S(2)}) collective-permute-start(bf16[384,768]{1,0:T(8,128)(2,1)S(1)} %bitcast.92), channel_id=1, source_target_pairs={{0,64},{32,96},{64,0},{96,32},{1,65},{33,97},{65,1},{97,33},{2,66}... | collective-permute-start | bytes 1769480 | tf_op jit(solution)/shard_map/ppermute | solution.py:18
  66.7 1.9 fusion.7
  68.7 2.8 %collective-permute-done.8 = bf16[384,384]{0,1:T(8,128)(2,1)S(1)} collective-permute-done((bf16[384,384]{0,1:T(8,128)(2,1)S(1)}, bf16[384,384]{0,1:T(8,128)(2,1)S(1)}, u32[]{:S(2)}, u32[]{:S(2)}) %collective-permute-start.8) | collective-permute-done | bytes 294944 | tf_op jit(solution)/shard_map/ppermute | solution.py:18
  71.5 1.5 collective-permute-done.9
  75.6 2.0 fusion.8
  79.3 1.8 dynamic-slice_bitcast_fusion.3
  81.0 1.8 pad_maximum_fusion.refs_4_.t_ref
  82.8 7.2 %collective-permute-done.4.refs_2_ = bf16[384,768]{1,0:T(8,128)(2,1)S(1)} collective-permute-done((bf16[384,768]{1,0:T(8,128)(2,1)S(1)}, bf16[384,768]{1,0:T(8,128)(2,1)S(1)}, u32[]{:S(2)}, u32[]{:S(2)}) %collective-permute-start.4) | collective-permute-done | bytes 589856 | tf_op jit(solution)/shard_map/ppermute | solution.py:18
  90.8 10.2 %all-gather.2.cloned.1.call-done = bf16[24576,384]{1,0:T(8,128)(2,1)} async-done(((bf16[768,384]{1,0:T(8,128)(2,1)}), bf16[24576,384]{1,0:T(8,128)(2,1)}) %all-gather.2.cloned.1.call-update) | async-done | bytes 18874384 | tf_op jit(solution)/shard_map/all_gather | solution.py:291
  101.1 19.0 %shard_map.38 = (f32[384,3072]{1,0:T(8,128)}, bf16[384,3072]{1,0:T(8,128)(2,1)}, bf16[384,768]{1,0:T(8,128)(2,1)S(1)}) custom-call(s32[4]{0:T(128)S(1)} %pad_add_fusion.which_ref, bf16[8,3072,384]{2,1,0:T(8,128)(2,1)} %bitcast.95, bf16[384,768]{1,0:T(8,128)(2,1)S(1)} %bitcast.94, bf16[384,768]{1,0:T(8,128)(2,1)S(1)} %collective-permute-done.3.refs_1_, ...), custom_call_target="tpu_custom_call" | custom-call | flops 9059696640 | bytes 31260672 | tf_op jit(solution)/shard_map/pallas_call | solution.py:80
  120.1 1.6 collective-permute-start.10
  121.6 1.8 collective-permute-start.14
  123.4 1.7 copy-done.3
  125.1 7.2 %shard_map.40 = (f32[192,768]{1,0:T(8,128)S(1)}, bf16[192,768]{1,0:T(8,128)(2,1)S(1)}, bf16[192,768]{1,0:T(8,128)(2,1)S(1)}, f32[192,768]{1,0:T(8,128)S(1)}) custom-call(s32[2]{0:T(128)S(1)} %pad_add_fusion.2.which_ref, bf16[8,3072,384]{2,1,0:T(8,128)(2,1)} %bitcast.96, bf16[8,3072,384]{2,1,0:T(8,128)(2,1)} %bitcast.97, bf16[384,3072]{1,0:T(8,128)(2,1)S(1)} %copy-done.3), custom_call_target="tpu_custom_call" | custom-call | flops 3623878656 | bytes 11796480 | tf_op jit(solution)/shard_map/pallas_call | solution.py:193
  132.3 1.6 collective-permute-start.12
  134.9 3.0 %collective-permute-start.15 = (bf16[192,768]{1,0:T(8,128)(2,1)S(1)}, bf16[192,768]{1,0:T(8,128)(2,1)S(1)}, u32[]{:S(2)}, u32[]{:S(2)}) collective-permute-start(bf16[192,768]{1,0:T(8,128)(2,1)S(1)} %add_convert_fusion.2), channel_id=1, source_target_pairs={{0,96},{32,0},{64,32},{96,64},{1,97},{33,1},{65,33},{97,65},{2,98}... | collective-permute-start | bytes 884744 | tf_op jit(solution)/shard_map/ppermute | solution.py:18
  137.9 4.0 %shard_map.39 = f32[384,768]{1,0:T(8,128)S(1)} custom-call(s32[1]{0:T(128)} %bitcast.which_ref, bf16[8,3072,384]{2,1,0:T(8,128)(2,1)} %bitcast.98, bf16[384,3072]{1,0:T(8,128)(2,1)S(1)} %copy-done.3), custom_call_target="tpu_custom_call" | custom-call | flops 1811939328 | bytes 8257536 | tf_op jit(solution)/shard_map/pallas_call | solution.py:193
  142.3 2.7 %collective-permute-done.13 = bf16[192,768]{1,0:T(8,128)(2,1)S(1)} collective-permute-done((bf16[192,768]{1,0:T(8,128)(2,1)S(1)}, bf16[192,768]{1,0:T(8,128)(2,1)S(1)}, u32[]{:S(2)}, u32[]{:S(2)}) %collective-permute-start.13) | collective-permute-done | bytes 294944 | tf_op jit(solution)/shard_map/ppermute | solution.py:18
  145.0 4.7 %collective-permute-done.11 = bf16[192,768]{1,0:T(8,128)(2,1)S(1)} collective-permute-done((bf16[192,768]{1,0:T(8,128)(2,1)S(1)}, bf16[192,768]{1,0:T(8,128)(2,1)S(1)}, u32[]{:S(2)}, u32[]{:S(2)}) %collective-permute-start.11) | collective-permute-done | bytes 294944 | tf_op jit(solution)/shard_map/ppermute | solution.py:18
  150.1 3.2 %collective-permute-start.17 = (bf16[384,768]{1,0:T(8,128)(2,1)S(1)}, bf16[384,768]{1,0:T(8,128)(2,1)S(1)}, u32[]{:S(2)}, u32[]{:S(2)}) collective-permute-start(bf16[384,768]{1,0:T(8,128)(2,1)S(1)} %fusion.1.refs_3_), channel_id=1, source_target_pairs={{0,96},{32,0},{64,32},{96,64},{1,97},{33,1},{65,33},{97,65},{2,98}... | collective-permute-start | bytes 1769480 | tf_op jit(solution)/shard_map/ppermute | solution.py:18
  157.4 6.4 %all-to-all-start = ((f32[64,1,128]{2,1,0:T(1,128)}), f32[64,1,128]{2,1,0:T(1,128)}, u32[]{:S(2)}, u32[]{:S(2)}) async-start(f32[64,1,128]{2,1,0:T(1,128)} %bitcast.27), calls=%async_computation | async-start | bytes 65536 | tf_op jit(solution)/shard_map/all_to_all | solution.py:278
  167.0 2.9 %collective-permute-start.20 = (bf16[192,768]{1,0:T(8,128)(2,1)}, bf16[192,768]{1,0:T(8,128)(2,1)}, u32[]{:S(2)}, u32[]{:S(2)}) collective-permute-start(bf16[192,768]{1,0:T(8,128)(2,1)} %slice.103), channel_id=1, source_target_pairs={{0,96},{32,0},{64,32},{96,64},{1,97},{33,1},{65,33},{97,65},{2,98}... | collective-permute-start | bytes 884744 | tf_op jit(solution)/shard_map/ppermute | solution.py:18
  171.0 11.1 %shard_map.41.part_ref = f32[384,3072]{1,0:T(8,128)} custom-call(s32[3]{0:T(128)S(1)} %pad_add_fusion.3.which_ref, bf16[8,3072,384]{2,1,0:T(8,128)(2,1)} %bitcast.99, bf16[8,3072,384]{2,1,0:T(8,128)(2,1)} %bitcast.100, bf16[8,3072,384]{2,1,0:T(8,128)(2,1)} %bitcast.101, bf16[384,768]{1,0:T(8,128)(2,1)S(1)} %fusion.1.refs_3_, bf16[384,768]{1,0:T(8,128)(2,1)S(1)} %copy-done.5, ...), custom_call_target="tpu_custom_call" | custom-call | flops 5435817984 | bytes 20643840 | tf_op jit(solution)/shard_map/pallas_call | solution.py:113
  185.3 9.7 %shard_map.42 = (bf16[384,3072]{1,0:T(8,128)(2,1)S(1)}, bf16[384,768]{1,0:T(8,128)(2,1)S(1)}) custom-call(s32[1]{0:T(128)} %bitcast.2.which_ref, f32[1,1]{1,0:T(1,128)} %bitcast.29.scale_ref, bf16[8,3072,384]{2,1,0:T(8,128)(2,1)} %bitcast.102, bf16[384,768]{1,0:T(8,128)(2,1)S(1)} %pad_maximum_fusion.3.f_ref, f32[384,3072]{1,0:T(8,128)} %shard_map.41.part_ref, ...), custom_call_target="tpu_custom_call" | custom-call | flops 3623878656 | bytes 15335424 | tf_op jit(solution)/shard_map/pallas_call | solution.py:142
  195.1 3.2 %collective-permute-start.25 = (bf16[192,768]{1,0:T(8,128)(2,1)S(1)}, bf16[192,768]{1,0:T(8,128)(2,1)S(1)}, u32[]{:S(2)}, u32[]{:S(2)}) collective-permute-start(bf16[192,768]{1,0:T(8,128)(2,1)S(1)} %get-tuple-element.64), channel_id=1, source_target_pairs={{0,96},{32,0},{64,32},{96,64},{1,97},{33,1},{65,33},{97,65},{2,98}... | collective-permute-start | bytes 884744 | tf_op jit(solution)/shard_map/ppermute | solution.py:18
  198.4 7.2 %shard_map.44 = (f32[192,768]{1,0:T(8,128)S(1)}, bf16[192,768]{1,0:T(8,128)(2,1)S(1)}, bf16[192,768]{1,0:T(8,128)(2,1)S(1)}, f32[192,768]{1,0:T(8,128)S(1)}) custom-call(s32[2]{0:T(128)S(1)} %pad_add_fusion.2.which_ref, bf16[8,3072,384]{2,1,0:T(8,128)(2,1)} %bitcast.103, bf16[8,3072,384]{2,1,0:T(8,128)(2,1)} %bitcast.104, ...), custom_call_target="tpu_custom_call" | custom-call | flops 3623878656 | bytes 11796480 | tf_op jit(solution)/shard_map/pallas_call | solution.py:193
  205.7 2.0 collective-permute-start.24
  209.3 3.2 %collective-permute-start.26 = (bf16[192,768]{1,0:T(8,128)(2,1)}, bf16[192,768]{1,0:T(8,128)(2,1)}, u32[]{:S(2)}, u32[]{:S(2)}) collective-permute-start(bf16[192,768]{1,0:T(8,128)(2,1)} %add_convert_fusion), channel_id=1, source_target_pairs={{0,96},{32,0},{64,32},{96,64},{1,97},{33,1},{65,33},{97,65},{2,98}... | collective-permute-start | bytes 884744 | tf_op jit(solution)/shard_map/ppermute | solution.py:18
  212.5 4.0 %shard_map.43 = f32[384,768]{1,0:T(8,128)S(1)} custom-call(s32[1]{0:T(128)} %bitcast.which_ref, bf16[8,3072,384]{2,1,0:T(8,128)(2,1)} %bitcast.105, bf16[384,3072]{1,0:T(8,128)(2,1)S(1)} %copy-done.2), custom_call_target="tpu_custom_call" | custom-call | flops 1811939328 | bytes 8257536 | tf_op jit(solution)/shard_map/pallas_call | solution.py:193
  216.6 3.3 %collective-permute-done.22 = bf16[192,768]{1,0:T(8,128)(2,1)} collective-permute-done((bf16[192,768]{1,0:T(8,128)(2,1)}, bf16[192,768]{1,0:T(8,128)(2,1)}, u32[]{:S(2)}, u32[]{:S(2)}) %collective-permute-start.22) | collective-permute-done | bytes 294944 | tf_op jit(solution)/shard_map/ppermute | solution.py:18
  223.3 2.7 %collective-permute-start.27 = (bf16[192,384]{1,0:T(8,128)(2,1)S(1)}, bf16[192,384]{1,0:T(8,128)(2,1)S(1)}, u32[]{:S(2)}, u32[]{:S(2)}) collective-permute-start(bf16[192,384]{1,0:T(8,128)(2,1)S(1)} %get-tuple-element.62), channel_id=1, source_target_pairs={{0,24},{8,0},{16,8},{24,16},{1,25},{9,1},{17,9},{25,17},{2,26},{10... | collective-permute-start | bytes 442376 | tf_op jit(solution)/shard_map/ppermute | solution.py:18
  227.2 6.0 %all-to-all-start.1 = ((f32[64,1,128]{2,1,0:T(1,128)}), f32[64,1,128]{2,1,0:T(1,128)S(1)}, u32[]{:S(2)}, u32[]{:S(2)}) async-start(f32[64,1,128]{2,1,0:T(1,128)} %bitcast.42), calls=%async_computation.1 | async-start | bytes 65536 | tf_op jit(solution)/shard_map/all_to_all | solution.py:278
  233.3 1.6 collective-permute-start.29
  234.9 2.7 %collective-permute-start.28 = (bf16[192,384]{1,0:T(8,128)(2,1)S(1)}, bf16[192,384]{1,0:T(8,128)(2,1)S(1)}, u32[]{:S(2)}, u32[]{:S(2)}) collective-permute-start(bf16[192,384]{1,0:T(8,128)(2,1)S(1)} %get-tuple-element.61), channel_id=1, source_target_pairs={{0,16},{8,24},{16,0},{24,8},{1,17},{9,25},{17,1},{25,9},{2,18},{10... | collective-permute-start | bytes 442376 | tf_op jit(solution)/shard_map/ppermute | solution.py:18
  237.6 5.2 %all-to-all-done.1 = f32[64,1,128]{2,1,0:T(1,128)S(1)} async-done(((f32[64,1,128]{2,1,0:T(1,128)}), f32[64,1,128]{2,1,0:T(1,128)S(1)}, u32[]{:S(2)}, u32[]{:S(2)}) %all-to-all-start.1) | async-done | bytes 32800 | tf_op jit(solution)/shard_map/all_to_all | solution.py:278
  (109 shorter events, 37.3 us)
Async XLA Ops:
  6.5 94.6 %all-gather.2.cloned.1.call-start = ((), (), s32[]{:S(2)}) async-start(), calls=%async_computation.2 | async-start | bytes 19464192 | tf_op jit(solution)/shard_map/all_gather | solution.py:291
  9.2 11.5 %collective-permute-start.2 = (bf16[192,384]{1,0:T(8,128)(2,1)}, bf16[192,384]{1,0:T(8,128)(2,1)S(1)}, u32[]{:S(2)}, u32[]{:S(2)}) collective-permute-start(bf16[192,384]{1,0:T(8,128)(2,1)} %get-tuple-element.67), channel_id=1, source_target_pairs={{0,8},{8,16},{16,24},{24,0},{1,9},{9,17},{17,25},{25,1},{2,10},{10... | collective-permute-start | bytes 442376 | tf_op jit(solution)/shard_map/ppermute | solution.py:18
  10.8 9.8 %collective-permute-start = (bf16[192,384]{1,0:T(8,128)(2,1)}, bf16[192,384]{1,0:T(8,128)(2,1)S(1)}, u32[]{:S(2)}, u32[]{:S(2)}) collective-permute-start(bf16[192,384]{1,0:T(8,128)(2,1)} %get-tuple-element.68), channel_id=1, source_target_pairs={{0,24},{8,0},{16,8},{24,16},{1,25},{9,1},{17,9},{25,17},{2,26},{10... | collective-permute-start | bytes 442376 | tf_op jit(solution)/shard_map/ppermute | solution.py:18
  12.4 8.3 %collective-permute-start.1 = (bf16[192,384]{1,0:T(8,128)(2,1)}, bf16[192,384]{1,0:T(8,128)(2,1)S(1)}, u32[]{:S(2)}, u32[]{:S(2)}) collective-permute-start(bf16[192,384]{1,0:T(8,128)(2,1)} %get-tuple-element.69), channel_id=1, source_target_pairs={{0,16},{8,24},{16,0},{24,8},{1,17},{9,25},{17,1},{25,9},{2,18},{10... | collective-permute-start | bytes 442376 | tf_op jit(solution)/shard_map/ppermute | solution.py:18
  17.8 2.9 %copy-start.6 = (bf16[1152,384]{1,0:T(8,128)(2,1)S(1)}, bf16[1152,384]{1,0:T(8,128)(2,1)}, u32[]{:S(2)}) copy-start(bf16[1152,384]{1,0:T(8,128)(2,1)} %get-tuple-element.28) | copy-start | bytes 2654212
  23.8 30.8 %collective-permute-start.7 = (bf16[1152,384]{0,1:T(8,128)(2,1)}, bf16[1152,384]{0,1:T(8,128)(2,1)S(1)}, u32[]{:S(2)}, u32[]{:S(2)}) collective-permute-start(bf16[1152,384]{0,1:T(8,128)(2,1)} %copy.20), channel_id=1, source_target_pairs={{0,8},{8,16},{16,24},{24,0},{1,9},{9,17},{17,25},{25,1},{2,10},{10... | collective-permute-start | bytes 2654216 | tf_op jit(solution)/shard_map/ppermute | solution.py:18
  24.9 29.8 %collective-permute-start.6 = (bf16[1152,384]{0,1:T(8,128)(2,1)}, bf16[1152,384]{0,1:T(8,128)(2,1)}, u32[]{:S(2)}, u32[]{:S(2)}) collective-permute-start(bf16[1152,384]{0,1:T(8,128)(2,1)} %copy.19), channel_id=1, source_target_pairs={{0,24},{8,0},{16,8},{24,16},{1,25},{9,1},{17,9},{25,17},{2,26},{10... | collective-permute-start | bytes 2654216 | tf_op jit(solution)/shard_map/ppermute | solution.py:18
  54.6 16.9 %collective-permute-start.8 = (bf16[384,384]{0,1:T(8,128)(2,1)S(1)}, bf16[384,384]{0,1:T(8,128)(2,1)S(1)}, u32[]{:S(2)}, u32[]{:S(2)}) collective-permute-start(bf16[384,384]{0,1:T(8,128)(2,1)S(1)} %slice.97), channel_id=1, source_target_pairs={{0,8},{8,16},{16,24},{24,0},{1,9},{9,17},{17,25},{25,1},{2,10},{10... | collective-permute-start | bytes 884744 | tf_op jit(solution)/shard_map/ppermute | solution.py:18
  56.4 16.6 %collective-permute-start.9 = (bf16[384,384]{0,1:T(8,128)(2,1)}, bf16[384,384]{0,1:T(8,128)(2,1)S(1)}, u32[]{:S(2)}, u32[]{:S(2)}) collective-permute-start(bf16[384,384]{0,1:T(8,128)(2,1)} %slice.98), channel_id=1, source_target_pairs={{0,24},{8,0},{16,8},{24,16},{1,25},{9,1},{17,9},{25,17},{2,26},{10... | collective-permute-start | bytes 884744 | tf_op jit(solution)/shard_map/ppermute | solution.py:18
  61.1 21.7 %collective-permute-start.5 = (bf16[384,768]{1,0:T(8,128)(2,1)S(1)}, bf16[384,768]{1,0:T(8,128)(2,1)S(1)}, u32[]{:S(2)}, u32[]{:S(2)}) collective-permute-start(bf16[384,768]{1,0:T(8,128)(2,1)S(1)} %bitcast.91), channel_id=1, source_target_pairs={{0,32},{32,64},{64,96},{96,0},{1,33},{33,65},{65,97},{97,1},{2,34}... | collective-permute-start | bytes 1769480 | tf_op jit(solution)/shard_map/ppermute | solution.py:18
  62.6 27.4 %collective-permute-start.4 = (bf16[384,768]{1,0:T(8,128)(2,1)S(1)}, bf16[384,768]{1,0:T(8,128)(2,1)S(1)}, u32[]{:S(2)}, u32[]{:S(2)}) collective-permute-start(bf16[384,768]{1,0:T(8,128)(2,1)S(1)} %bitcast.92), channel_id=1, source_target_pairs={{0,64},{32,96},{64,0},{96,32},{1,65},{33,97},{65,1},{97,33},{2,66}... | collective-permute-start | bytes 1769480 | tf_op jit(solution)/shard_map/ppermute | solution.py:18
  65.3 25.5 %collective-permute-start.3 = (bf16[384,768]{1,0:T(8,128)(2,1)S(1)}, bf16[384,768]{1,0:T(8,128)(2,1)S(1)}, u32[]{:S(2)}, u32[]{:S(2)}) collective-permute-start(bf16[384,768]{1,0:T(8,128)(2,1)S(1)} %bitcast.93), channel_id=1, source_target_pairs={{0,96},{32,0},{64,32},{96,64},{1,97},{33,1},{65,33},{97,65},{2,98}... | collective-permute-start | bytes 1769480 | tf_op jit(solution)/shard_map/ppermute | solution.py:18
  82.8 7.2 %copy-start.7 = (bf16[384,768]{1,0:T(8,128)(2,1)}, bf16[384,768]{1,0:T(8,128)(2,1)S(1)}, u32[]{:S(2)}) copy-start(bf16[384,768]{1,0:T(8,128)(2,1)S(1)} %collective-permute-done.5.refs_3_) | copy-start | bytes 1769476
  90.0 0.8 copy-start.8
  120.1 14.3 %collective-permute-start.10 = (bf16[192,768]{1,0:T(8,128)(2,1)S(1)}, bf16[192,768]{1,0:T(8,128)(2,1)S(1)}, u32[]{:S(2)}, u32[]{:S(2)}) collective-permute-start(bf16[192,768]{1,0:T(8,128)(2,1)S(1)} %get-tuple-element.65), channel_id=1, source_target_pairs={{0,32},{32,64},{64,96},{96,0},{1,33},{33,65},{65,97},{97,1},{2,34}... | collective-permute-start | bytes 884744 | tf_op jit(solution)/shard_map/ppermute | solution.py:18
  121.6 13.2 %collective-permute-start.14 = (bf16[192,768]{1,0:T(8,128)(2,1)S(1)}, bf16[192,768]{1,0:T(8,128)(2,1)S(1)}, u32[]{:S(2)}, u32[]{:S(2)}) collective-permute-start(bf16[192,768]{1,0:T(8,128)(2,1)S(1)} %get-tuple-element.66), channel_id=1, source_target_pairs={{0,96},{32,0},{64,32},{96,64},{1,97},{33,1},{65,33},{97,65},{2,98}... | collective-permute-start | bytes 884744 | tf_op jit(solution)/shard_map/ppermute | solution.py:18
  123.4 1.7 copy-start.3
  132.3 10.0 %collective-permute-start.12 = (bf16[192,768]{1,0:T(8,128)(2,1)S(1)}, bf16[192,768]{1,0:T(8,128)(2,1)S(1)}, u32[]{:S(2)}, u32[]{:S(2)}) collective-permute-start(bf16[192,768]{1,0:T(8,128)(2,1)S(1)} %get-tuple-element.33), channel_id=1, source_target_pairs={{0,96},{32,0},{64,32},{96,64},{1,97},{33,1},{65,33},{97,65},{2,98}... | collective-permute-start | bytes 884744 | tf_op jit(solution)/shard_map/ppermute | solution.py:18
  133.9 11.2 %collective-permute-start.13 = (bf16[192,768]{1,0:T(8,128)(2,1)S(1)}, bf16[192,768]{1,0:T(8,128)(2,1)S(1)}, u32[]{:S(2)}, u32[]{:S(2)}) collective-permute-start(bf16[192,768]{1,0:T(8,128)(2,1)S(1)} %get-tuple-element.34), channel_id=1, source_target_pairs={{0,32},{32,64},{64,96},{96,0},{1,33},{33,65},{65,97},{97,1},{2,34}... | collective-permute-start | bytes 884744 | tf_op jit(solution)/shard_map/ppermute | solution.py:18
  134.5 15.3 %collective-permute-start.11 = (bf16[192,768]{1,0:T(8,128)(2,1)S(1)}, bf16[192,768]{1,0:T(8,128)(2,1)S(1)}, u32[]{:S(2)}, u32[]{:S(2)}) collective-permute-start(bf16[192,768]{1,0:T(8,128)(2,1)S(1)} %add_convert_fusion.3), channel_id=1, source_target_pairs={{0,32},{32,64},{64,96},{96,0},{1,33},{33,65},{65,97},{97,1},{2,34}... | collective-permute-start | bytes 884744 | tf_op jit(solution)/shard_map/ppermute | solution.py:18
  134.9 14.9 %collective-permute-start.15 = (bf16[192,768]{1,0:T(8,128)(2,1)S(1)}, bf16[192,768]{1,0:T(8,128)(2,1)S(1)}, u32[]{:S(2)}, u32[]{:S(2)}) collective-permute-start(bf16[192,768]{1,0:T(8,128)(2,1)S(1)} %add_convert_fusion.2), channel_id=1, source_target_pairs={{0,96},{32,0},{64,32},{96,64},{1,97},{33,1},{65,33},{97,65},{2,98}... | collective-permute-start | bytes 884744 | tf_op jit(solution)/shard_map/ppermute | solution.py:18
  150.0 15.0 %collective-permute-start.18 = (bf16[384,768]{1,0:T(8,128)(2,1)S(1)}, bf16[384,768]{1,0:T(8,128)(2,1)S(1)}, u32[]{:S(2)}, u32[]{:S(2)}) collective-permute-start(bf16[384,768]{1,0:T(8,128)(2,1)S(1)} %fusion.1.refs_3_), channel_id=1, source_target_pairs={{0,32},{32,64},{64,96},{96,0},{1,33},{33,65},{65,97},{97,1},{2,34}... | collective-permute-start | bytes 1769480 | tf_op jit(solution)/shard_map/ppermute | solution.py:18
  150.1 16.0 %collective-permute-start.17 = (bf16[384,768]{1,0:T(8,128)(2,1)S(1)}, bf16[384,768]{1,0:T(8,128)(2,1)S(1)}, u32[]{:S(2)}, u32[]{:S(2)}) collective-permute-start(bf16[384,768]{1,0:T(8,128)(2,1)S(1)} %fusion.1.refs_3_), channel_id=1, source_target_pairs={{0,96},{32,0},{64,32},{96,64},{1,97},{33,1},{65,33},{97,65},{2,98}... | collective-permute-start | bytes 1769480 | tf_op jit(solution)/shard_map/ppermute | solution.py:18
  154.9 1.3 collective-permute-start.16
  157.4 24.7 %all-to-all-start = ((f32[64,1,128]{2,1,0:T(1,128)}), f32[64,1,128]{2,1,0:T(1,128)}, u32[]{:S(2)}, u32[]{:S(2)}) async-start(f32[64,1,128]{2,1,0:T(1,128)} %bitcast.27), calls=%async_computation | async-start | bytes 65536 | tf_op jit(solution)/shard_map/all_to_all | solution.py:278
  165.7 18.4 %collective-permute-start.19 = (bf16[192,768]{1,0:T(8,128)(2,1)}, bf16[192,768]{1,0:T(8,128)(2,1)}, u32[]{:S(2)}, u32[]{:S(2)}) collective-permute-start(bf16[192,768]{1,0:T(8,128)(2,1)} %slice.102), channel_id=1, source_target_pairs={{0,32},{32,64},{64,96},{96,0},{1,33},{33,65},{65,97},{97,1},{2,34}... | collective-permute-start | bytes 884744 | tf_op jit(solution)/shard_map/ppermute | solution.py:18
  166.1 0.9 copy-start.4
  167.0 17.2 %collective-permute-start.20 = (bf16[192,768]{1,0:T(8,128)(2,1)}, bf16[192,768]{1,0:T(8,128)(2,1)}, u32[]{:S(2)}, u32[]{:S(2)}) collective-permute-start(bf16[192,768]{1,0:T(8,128)(2,1)} %slice.103), channel_id=1, source_target_pairs={{0,96},{32,0},{64,32},{96,64},{1,97},{33,1},{65,33},{97,65},{2,98}... | collective-permute-start | bytes 884744 | tf_op jit(solution)/shard_map/ppermute | solution.py:18
  169.9 1.1 copy-start.5
  171.0 14.3 %copy-start = (bf16[384,3072]{1,0:T(8,128)(2,1)S(1)}, bf16[384,3072]{1,0:T(8,128)(2,1)}, u32[]{:S(2)}) copy-start(bf16[384,3072]{1,0:T(8,128)(2,1)} %pad_maximum_fusion.refs_4_.t_ref) | copy-start | bytes 7077892
  195.0 10.6 %copy-start.1 = (bf16[384,3072]{1,0:T(8,128)(2,1)}, bf16[384,3072]{1,0:T(8,128)(2,1)S(1)}, u32[]{:S(2)}) copy-start(bf16[384,3072]{1,0:T(8,128)(2,1)S(1)} %get-tuple-element.39.refs_1_.refs_2_) | copy-start | bytes 7077892
  195.1 12.7 %collective-permute-start.21 = (bf16[192,768]{1,0:T(8,128)(2,1)S(1)}, bf16[192,768]{1,0:T(8,128)(2,1)S(1)}, u32[]{:S(2)}, u32[]{:S(2)}) collective-permute-start(bf16[192,768]{1,0:T(8,128)(2,1)S(1)} %get-tuple-element.63), channel_id=1, source_target_pairs={{0,32},{32,64},{64,96},{96,0},{1,33},{33,65},{65,97},{97,1},{2,34}... | collective-permute-start | bytes 884744 | tf_op jit(solution)/shard_map/ppermute | solution.py:18
  195.1 13.3 %collective-permute-start.25 = (bf16[192,768]{1,0:T(8,128)(2,1)S(1)}, bf16[192,768]{1,0:T(8,128)(2,1)S(1)}, u32[]{:S(2)}, u32[]{:S(2)}) collective-permute-start(bf16[192,768]{1,0:T(8,128)(2,1)S(1)} %get-tuple-element.64), channel_id=1, source_target_pairs={{0,96},{32,0},{64,32},{96,64},{1,97},{33,1},{65,33},{97,65},{2,98}... | collective-permute-start | bytes 884744 | tf_op jit(solution)/shard_map/ppermute | solution.py:18
  205.6 10.9 %collective-permute-start.23 = (bf16[192,768]{1,0:T(8,128)(2,1)S(1)}, bf16[192,768]{1,0:T(8,128)(2,1)S(1)}, u32[]{:S(2)}, u32[]{:S(2)}) collective-permute-start(bf16[192,768]{1,0:T(8,128)(2,1)S(1)} %get-tuple-element.42), channel_id=1, source_target_pairs={{0,96},{32,0},{64,32},{96,64},{1,97},{33,1},{65,33},{97,65},{2,98}... | collective-permute-start | bytes 884744 | tf_op jit(solution)/shard_map/ppermute | solution.py:18
  205.7 10.9 %collective-permute-start.24 = (bf16[192,768]{1,0:T(8,128)(2,1)S(1)}, bf16[192,768]{1,0:T(8,128)(2,1)S(1)}, u32[]{:S(2)}, u32[]{:S(2)}) collective-permute-start(bf16[192,768]{1,0:T(8,128)(2,1)S(1)} %get-tuple-element.43), channel_id=1, source_target_pairs={{0,32},{32,64},{64,96},{96,0},{1,33},{33,65},{65,97},{97,1},{2,34}... | collective-permute-start | bytes 884744 | tf_op jit(solution)/shard_map/ppermute | solution.py:18
  207.7 4.8 %copy-start.2 = (bf16[384,3072]{1,0:T(8,128)(2,1)S(1)}, bf16[384,3072]{1,0:T(8,128)(2,1)}, u32[]{:S(2)}) copy-start(bf16[384,3072]{1,0:T(8,128)(2,1)} %copy-done.1) | copy-start | bytes 7077892
  208.5 11.4 %collective-permute-start.22 = (bf16[192,768]{1,0:T(8,128)(2,1)}, bf16[192,768]{1,0:T(8,128)(2,1)}, u32[]{:S(2)}, u32[]{:S(2)}) collective-permute-start(bf16[192,768]{1,0:T(8,128)(2,1)} %add_convert_fusion.1), channel_id=1, source_target_pairs={{0,32},{32,64},{64,96},{96,0},{1,33},{33,65},{65,97},{97,1},{2,34}... | collective-permute-start | bytes 884744 | tf_op jit(solution)/shard_map/ppermute | solution.py:18
  209.3 10.6 %collective-permute-start.26 = (bf16[192,768]{1,0:T(8,128)(2,1)}, bf16[192,768]{1,0:T(8,128)(2,1)}, u32[]{:S(2)}, u32[]{:S(2)}) collective-permute-start(bf16[192,768]{1,0:T(8,128)(2,1)} %add_convert_fusion), channel_id=1, source_target_pairs={{0,96},{32,0},{64,32},{96,64},{1,97},{33,1},{65,33},{97,65},{2,98}... | collective-permute-start | bytes 884744 | tf_op jit(solution)/shard_map/ppermute | solution.py:18
  223.1 2.9 %collective-permute-start.30 = (f32[64,128]{1,0:T(8,128)S(1)}, f32[64,128]{1,0:T(8,128)S(1)}, u32[]{:S(2)}, u32[]{:S(2)}) collective-permute-start(f32[64,128]{1,0:T(8,128)S(1)} %broadcast_in_dim.7), channel_id=1, source_target_pairs={{0,1},{1,0},{2,3},{3,2},{4,5},{5,4},{6,7},{7,6},{8,9},{9,8},{10,11... | collective-permute-start | bytes 98312 | tf_op jit(solution)/shard_map/ppermute | solution.py:277
  223.3 20.8 %collective-permute-start.27 = (bf16[192,384]{1,0:T(8,128)(2,1)S(1)}, bf16[192,384]{1,0:T(8,128)(2,1)S(1)}, u32[]{:S(2)}, u32[]{:S(2)}) collective-permute-start(bf16[192,384]{1,0:T(8,128)(2,1)S(1)} %get-tuple-element.62), channel_id=1, source_target_pairs={{0,24},{8,0},{16,8},{24,16},{1,25},{9,1},{17,9},{25,17},{2,26},{10... | collective-permute-start | bytes 442376 | tf_op jit(solution)/shard_map/ppermute | solution.py:18
  227.2 15.5 %all-to-all-start.1 = ((f32[64,1,128]{2,1,0:T(1,128)}), f32[64,1,128]{2,1,0:T(1,128)S(1)}, u32[]{:S(2)}, u32[]{:S(2)}) async-start(f32[64,1,128]{2,1,0:T(1,128)} %bitcast.42), calls=%async_computation.1 | async-start | bytes 65536 | tf_op jit(solution)/shard_map/all_to_all | solution.py:278
  233.3 11.1 %collective-permute-start.29 = (bf16[192,384]{1,0:T(8,128)(2,1)S(1)}, bf16[192,384]{1,0:T(8,128)(2,1)S(1)}, u32[]{:S(2)}, u32[]{:S(2)}) collective-permute-start(bf16[192,384]{1,0:T(8,128)(2,1)S(1)} %get-tuple-element.59), channel_id=1, source_target_pairs={{0,8},{8,16},{16,24},{24,0},{1,9},{9,17},{17,25},{25,1},{2,10},{10... | collective-permute-start | bytes 442376 | tf_op jit(solution)/shard_map/ppermute | solution.py:18
  234.9 9.4 %collective-permute-start.28 = (bf16[192,384]{1,0:T(8,128)(2,1)S(1)}, bf16[192,384]{1,0:T(8,128)(2,1)S(1)}, u32[]{:S(2)}, u32[]{:S(2)}) collective-permute-start(bf16[192,384]{1,0:T(8,128)(2,1)S(1)} %get-tuple-element.61), channel_id=1, source_target_pairs={{0,16},{8,24},{16,0},{24,8},{1,17},{9,25},{17,1},{25,9},{2,18},{10... | collective-permute-start | bytes 442376 | tf_op jit(solution)/shard_map/ppermute | solution.py:18
Sparse Core Ops, SparseCore 0:
  9.6 91.4 all-gather.1

commit v14 on v5

--- a/solution.py
+++ b/solution.py
@@ -66,11 +66,15 @@
     whole = pl.BlockSpec((cols, deep), lambda i, which: (0, 0), pipeline_mode=pl.Buffered(1))
 
     def kernel(which_ref, x_ref, *refs):
-        w_refs, (t_ref, h_ref, s_ref, far_ref, total_ref) = refs[:N], refs[N:]
+        w_refs, (t_ref, h_ref, s_ref, far_ref, total_ref, w_all) = refs[:N], refs[N:]
+
+        @pl.when(pl.program_id(0) == 0)
+        def _():
+            w_all[...] = jnp.concatenate([w_ref[...] for w_ref in w_refs], axis=1)
+
         block = lambda j: [x_ref[per * which_ref[j] + k] for k in range(per)]
         x = jnp.concatenate([part for j in range(N) for part in block(j)], axis=1)
-        w = jnp.concatenate([w_ref[...] for w_ref in w_refs], axis=1)
-        hidden = lax.dot_general(w, x, NT, preferred_element_type=F32)
+        hidden = lax.dot_general(w_all[...], x, NT, preferred_element_type=F32)
         h_ref[...] = hidden
         s = slope_of(hidden, t_ref[...])
         s_ref[...] = s
@@ -83,7 +87,7 @@
             grid=(N,),
             in_specs=[pl.BlockSpec((blocks, tile, wide), lambda i, which: (0, i, 0))] + [whole] * N + [out],
             out_specs=[out, out, pl.BlockSpec((cols, deep), lambda i, which: (0, 0))],
-            scratch_shapes=[pltpu.VMEM((cols, deep), F32)],
+            scratch_shapes=[pltpu.VMEM((cols, deep), F32), pltpu.VMEM((cols, N * deep), BF16)],
         ),
         out_shape=[
             jax.ShapeDtypeStruct((cols, rows), F32),

time: 248 us -> 248 us (level)
  no operation moved by 1% of the time
where the time goes in v14:
time: 248 us
  Pallas kernels  68.3 us (28%)
  waiting for transfers between devices  62.4 us (25%)
  starting transfers between devices  61.3 us (25%)
  local copies, waits for them, and re-layouts  27.1 us (11%)
  between operations  15.2 us (6%)
  other arithmetic  13.4 us (5%)
    ppermute x29, starting transfers between devices, shift(): return lax.ppermute(value, axis, [(i, (i + step) % N) for i in range(N)])  48.9 us
    ppermute x29, waiting for transfers between devices, shift(): return lax.ppermute(value, axis, [(i, (i + step) % N) for i in range(N)])  44.5 us
    pallas_call x4, Pallas kernels, terms(): pl.pallas_call(kernel, grid_spec=pltpu.PrefetchScalarGridSpec(num_scalar_...  23.8 us
    pallas_call x1, Pallas kernels, first_slopes(): pl.pallas_call(kernel, grid_spec=pltpu.PrefetchScalarGridSpec(num_scalar_...  19.2 us
    unnamed x26, local copies, waits for them, and re-layouts  13.7 us
    all_to_all x2, starting transfers between devices, total_of(): lax.all_to_all(total, ('x', 'y', 'z'), split_axis=0, concat_axis=0, tiled...  12.3 us
    pallas_call x1, Pallas kernels, moved(): pl.pallas_call(kernel, grid_spec=pltpu.PrefetchScalarGridSpec(num_scalar_...  11 us
    pallas_call x1, Pallas kernels, second_slopes(): pl.pallas_call(kernel, grid_spec=pltpu.PrefetchScalarGridSpec(num_scalar_...  11 us
  transfers between devices with their start and end apart: 34, of which 14 were waited for; matrix products, arithmetic and copies ran while one was open for 14% of the time, Pallas kernels for 15%

profile of v14, /device:TPU:0, one launch (start us, length us, event | category | flops | bytes accessed | tf_op | source)
XLA Modules:
  0.0 247.8 jit_solution(11415981232878227916)
XLA Ops:
  7.3 1.8 constant_dynamic-slice_fusion.1
  9.1 1.7 collective-permute-start.2
  10.7 1.6 collective-permute-start
  12.3 2.1 collective-permute-start.1
  14.5 3.2 %shard_map.37 = (bf16[1152,384]{1,0:T(8,128)(2,1)S(1)}, bf16[1152,384]{1,0:T(8,128)(2,1)}, bf16[768,384]{1,0:T(8,128)(2,1)S(1)}) custom-call(s32[4]{0:T(128)S(1)} %pad_add_fusion.1.which_ref, bf16[768,1536]{1,0:T(8,128)(2,1)} %before.1, bf16[768,1536]{1,0:T(8,128)(2,1)} %before.1, bf16[768,1536]{1,0:T(8,128)(2,1)} %before.1, bf16[768,1536]{1,0:T(8,128)(2,1)} %before.1), custom_call_target="tpu_custom_call" | custom-call | tf_op jit(solution)/shard_map/pallas_call | solution.py:252
  18.9 1.6 bitcast_dynamic-update-slice_fusion.14
  20.7 1.6 copy.19
  22.2 1.5 copy.20
  24.7 2.3 collective-permute-start.6
  27.7 1.6 bitcast_dynamic-update-slice_fusion.10
  29.9 1.6 bitcast_dynamic-update-slice_fusion.15
  32.2 1.6 bitcast_dynamic-update-slice_fusion.11
  34.4 20.1 %collective-permute-done.7 = bf16[1152,384]{0,1:T(8,128)(2,1)S(1)} collective-permute-done((bf16[1152,384]{0,1:T(8,128)(2,1)}, bf16[1152,384]{0,1:T(8,128)(2,1)S(1)}, u32[]{:S(2)}, u32[]{:S(2)}) %collective-permute-start.7) | collective-permute-done | bytes 884768 | tf_op jit(solution)/shard_map/ppermute | solution.py:17
  56.1 3.2 %collective-permute-start.9 = (bf16[384,384]{0,1:T(8,128)(2,1)}, bf16[384,384]{0,1:T(8,128)(2,1)}, u32[]{:S(2)}, u32[]{:S(2)}) collective-permute-start(bf16[384,384]{0,1:T(8,128)(2,1)} %slice.98), channel_id=1, source_target_pairs={{0,24},{8,0},{16,8},{24,16},{1,25},{9,1},{17,9},{25,17},{2,26},{10... | collective-permute-start | bytes 884744 | tf_op jit(solution)/shard_map/ppermute | solution.py:17
  60.9 1.5 collective-permute-start.5
  62.4 2.7 %collective-permute-start.4 = (bf16[384,768]{1,0:T(8,128)(2,1)S(1)}, bf16[384,768]{1,0:T(8,128)(2,1)S(1)}, u32[]{:S(2)}, u32[]{:S(2)}) collective-permute-start(bf16[384,768]{1,0:T(8,128)(2,1)S(1)} %bitcast.92), channel_id=1, source_target_pairs={{0,64},{32,96},{64,0},{96,32},{1,65},{33,97},{65,1},{97,33},{2,66}... | collective-permute-start | bytes 1769480 | tf_op jit(solution)/shard_map/ppermute | solution.py:17
  67.4 5.1 %collective-permute-done.8 = bf16[384,384]{0,1:T(8,128)(2,1)} collective-permute-done((bf16[384,384]{0,1:T(8,128)(2,1)}, bf16[384,384]{0,1:T(8,128)(2,1)}, u32[]{:S(2)}, u32[]{:S(2)}) %collective-permute-start.8) | collective-permute-done | bytes 294944 | tf_op jit(solution)/shard_map/ppermute | solution.py:17
  72.7 1.9 fusion.11
  77.3 1.9 fusion.12
  80.0 1.8 dynamic-slice_bitcast_fusion.3
  81.8 1.8 pad_maximum_fusion.refs_4_.t_ref
  83.6 6.1 %collective-permute-done.4.refs_2_ = bf16[384,768]{1,0:T(8,128)(2,1)S(1)} collective-permute-done((bf16[384,768]{1,0:T(8,128)(2,1)S(1)}, bf16[384,768]{1,0:T(8,128)(2,1)S(1)}, u32[]{:S(2)}, u32[]{:S(2)}) %collective-permute-start.4) | collective-permute-done | bytes 589856 | tf_op jit(solution)/shard_map/ppermute | solution.py:17
  90.5 11.0 %all-gather.2.cloned.1.call-done = bf16[24576,384]{1,0:T(8,128)(2,1)} async-done(((bf16[768,384]{1,0:T(8,128)(2,1)}), bf16[24576,384]{1,0:T(8,128)(2,1)}) %all-gather.2.cloned.1.call-update) | async-done | bytes 18874384 | tf_op jit(solution)/shard_map/all_gather | solution.py:294
  101.4 19.2 %shard_map.38 = (f32[384,3072]{1,0:T(8,128)}, bf16[384,3072]{1,0:T(8,128)(2,1)}, bf16[384,768]{1,0:T(8,128)(2,1)S(1)}) custom-call(s32[4]{0:T(128)S(1)} %pad_add_fusion.which_ref, bf16[8,3072,384]{2,1,0:T(8,128)(2,1)} %bitcast.95, bf16[384,768]{1,0:T(8,128)(2,1)S(1)} %bitcast.94, bf16[384,768]{1,0:T(8,128)(2,1)S(1)} %collective-permute-done.3.refs_1_, ...), custom_call_target="tpu_custom_call" | custom-call | flops 9059696640 | bytes 31260672 | tf_op jit(solution)/shard_map/pallas_call | solution.py:83
  120.7 1.5 collective-permute-start.10
  122.2 1.8 collective-permute-start.14
  124.0 7.6 %shard_map.40 = (f32[192,768]{1,0:T(8,128)S(1)}, bf16[192,768]{1,0:T(8,128)(2,1)S(1)}, bf16[192,768]{1,0:T(8,128)(2,1)S(1)}, f32[192,768]{1,0:T(8,128)S(1)}) custom-call(s32[2]{0:T(128)S(1)} %pad_add_fusion.2.which_ref, bf16[8,3072,384]{2,1,0:T(8,128)(2,1)} %bitcast.96, bf16[8,3072,384]{2,1,0:T(8,128)(2,1)} %bitcast.97, ...), custom_call_target="tpu_custom_call" | custom-call | flops 3623878656 | bytes 11796480 | tf_op jit(solution)/shard_map/pallas_call | solution.py:196
  131.6 1.5 collective-permute-start.12
  134.1 3.1 %collective-permute-start.15 = (bf16[192,768]{1,0:T(8,128)(2,1)S(1)}, bf16[192,768]{1,0:T(8,128)(2,1)S(1)}, u32[]{:S(2)}, u32[]{:S(2)}) collective-permute-start(bf16[192,768]{1,0:T(8,128)(2,1)S(1)} %add_convert_fusion.2), channel_id=1, source_target_pairs={{0,96},{32,0},{64,32},{96,64},{1,97},{33,1},{65,33},{97,65},{2,98}... | collective-permute-start | bytes 884744 | tf_op jit(solution)/shard_map/ppermute | solution.py:17
  137.2 4.3 %shard_map.39 = f32[384,768]{1,0:T(8,128)S(1)} custom-call(s32[1]{0:T(128)} %bitcast.which_ref, bf16[8,3072,384]{2,1,0:T(8,128)(2,1)} %bitcast.98, bf16[384,3072]{1,0:T(8,128)(2,1)} %get-tuple-element.30.refs_1_.refs_2_), custom_call_target="tpu_custom_call" | custom-call | flops 1811939328 | bytes 8257536 | tf_op jit(solution)/shard_map/pallas_call | solution.py:196
  141.6 2.7 %collective-permute-done.13 = bf16[192,768]{1,0:T(8,128)(2,1)S(1)} collective-permute-done((bf16[192,768]{1,0:T(8,128)(2,1)S(1)}, bf16[192,768]{1,0:T(8,128)(2,1)S(1)}, u32[]{:S(2)}, u32[]{:S(2)}) %collective-permute-start.13) | collective-permute-done | bytes 294944 | tf_op jit(solution)/shard_map/ppermute | solution.py:17
  144.3 4.7 %collective-permute-done.11 = bf16[192,768]{1,0:T(8,128)(2,1)S(1)} collective-permute-done((bf16[192,768]{1,0:T(8,128)(2,1)S(1)}, bf16[192,768]{1,0:T(8,128)(2,1)S(1)}, u32[]{:S(2)}, u32[]{:S(2)}) %collective-permute-start.11) | collective-permute-done | bytes 294944 | tf_op jit(solution)/shard_map/ppermute | solution.py:17
  149.3 3.2 %collective-permute-start.17 = (bf16[384,768]{1,0:T(8,128)(2,1)S(1)}, bf16[384,768]{1,0:T(8,128)(2,1)S(1)}, u32[]{:S(2)}, u32[]{:S(2)}) collective-permute-start(bf16[384,768]{1,0:T(8,128)(2,1)S(1)} %fusion.1.refs_3_), channel_id=1, source_target_pairs={{0,96},{32,0},{64,32},{96,64},{1,97},{33,1},{65,33},{97,65},{2,98}... | collective-permute-start | bytes 1769480 | tf_op jit(solution)/shard_map/ppermute | solution.py:17
  156.7 6.2 %all-to-all-start = ((f32[64,1,128]{2,1,0:T(1,128)}), f32[64,1,128]{2,1,0:T(1,128)S(1)}, u32[]{:S(2)}, u32[]{:S(2)}) async-start(f32[64,1,128]{2,1,0:T(1,128)} %bitcast.27), calls=%async_computation | async-start | bytes 65536 | tf_op jit(solution)/shard_map/all_to_all | solution.py:281
  164.6 3.0 %collective-permute-start.20 = (bf16[192,768]{1,0:T(8,128)(2,1)S(1)}, bf16[192,768]{1,0:T(8,128)(2,1)S(1)}, u32[]{:S(2)}, u32[]{:S(2)}) collective-permute-start(bf16[192,768]{1,0:T(8,128)(2,1)S(1)} %slice.103), channel_id=1, source_target_pairs={{0,96},{32,0},{64,32},{96,64},{1,97},{33,1},{65,33},{97,65},{2,98}... | collective-permute-start | bytes 884744 | tf_op jit(solution)/shard_map/ppermute | solution.py:17
  167.6 11.0 %shard_map.41.part_ref = f32[384,3072]{1,0:T(8,128)} custom-call(s32[3]{0:T(128)S(1)} %pad_add_fusion.3.which_ref, bf16[8,3072,384]{2,1,0:T(8,128)(2,1)} %bitcast.99, bf16[8,3072,384]{2,1,0:T(8,128)(2,1)} %bitcast.100, bf16[8,3072,384]{2,1,0:T(8,128)(2,1)} %bitcast.101, bf16[384,768]{1,0:T(8,128)(2,1)S(1)} %fusion.1.refs_3_, ...), custom_call_target="tpu_custom_call" | custom-call | flops 5435817984 | bytes 20643840 | tf_op jit(solution)/shard_map/pallas_call | solution.py:116
  180.0 11.0 %shard_map.42 = (bf16[384,3072]{1,0:T(8,128)(2,1)}, bf16[384,768]{1,0:T(8,128)(2,1)S(1)}) custom-call(s32[1]{0:T(128)} %bitcast.2.which_ref, f32[1,1]{1,0:T(1,128)} %bitcast.29.scale_ref, bf16[8,3072,384]{2,1,0:T(8,128)(2,1)} %bitcast.102, bf16[384,768]{1,0:T(8,128)(2,1)S(1)} %pad_maximum_fusion.3.f_ref, f32[384,3072]{1,0:T(8,128)} %shard_map.41.part_ref, ...), custom_call_target="tpu_custom_call" | custom-call | flops 3623878656 | bytes 15335424 | tf_op jit(solution)/shard_map/pallas_call | solution.py:145
  191.2 3.2 %collective-permute-start.25 = (bf16[192,768]{1,0:T(8,128)(2,1)S(1)}, bf16[192,768]{1,0:T(8,128)(2,1)S(1)}, u32[]{:S(2)}, u32[]{:S(2)}) collective-permute-start(bf16[192,768]{1,0:T(8,128)(2,1)S(1)} %get-tuple-element.64), channel_id=1, source_target_pairs={{0,96},{32,0},{64,32},{96,64},{1,97},{33,1},{65,33},{97,65},{2,98}... | collective-permute-start | bytes 884744 | tf_op jit(solution)/shard_map/ppermute | solution.py:17
  194.4 7.6 %shard_map.44 = (f32[192,768]{1,0:T(8,128)S(1)}, bf16[192,768]{1,0:T(8,128)(2,1)S(1)}, bf16[192,768]{1,0:T(8,128)(2,1)S(1)}, f32[192,768]{1,0:T(8,128)S(1)}) custom-call(s32[2]{0:T(128)S(1)} %pad_add_fusion.2.which_ref, bf16[8,3072,384]{2,1,0:T(8,128)(2,1)} %bitcast.103, bf16[8,3072,384]{2,1,0:T(8,128)(2,1)} %bitcast.104, ...), custom_call_target="tpu_custom_call" | custom-call | flops 3623878656 | bytes 11796480 | tf_op jit(solution)/shard_map/pallas_call | solution.py:196
  202.0 2.0 collective-permute-start.24
  204.2 3.5 %collective-permute-start.26 = (bf16[192,768]{1,0:T(8,128)(2,1)S(1)}, bf16[192,768]{1,0:T(8,128)(2,1)S(1)}, u32[]{:S(2)}, u32[]{:S(2)}) collective-permute-start(bf16[192,768]{1,0:T(8,128)(2,1)S(1)} %add_convert_fusion), channel_id=1, source_target_pairs={{0,96},{32,0},{64,32},{96,64},{1,97},{33,1},{65,33},{97,65},{2,98}... | collective-permute-start | bytes 884744 | tf_op jit(solution)/shard_map/ppermute | solution.py:17
  207.7 4.3 %shard_map.43 = f32[384,768]{1,0:T(8,128)S(1)} custom-call(s32[1]{0:T(128)} %bitcast.which_ref, bf16[8,3072,384]{2,1,0:T(8,128)(2,1)} %bitcast.105, bf16[384,3072]{1,0:T(8,128)(2,1)} %get-tuple-element.39.refs_1_.refs_2_), custom_call_target="tpu_custom_call" | custom-call | flops 1811939328 | bytes 8257536 | tf_op jit(solution)/shard_map/pallas_call | solution.py:196
  212.9 3.2 %collective-permute-done.22 = bf16[192,768]{1,0:T(8,128)(2,1)S(1)} collective-permute-done((bf16[192,768]{1,0:T(8,128)(2,1)S(1)}, bf16[192,768]{1,0:T(8,128)(2,1)S(1)}, u32[]{:S(2)}, u32[]{:S(2)}) %collective-permute-start.22) | collective-permute-done | bytes 294944 | tf_op jit(solution)/shard_map/ppermute | solution.py:17
  218.3 2.7 %collective-permute-start.27 = (bf16[192,384]{1,0:T(8,128)(2,1)S(1)}, bf16[192,384]{1,0:T(8,128)(2,1)S(1)}, u32[]{:S(2)}, u32[]{:S(2)}) collective-permute-start(bf16[192,384]{1,0:T(8,128)(2,1)S(1)} %get-tuple-element.62), channel_id=1, source_target_pairs={{0,24},{8,0},{16,8},{24,16},{1,25},{9,1},{17,9},{25,17},{2,26},{10... | collective-permute-start | bytes 442376 | tf_op jit(solution)/shard_map/ppermute | solution.py:17
  222.3 6.1 %all-to-all-start.1 = ((f32[64,1,128]{2,1,0:T(1,128)}), f32[64,1,128]{2,1,0:T(1,128)S(1)}, u32[]{:S(2)}, u32[]{:S(2)}) async-start(f32[64,1,128]{2,1,0:T(1,128)} %bitcast.42), calls=%async_computation.1 | async-start | bytes 65536 | tf_op jit(solution)/shard_map/all_to_all | solution.py:281
  228.4 1.6 collective-permute-start.29
  230.1 2.7 %collective-permute-start.28 = (bf16[192,384]{1,0:T(8,128)(2,1)S(1)}, bf16[192,384]{1,0:T(8,128)(2,1)S(1)}, u32[]{:S(2)}, u32[]{:S(2)}) collective-permute-start(bf16[192,384]{1,0:T(8,128)(2,1)S(1)} %get-tuple-element.61), channel_id=1, source_target_pairs={{0,16},{8,24},{16,0},{24,8},{1,17},{9,25},{17,1},{25,9},{2,18},{10... | collective-permute-start | bytes 442376 | tf_op jit(solution)/shard_map/ppermute | solution.py:17
  232.7 5.2 %all-to-all-done.1 = f32[64,1,128]{2,1,0:T(1,128)S(1)} async-done(((f32[64,1,128]{2,1,0:T(1,128)}), f32[64,1,128]{2,1,0:T(1,128)S(1)}, u32[]{:S(2)}, u32[]{:S(2)}) %all-to-all-start.1) | async-done | bytes 32800 | tf_op jit(solution)/shard_map/all_to_all | solution.py:281
  (99 shorter events, 30.6 us)
Async XLA Ops:
  6.5 94.9 %all-gather.2.cloned.1.call-start = ((), (), s32[]{:S(2)}) async-start(), calls=%async_computation.2 | async-start | bytes 19464192 | tf_op jit(solution)/shard_map/all_gather | solution.py:294
  9.1 11.5 %collective-permute-start.2 = (bf16[192,384]{1,0:T(8,128)(2,1)}, bf16[192,384]{1,0:T(8,128)(2,1)S(1)}, u32[]{:S(2)}, u32[]{:S(2)}) collective-permute-start(bf16[192,384]{1,0:T(8,128)(2,1)} %get-tuple-element.67), channel_id=1, source_target_pairs={{0,8},{8,16},{16,24},{24,0},{1,9},{9,17},{17,25},{25,1},{2,10},{10... | collective-permute-start | bytes 442376 | tf_op jit(solution)/shard_map/ppermute | solution.py:17
  10.7 9.9 %collective-permute-start = (bf16[192,384]{1,0:T(8,128)(2,1)S(1)}, bf16[192,384]{1,0:T(8,128)(2,1)S(1)}, u32[]{:S(2)}, u32[]{:S(2)}) collective-permute-start(bf16[192,384]{1,0:T(8,128)(2,1)S(1)} %get-tuple-element.68), channel_id=1, source_target_pairs={{0,24},{8,0},{16,8},{24,16},{1,25},{9,1},{17,9},{25,17},{2,26},{10... | collective-permute-start | bytes 442376 | tf_op jit(solution)/shard_map/ppermute | solution.py:17
  12.3 8.4 %collective-permute-start.1 = (bf16[192,384]{1,0:T(8,128)(2,1)S(1)}, bf16[192,384]{1,0:T(8,128)(2,1)}, u32[]{:S(2)}, u32[]{:S(2)}) collective-permute-start(bf16[192,384]{1,0:T(8,128)(2,1)S(1)} %get-tuple-element.69), channel_id=1, source_target_pairs={{0,16},{8,24},{16,0},{24,8},{1,17},{9,25},{17,1},{25,9},{2,18},{10... | collective-permute-start | bytes 442376 | tf_op jit(solution)/shard_map/ppermute | solution.py:17
  17.6 3.0 %copy-start = (bf16[1152,384]{1,0:T(8,128)(2,1)S(1)}, bf16[1152,384]{1,0:T(8,128)(2,1)}, u32[]{:S(2)}) copy-start(bf16[1152,384]{1,0:T(8,128)(2,1)} %get-tuple-element.28) | copy-start | bytes 2654212
  22.2 2.5 copy-start.1
  23.7 30.8 %collective-permute-start.7 = (bf16[1152,384]{0,1:T(8,128)(2,1)}, bf16[1152,384]{0,1:T(8,128)(2,1)S(1)}, u32[]{:S(2)}, u32[]{:S(2)}) collective-permute-start(bf16[1152,384]{0,1:T(8,128)(2,1)} %copy.20), channel_id=1, source_target_pairs={{0,8},{8,16},{16,24},{24,0},{1,9},{9,17},{17,25},{25,1},{2,10},{10... | collective-permute-start | bytes 2654216 | tf_op jit(solution)/shard_map/ppermute | solution.py:17
  24.7 30.7 %collective-permute-start.6 = (bf16[1152,384]{0,1:T(8,128)(2,1)S(1)}, bf16[1152,384]{0,1:T(8,128)(2,1)S(1)}, u32[]{:S(2)}, u32[]{:S(2)}) collective-permute-start(bf16[1152,384]{0,1:T(8,128)(2,1)S(1)} %copy-done.1), channel_id=1, source_target_pairs={{0,24},{8,0},{16,8},{24,16},{1,25},{9,1},{17,9},{25,17},{2,26},{10... | collective-permute-start | bytes 2654216 | tf_op jit(solution)/shard_map/ppermute | solution.py:17
  55.4 17.2 %collective-permute-start.8 = (bf16[384,384]{0,1:T(8,128)(2,1)}, bf16[384,384]{0,1:T(8,128)(2,1)}, u32[]{:S(2)}, u32[]{:S(2)}) collective-permute-start(bf16[384,384]{0,1:T(8,128)(2,1)} %slice.97), channel_id=1, source_target_pairs={{0,8},{8,16},{16,24},{24,0},{1,9},{9,17},{17,25},{25,1},{2,10},{10... | collective-permute-start | bytes 884744 | tf_op jit(solution)/shard_map/ppermute | solution.py:17
  56.1 16.6 %collective-permute-start.9 = (bf16[384,384]{0,1:T(8,128)(2,1)}, bf16[384,384]{0,1:T(8,128)(2,1)}, u32[]{:S(2)}, u32[]{:S(2)}) collective-permute-start(bf16[384,384]{0,1:T(8,128)(2,1)} %slice.98), channel_id=1, source_target_pairs={{0,24},{8,0},{16,8},{24,16},{1,25},{9,1},{17,9},{25,17},{2,26},{10... | collective-permute-start | bytes 884744 | tf_op jit(solution)/shard_map/ppermute | solution.py:17
  60.9 22.7 %collective-permute-start.5 = (bf16[384,768]{1,0:T(8,128)(2,1)S(1)}, bf16[384,768]{1,0:T(8,128)(2,1)S(1)}, u32[]{:S(2)}, u32[]{:S(2)}) collective-permute-start(bf16[384,768]{1,0:T(8,128)(2,1)S(1)} %bitcast.91), channel_id=1, source_target_pairs={{0,32},{32,64},{64,96},{96,0},{1,33},{33,65},{65,97},{97,1},{2,34}... | collective-permute-start | bytes 1769480 | tf_op jit(solution)/shard_map/ppermute | solution.py:17
  62.4 27.2 %collective-permute-start.4 = (bf16[384,768]{1,0:T(8,128)(2,1)S(1)}, bf16[384,768]{1,0:T(8,128)(2,1)S(1)}, u32[]{:S(2)}, u32[]{:S(2)}) collective-permute-start(bf16[384,768]{1,0:T(8,128)(2,1)S(1)} %bitcast.92), channel_id=1, source_target_pairs={{0,64},{32,96},{64,0},{96,32},{1,65},{33,97},{65,1},{97,33},{2,66}... | collective-permute-start | bytes 1769480 | tf_op jit(solution)/shard_map/ppermute | solution.py:17
  65.1 25.3 %collective-permute-start.3 = (bf16[384,768]{1,0:T(8,128)(2,1)S(1)}, bf16[384,768]{1,0:T(8,128)(2,1)S(1)}, u32[]{:S(2)}, u32[]{:S(2)}) collective-permute-start(bf16[384,768]{1,0:T(8,128)(2,1)S(1)} %bitcast.93), channel_id=1, source_target_pairs={{0,96},{32,0},{64,32},{96,64},{1,97},{33,1},{65,33},{97,65},{2,98}... | collective-permute-start | bytes 1769480 | tf_op jit(solution)/shard_map/ppermute | solution.py:17
  83.6 6.1 %copy-start.2 = (bf16[384,768]{1,0:T(8,128)(2,1)}, bf16[384,768]{1,0:T(8,128)(2,1)S(1)}, u32[]{:S(2)}) copy-start(bf16[384,768]{1,0:T(8,128)(2,1)S(1)} %collective-permute-done.5.refs_3_) | copy-start | bytes 1769476
  89.6 0.8 copy-start.3
  120.7 13.0 %collective-permute-start.10 = (bf16[192,768]{1,0:T(8,128)(2,1)S(1)}, bf16[192,768]{1,0:T(8,128)(2,1)S(1)}, u32[]{:S(2)}, u32[]{:S(2)}) collective-permute-start(bf16[192,768]{1,0:T(8,128)(2,1)S(1)} %get-tuple-element.65), channel_id=1, source_target_pairs={{0,32},{32,64},{64,96},{96,0},{1,33},{33,65},{65,97},{97,1},{2,34}... | collective-permute-start | bytes 884744 | tf_op jit(solution)/shard_map/ppermute | solution.py:17
  122.2 11.8 %collective-permute-start.14 = (bf16[192,768]{1,0:T(8,128)(2,1)S(1)}, bf16[192,768]{1,0:T(8,128)(2,1)S(1)}, u32[]{:S(2)}, u32[]{:S(2)}) collective-permute-start(bf16[192,768]{1,0:T(8,128)(2,1)S(1)} %get-tuple-element.66), channel_id=1, source_target_pairs={{0,96},{32,0},{64,32},{96,64},{1,97},{33,1},{65,33},{97,65},{2,98}... | collective-permute-start | bytes 884744 | tf_op jit(solution)/shard_map/ppermute | solution.py:17
  131.6 10.0 %collective-permute-start.12 = (bf16[192,768]{1,0:T(8,128)(2,1)S(1)}, bf16[192,768]{1,0:T(8,128)(2,1)S(1)}, u32[]{:S(2)}, u32[]{:S(2)}) collective-permute-start(bf16[192,768]{1,0:T(8,128)(2,1)S(1)} %get-tuple-element.33), channel_id=1, source_target_pairs={{0,96},{32,0},{64,32},{96,64},{1,97},{33,1},{65,33},{97,65},{2,98}... | collective-permute-start | bytes 884744 | tf_op jit(solution)/shard_map/ppermute | solution.py:17
  133.1 11.2 %collective-permute-start.13 = (bf16[192,768]{1,0:T(8,128)(2,1)S(1)}, bf16[192,768]{1,0:T(8,128)(2,1)S(1)}, u32[]{:S(2)}, u32[]{:S(2)}) collective-permute-start(bf16[192,768]{1,0:T(8,128)(2,1)S(1)} %get-tuple-element.34), channel_id=1, source_target_pairs={{0,32},{32,64},{64,96},{96,0},{1,33},{33,65},{65,97},{97,1},{2,34}... | collective-permute-start | bytes 884744 | tf_op jit(solution)/shard_map/ppermute | solution.py:17
  133.8 15.2 %collective-permute-start.11 = (bf16[192,768]{1,0:T(8,128)(2,1)S(1)}, bf16[192,768]{1,0:T(8,128)(2,1)S(1)}, u32[]{:S(2)}, u32[]{:S(2)}) collective-permute-start(bf16[192,768]{1,0:T(8,128)(2,1)S(1)} %add_convert_fusion.3), channel_id=1, source_target_pairs={{0,32},{32,64},{64,96},{96,0},{1,33},{33,65},{65,97},{97,1},{2,34}... | collective-permute-start | bytes 884744 | tf_op jit(solution)/shard_map/ppermute | solution.py:17
  134.1 14.8 %collective-permute-start.15 = (bf16[192,768]{1,0:T(8,128)(2,1)S(1)}, bf16[192,768]{1,0:T(8,128)(2,1)S(1)}, u32[]{:S(2)}, u32[]{:S(2)}) collective-permute-start(bf16[192,768]{1,0:T(8,128)(2,1)S(1)} %add_convert_fusion.2), channel_id=1, source_target_pairs={{0,96},{32,0},{64,32},{96,64},{1,97},{33,1},{65,33},{97,65},{2,98}... | collective-permute-start | bytes 884744 | tf_op jit(solution)/shard_map/ppermute | solution.py:17
  149.2 15.0 %collective-permute-start.18 = (bf16[384,768]{1,0:T(8,128)(2,1)S(1)}, bf16[384,768]{1,0:T(8,128)(2,1)S(1)}, u32[]{:S(2)}, u32[]{:S(2)}) collective-permute-start(bf16[384,768]{1,0:T(8,128)(2,1)S(1)} %fusion.1.refs_3_), channel_id=1, source_target_pairs={{0,32},{32,64},{64,96},{96,0},{1,33},{33,65},{65,97},{97,1},{2,34}... | collective-permute-start | bytes 1769480 | tf_op jit(solution)/shard_map/ppermute | solution.py:17
  149.3 15.3 %collective-permute-start.17 = (bf16[384,768]{1,0:T(8,128)(2,1)S(1)}, bf16[384,768]{1,0:T(8,128)(2,1)S(1)}, u32[]{:S(2)}, u32[]{:S(2)}) collective-permute-start(bf16[384,768]{1,0:T(8,128)(2,1)S(1)} %fusion.1.refs_3_), channel_id=1, source_target_pairs={{0,96},{32,0},{64,32},{96,64},{1,97},{33,1},{65,33},{97,65},{2,98}... | collective-permute-start | bytes 1769480 | tf_op jit(solution)/shard_map/ppermute | solution.py:17
  154.2 1.3 collective-permute-start.16
  156.7 21.9 %all-to-all-start = ((f32[64,1,128]{2,1,0:T(1,128)}), f32[64,1,128]{2,1,0:T(1,128)S(1)}, u32[]{:S(2)}, u32[]{:S(2)}) async-start(f32[64,1,128]{2,1,0:T(1,128)} %bitcast.27), calls=%async_computation | async-start | bytes 65536 | tf_op jit(solution)/shard_map/all_to_all | solution.py:281
  164.2 15.7 %collective-permute-start.19 = (bf16[192,768]{1,0:T(8,128)(2,1)S(1)}, bf16[192,768]{1,0:T(8,128)(2,1)S(1)}, u32[]{:S(2)}, u32[]{:S(2)}) collective-permute-start(bf16[192,768]{1,0:T(8,128)(2,1)S(1)} %slice.102), channel_id=1, source_target_pairs={{0,32},{32,64},{64,96},{96,0},{1,33},{33,65},{65,97},{97,1},{2,34}... | collective-permute-start | bytes 884744 | tf_op jit(solution)/shard_map/ppermute | solution.py:17
  164.6 15.3 %collective-permute-start.20 = (bf16[192,768]{1,0:T(8,128)(2,1)S(1)}, bf16[192,768]{1,0:T(8,128)(2,1)S(1)}, u32[]{:S(2)}, u32[]{:S(2)}) collective-permute-start(bf16[192,768]{1,0:T(8,128)(2,1)S(1)} %slice.103), channel_id=1, source_target_pairs={{0,96},{32,0},{64,32},{96,64},{1,97},{33,1},{65,33},{97,65},{2,98}... | collective-permute-start | bytes 884744 | tf_op jit(solution)/shard_map/ppermute | solution.py:17
  191.1 13.0 %collective-permute-start.21 = (bf16[192,768]{1,0:T(8,128)(2,1)S(1)}, bf16[192,768]{1,0:T(8,128)(2,1)S(1)}, u32[]{:S(2)}, u32[]{:S(2)}) collective-permute-start(bf16[192,768]{1,0:T(8,128)(2,1)S(1)} %get-tuple-element.63), channel_id=1, source_target_pairs={{0,32},{32,64},{64,96},{96,0},{1,33},{33,65},{65,97},{97,1},{2,34}... | collective-permute-start | bytes 884744 | tf_op jit(solution)/shard_map/ppermute | solution.py:17
  191.2 13.0 %collective-permute-start.25 = (bf16[192,768]{1,0:T(8,128)(2,1)S(1)}, bf16[192,768]{1,0:T(8,128)(2,1)S(1)}, u32[]{:S(2)}, u32[]{:S(2)}) collective-permute-start(bf16[192,768]{1,0:T(8,128)(2,1)S(1)} %get-tuple-element.64), channel_id=1, source_target_pairs={{0,96},{32,0},{64,32},{96,64},{1,97},{33,1},{65,33},{97,65},{2,98}... | collective-permute-start | bytes 884744 | tf_op jit(solution)/shard_map/ppermute | solution.py:17
  201.9 10.1 %collective-permute-start.23 = (bf16[192,768]{1,0:T(8,128)(2,1)S(1)}, bf16[192,768]{1,0:T(8,128)(2,1)S(1)}, u32[]{:S(2)}, u32[]{:S(2)}) collective-permute-start(bf16[192,768]{1,0:T(8,128)(2,1)S(1)} %get-tuple-element.42), channel_id=1, source_target_pairs={{0,96},{32,0},{64,32},{96,64},{1,97},{33,1},{65,33},{97,65},{2,98}... | collective-permute-start | bytes 884744 | tf_op jit(solution)/shard_map/ppermute | solution.py:17
  202.0 10.9 %collective-permute-start.24 = (bf16[192,768]{1,0:T(8,128)(2,1)S(1)}, bf16[192,768]{1,0:T(8,128)(2,1)S(1)}, u32[]{:S(2)}, u32[]{:S(2)}) collective-permute-start(bf16[192,768]{1,0:T(8,128)(2,1)S(1)} %get-tuple-element.43), channel_id=1, source_target_pairs={{0,32},{32,64},{64,96},{96,0},{1,33},{33,65},{65,97},{97,1},{2,34}... | collective-permute-start | bytes 884744 | tf_op jit(solution)/shard_map/ppermute | solution.py:17
  204.1 12.0 %collective-permute-start.22 = (bf16[192,768]{1,0:T(8,128)(2,1)S(1)}, bf16[192,768]{1,0:T(8,128)(2,1)S(1)}, u32[]{:S(2)}, u32[]{:S(2)}) collective-permute-start(bf16[192,768]{1,0:T(8,128)(2,1)S(1)} %add_convert_fusion.1), channel_id=1, source_target_pairs={{0,32},{32,64},{64,96},{96,0},{1,33},{33,65},{65,97},{97,1},{2,34}... | collective-permute-start | bytes 884744 | tf_op jit(solution)/shard_map/ppermute | solution.py:17
  204.2 11.8 %collective-permute-start.26 = (bf16[192,768]{1,0:T(8,128)(2,1)S(1)}, bf16[192,768]{1,0:T(8,128)(2,1)S(1)}, u32[]{:S(2)}, u32[]{:S(2)}) collective-permute-start(bf16[192,768]{1,0:T(8,128)(2,1)S(1)} %add_convert_fusion), channel_id=1, source_target_pairs={{0,96},{32,0},{64,32},{96,64},{1,97},{33,1},{65,33},{97,65},{2,98}... | collective-permute-start | bytes 884744 | tf_op jit(solution)/shard_map/ppermute | solution.py:17
  218.2 2.9 %collective-permute-start.30 = (f32[64,128]{1,0:T(8,128)S(1)}, f32[64,128]{1,0:T(8,128)S(1)}, u32[]{:S(2)}, u32[]{:S(2)}) collective-permute-start(f32[64,128]{1,0:T(8,128)S(1)} %broadcast_in_dim.7), channel_id=1, source_target_pairs={{0,1},{1,0},{2,3},{3,2},{4,5},{5,4},{6,7},{7,6},{8,9},{9,8},{10,11... | collective-permute-start | bytes 98312 | tf_op jit(solution)/shard_map/ppermute | solution.py:280
  218.3 20.8 %collective-permute-start.27 = (bf16[192,384]{1,0:T(8,128)(2,1)S(1)}, bf16[192,384]{1,0:T(8,128)(2,1)S(1)}, u32[]{:S(2)}, u32[]{:S(2)}) collective-permute-start(bf16[192,384]{1,0:T(8,128)(2,1)S(1)} %get-tuple-element.62), channel_id=1, source_target_pairs={{0,24},{8,0},{16,8},{24,16},{1,25},{9,1},{17,9},{25,17},{2,26},{10... | collective-permute-start | bytes 442376 | tf_op jit(solution)/shard_map/ppermute | solution.py:17
  222.3 15.6 %all-to-all-start.1 = ((f32[64,1,128]{2,1,0:T(1,128)}), f32[64,1,128]{2,1,0:T(1,128)S(1)}, u32[]{:S(2)}, u32[]{:S(2)}) async-start(f32[64,1,128]{2,1,0:T(1,128)} %bitcast.42), calls=%async_computation.1 | async-start | bytes 65536 | tf_op jit(solution)/shard_map/all_to_all | solution.py:281
  228.4 11.1 %collective-permute-start.29 = (bf16[192,384]{1,0:T(8,128)(2,1)S(1)}, bf16[192,384]{1,0:T(8,128)(2,1)S(1)}, u32[]{:S(2)}, u32[]{:S(2)}) collective-permute-start(bf16[192,384]{1,0:T(8,128)(2,1)S(1)} %get-tuple-element.59), channel_id=1, source_target_pairs={{0,8},{8,16},{16,24},{24,0},{1,9},{9,17},{17,25},{25,1},{2,10},{10... | collective-permute-start | bytes 442376 | tf_op jit(solution)/shard_map/ppermute | solution.py:17
  230.1 9.4 %collective-permute-start.28 = (bf16[192,384]{1,0:T(8,128)(2,1)S(1)}, bf16[192,384]{1,0:T(8,128)(2,1)S(1)}, u32[]{:S(2)}, u32[]{:S(2)}) collective-permute-start(bf16[192,384]{1,0:T(8,128)(2,1)S(1)} %get-tuple-element.61), channel_id=1, source_target_pairs={{0,16},{8,24},{16,0},{24,8},{1,17},{9,25},{17,1},{25,9},{2,18},{10... | collective-permute-start | bytes 442376 | tf_op jit(solution)/shard_map/ppermute | solution.py:17
Sparse Core Ops, SparseCore 0:
  9.6 91.7 all-gather.1
